TPU v7x, 32 devices: a whole 2x2x4 slice. The times are simulated.
32 devices in a mesh: groups: 2 (over x), expert: 4 (over y, core), tensor: 4 (over z).
Axes of the slice: x: 2, y: 2, z: 4, core: 2. Of those that a mesh axis runs over, the one named last changes fastest.
Arguments:
- tokens: bfloat16 [2, 128, 7168], P(None, ('groups', 'expert')), parts along dimension 1, may hold values from -6 to 6
- expert_ids: int32 [2, 128, 2], P(None, ('groups', 'expert')), parts along dimension 1, may hold values from 0 to 3, all different within a row; in each aligned block of 16 rows (0 to 15, 16 to 31, ..., all dimensions but the last counted through in order) at most 12 rows name the same one
- gate_values: float32 [2, 128, 2], P(None, ('groups', 'expert')), parts along dimension 1, may hold values from 0.05 to 0.3
- tenant_ids: int32 [128], P(('groups', 'expert')), parts along dimension 0, may hold values from 0 to 15
- w_gate: bfloat16 [4, 7168, 1024], P('expert', None, 'tensor'), may hold values from -0.0625 to 0.0625
- w_up: bfloat16 [4, 7168, 1024], P('expert', None, 'tensor'), may hold values from -0.0625 to 0.0625
- routed_down_weight: bfloat16 [4, 1024, 7168], P('expert', 'tensor'), may hold values from -0.1875 to 0.1875
- shared_gate: bfloat16 [7168, 1024], P(None, 'tensor'), may hold values from -0.0625 to 0.0625
- shared_up: bfloat16 [7168, 1024], P(None, 'tensor'), may hold values from -0.0625 to 0.0625
- shared_down: bfloat16 [1024, 7168], P('tensor'), may hold values from -0.1875 to 0.1875
- store_a: bfloat16 [8, 16, 7168], P('expert'), may hold values from -0.0625 to 0.0625
- store_b: bfloat16 [8, 16, 1024], P('expert', None, 'tensor'), may hold values from -1.5 to 1.5
- pair_slot: int32 [4, 16], replicated, may hold values from -1 to 7, as said below
- shared_a: bfloat16 [16, 16, 7168], P('expert'), may hold values from -0.0625 to 0.0625
- shared_b: bfloat16 [16, 16, 1024], P('expert', None, 'tensor'), may hold values from -1.5 to 1.5
Outputs:
- mixed: bfloat16 [2, 128, 7168], P(None, ('groups', 'expert'), 'tensor'), parts along dimension 1
There are 2 independent parts, one for each index of `groups`. A program takes and returns all parts, laid end to end along the dimension named above; an argument that names none is the same for every part. Nothing has to cross between parts.
Inputs may be any that keep to these rules, and one draw needn't show every extreme that they name: `expert_ids`: each row names 2 different experts. In each step, among the 16 rows of one index of expert, no expert is named by more than 12 rows, a bound that some block reaches. pair_slot[e, t] is the store slot that holds tenant t's adapter of routed expert e, or -1 where that pair has none. Store slot j lies on index j // 2 of expert. Every slot holds exactly one pair; each routed expert has exactly 2 adapted tenants, no two of them on the same index of expert.
All inputs are finite; a program needn't handle non-finite values.
Results may differ from a plain program's by a relative error of at most 0.017.
Values may be sent and summed in bfloat16 or wider, within the bound.
No kernel may reach another device: no remote copies, remote signals or barrier semaphores. Data moves between devices by JAX's collectives and lax.ppermute only.
A program may use at most 128 MiB of HBM per device.

v0:
```python
import jax
import jax.numpy as jnp
from jax import lax
from jax.sharding import PartitionSpec as P


def contract(token_row_block, factor):
    return lax.dot_general(
        token_row_block, factor, (((1,), (1,)), ((), ())), preferred_element_type=jnp.float32
    )


def feed_forward(token_row_block, inner, tenant_hot, gate_weight, up_weight, down_weight, factor_b):
    gate = jnp.dot(token_row_block, gate_weight, preferred_element_type=jnp.float32)
    lifted = jnp.where(tenant_hot, inner, 0.0).astype(jnp.bfloat16)
    upward = jnp.dot(token_row_block, up_weight, preferred_element_type=jnp.float32) + jnp.dot(
        lifted, factor_b, preferred_element_type=jnp.float32
    )
    hidden = (jax.nn.silu(gate) * upward).astype(jnp.bfloat16)
    return jnp.dot(hidden, down_weight, preferred_element_type=jnp.float32)


def local(
    tokens,
    expert_ids,
    gate_values,
    tenant_ids,
    w_gate,
    w_up,
    routed_down_weight,
    shared_gate,
    shared_up,
    shared_down,
    store_a,
    store_b,
    pair_slot,
    shared_a,
    shared_b,
):
    experts = pair_slot.shape[0]
    tenants = pair_slot.shape[1]
    adapted = store_a.shape[0]
    adapter_rank = store_a.shape[1]
    model_width = store_a.shape[2]
    block_width = store_b.shape[2]
    step_count, tok_dev, top_count = expert_ids.shape
    n_expert = lax.axis_size("expert")
    n_tensor = lax.axis_size("tensor")
    own_expert = lax.axis_index("expert")
    part_width = model_width // n_tensor
    capacity = tok_dev * top_count * 3 // (2 * n_expert)
    valid = pair_slot >= 0
    holder = jnp.where(valid, pair_slot // adapted, -1)
    within = jnp.where(valid, pair_slot % adapted, -1)
    held = (holder == own_expert)[:, :, None] & (
        within[:, :, None] == jnp.arange(adapted, dtype=jnp.int32)[None, None, :]
    )
    picker = jnp.any(held, axis=1).astype(jnp.bfloat16)
    send_b = jnp.einsum("ej,jrh->erh", picker, store_b, preferred_element_type=jnp.bfloat16)
    send_a = jnp.einsum("ej,jrd->erd", picker, store_a, preferred_element_type=jnp.bfloat16)
    arrived_a, received_factor_b = (
        lax.all_to_all(send_a, "expert", split_axis=0, concat_axis=0, tiled=True),
        lax.all_to_all(send_b, "expert", split_axis=0, concat_axis=0, tiled=True),
    )
    gathered_a, gathered_b = (
        lax.all_gather(shared_a, "expert", axis=0, tiled=True),
        lax.all_gather(shared_b, "expert", axis=0, tiled=True),
    )
    own_row = lax.dynamic_index_in_dim(pair_slot, own_expert, 0, keepdims=False)
    source = jnp.where(own_row >= 0, own_row // adapted, -1)
    chooser = (source[:, None] == jnp.arange(n_expert, dtype=jnp.int32)[None, :]).astype(
        jnp.bfloat16
    )
    routed_a = jnp.einsum(
        "ts,srd->trd", chooser, arrived_a, preferred_element_type=jnp.bfloat16
    ).reshape(tenants * adapter_rank, -1)
    routed_b = jnp.einsum(
        "ts,srh->trh", chooser, received_factor_b, preferred_element_type=jnp.bfloat16
    ).reshape(tenants * adapter_rank, block_width)
    shared_flat_a = gathered_a.reshape(tenants * adapter_rank, -1)
    shared_flat_b = gathered_b.reshape(tenants * adapter_rank, block_width)
    tenant_columns = jnp.arange(tenants * adapter_rank, dtype=jnp.int32) // adapter_rank
    local_hot = tenant_ids[:, None] == tenant_columns[None, :]
    tenant_value_entry = tenant_ids.astype(jnp.float32)
    slot_count = n_expert * capacity
    results = []
    for step_index in range(step_count):
        token_row_block = tokens[step_index]
        picks = expert_ids[step_index]
        weights = gate_values[step_index]
        hits = picks[:, :, None] == jnp.arange(experts, dtype=jnp.int32)[None, None, :]
        chosen = jnp.any(hits, axis=1).astype(jnp.int32)
        share = jnp.sum(jnp.where(hits, weights[:, :, None], 0.0), axis=1)
        before = jnp.cumsum(chosen, axis=0) - chosen
        positioned_rows = (chosen[:, :, None] == 1) & (
            before[:, :, None] == jnp.arange(capacity, dtype=jnp.int32)[None, None, :]
        )
        position_pass = positioned_rows.astype(jnp.bfloat16)
        slot_owner_tenant = jnp.einsum(
            "mzu,m->zu", positioned_rows.astype(jnp.float32), tenant_value_entry
        ).astype(jnp.bfloat16)
        outgoing = jnp.einsum(
            "zvw,zq->vwq", position_pass, token_row_block, preferred_element_type=jnp.bfloat16
        )
        incoming, incoming_tenant = (
            lax.all_to_all(outgoing, "expert", split_axis=0, concat_axis=0, tiled=True),
            lax.all_to_all(slot_owner_tenant, "expert", split_axis=0, concat_axis=0, tiled=True),
        )
        slot_rows = incoming.reshape(slot_count, model_width)
        slot_hot = (
            incoming_tenant.reshape(slot_count).astype(jnp.int32)[:, None]
            == tenant_columns[None, :]
        )
        inner_slots = contract(slot_rows, routed_a)
        inner_local = contract(token_row_block, shared_flat_a)
        routed_terms = feed_forward(
            slot_rows, inner_slots, slot_hot, w_gate[0], w_up[0], routed_down_weight[0], routed_b
        )
        shared_terms = feed_forward(
            token_row_block,
            inner_local,
            local_hot,
            shared_gate,
            shared_up,
            shared_down,
            shared_flat_b,
        )
        summed = lax.psum_scatter(
            jnp.concatenate([routed_terms, shared_terms], axis=0).astype(jnp.bfloat16),
            "tensor",
            scatter_dimension=1,
            tiled=True,
        ).astype(jnp.float32)
        expert_result = (
            summed[:slot_count].astype(jnp.bfloat16).reshape(n_expert, capacity, part_width)
        )
        returned_rows = lax.all_to_all(
            expert_result, "expert", split_axis=0, concat_axis=0, tiled=True
        )
        combine = jnp.where(positioned_rows, share[:, :, None], 0.0)
        routed_out = jnp.einsum(
            "bqr,qrg->bg",
            combine,
            returned_rows.astype(jnp.float32),
            precision=lax.Precision.HIGHEST,
        )
        results.append((summed[slot_count:] + routed_out).astype(jnp.bfloat16))
    return jnp.stack(results, axis=0)


def solution(mesh):
    return jax.shard_map(
        local,
        mesh=mesh,
        in_specs=(
            P(None, ("groups", "expert"), None),
            P(None, ("groups", "expert"), None),
            P(None, ("groups", "expert"), None),
            P(("groups", "expert")),
            P("expert", None, "tensor"),
            P("expert", None, "tensor"),
            P("expert", "tensor", None),
            P(None, "tensor"),
            P(None, "tensor"),
            P("tensor", None),
            P("expert", None, None),
            P("expert", None, "tensor"),
            P(),
            P("expert", None, None),
            P("expert", None, "tensor"),
        ),
        out_specs=P(None, ("groups", "expert"), "tensor"),
        check_vma=False,
    )
```

profile of v0, /device:TPU:0, one launch (start us, length us, event | category | flops | bytes accessed | tf_op | source)
XLA Modules:
  0.0 187.5 jit_solution(438040607665719393)
XLA Ops:
  9.6 4.2 %all-to-all-start.1 = ((bf16[4,1,12]{2,1,0:T(2,128)(2,1)}), bf16[4,1,12]{2,1,0:T(2,128)(2,1)S(1)}, u32[]{:S(2)}, u32[]{:S(2)}) async-start(bf16[4,1,12]{2,1,0:T(2,128)(2,1)} %copy.62), calls=%async_computation.1 | async-start | bytes 4096 | tf_op jit(solution)/shard_map/all_to_all | solution.py:107
  19.8 2.4 %fusion.39 = bf16[4,12,7168]{2,1,0:T(8,128)(2,1)} fusion(bf16[2,16,7168]{2,1,0:T(8,128)(2,1)} %param.15, s32[16,4]{0,1:T(4,128)S(1)} %copy.60, pred[16,4]{0,1:T(4,128)(4,1)S(1)} %copy.59), kind=kOutput, calls=%fused_computation.55 | convolution fusion | flops 11011584 | bytes 917824 | tf_op jit(solution)/shard_map/zvw,zq->vwq/dot_general | solution.py:102
  22.2 2.4 %fusion.32 = bf16[4,12,7168]{2,1,0:T(8,128)(2,1)} fusion(bf16[2,16,7168]{2,1,0:T(8,128)(2,1)} %param.15, s32[16,4]{0,1:T(4,128)S(1)} %copy.73, pred[16,4]{0,1:T(4,128)(4,1)S(1)} %copy.72), kind=kOutput, calls=%fused_computation.48 | convolution fusion | flops 11011584 | bytes 917824 | tf_op jit(solution)/shard_map/zvw,zq->vwq/dot_general | solution.py:102
  30.0 3.3 %all-to-all-start.6 = ((bf16[4,1,12]{2,1,0:T(2,128)(2,1)}), bf16[4,1,12]{2,1,0:T(2,128)(2,1)S(1)}, u32[]{:S(2)}, u32[]{:S(2)}) async-start(bf16[4,1,12]{2,1,0:T(2,128)(2,1)} %copy.75), calls=%async_computation.7 | async-start | bytes 4096 | tf_op jit(solution)/shard_map/all_to_all | solution.py:107
  34.0 3.1 %all-to-all-done.6 = bf16[4,1,12]{2,1,0:T(2,128)(2,1)S(1)} async-done(((bf16[4,1,12]{2,1,0:T(2,128)(2,1)}), bf16[4,1,12]{2,1,0:T(2,128)(2,1)S(1)}, u32[]{:S(2)}, u32[]{:S(2)}) %all-to-all-start.6) | async-done | bytes 128 | tf_op jit(solution)/shard_map/all_to_all | solution.py:107
  37.1 3.3 %all-to-all-start.3 = ((bf16[4,16,256]{2,1,0:T(8,128)(2,1)}), bf16[4,16,256]{2,1,0:T(8,128)(2,1)S(1)}, u32[]{:S(2)}, u32[]{:S(2)}) async-start(bf16[4,16,256]{2,1,0:T(8,128)(2,1)} %copy.68), calls=%async_computation.3 | async-start | bytes 65536 | tf_op jit(solution)/shard_map/all_to_all | solution.py:63
  40.4 6.5 %all_gather.7 = bf16[16,16,256]{2,1,0:T(8,128)(2,1)S(1)} all-gather(bf16[4,16,256]{2,1,0:T(8,128)(2,1)S(1)} %copy-done.11), channel_id=1, replica_groups=mesh['groups'=2,'expert'=4,'tensor'=4] {'expert'}, dimensions={0}, use_global_device_ids=true | all-gather | bytes 163840 | tf_op jit(solution)/shard_map/all_gather | solution.py:67
  48.1 3.5 %all-to-all-start = ((bf16[4,12,7168]{2,1,0:T(8,128)(2,1)}), bf16[4,12,7168]{2,1,0:T(8,128)(2,1)S(1)}, u32[]{:S(2)}, u32[]{:S(2)}) async-start(bf16[4,12,7168]{2,1,0:T(8,128)(2,1)} %fusion.39), calls=%async_computation | async-start | bytes 1835008 | tf_op jit(solution)/shard_map/all_to_all | solution.py:106
  51.6 3.2 %fusion.36 = f32[16,256]{1,0:T(8,128)} fusion(bf16[7168,256]{1,0:T(8,128)(2,1)} %param.22, bf16[2,16,7168]{2,1,0:T(8,128)(2,1)S(1)} %copy-done.5), kind=kOutput, calls=%fused_computation.52 | convolution fusion | flops 58720256 | bytes 3915776 | tf_op jit(solution)/shard_map/dot_general | solution.py:14
  56.0 8.6 %all-to-all-done = bf16[4,12,7168]{2,1,0:T(8,128)(2,1)S(1)} async-done(((bf16[4,12,7168]{2,1,0:T(8,128)(2,1)}), bf16[4,12,7168]{2,1,0:T(8,128)(2,1)S(1)}, u32[]{:S(2)}, u32[]{:S(2)}) %all-to-all-start) | async-done | bytes 688160 | tf_op jit(solution)/shard_map/all_to_all | solution.py:106
  64.6 4.2 %all-to-all-start.5 = ((bf16[4,12,7168]{2,1,0:T(8,128)(2,1)}), bf16[4,12,7168]{2,1,0:T(8,128)(2,1)}, u32[]{:S(2)}, u32[]{:S(2)}) async-start(bf16[4,12,7168]{2,1,0:T(8,128)(2,1)} %fusion.32), calls=%async_computation.6 | async-start | bytes 1835008 | tf_op jit(solution)/shard_map/all_to_all | solution.py:106
  69.3 3.4 %fusion.4 = f32[48,256]{1,0:T(8,128)} fusion(bf16[48,7168]{1,0:T(8,128)(2,1)S(1)} %reshape.133, bf16[1,7168,256]{2,1,0:T(8,128)(2,1)} %param.20), kind=kOutput, calls=%fused_computation.8 | convolution fusion | flops 176160768 | bytes 4407296 | tf_op jit(solution)/shard_map/dot_general | solution.py:16
  72.7 9.2 %all-to-all-done.5 = bf16[4,12,7168]{2,1,0:T(8,128)(2,1)} async-done(((bf16[4,12,7168]{2,1,0:T(8,128)(2,1)}), bf16[4,12,7168]{2,1,0:T(8,128)(2,1)}, u32[]{:S(2)}, u32[]{:S(2)}) %all-to-all-start.5) | async-done | bytes 688160 | tf_op jit(solution)/shard_map/all_to_all | solution.py:106
  82.0 3.5 %all-to-all-start.2 = ((bf16[4,16,7168]{2,1,0:T(8,128)(2,1)}), bf16[4,16,7168]{2,1,0:T(8,128)(2,1)S(1)}, u32[]{:S(2)}, u32[]{:S(2)}) async-start(bf16[4,16,7168]{2,1,0:T(8,128)(2,1)} %copy.64), calls=%async_computation.2 | async-start | bytes 1835008 | tf_op jit(solution)/shard_map/all_to_all | solution.py:62
  85.7 3.4 %fusion.8 = f32[48,256]{1,0:T(8,128)} fusion(bf16[48,7168]{1,0:T(8,128)(2,1)S(1)} %reshape.133, bf16[1,7168,256]{2,1,0:T(8,128)(2,1)} %param.19), kind=kOutput, calls=%fused_computation.12 | convolution fusion | flops 176160768 | bytes 4407296 | tf_op jit(solution)/shard_map/dot_general | solution.py:14
  90.5 2.9 %fusion.2 = f32[48,256]{1,0:T(8,128)S(1)} fusion(bf16[48,7168]{1,0:T(8,128)(2,1)S(1)} %reshape.139, bf16[1,7168,256]{2,1,0:T(8,128)(2,1)} %param.20), kind=kOutput, calls=%fused_computation.6 | convolution fusion | flops 176160768 | bytes 4407296 | tf_op jit(solution)/shard_map/dot_general | solution.py:16
  95.0 3.5 %all-to-all-done.2 = bf16[4,16,7168]{2,1,0:T(8,128)(2,1)S(1)} async-done(((bf16[4,16,7168]{2,1,0:T(8,128)(2,1)}), bf16[4,16,7168]{2,1,0:T(8,128)(2,1)S(1)}, u32[]{:S(2)}, u32[]{:S(2)}) %all-to-all-start.2) | async-done | bytes 917536 | tf_op jit(solution)/shard_map/all_to_all | solution.py:62
  98.5 2.5 %fusion.28 = bf16[16,16,7168]{2,0,1:T(8,128)(2,1)S(1)} fusion(bf16[4,16,7168]{2,1,0:T(8,128)(2,1)S(1)} %all-to-all-done.2, s32[16]{0:T(128)} %copy-done.22), kind=kOutput, calls=%fused_computation.44 | convolution fusion | flops 14680128 | bytes 4587584 | tf_op jit(solution)/shard_map/ts,srd->trd/dot_general | solution.py:74
  101.0 2.0 %copy.66 = bf16[16,16,7168]{2,1,0:T(8,128)(2,1)S(1)} copy(bf16[16,16,7168]{2,0,1:T(8,128)(2,1)S(1)} %fusion.28) | data formatting | bytes 7340032 | tf_op jit(solution)/shard_map/ts,srd->trd/dot_general | solution.py:74
  103.0 1.8 copy-done.1
  106.1 2.9 %convolution_convert_fusion.1 = bf16[48,7168]{1,0:T(8,128)(2,1)S(1)} fusion(bf16[1,256,7168]{2,1,0:T(8,128)(2,1)} %param.21, f32[48,256]{1,0:T(8,128)S(1)} %copy-done.7, bf16[48,256]{1,0:T(8,128)(2,1)S(1)} %fusion.20, bf16[256,256]{1,0:T(8,128)(2,1)S(1)} %bitcast.129, f32[48,256]{1,0:T(8,128)S(1)} %copy-done.8), kind=kOutput, calls=%fused_computation.1 | convolution fusion | flops 182882304 | bytes 4612096 | tf_op jit(solution)/shard_map/dot_general | solution.py:20
  109.1 3.1 %fusion.24 = bf16[16,256]{1,0:T(8,128)(2,1)S(1)} fusion(bf16[256,7168]{1,0:T(8,128)(2,1)} %bitcast.125, bf16[2,16,7168]{2,1,0:T(8,128)(2,1)S(1)} %copy-done.5, s32[256]{0:T(256)S(1)} %copy-done.12, s32[16]{0:T(128)S(1)} %copy-done.21), kind=kOutput, calls=%fused_computation.38 | convolution fusion | flops 58732544 | bytes 3909120 | tf_op jit(solution)/shard_map/dot_general | solution.py:8
  112.2 2.7 %convolution_convert_fusion.3 = bf16[16,7168]{1,0:T(8,128)(2,1)S(1)} fusion(bf16[256,7168]{1,0:T(8,128)(2,1)} %param.24, f32[16,256]{1,0:T(8,128)S(1)} %fusion.41, bf16[16,256]{1,0:T(8,128)(2,1)S(1)} %fusion.24, bf16[256,256]{1,0:T(8,128)(2,1)S(1)} %bitcast.127, f32[16,256]{1,0:T(8,128)S(1)} %copy-done.9), kind=kOutput, calls=%fused_computation.3 | convolution fusion | flops 60960768 | bytes 4071424 | tf_op jit(solution)/shard_map/dot_general | solution.py:20
  116.1 3.3 %fusion.21 = bf16[48,256]{1,0:T(8,128)(2,1)S(1)} fusion(bf16[48,7168]{1,0:T(8,128)(2,1)S(1)} %reshape.139, bf16[256,7168]{1,0:T(8,128)(2,1)} %bitcast.124, s32[256]{0:T(256)S(1)} %copy-done.12, s32[48]{0:T(128)S(1)} %copy-done.27), kind=kOutput, calls=%fused_computation.31 | convolution fusion | flops 176197632 | bytes 4383936 | tf_op jit(solution)/shard_map/dot_general | solution.py:8
  119.4 2.9 %convolution_convert_fusion = bf16[48,7168]{1,0:T(8,128)(2,1)S(1)} fusion(bf16[1,256,7168]{2,1,0:T(8,128)(2,1)} %param.21, f32[48,256]{1,0:T(8,128)S(1)} %fusion.2, bf16[48,256]{1,0:T(8,128)(2,1)S(1)} %fusion.21, bf16[256,256]{1,0:T(8,128)(2,1)S(1)} %bitcast.130, f32[48,256]{1,0:T(8,128)S(1)} %copy-done.6), kind=kOutput, calls=%fused_computation | convolution fusion | flops 182882304 | bytes 4612096 | tf_op jit(solution)/shard_map/dot_general | solution.py:20
  122.3 3.1 %fusion.26 = bf16[16,256]{1,0:T(8,128)(2,1)S(1)} fusion(bf16[256,7168]{1,0:T(8,128)(2,1)} %bitcast.126, bf16[2,16,7168]{2,1,0:T(8,128)(2,1)S(1)} %copy-done.5, s32[256]{0:T(256)S(1)} %copy-done.12, s32[16]{0:T(128)S(1)} %copy-done.21), kind=kOutput, calls=%fused_computation.40 | convolution fusion | flops 58732544 | bytes 3909120 | tf_op jit(solution)/shard_map/dot_general | solution.py:8
  125.5 2.7 %convolution_convert_fusion.2 = bf16[16,7168]{1,0:T(8,128)(2,1)S(1)} fusion(bf16[256,7168]{1,0:T(8,128)(2,1)} %param.24, f32[16,256]{1,0:T(8,128)S(1)} %fusion.34, bf16[16,256]{1,0:T(8,128)(2,1)S(1)} %fusion.26, bf16[256,256]{1,0:T(8,128)(2,1)S(1)} %bitcast.128, f32[16,256]{1,0:T(8,128)S(1)} %copy-done.10), kind=kOutput, calls=%fused_computation.2 | convolution fusion | flops 60960768 | bytes 4071424 | tf_op jit(solution)/shard_map/dot_general | solution.py:20
  129.3 12.5 %reduce-scatter.3.cloned.1.call-done = bf16[64,1792]{1,0:T(8,128)(2,1)} async-done(((bf16[64,7168]{1,0:T(8,128)(2,1)}), bf16[64,1792]{1,0:T(8,128)(2,1)}) %reduce-scatter.3.cloned.1.call-update) | async-done | bytes 229392 | tf_op jit(solution)/shard_map/reduce_scatter | solution.py:128
  143.5 3.4 %all-to-all-start.4 = ((bf16[4,12,1792]{2,1,0:T(8,128)(2,1)}), bf16[4,12,1792]{2,1,0:T(8,128)(2,1)S(1)}, u32[]{:S(2)}, u32[]{:S(2)}) async-start(bf16[4,12,1792]{2,1,0:T(8,128)(2,1)} %reshape.138), calls=%async_computation.5 | async-start | bytes 458752 | tf_op jit(solution)/shard_map/all_to_all | solution.py:137
  146.9 21.3 %reduce-scatter.5.cloned.1.call-done = bf16[64,1792]{1,0:T(8,128)(2,1)} async-done(((bf16[64,7168]{1,0:T(8,128)(2,1)}), bf16[64,1792]{1,0:T(8,128)(2,1)}) %reduce-scatter.5.cloned.1.call-update) | async-done | bytes 229392 | tf_op jit(solution)/shard_map/reduce_scatter | solution.py:128
  169.9 3.4 %all-to-all-start.7 = ((bf16[4,12,1792]{2,1,0:T(8,128)(2,1)}), bf16[4,12,1792]{2,1,0:T(8,128)(2,1)S(1)}, u32[]{:S(2)}, u32[]{:S(2)}) async-start(bf16[4,12,1792]{2,1,0:T(8,128)(2,1)} %reshape.140), calls=%async_computation.9 | async-start | bytes 458752 | tf_op jit(solution)/shard_map/all_to_all | solution.py:137
  174.7 4.3 %all-to-all-done.7 = bf16[4,12,1792]{2,1,0:T(8,128)(2,1)S(1)} async-done(((bf16[4,12,1792]{2,1,0:T(8,128)(2,1)}), bf16[4,12,1792]{2,1,0:T(8,128)(2,1)S(1)}, u32[]{:S(2)}, u32[]{:S(2)}) %all-to-all-start.7) | async-done | bytes 172064 | tf_op jit(solution)/shard_map/all_to_all | solution.py:137
  (122 shorter events, 31.1 us)
Async XLA Ops:
  6.5 18.1 %copy-start = (bf16[2,16,7168]{2,1,0:T(8,128)(2,1)S(1)}, bf16[2,16,7168]{2,1,0:T(8,128)(2,1)}, u32[]{:S(2)}) copy-start(bf16[2,16,7168]{2,1,0:T(8,128)(2,1)} %param.25) | copy-start | bytes 1376260
  6.5 19.0 %copy-start.5 = (bf16[2,16,7168]{2,1,0:T(8,128)(2,1)S(1)}, bf16[2,16,7168]{2,1,0:T(8,128)(2,1)}, u32[]{:S(2)}) copy-start(bf16[2,16,7168]{2,1,0:T(8,128)(2,1)} %param.15) | copy-start | bytes 1376260
  8.1 14.1 %copy-start.17 = (s32[16,4]{0,1:T(4,128)}, s32[16,4]{0,1:T(4,128)S(1)}, u32[]{:S(2)}) copy-start(s32[16,4]{0,1:T(4,128)S(1)} %copy.60) | copy-start | bytes 772
  8.2 18.0 %copy-start.23 = (pred[16,4]{0,1:T(4,128)(4,1)}, pred[16,4]{0,1:T(4,128)(4,1)S(1)}, u32[]{:S(2)}) copy-start(pred[16,4]{0,1:T(4,128)(4,1)S(1)} %copy.59) | copy-start | bytes 196
  9.6 20.4 %all-to-all-start.1 = ((bf16[4,1,12]{2,1,0:T(2,128)(2,1)}), bf16[4,1,12]{2,1,0:T(2,128)(2,1)S(1)}, u32[]{:S(2)}, u32[]{:S(2)}) async-start(bf16[4,1,12]{2,1,0:T(2,128)(2,1)} %copy.62), calls=%async_computation.1 | async-start | bytes 4096 | tf_op jit(solution)/shard_map/all_to_all | solution.py:107
  13.9 95.2 %all-gather.2.cloned.1.call-start = ((), (), s32[]{:S(2)}) async-start(), calls=%async_computation.10 | async-start | bytes 4587520 | tf_op jit(solution)/shard_map/all_gather | solution.py:66
  16.8 5.4 %copy-start.19 = (s32[16,4]{0,1:T(4,128)}, s32[16,4]{0,1:T(4,128)S(1)}, u32[]{:S(2)}) copy-start(s32[16,4]{0,1:T(4,128)S(1)} %copy.73) | copy-start | bytes 772
  16.9 9.3 %copy-start.25 = (pred[16,4]{0,1:T(4,128)(4,1)}, pred[16,4]{0,1:T(4,128)(4,1)S(1)}, u32[]{:S(2)}) copy-start(pred[16,4]{0,1:T(4,128)(4,1)S(1)} %copy.72) | copy-start | bytes 196
  16.9 8.7 %copy-start.2 = (bf16[7168,256]{1,0:T(8,128)(2,1)S(1)}, bf16[7168,256]{1,0:T(8,128)(2,1)}, u32[]{:S(2)}) copy-start(bf16[7168,256]{1,0:T(8,128)(2,1)} %param.23) | copy-start | bytes 11010052
  18.7 50.1 %copy-start.22 = (s32[16]{0:T(128)}, s32[16]{0:T(128)S(1)}, u32[]{:S(2)}) copy-start(s32[16]{0:T(128)S(1)} %compare_select_fusion) | copy-start | bytes 196
  26.2 14.2 %copy-start.11 = (bf16[4,16,256]{2,1,0:T(8,128)(2,1)S(1)}, bf16[4,16,256]{2,1,0:T(8,128)(2,1)}, u32[]{:S(2)}) copy-start(bf16[4,16,256]{2,1,0:T(8,128)(2,1)} %param.29) | copy-start | bytes 98308
  30.0 7.1 %all-to-all-start.6 = ((bf16[4,1,12]{2,1,0:T(2,128)(2,1)}), bf16[4,1,12]{2,1,0:T(2,128)(2,1)S(1)}, u32[]{:S(2)}, u32[]{:S(2)}) async-start(bf16[4,1,12]{2,1,0:T(2,128)(2,1)} %copy.75), calls=%async_computation.7 | async-start | bytes 4096 | tf_op jit(solution)/shard_map/all_to_all | solution.py:107
  37.1 11.0 %all-to-all-start.3 = ((bf16[4,16,256]{2,1,0:T(8,128)(2,1)}), bf16[4,16,256]{2,1,0:T(8,128)(2,1)S(1)}, u32[]{:S(2)}, u32[]{:S(2)}) async-start(bf16[4,16,256]{2,1,0:T(8,128)(2,1)} %copy.68), calls=%async_computation.3 | async-start | bytes 65536 | tf_op jit(solution)/shard_map/all_to_all | solution.py:63
  48.1 16.5 %all-to-all-start = ((bf16[4,12,7168]{2,1,0:T(8,128)(2,1)}), bf16[4,12,7168]{2,1,0:T(8,128)(2,1)S(1)}, u32[]{:S(2)}, u32[]{:S(2)}) async-start(bf16[4,12,7168]{2,1,0:T(8,128)(2,1)} %fusion.39), calls=%async_computation | async-start | bytes 1835008 | tf_op jit(solution)/shard_map/all_to_all | solution.py:106
  64.6 17.4 %all-to-all-start.5 = ((bf16[4,12,7168]{2,1,0:T(8,128)(2,1)}), bf16[4,12,7168]{2,1,0:T(8,128)(2,1)}, u32[]{:S(2)}, u32[]{:S(2)}) async-start(bf16[4,12,7168]{2,1,0:T(8,128)(2,1)} %fusion.32), calls=%async_computation.6 | async-start | bytes 1835008 | tf_op jit(solution)/shard_map/all_to_all | solution.py:106
  82.0 16.5 %all-to-all-start.2 = ((bf16[4,16,7168]{2,1,0:T(8,128)(2,1)}), bf16[4,16,7168]{2,1,0:T(8,128)(2,1)S(1)}, u32[]{:S(2)}, u32[]{:S(2)}) async-start(bf16[4,16,7168]{2,1,0:T(8,128)(2,1)} %copy.64), calls=%async_computation.2 | async-start | bytes 1835008 | tf_op jit(solution)/shard_map/all_to_all | solution.py:62
  85.5 56.4 %reduce-scatter.3.cloned.1.call-start = ((), (), s32[]{:S(2)}) async-start(), calls=%async_computation.11 | async-start | bytes 1146880 | tf_op jit(solution)/shard_map/reduce_scatter | solution.py:128
  104.9 4.2 %copy-start.21 = (s32[16]{0:T(128)S(1)}, s32[16]{0:T(128)}, u32[]{:S(2)}) copy-start(s32[16]{0:T(128)} %param.18) | copy-start | bytes 196
  106.1 6.1 %copy-start.9 = (f32[16,256]{1,0:T(8,128)S(1)}, f32[16,256]{1,0:T(8,128)}, u32[]{:S(2)}) copy-start(f32[16,256]{1,0:T(8,128)} %fusion.43) | copy-start | bytes 49156
  112.2 3.9 %copy-start.27 = (s32[48]{0:T(128)S(1)}, s32[48]{0:T(128)}, u32[]{:S(2)}) copy-start(s32[48]{0:T(128)} %reshape.142) | copy-start | bytes 580
  114.9 4.4 %copy-start.6 = (f32[48,256]{1,0:T(8,128)S(1)}, f32[48,256]{1,0:T(8,128)}, u32[]{:S(2)}) copy-start(f32[48,256]{1,0:T(8,128)} %fusion.6) | copy-start | bytes 147460
  116.0 52.2 %reduce-scatter.5.cloned.1.call-start = ((), (), s32[]{:S(2)}) async-start(), calls=%async_computation.12 | async-start | bytes 1146880 | tf_op jit(solution)/shard_map/reduce_scatter | solution.py:128
  119.4 6.1 %copy-start.10 = (f32[16,256]{1,0:T(8,128)S(1)}, f32[16,256]{1,0:T(8,128)}, u32[]{:S(2)}) copy-start(f32[16,256]{1,0:T(8,128)} %fusion.36) | copy-start | bytes 49156
  125.5 21.5 %copy-start.29 = (f32[2,16,2]{1,2,0:T(2,128)S(1)}, f32[2,16,2]{1,2,0:T(2,128)}, u32[]{:S(2)}) copy-start(f32[2,16,2]{1,2,0:T(2,128)} %param.17) | copy-start | bytes 772
  125.5 47.8 %copy-start.14 = (s32[16,2]{0,1:T(2,128)S(1)}, s32[16,2]{0,1:T(2,128)}, u32[]{:S(2)}) copy-start(s32[16,2]{0,1:T(2,128)} %copy-done.13) | copy-start | bytes 388
  125.5 47.8 %copy-start.16 = (s32[16,2]{0,1:T(2,128)S(1)}, s32[16,2]{0,1:T(2,128)}, u32[]{:S(2)}) copy-start(s32[16,2]{0,1:T(2,128)} %copy-done.15) | copy-start | bytes 388
  125.5 47.9 %copy-start.18 = (s32[16,4]{0,1:T(4,128)S(1)}, s32[16,4]{0,1:T(4,128)}, u32[]{:S(2)}) copy-start(s32[16,4]{0,1:T(4,128)} %copy-done.17) | copy-start | bytes 772
  125.5 47.9 %copy-start.24 = (pred[16,4]{0,1:T(4,128)(4,1)S(1)}, pred[16,4]{0,1:T(4,128)(4,1)}, u32[]{:S(2)}) copy-start(pred[16,4]{0,1:T(4,128)(4,1)} %copy-done.23) | copy-start | bytes 196
  128.3 50.7 %copy-start.20 = (s32[16,4]{0,1:T(4,128)S(1)}, s32[16,4]{0,1:T(4,128)}, u32[]{:S(2)}) copy-start(s32[16,4]{0,1:T(4,128)} %copy-done.19) | copy-start | bytes 772
  128.3 50.7 %copy-start.26 = (pred[16,4]{0,1:T(4,128)(4,1)S(1)}, pred[16,4]{0,1:T(4,128)(4,1)}, u32[]{:S(2)}) copy-start(pred[16,4]{0,1:T(4,128)(4,1)} %copy-done.25) | copy-start | bytes 196
  143.5 26.4 %all-to-all-start.4 = ((bf16[4,12,1792]{2,1,0:T(8,128)(2,1)}), bf16[4,12,1792]{2,1,0:T(8,128)(2,1)S(1)}, u32[]{:S(2)}, u32[]{:S(2)}) async-start(bf16[4,12,1792]{2,1,0:T(8,128)(2,1)} %reshape.138), calls=%async_computation.5 | async-start | bytes 458752 | tf_op jit(solution)/shard_map/all_to_all | solution.py:137
  169.9 9.0 %all-to-all-start.7 = ((bf16[4,12,1792]{2,1,0:T(8,128)(2,1)}), bf16[4,12,1792]{2,1,0:T(8,128)(2,1)S(1)}, u32[]{:S(2)}, u32[]{:S(2)}) async-start(bf16[4,12,1792]{2,1,0:T(8,128)(2,1)} %reshape.140), calls=%async_computation.9 | async-start | bytes 458752 | tf_op jit(solution)/shard_map/all_to_all | solution.py:137
  (9 other events, 22.6 us)
Sparse Core Ops, SparseCore 0:
  16.3 34.7 all-gather.1
  116.2 25.6 reduce-scatter.2
  144.2 24.0 reduce-scatter.4
where the time goes:
time: 189 us; the launch traced here: 187 us
  waiting for transfers between devices  63.4 us (34%)
  matrix products  52.6 us (28%)
  starting transfers between devices  29.1 us (15%)
  local copies, waits for them, and re-layouts  16.5 us (9%)
  between operations  13.5 us (7%)
  blocking collectives  6.46 us (3%)
  other arithmetic  5.88 us (3%)
    reduce_scatter x2, waiting for transfers between devices, local(): lax.psum_scatter(jnp.concatenate([routed_terms, shared_terms], axis=0).as...  33.8 us
    all_to_all x2, waiting for transfers between devices, local(): lax.all_to_all(outgoing, 'expert', split_axis=0, concat_axis=0, tiled=True)  17.8 us
    dot_general x4, matrix products, feed_forward(): return jnp.dot(hidden, down_weight, preferred_element_type=jnp.float32)  11.4 us
    dot_general x4, matrix products, contract(): lax.dot_general(token_row_block, factor, (((1,), (1,)), ((), ())), prefer...  10.7 us
    dot_general x4, matrix products, feed_forward(): jnp.dot(token_row_block, gate_weight, preferred_element_type=jnp.float32)  9.19 us
    all_to_all x2, starting transfers between devices, local(): lax.all_to_all(outgoing, 'expert', split_axis=0, concat_axis=0, tiled=True)  7.75 us
    all_to_all x2, starting transfers between devices, local(): lax.all_to_all(slot_owner_tenant, 'expert', split_axis=0, concat_axis=0,...  7.57 us
    dot_general x4, matrix products, feed_forward(): jnp.dot(token_row_block, up_weight, preferred_element_type=jnp.float32)  7.5 us
  transfers between devices with their start and end apart: 11, of which 7 were waited for; matrix products, arithmetic and copies ran while one was open for 32% of the time, Pallas kernels for 0%

commit v1 on v0

v1 whole, which is shorter than its diff:
```python
import functools

import jax
import jax.numpy as jnp
from jax import lax
from jax.experimental import pallas as pl
from jax.experimental.pallas import tpu as pltpu
from jax.sharding import PartitionSpec as P

F32 = jnp.float32
BF16 = jnp.bfloat16
VMEM_LIMIT = 24 * 1024 * 1024


def params():
    return pltpu.CompilerParams(
        dimension_semantics=("arbitrary",), vmem_limit_bytes=VMEM_LIMIT
    )


def cost(flops, moved):
    return pl.CostEstimate(flops=int(flops), bytes_accessed=int(moved), transcendentals=0)


def swap(value, bit):
    count = lax.axis_size("expert")
    return lax.ppermute(value, "expert", [(i, i ^ bit) for i in range(count)])


def exchange_all(value):
    count = lax.axis_size("expert")
    pieces = {0: value}
    bit = count // 2
    while bit >= 1:
        pieces.update({r ^ bit: swap(piece, bit) for r, piece in list(pieces.items())})
        bit //= 2
    return [pieces[r] for r in range(count)]


def rows_of(refs):
    return jnp.concatenate([ref[...] for ref in refs], axis=0)


def gate_up_kernel(count, *refs):
    rows, gate_weight, up_weight, gate, up = refs[:count], *refs[count:]

    @pl.when(pl.program_id(0) == 0)
    def _():
        gate[...] = jnp.zeros_like(gate)
        up[...] = jnp.zeros_like(up)

    block = rows_of(rows)
    gate[...] += jnp.dot(block, gate_weight[...], preferred_element_type=F32)
    up[...] += jnp.dot(block, up_weight[...], preferred_element_type=F32)


def gate_up(rows, gate_weight, up_weight):
    depth, width = gate_weight.shape
    size = rows[0].shape[0]
    total = size * len(rows)
    chunk = 1024
    out = jax.ShapeDtypeStruct((total, width), F32)
    return pl.pallas_call(
        functools.partial(gate_up_kernel, len(rows)),
        grid=(depth // chunk,),
        in_specs=[pl.BlockSpec((size, chunk), lambda k: (0, k))] * len(rows)
        + [pl.BlockSpec((chunk, width), lambda k: (k, 0))] * 2,
        out_specs=[pl.BlockSpec((total, width), lambda k: (0, 0))] * 2,
        out_shape=[out, out],
        compiler_params=params(),
        cost_estimate=cost(4 * total * depth * width, 4 * depth * width),
    )(*rows, gate_weight, up_weight)


def inner_kernel(count, *refs):
    rows, factor_shared, factor_store, inner, total = refs[:count], *refs[count:]

    @pl.when(pl.program_id(0) == 0)
    def _():
        total[...] = jnp.zeros_like(total)

    block = rows_of(rows)
    factors = jnp.concatenate([factor_shared[...], factor_store[...]], axis=0)
    total[...] += lax.dot_general(
        block, factors, (((1,), (1,)), ((), ())), preferred_element_type=F32
    )

    @pl.when(pl.program_id(0) == pl.num_programs(0) - 1)
    def _():
        inner[...] = total[...].astype(BF16)


def inner_products(rows, factor_shared, factor_store):
    depth = factor_shared.shape[1]
    size = rows[0].shape[0]
    total = size * len(rows)
    shared_count, store_count = factor_shared.shape[0], factor_store.shape[0]
    width = shared_count + store_count
    chunk = 1792
    return pl.pallas_call(
        functools.partial(inner_kernel, len(rows)),
        grid=(depth // chunk,),
        in_specs=[pl.BlockSpec((size, chunk), lambda k: (0, k))] * len(rows)
        + [
            pl.BlockSpec((shared_count, chunk), lambda k: (0, k)),
            pl.BlockSpec((store_count, chunk), lambda k: (0, k)),
        ],
        out_specs=pl.BlockSpec((total, width), lambda k: (0, 0)),
        out_shape=jax.ShapeDtypeStruct((total, width), BF16),
        scratch_shapes=[pltpu.VMEM((total, width), F32)],
        compiler_params=params(),
        cost_estimate=cost(2 * total * depth * width, 2 * depth * width),
    )(*rows, factor_shared, factor_store)


def silu(value):
    return value / (1.0 + jnp.exp(-value))


def down_kernel(count, size, shared_count, *refs):
    gate, up, gate_own, up_own = refs[:4]
    inner = refs[4 : 4 + count]
    factors = refs[4 + count : 4 + 2 * count]
    row_tenant, slot_tenant, shared_tenant, share, down, down_own = refs[
        4 + 2 * count : 10 + 2 * count
    ]
    outs = refs[10 + 2 * count : 10 + 3 * count]
    hidden, hidden_own = refs[10 + 3 * count :]

    @pl.when(pl.program_id(0) == 0)
    def _():
        width = inner[0].shape[1]
        parts, parts_own = [], []
        for r in range(count):
            held = inner[r][...]
            blocks = [held[(k ^ r) * size : ((k ^ r) + 1) * size] for k in range(count)]
            parts.append(jnp.concatenate(blocks, axis=0)[:, shared_count:])
            parts_own.append(blocks[0][:, :shared_count])
        lifted = jnp.concatenate(parts, axis=1)
        lifted_own = jnp.concatenate(parts_own, axis=1)
        tenants = row_tenant[...]
        zero = jnp.zeros((), BF16)
        lifted = jnp.where(tenants == slot_tenant[...], lifted, zero)
        lifted_own = jnp.where(tenants[:size] == shared_tenant[...], lifted_own, zero)
        factor = jnp.concatenate([ref[shared_count:width] for ref in factors], axis=0)
        factor_own = jnp.concatenate([ref[:shared_count] for ref in factors], axis=0)
        upward = up[...] + jnp.dot(lifted, factor, preferred_element_type=F32)
        hidden[...] = (silu(gate[...]) * upward).astype(BF16)
        upward_own = up_own[...] + jnp.dot(lifted_own, factor_own, preferred_element_type=F32)
        hidden_own[...] = (silu(gate_own[...]) * upward_own).astype(BF16)

    routed = jnp.dot(hidden[...], down[...], preferred_element_type=F32) * share[...]
    own = jnp.dot(hidden_own[...], down_own[...], preferred_element_type=F32)
    outs[0][0] = (routed[:size] + own).astype(BF16)
    for r in range(1, count):
        outs[r][0] = routed[r * size : (r + 1) * size].astype(BF16)


def down_products(
    gate, up, gate_own, up_own, inner, factors, row_tenant, slot_tenant, shared_tenant, share,
    down, down_own, size, shared_count, blocks,
):
    count = len(inner)
    total, hid = gate.shape
    depth = down.shape[1]
    part = depth // blocks
    whole = [gate, up, gate_own, up_own, *inner, *factors, row_tenant, slot_tenant, shared_tenant, share]
    return pl.pallas_call(
        functools.partial(down_kernel, count, size, shared_count),
        grid=(blocks,),
        in_specs=[pl.BlockSpec(x.shape, lambda j: (0, 0)) for x in whole]
        + [pl.BlockSpec((hid, part), lambda j: (0, j))] * 2,
        out_specs=[pl.BlockSpec((1, size, part), lambda j: (j, 0, 0))] * count,
        out_shape=[jax.ShapeDtypeStruct((blocks, size, part), BF16)] * count,
        scratch_shapes=[pltpu.VMEM((total, hid), BF16), pltpu.VMEM((size, hid), BF16)],
        compiler_params=params(),
        cost_estimate=cost(2 * (total + size) * depth * hid, 4 * depth * hid),
    )(*whole, down, down_own)


def split3(value):
    first = lax.reduce_precision(value, 8, 7)
    second = lax.reduce_precision(value - first, 8, 7)
    return jnp.stack([first, second, value - first - second]).astype(BF16)


def local(
    tokens,
    expert_ids,
    gate_values,
    tenant_ids,
    w_gate,
    w_up,
    routed_down_weight,
    shared_gate,
    shared_up,
    shared_down,
    store_a,
    store_b,
    pair_slot,
    shared_a,
    shared_b,
):
    experts, tenants = pair_slot.shape
    adapted, rank, model_width = store_a.shape
    own_tenants = shared_a.shape[0]
    hid = store_b.shape[2]
    steps, size, _ = expert_ids.shape
    count = lax.axis_size("expert")
    n_tensor = lax.axis_size("tensor")
    own = lax.axis_index("expert")
    shared_count = own_tenants * rank

    gathered = [exchange_all(tokens[s]) for s in range(steps)]

    hits = expert_ids[..., None] == jnp.arange(experts, dtype=jnp.int32)
    dense = jnp.sum(jnp.where(hits, gate_values[..., None], 0.0), axis=2)
    dense = dense.reshape(steps * size * experts)
    extra = jnp.concatenate([split3(dense).reshape(-1), tenant_ids.astype(BF16)])
    extra_rows = -(-extra.shape[0] // (16 * hid)) * 16
    extra = jnp.pad(extra, (0, extra_rows * hid - extra.shape[0])).reshape(extra_rows, hid)
    pack = jnp.concatenate(
        [shared_b.reshape(shared_count, hid), store_b.reshape(adapted * rank, hid), extra], axis=0
    )
    packs = exchange_all(pack)
    base = shared_count + adapted * rank
    number = steps * size * experts
    shares, row_tenants = [], []
    for r in range(count):
        flat = packs[r][base:].reshape(-1)
        three = flat[: 3 * number].astype(F32).reshape(3, steps, size, experts)
        shares.append(three[0] + three[1] + three[2])
        row_tenants.append(flat[3 * number : 3 * number + size].astype(jnp.int32))
    share = jnp.concatenate(shares, axis=1)
    share = lax.dynamic_slice_in_dim(share, own, 1, axis=2)
    row_tenant = jnp.concatenate(row_tenants).reshape(count * size, 1)

    holders = own ^ jnp.arange(count, dtype=jnp.int32)
    slots = (holders[:, None] * adapted + jnp.arange(adapted, dtype=jnp.int32)).reshape(-1)
    own_row = lax.dynamic_index_in_dim(pair_slot, own, 0, keepdims=False)
    same = own_row[None, :] == slots[:, None]
    slot_tenant = jnp.max(
        jnp.where(same, jnp.arange(tenants, dtype=jnp.int32)[None, :], -1), axis=1
    )
    slot_tenant = jnp.repeat(slot_tenant, rank).reshape(1, -1)
    shared_tenant = (
        holders[:, None] * own_tenants + jnp.arange(own_tenants, dtype=jnp.int32)
    ).reshape(-1)
    shared_tenant = jnp.repeat(shared_tenant, rank).reshape(1, -1)

    gate_own, up_own = gate_up([tokens.reshape(steps * size, model_width)], shared_gate, shared_up)
    factor_shared = shared_a.reshape(shared_count, model_width)
    factor_store = store_a.reshape(adapted * rank, model_width)
    results = []
    for s in range(steps):
        rows = gathered[s]
        inner = exchange_all(inner_products(rows, factor_shared, factor_store))
        gate, up = gate_up(rows, w_gate[0], w_up[0])
        pieces = down_products(
            gate,
            up,
            gate_own[s * size : (s + 1) * size],
            up_own[s * size : (s + 1) * size],
            inner,
            packs,
            row_tenant,
            slot_tenant,
            shared_tenant,
            share[s],
            routed_down_weight[0],
            shared_down,
            size,
            shared_count,
            n_tensor,
        )
        held = dict(enumerate(pieces))
        bit = 1
        while bit < count:
            for r in sorted([r for r in held if r & bit], reverse=True):
                arrived = swap(held.pop(r), bit)
                held[r ^ bit] = (held[r ^ bit].astype(F32) + arrived.astype(F32)).astype(BF16)
            bit *= 2
        parts = lax.all_to_all(held[0], "tensor", split_axis=0, concat_axis=0, tiled=True)
        results.append(jnp.sum(parts.astype(F32), axis=0).astype(BF16))
    return jnp.stack(results, axis=0)


def solution(mesh):
    return jax.shard_map(
        local,
        mesh=mesh,
        in_specs=(
            P(None, ("groups", "expert"), None),
            P(None, ("groups", "expert"), None),
            P(None, ("groups", "expert"), None),
            P(("groups", "expert")),
            P("expert", None, "tensor"),
            P("expert", None, "tensor"),
            P("expert", "tensor", None),
            P(None, "tensor"),
            P(None, "tensor"),
            P("tensor", None),
            P("expert", None, None),
            P("expert", None, "tensor"),
            P(),
            P("expert", None, None),
            P("expert", None, "tensor"),
        ),
        out_specs=P(None, ("groups", "expert"), "tensor"),
        check_vma=False,
    )
```

time: 189 us -> 88.5 us (0.47)
  matrix products: 52.6 us -> 0 us
  waiting for transfers between devices: 63.4 us -> 26.4 us
  Pallas kernels: 0 us -> 15 us
  between operations: 13.5 us -> 0.33 us
  starting transfers between devices: 29.1 us -> 19.5 us
  blocking collectives: 6.46 us -> 0 us
  local copies, waits for them, and re-layouts: 16.5 us -> 20.3 us
    dot_general x26 -> x0, matrix products: 52.6 us -> none  [the longest x4 11.4 us: feed_forward(): return jnp.dot(hidden, down_weight, preferred_element_type=jnp.float32)]
    reduce_scatter x2 -> x0, waiting for transfers between devices: 33.8 us -> none  [local(): lax.psum_scatter(jnp.concatenate([routed_terms, shared_terms], axis=0).as...]
    all_to_all x8 -> x2, starting transfers between devices: 28.9 us -> 8.25 us  [local(): lax.all_to_all(held[0], 'tensor', split_axis=0, concat_axis=0, tiled=True)]
    all_to_all x8 -> x2, waiting for transfers between devices: 28.8 us -> 13.4 us  [local(): lax.all_to_all(held[0], 'tensor', split_axis=0, concat_axis=0, tiled=True)]
    pallas_call x0 -> x7, Pallas kernels: none -> 15 us  [the longest x3 6.76 us: gate_up(): pl.pallas_call(functools.partial(gate_up_kernel, len(rows)), grid=(depth...]
    ppermute x0 -> x21, waiting for transfers between devices: none -> 13 us  [swap(): return lax.ppermute(value, 'expert', [(i, i ^ bit) for i in range(count)])]
    ppermute x0 -> x21, starting transfers between devices: none -> 11.3 us  [swap(): return lax.ppermute(value, 'expert', [(i, i ^ bit) for i in range(count)])]
    unnamed x60 -> x37, local copies, waits for them, and re-layouts: 4.08 us -> 14.3 us
  transfers between devices with their start and end apart: 11 -> 23, of which waited for: 7 -> 7; matrix products, arithmetic and copies ran while one was open for 32% -> 10% of each run, Pallas kernels for 0% -> 17%
where the time goes in v1:
time: 88.5 us; the launch traced here: 87.7 us
  waiting for transfers between devices  26.4 us (30%)
  local copies, waits for them, and re-layouts  20.3 us (23%)
  starting transfers between devices  19.5 us (22%)
  Pallas kernels  15 us (17%)
  other arithmetic  6.11 us (7%)
    unnamed x37, local copies, waits for them, and re-layouts  14.3 us
    all_to_all x2, waiting for transfers between devices, local(): lax.all_to_all(held[0], 'tensor', split_axis=0, concat_axis=0, tiled=True)  13.4 us
    ppermute x21, waiting for transfers between devices, swap(): return lax.ppermute(value, 'expert', [(i, i ^ bit) for i in range(count)])  13 us
    ppermute x21, starting transfers between devices, swap(): return lax.ppermute(value, 'expert', [(i, i ^ bit) for i in range(count)])  11.3 us
    all_to_all x2, starting transfers between devices, local(): lax.all_to_all(held[0], 'tensor', split_axis=0, concat_axis=0, tiled=True)  8.25 us
    pallas_call x3, Pallas kernels, gate_up(): pl.pallas_call(functools.partial(gate_up_kernel, len(rows)), grid=(depth...  6.76 us
    pallas_call x2, Pallas kernels, down_products(): pl.pallas_call(functools.partial(down_kernel, count, size, shared_count),...  5.76 us
    convert_element_type x4, other arithmetic, local(): (held[r ^ bit].astype(F32) + arrived.astype(F32)).astype(BF16)  2.63 us
  transfers between devices with their start and end apart: 23, of which 7 were waited for; matrix products, arithmetic and copies ran while one was open for 10% of the time, Pallas kernels for 17%

profile of v1, /device:TPU:0, one launch (start us, length us, event | category | flops | bytes accessed | tf_op | source)
XLA Modules:
  0.0 87.7 jit_solution(7209259878077646355)
XLA Ops:
  0.7 0.7 select_reduce_fusion
  1.6 0.8 pad_maximum_fusion.1.refs_8_
  2.4 3.0 %collective-permute-start.7 = (bf16[112,256]{1,0:T(8,128)(2,1)S(1)}, bf16[112,256]{1,0:T(8,128)(2,1)S(1)}, u32[]{:S(2)}, u32[]{:S(2)}) collective-permute-start(bf16[112,256]{1,0:T(8,128)(2,1)S(1)} %pad_maximum_fusion.1.refs_8_), channel_id=1, source_target_pairs={{0,8},{4,12},{8,0},{12,4},{1,9},{5,13},{9,1},{13,5},{2,10},{6,14},... | collective-permute-start | bytes 172040 | tf_op jit(solution)/shard_map/ppermute | solution.py:27
  5.4 1.1 %slice_bitcast_fusion.1 = (bf16[16,7168]{1,0:T(8,128)(2,1)S(1)}, bf16[16,7168]{1,0:T(8,128)(2,1)S(1)}) fusion(bf16[2,16,7168]{2,1,0:T(8,128)(2,1)} %param.15), kind=kLoop, calls=%fused_computation.7 | loop fusion | bytes 917504 | tf_op jit(solution)/shard_map/squeeze | solution.py:214
  7.1 1.7 %collective-permute-start.13 = (bf16[16,7168]{1,0:T(8,128)(2,1)S(1)}, bf16[16,7168]{1,0:T(8,128)(2,1)S(1)}, u32[]{:S(2)}, u32[]{:S(2)}) collective-permute-start(bf16[16,7168]{1,0:T(8,128)(2,1)S(1)} %get-tuple-element.34.refs_0_), channel_id=1, source_target_pairs={{0,8},{4,12},{8,0},{12,4},{1,9},{5,13},{9,1},{13,5},{2,10},{6,14},... | collective-permute-start | bytes 688136 | tf_op jit(solution)/shard_map/ppermute | solution.py:27
  9.6 2.0 %copy-done.10 = bf16[7168,256]{1,0:T(8,128)(2,1)S(1)} copy-done((bf16[7168,256]{1,0:T(8,128)(2,1)S(1)}, bf16[7168,256]{1,0:T(8,128)(2,1)}, u32[]{:S(2)}) %copy-start.10) | copy-done | bytes 3670040
  11.7 2.0 %copy-done.11 = bf16[7168,256]{1,0:T(8,128)(2,1)S(1)} copy-done((bf16[7168,256]{1,0:T(8,128)(2,1)S(1)}, bf16[7168,256]{1,0:T(8,128)(2,1)}, u32[]{:S(2)}) %copy-start.11) | copy-done | bytes 3670040
  13.7 1.0 %copy-done.13 = bf16[2,16,7168]{2,1,0:T(8,128)(2,1)S(1)} copy-done((bf16[2,16,7168]{2,1,0:T(8,128)(2,1)S(1)}, bf16[2,16,7168]{2,1,0:T(8,128)(2,1)}, u32[]{:S(2)}) %copy-start.13) | copy-done | bytes 458776
  14.7 2.1 %shard_map.146 = (f32[32,256]{1,0:T(8,128)S(1)}, f32[32,256]{1,0:T(8,128)S(1)}) custom-call(bf16[32,7168]{1,0:T(8,128)(2,1)S(1)} %bitcast.46, bf16[7168,256]{1,0:T(8,128)(2,1)S(1)} %copy-done.10, bf16[7168,256]{1,0:T(8,128)(2,1)S(1)} %copy-done.11), custom_call_target="tpu_custom_call" | custom-call | flops 234881024 | bytes 7340032 | tf_op jit(solution)/shard_map/pallas_call | solution.py:63
  22.6 1.2 %shard_map.150.refs_4_ = bf16[64,96]{1,0:T(8,128)(2,1)S(1)} custom-call(bf16[16,7168]{1,0:T(8,128)(2,1)S(1)} %get-tuple-element.34.refs_0_, bf16[16,7168]{1,0:T(8,128)(2,1)S(1)} %collective-permute-done.12.refs_1_, bf16[16,7168]{1,0:T(8,128)(2,1)S(1)} %collective-permute-done.13.refs_2_, bf16[16,7168]{1,0:T(8,128)(2,1)S(1)} %collective-permute-done.14.refs_3_, ...), custom_call_target="tpu_custom_call" | custom-call | flops 88080384 | bytes 1376256 | tf_op jit(solution)/shard_map/pallas_call | solution.py:100
  24.5 0.7 copy.46.refs_15_
  25.3 2.5 %collective-permute-done.16.refs_6_ = bf16[64,96]{1,0:T(8,128)(2,1)} collective-permute-done((bf16[64,96]{1,0:T(8,128)(2,1)S(1)}, bf16[64,96]{1,0:T(8,128)(2,1)}, u32[]{:S(2)}, u32[]{:S(2)}) %collective-permute-start.16) | collective-permute-done | bytes 12320 | tf_op jit(solution)/shard_map/ppermute | solution.py:27
  27.8 2.0 %copy-done.1 = bf16[1,7168,256]{2,1,0:T(8,128)(2,1)S(1)} copy-done((bf16[1,7168,256]{2,1,0:T(8,128)(2,1)S(1)}, bf16[1,7168,256]{2,1,0:T(8,128)(2,1)}, u32[]{:S(2)}) %copy-start.1) | copy-done | bytes 3670040
  29.8 2.0 %copy-done.3 = bf16[1,7168,256]{2,1,0:T(8,128)(2,1)S(1)} copy-done((bf16[1,7168,256]{2,1,0:T(8,128)(2,1)S(1)}, bf16[1,7168,256]{2,1,0:T(8,128)(2,1)}, u32[]{:S(2)}) %copy-start.3) | copy-done | bytes 3670040
  31.9 2.3 %shard_map.149 = (f32[64,256]{1,0:T(8,128)S(1)}, f32[64,256]{1,0:T(8,128)S(1)}) custom-call(bf16[16,7168]{1,0:T(8,128)(2,1)S(1)} %get-tuple-element.34.refs_0_, bf16[16,7168]{1,0:T(8,128)(2,1)S(1)} %collective-permute-done.12.refs_1_, bf16[16,7168]{1,0:T(8,128)(2,1)S(1)} %collective-permute-done.13.refs_2_, ...), custom_call_target="tpu_custom_call" | custom-call | flops 469762048 | bytes 7340032 | tf_op jit(solution)/shard_map/pallas_call | solution.py:63
  34.2 0.8 copy-done.7
  35.0 3.4 %shard_map.151 = (bf16[4,16,1792]{2,1,0:T(8,128)(2,1)S(1)}, bf16[4,16,1792]{2,1,0:T(8,128)(2,1)S(1)}, bf16[4,16,1792]{2,1,0:T(8,128)(2,1)S(1)}, bf16[4,16,1792]{2,1,0:T(8,128)(2,1)}) custom-call(f32[64,256]{1,0:T(8,128)S(1)} %get-tuple-element.27.refs_0_, f32[64,256]{1,0:T(8,128)S(1)} %get-tuple-element.28.refs_1_, f32[16,256]{1,0:T(8,128)S(1)} %copy-done.16, ...), custom_call_target="tpu_custom_call" | custom-call | flops 293601280 | bytes 7340032 | tf_op jit(solution)/shard_map/pallas_call | solution.py:168
  39.0 1.2 %shard_map.147.refs_4_ = bf16[64,96]{1,0:T(8,128)(2,1)S(1)} custom-call(bf16[16,7168]{1,0:T(8,128)(2,1)S(1)} %get-tuple-element.33.refs_0_, bf16[16,7168]{1,0:T(8,128)(2,1)S(1)} %collective-permute-done.refs_1_, bf16[16,7168]{1,0:T(8,128)(2,1)S(1)} %collective-permute-done.1.refs_2_, bf16[16,7168]{1,0:T(8,128)(2,1)S(1)} %collective-permute-done.2.refs_3_, ...), custom_call_target="tpu_custom_call" | custom-call | flops 88080384 | bytes 1376256 | tf_op jit(solution)/shard_map/pallas_call | solution.py:100
  40.8 3.2 %collective-permute-done.4.refs_6_ = bf16[64,96]{1,0:T(8,128)(2,1)S(1)} collective-permute-done((bf16[64,96]{1,0:T(8,128)(2,1)S(1)}, bf16[64,96]{1,0:T(8,128)(2,1)S(1)}, u32[]{:S(2)}, u32[]{:S(2)}) %collective-permute-start.4) | collective-permute-done | bytes 12320 | tf_op jit(solution)/shard_map/ppermute | solution.py:27
  44.0 2.0 %copy-done.2 = bf16[1,7168,256]{2,1,0:T(8,128)(2,1)S(1)} copy-done((bf16[1,7168,256]{2,1,0:T(8,128)(2,1)S(1)}, bf16[1,7168,256]{2,1,0:T(8,128)(2,1)}, u32[]{:S(2)}) %copy-start.2) | copy-done | bytes 3670040
  46.1 2.0 %copy-done.4 = bf16[1,7168,256]{2,1,0:T(8,128)(2,1)S(1)} copy-done((bf16[1,7168,256]{2,1,0:T(8,128)(2,1)S(1)}, bf16[1,7168,256]{2,1,0:T(8,128)(2,1)}, u32[]{:S(2)}) %copy-start.4) | copy-done | bytes 3670040
  48.1 2.3 %shard_map.145 = (f32[64,256]{1,0:T(8,128)S(1)}, f32[64,256]{1,0:T(8,128)S(1)}) custom-call(bf16[16,7168]{1,0:T(8,128)(2,1)S(1)} %get-tuple-element.33.refs_0_, bf16[16,7168]{1,0:T(8,128)(2,1)S(1)} %collective-permute-done.refs_1_, bf16[16,7168]{1,0:T(8,128)(2,1)S(1)} %collective-permute-done.1.refs_2_, bf16[16,7168]{1,0:T(8,128)(2,1)S(1)} %collective-permute-done.2.refs_3_, ...), custom_call_target="tpu_custom_call" | custom-call | flops 469762048 | bytes 7340032 | tf_op jit(solution)/shard_map/pallas_call | solution.py:63
  51.3 2.3 %shard_map.148 = (bf16[4,16,1792]{2,1,0:T(8,128)(2,1)S(1)}, bf16[4,16,1792]{2,1,0:T(8,128)(2,1)S(1)}, bf16[4,16,1792]{2,1,0:T(8,128)(2,1)S(1)}, bf16[4,16,1792]{2,1,0:T(8,128)(2,1)S(1)}) custom-call(f32[64,256]{1,0:T(8,128)S(1)} %get-tuple-element.19.refs_0_, f32[64,256]{1,0:T(8,128)S(1)} %get-tuple-element.20.refs_1_, f32[16,256]{1,0:T(8,128)S(1)} %copy-done.14, ...), custom_call_target="tpu_custom_call" | custom-call | flops 293601280 | bytes 7340032 | tf_op jit(solution)/shard_map/pallas_call | solution.py:168
  54.2 1.0 %add_convert_fusion.1 = bf16[4,16,1792]{2,1,0:T(8,128)(2,1)S(1)} fusion(bf16[4,16,1792]{2,1,0:T(8,128)(2,1)} %collective-permute-done.19, bf16[4,16,1792]{2,1,0:T(8,128)(2,1)S(1)} %get-tuple-element.31), kind=kLoop, calls=%fused_computation.1 | loop fusion | flops 458752 | bytes 688128 | tf_op jit(solution)/shard_map/convert_element_type | solution.py:281
  55.7 1.7 %collective-permute-start.11 = (bf16[4,16,1792]{2,1,0:T(8,128)(2,1)S(1)}, bf16[4,16,1792]{2,1,0:T(8,128)(2,1)S(1)}, u32[]{:S(2)}, u32[]{:S(2)}) collective-permute-start(bf16[4,16,1792]{2,1,0:T(8,128)(2,1)S(1)} %add_convert_fusion.4), channel_id=1, source_target_pairs={{0,8},{4,12},{8,0},{12,4},{1,9},{5,13},{9,1},{13,5},{2,10},{6,14},... | collective-permute-start | bytes 688136 | tf_op jit(solution)/shard_map/ppermute | solution.py:27
  57.5 6.2 %collective-permute-done.20 = bf16[4,16,1792]{2,1,0:T(8,128)(2,1)S(1)} collective-permute-done((bf16[4,16,1792]{2,1,0:T(8,128)(2,1)S(1)}, bf16[4,16,1792]{2,1,0:T(8,128)(2,1)S(1)}, u32[]{:S(2)}, u32[]{:S(2)}) %collective-permute-start.20) | collective-permute-done | bytes 229408 | tf_op jit(solution)/shard_map/ppermute | solution.py:27
  63.7 0.8 add_convert_fusion
  64.5 4.9 %all-to-all-start.1 = ((bf16[4,16,1792]{2,1,0:T(8,128)(2,1)}), bf16[4,16,1792]{2,1,0:T(8,128)(2,1)S(1)}, u32[]{:S(2)}, u32[]{:S(2)}) async-start(bf16[4,16,1792]{2,1,0:T(8,128)(2,1)} %add_convert_fusion), calls=%async_computation.1 | async-start | bytes 458752 | tf_op jit(solution)/shard_map/all_to_all | solution.py:283
  69.4 0.8 add_convert_fusion.3
  70.2 6.9 %all-to-all-done.1 = bf16[4,16,1792]{2,1,0:T(8,128)(2,1)S(1)} async-done(((bf16[4,16,1792]{2,1,0:T(8,128)(2,1)}), bf16[4,16,1792]{2,1,0:T(8,128)(2,1)S(1)}, u32[]{:S(2)}, u32[]{:S(2)}) %all-to-all-start.1) | async-done | bytes 229408 | tf_op jit(solution)/shard_map/all_to_all | solution.py:283
  77.1 3.4 %all-to-all-start = ((bf16[4,16,1792]{2,1,0:T(8,128)(2,1)}), bf16[4,16,1792]{2,1,0:T(8,128)(2,1)S(1)}, u32[]{:S(2)}, u32[]{:S(2)}) async-start(bf16[4,16,1792]{2,1,0:T(8,128)(2,1)} %add_convert_fusion.3), calls=%async_computation | async-start | bytes 458752 | tf_op jit(solution)/shard_map/all_to_all | solution.py:283
  80.6 6.4 %all-to-all-done = bf16[4,16,1792]{2,1,0:T(8,128)(2,1)S(1)} async-done(((bf16[4,16,1792]{2,1,0:T(8,128)(2,1)}), bf16[4,16,1792]{2,1,0:T(8,128)(2,1)S(1)}, u32[]{:S(2)}, u32[]{:S(2)}) %all-to-all-start) | async-done | bytes 229408 | tf_op jit(solution)/shard_map/all_to_all | solution.py:283
  (114 shorter events, 12.5 us)
Async XLA Ops:
  0.0 9.1 %copy-start = (s32[4,16]{1,0:T(4,128)S(1)}, s32[4,16]{1,0:T(4,128)}, u32[]{:S(2)}) copy-start(s32[4,16]{1,0:T(4,128)} %param.27) | copy-start | bytes 772
  2.4 15.9 %collective-permute-start.7 = (bf16[112,256]{1,0:T(8,128)(2,1)S(1)}, bf16[112,256]{1,0:T(8,128)(2,1)S(1)}, u32[]{:S(2)}, u32[]{:S(2)}) collective-permute-start(bf16[112,256]{1,0:T(8,128)(2,1)S(1)} %pad_maximum_fusion.1.refs_8_), channel_id=1, source_target_pairs={{0,8},{4,12},{8,0},{12,4},{1,9},{5,13},{9,1},{13,5},{2,10},{6,14},... | collective-permute-start | bytes 172040 | tf_op jit(solution)/shard_map/ppermute | solution.py:27
  5.4 12.3 %collective-permute-start.6 = (bf16[112,256]{1,0:T(8,128)(2,1)S(1)}, bf16[112,256]{1,0:T(8,128)(2,1)S(1)}, u32[]{:S(2)}, u32[]{:S(2)}) collective-permute-start(bf16[112,256]{1,0:T(8,128)(2,1)S(1)} %pad_maximum_fusion.1.refs_8_), channel_id=1, source_target_pairs={{0,4},{4,0},{8,12},{12,8},{1,5},{5,1},{9,13},{13,9},{2,6},{6,2},{1... | collective-permute-start | bytes 172040 | tf_op jit(solution)/shard_map/ppermute | solution.py:27
  6.5 15.6 %collective-permute-start.1 = (bf16[16,7168]{1,0:T(8,128)(2,1)S(1)}, bf16[16,7168]{1,0:T(8,128)(2,1)S(1)}, u32[]{:S(2)}, u32[]{:S(2)}) collective-permute-start(bf16[16,7168]{1,0:T(8,128)(2,1)S(1)} %get-tuple-element.33.refs_0_), channel_id=1, source_target_pairs={{0,8},{4,12},{8,0},{12,4},{1,9},{5,13},{9,1},{13,5},{2,10},{6,14},... | collective-permute-start | bytes 688136 | tf_op jit(solution)/shard_map/ppermute | solution.py:27
  6.6 32.4 %collective-permute-start = (bf16[16,7168]{1,0:T(8,128)(2,1)S(1)}, bf16[16,7168]{1,0:T(8,128)(2,1)S(1)}, u32[]{:S(2)}, u32[]{:S(2)}) collective-permute-start(bf16[16,7168]{1,0:T(8,128)(2,1)S(1)} %get-tuple-element.33.refs_0_), channel_id=1, source_target_pairs={{0,4},{4,0},{8,12},{12,8},{1,5},{5,1},{9,13},{13,9},{2,6},{6,2},{1... | collective-permute-start | bytes 688136 | tf_op jit(solution)/shard_map/ppermute | solution.py:27
  7.1 14.0 %collective-permute-start.13 = (bf16[16,7168]{1,0:T(8,128)(2,1)S(1)}, bf16[16,7168]{1,0:T(8,128)(2,1)S(1)}, u32[]{:S(2)}, u32[]{:S(2)}) collective-permute-start(bf16[16,7168]{1,0:T(8,128)(2,1)S(1)} %get-tuple-element.34.refs_0_), channel_id=1, source_target_pairs={{0,8},{4,12},{8,0},{12,4},{1,9},{5,13},{9,1},{13,5},{2,10},{6,14},... | collective-permute-start | bytes 688136 | tf_op jit(solution)/shard_map/ppermute | solution.py:27
  14.7 7.8 %copy-start.9 = (bf16[4,16,7168]{2,1,0:T(8,128)(2,1)S(1)}, bf16[4,16,7168]{2,1,0:T(8,128)(2,1)}, u32[]{:S(2)}) copy-start(bf16[4,16,7168]{2,1,0:T(8,128)(2,1)} %param.28) | copy-start | bytes 2752516
  14.7 7.8 %copy-start.12 = (bf16[2,16,7168]{2,1,0:T(8,128)(2,1)S(1)}, bf16[2,16,7168]{2,1,0:T(8,128)(2,1)}, u32[]{:S(2)}) copy-start(bf16[2,16,7168]{2,1,0:T(8,128)(2,1)} %param.25) | copy-start | bytes 1376260
  17.7 4.6 %collective-permute-start.12 = (bf16[16,7168]{1,0:T(8,128)(2,1)S(1)}, bf16[16,7168]{1,0:T(8,128)(2,1)S(1)}, u32[]{:S(2)}, u32[]{:S(2)}) collective-permute-start(bf16[16,7168]{1,0:T(8,128)(2,1)S(1)} %get-tuple-element.34.refs_0_), channel_id=1, source_target_pairs={{0,4},{4,0},{8,12},{12,8},{1,5},{5,1},{9,13},{13,9},{2,6},{6,2},{1... | collective-permute-start | bytes 688136 | tf_op jit(solution)/shard_map/ppermute | solution.py:27
  18.9 1.5 %collective-permute-start.8 = (bf16[112,256]{1,0:T(8,128)(2,1)S(1)}, bf16[112,256]{1,0:T(8,128)(2,1)S(1)}, u32[]{:S(2)}, u32[]{:S(2)}) collective-permute-start(bf16[112,256]{1,0:T(8,128)(2,1)S(1)} %collective-permute-done.7.refs_10_), channel_id=1, source_target_pairs={{0,4},{4,0},{8,12},{12,8},{1,5},{5,1},{9,13},{13,9},{2,6},{6,2},{1... | collective-permute-start | bytes 172040 | tf_op jit(solution)/shard_map/ppermute | solution.py:27
  21.1 1.5 %collective-permute-start.14 = (bf16[16,7168]{1,0:T(8,128)(2,1)S(1)}, bf16[16,7168]{1,0:T(8,128)(2,1)S(1)}, u32[]{:S(2)}, u32[]{:S(2)}) collective-permute-start(bf16[16,7168]{1,0:T(8,128)(2,1)S(1)} %collective-permute-done.13.refs_2_), channel_id=1, source_target_pairs={{0,4},{4,0},{8,12},{12,8},{1,5},{5,1},{9,13},{13,9},{2,6},{6,2},{1... | collective-permute-start | bytes 688136 | tf_op jit(solution)/shard_map/ppermute | solution.py:27
  22.1 16.9 %collective-permute-start.2 = (bf16[16,7168]{1,0:T(8,128)(2,1)S(1)}, bf16[16,7168]{1,0:T(8,128)(2,1)S(1)}, u32[]{:S(2)}, u32[]{:S(2)}) collective-permute-start(bf16[16,7168]{1,0:T(8,128)(2,1)S(1)} %collective-permute-done.1.refs_2_), channel_id=1, source_target_pairs={{0,4},{4,0},{8,12},{12,8},{1,5},{5,1},{9,13},{13,9},{2,6},{6,2},{1... | collective-permute-start | bytes 688136 | tf_op jit(solution)/shard_map/ppermute | solution.py:27
  23.8 3.9 %collective-permute-start.16 = (bf16[64,96]{1,0:T(8,128)(2,1)S(1)}, bf16[64,96]{1,0:T(8,128)(2,1)}, u32[]{:S(2)}, u32[]{:S(2)}) collective-permute-start(bf16[64,96]{1,0:T(8,128)(2,1)S(1)} %shard_map.150.refs_4_), channel_id=1, source_target_pairs={{0,8},{4,12},{8,0},{12,4},{1,9},{5,13},{9,1},{13,5},{2,10},{6,14},... | collective-permute-start | bytes 36872 | tf_op jit(solution)/shard_map/ppermute | solution.py:27
  25.2 9.1 %collective-permute-start.15 = (bf16[64,96]{1,0:T(8,128)(2,1)S(1)}, bf16[64,96]{1,0:T(8,128)(2,1)S(1)}, u32[]{:S(2)}, u32[]{:S(2)}) collective-permute-start(bf16[64,96]{1,0:T(8,128)(2,1)S(1)} %shard_map.150.refs_4_), channel_id=1, source_target_pairs={{0,4},{4,0},{8,12},{12,8},{1,5},{5,1},{9,13},{13,9},{2,6},{6,2},{1... | collective-permute-start | bytes 36872 | tf_op jit(solution)/shard_map/ppermute | solution.py:27
  27.8 6.5 %collective-permute-start.17 = (bf16[64,96]{1,0:T(8,128)(2,1)}, bf16[64,96]{1,0:T(8,128)(2,1)S(1)}, u32[]{:S(2)}, u32[]{:S(2)}) collective-permute-start(bf16[64,96]{1,0:T(8,128)(2,1)} %collective-permute-done.16.refs_6_), channel_id=1, source_target_pairs={{0,4},{4,0},{8,12},{12,8},{1,5},{5,1},{9,13},{13,9},{2,6},{6,2},{1... | collective-permute-start | bytes 36872 | tf_op jit(solution)/shard_map/ppermute | solution.py:27
  31.9 3.2 %copy-start.7 = (bf16[256,7168]{1,0:T(8,128)(2,1)S(1)}, bf16[256,7168]{1,0:T(8,128)(2,1)}, u32[]{:S(2)}) copy-start(bf16[256,7168]{1,0:T(8,128)(2,1)} %refs_17_.3) | copy-start | bytes 11010052
  31.9 3.2 %copy-start.15 = (f32[16,256]{1,0:T(8,128)S(1)}, f32[16,256]{1,0:T(8,128)}, u32[]{:S(2)}) copy-start(f32[16,256]{1,0:T(8,128)} %get-tuple-element.42.refs_3_) | copy-start | bytes 49156
  31.9 3.2 %copy-start.16 = (f32[16,256]{1,0:T(8,128)S(1)}, f32[16,256]{1,0:T(8,128)}, u32[]{:S(2)}) copy-start(f32[16,256]{1,0:T(8,128)} %get-tuple-element.52.refs_2_) | copy-start | bytes 49156
  38.5 15.8 %collective-permute-start.19 = (bf16[4,16,1792]{2,1,0:T(8,128)(2,1)}, bf16[4,16,1792]{2,1,0:T(8,128)(2,1)}, u32[]{:S(2)}, u32[]{:S(2)}) collective-permute-start(bf16[4,16,1792]{2,1,0:T(8,128)(2,1)} %get-tuple-element.32), channel_id=1, source_target_pairs={{0,4},{4,0},{8,12},{12,8},{1,5},{5,1},{9,13},{13,9},{2,6},{6,2},{1... | collective-permute-start | bytes 688136 | tf_op jit(solution)/shard_map/ppermute | solution.py:27
  40.2 3.8 %collective-permute-start.4 = (bf16[64,96]{1,0:T(8,128)(2,1)S(1)}, bf16[64,96]{1,0:T(8,128)(2,1)S(1)}, u32[]{:S(2)}, u32[]{:S(2)}) collective-permute-start(bf16[64,96]{1,0:T(8,128)(2,1)S(1)} %shard_map.147.refs_4_), channel_id=1, source_target_pairs={{0,8},{4,12},{8,0},{12,4},{1,9},{5,13},{9,1},{13,5},{2,10},{6,14},... | collective-permute-start | bytes 36872 | tf_op jit(solution)/shard_map/ppermute | solution.py:27
  40.7 10.4 %copy-start.14 = (f32[16,256]{1,0:T(8,128)S(1)}, f32[16,256]{1,0:T(8,128)}, u32[]{:S(2)}) copy-start(f32[16,256]{1,0:T(8,128)} %get-tuple-element.53.refs_2_) | copy-start | bytes 49156
  40.7 10.3 %collective-permute-start.3 = (bf16[64,96]{1,0:T(8,128)(2,1)S(1)}, bf16[64,96]{1,0:T(8,128)(2,1)S(1)}, u32[]{:S(2)}, u32[]{:S(2)}) collective-permute-start(bf16[64,96]{1,0:T(8,128)(2,1)S(1)} %shard_map.147.refs_4_), channel_id=1, source_target_pairs={{0,4},{4,0},{8,12},{12,8},{1,5},{5,1},{9,13},{13,9},{2,6},{6,2},{1... | collective-permute-start | bytes 36872 | tf_op jit(solution)/shard_map/ppermute | solution.py:27
  44.0 7.0 %collective-permute-start.5 = (bf16[64,96]{1,0:T(8,128)(2,1)S(1)}, bf16[64,96]{1,0:T(8,128)(2,1)S(1)}, u32[]{:S(2)}, u32[]{:S(2)}) collective-permute-start(bf16[64,96]{1,0:T(8,128)(2,1)S(1)} %collective-permute-done.4.refs_6_), channel_id=1, source_target_pairs={{0,4},{4,0},{8,12},{12,8},{1,5},{5,1},{9,13},{13,9},{2,6},{6,2},{1... | collective-permute-start | bytes 36872 | tf_op jit(solution)/shard_map/ppermute | solution.py:27
  48.1 2.9 %copy-start.6 = (bf16[1,256,7168]{2,1,0:T(8,128)(2,1)S(1)}, bf16[1,256,7168]{2,1,0:T(8,128)(2,1)}, u32[]{:S(2)}) copy-start(bf16[1,256,7168]{2,1,0:T(8,128)(2,1)} %param.21) | copy-start | bytes 11010052
  48.1 3.2 %copy-start.8 = (bf16[256,7168]{1,0:T(8,128)(2,1)S(1)}, bf16[256,7168]{1,0:T(8,128)(2,1)}, u32[]{:S(2)}) copy-start(bf16[256,7168]{1,0:T(8,128)(2,1)} %refs_17_.3) | copy-start | bytes 11010052
  50.5 7.0 %collective-permute-start.18 = (bf16[4,16,1792]{2,1,0:T(8,128)(2,1)S(1)}, bf16[4,16,1792]{2,1,0:T(8,128)(2,1)S(1)}, u32[]{:S(2)}, u32[]{:S(2)}) collective-permute-start(bf16[4,16,1792]{2,1,0:T(8,128)(2,1)S(1)} %get-tuple-element.30), channel_id=1, source_target_pairs={{0,4},{4,0},{8,12},{12,8},{1,5},{5,1},{9,13},{13,9},{2,6},{6,2},{1... | collective-permute-start | bytes 688136 | tf_op jit(solution)/shard_map/ppermute | solution.py:27
  53.6 15.8 %collective-permute-start.9 = (bf16[4,16,1792]{2,1,0:T(8,128)(2,1)S(1)}, bf16[4,16,1792]{2,1,0:T(8,128)(2,1)S(1)}, u32[]{:S(2)}, u32[]{:S(2)}) collective-permute-start(bf16[4,16,1792]{2,1,0:T(8,128)(2,1)S(1)} %get-tuple-element.24), channel_id=1, source_target_pairs={{0,4},{4,0},{8,12},{12,8},{1,5},{5,1},{9,13},{13,9},{2,6},{6,2},{1... | collective-permute-start | bytes 688136 | tf_op jit(solution)/shard_map/ppermute | solution.py:27
  54.2 1.5 %collective-permute-start.10 = (bf16[4,16,1792]{2,1,0:T(8,128)(2,1)S(1)}, bf16[4,16,1792]{2,1,0:T(8,128)(2,1)S(1)}, u32[]{:S(2)}, u32[]{:S(2)}) collective-permute-start(bf16[4,16,1792]{2,1,0:T(8,128)(2,1)S(1)} %get-tuple-element.26), channel_id=1, source_target_pairs={{0,4},{4,0},{8,12},{12,8},{1,5},{5,1},{9,13},{13,9},{2,6},{6,2},{1... | collective-permute-start | bytes 688136 | tf_op jit(solution)/shard_map/ppermute | solution.py:27
  55.2 8.5 %collective-permute-start.20 = (bf16[4,16,1792]{2,1,0:T(8,128)(2,1)S(1)}, bf16[4,16,1792]{2,1,0:T(8,128)(2,1)S(1)}, u32[]{:S(2)}, u32[]{:S(2)}) collective-permute-start(bf16[4,16,1792]{2,1,0:T(8,128)(2,1)S(1)} %add_convert_fusion.1), channel_id=1, source_target_pairs={{0,8},{4,12},{8,0},{12,4},{1,9},{5,13},{9,1},{13,5},{2,10},{6,14},... | collective-permute-start | bytes 688136 | tf_op jit(solution)/shard_map/ppermute | solution.py:27
  55.7 13.6 %collective-permute-start.11 = (bf16[4,16,1792]{2,1,0:T(8,128)(2,1)S(1)}, bf16[4,16,1792]{2,1,0:T(8,128)(2,1)S(1)}, u32[]{:S(2)}, u32[]{:S(2)}) collective-permute-start(bf16[4,16,1792]{2,1,0:T(8,128)(2,1)S(1)} %add_convert_fusion.4), channel_id=1, source_target_pairs={{0,8},{4,12},{8,0},{12,4},{1,9},{5,13},{9,1},{13,5},{2,10},{6,14},... | collective-permute-start | bytes 688136 | tf_op jit(solution)/shard_map/ppermute | solution.py:27
  64.5 12.6 %all-to-all-start.1 = ((bf16[4,16,1792]{2,1,0:T(8,128)(2,1)}), bf16[4,16,1792]{2,1,0:T(8,128)(2,1)S(1)}, u32[]{:S(2)}, u32[]{:S(2)}) async-start(bf16[4,16,1792]{2,1,0:T(8,128)(2,1)} %add_convert_fusion), calls=%async_computation.1 | async-start | bytes 458752 | tf_op jit(solution)/shard_map/all_to_all | solution.py:283
  77.1 9.9 %all-to-all-start = ((bf16[4,16,1792]{2,1,0:T(8,128)(2,1)}), bf16[4,16,1792]{2,1,0:T(8,128)(2,1)S(1)}, u32[]{:S(2)}, u32[]{:S(2)}) async-start(bf16[4,16,1792]{2,1,0:T(8,128)(2,1)} %add_convert_fusion.3), calls=%async_computation | async-start | bytes 458752 | tf_op jit(solution)/shard_map/all_to_all | solution.py:283
  (8 other events, 15.6 us)

commit v2 on v1

--- a/solution.py
+++ b/solution.py
@@ -9,7 +9,7 @@
 
 F32 = jnp.float32
 BF16 = jnp.bfloat16
-VMEM_LIMIT = 24 * 1024 * 1024
+VMEM_LIMIT = 56 * 1024 * 1024
 
 
 def params():
@@ -22,9 +22,13 @@
     return pl.CostEstimate(flops=int(flops), bytes_accessed=int(moved), transcendentals=0)
 
 
-def swap(value, bit):
-    count = lax.axis_size("expert")
-    return lax.ppermute(value, "expert", [(i, i ^ bit) for i in range(count)])
+def swap(value, bits, axis="expert"):
+    count = lax.axis_size(axis)
+    return lax.ppermute(value, axis, [(i, i ^ bits) for i in range(count)])
+
+
+def add(one, other):
+    return (one.astype(F32) + other.astype(F32)).astype(BF16)
 
 
 def exchange_all(value):
@@ -117,15 +121,14 @@
     return value / (1.0 + jnp.exp(-value))
 
 
-def down_kernel(count, size, shared_count, *refs):
+def down_kernel(count, size, shared_count, order, place, *refs):
     gate, up, gate_own, up_own = refs[:4]
     inner = refs[4 : 4 + count]
     factors = refs[4 + count : 4 + 2 * count]
-    row_tenant, slot_tenant, shared_tenant, share, down, down_own = refs[
-        4 + 2 * count : 10 + 2 * count
+    row_tenant, slot_tenant, shared_tenant, share, down, down_own, keep, send = refs[
+        4 + 2 * count : 12 + 2 * count
     ]
-    outs = refs[10 + 2 * count : 10 + 3 * count]
-    hidden, hidden_own = refs[10 + 3 * count :]
+    hidden, hidden_own = refs[12 + 2 * count :]
 
     @pl.when(pl.program_id(0) == 0)
     def _():
@@ -151,31 +154,42 @@
 
     routed = jnp.dot(hidden[...], down[...], preferred_element_type=F32) * share[...]
     own = jnp.dot(hidden_own[...], down_own[...], preferred_element_type=F32)
-    outs[0][0] = (routed[:size] + own).astype(BF16)
-    for r in range(1, count):
-        outs[r][0] = routed[r * size : (r + 1) * size].astype(BF16)
+    half = count // 2
+    for place_of, r in enumerate(order):
+        block = routed[r * size : (r + 1) * size]
+        if r == 0:
+            block = block + own
+        target, row = (keep, place_of) if place_of < half else (send, place_of - half)
+        target[0, row] = block.astype(BF16)
 
 
 def down_products(
     gate, up, gate_own, up_own, inner, factors, row_tenant, slot_tenant, shared_tenant, share,
-    down, down_own, size, shared_count, blocks,
+    down, down_own, place, first, blocks, parts, order, shared_count,
 ):
     count = len(inner)
     total, hid = gate.shape
+    size = total // count
     depth = down.shape[1]
-    part = depth // blocks
+    part = depth // parts
     whole = [gate, up, gate_own, up_own, *inner, *factors, row_tenant, slot_tenant, shared_tenant, share]
+    out = jax.ShapeDtypeStruct((blocks, count // 2, size, part), BF16)
     return pl.pallas_call(
-        functools.partial(down_kernel, count, size, shared_count),
-        grid=(blocks,),
-        in_specs=[pl.BlockSpec(x.shape, lambda j: (0, 0)) for x in whole]
-        + [pl.BlockSpec((hid, part), lambda j: (0, j))] * 2,
-        out_specs=[pl.BlockSpec((1, size, part), lambda j: (j, 0, 0))] * count,
-        out_shape=[jax.ShapeDtypeStruct((blocks, size, part), BF16)] * count,
-        scratch_shapes=[pltpu.VMEM((total, hid), BF16), pltpu.VMEM((size, hid), BF16)],
+        functools.partial(down_kernel, count, size, shared_count, order),
+        grid_spec=pltpu.PrefetchScalarGridSpec(
+            num_scalar_prefetch=1,
+            grid=(blocks,),
+            in_specs=[pl.BlockSpec(x.shape, lambda j, place: (0, 0)) for x in whole]
+            + [pl.BlockSpec((hid, part), lambda j, place: (0, (first + j) ^ place[0]))] * 2,
+            out_specs=[pl.BlockSpec((1, count // 2, size, part), lambda j, place: (j, 0, 0, 0))] * 2,
+            scratch_shapes=[pltpu.VMEM((total, hid), BF16), pltpu.VMEM((size, hid), BF16)],
+        ),
+        out_shape=[out, out],
         compiler_params=params(),
-        cost_estimate=cost(2 * (total + size) * depth * hid, 4 * depth * hid),
-    )(*whole, down, down_own)
+        cost_estimate=cost(
+            2 * (total + size) * part * blocks * hid, 4 * part * blocks * hid
+        ),
+    )(place, *whole, down, down_own)
 
 
 def split3(value):
@@ -211,7 +225,8 @@
     own = lax.axis_index("expert")
     shared_count = own_tenants * rank
 
-    gathered = [exchange_all(tokens[s]) for s in range(steps)]
+    rows_own = tokens.reshape(steps * size, model_width)
+    rows = exchange_all(rows_own)
 
     hits = expert_ids[..., None] == jnp.arange(experts, dtype=jnp.int32)
     dense = jnp.sum(jnp.where(hits, gate_values[..., None], 0.0), axis=2)
@@ -228,12 +243,12 @@
     shares, row_tenants = [], []
     for r in range(count):
         flat = packs[r][base:].reshape(-1)
-        three = flat[: 3 * number].astype(F32).reshape(3, steps, size, experts)
+        three = flat[: 3 * number].astype(F32).reshape(3, steps * size, experts)
         shares.append(three[0] + three[1] + three[2])
-        row_tenants.append(flat[3 * number : 3 * number + size].astype(jnp.int32))
-    share = jnp.concatenate(shares, axis=1)
-    share = lax.dynamic_slice_in_dim(share, own, 1, axis=2)
-    row_tenant = jnp.concatenate(row_tenants).reshape(count * size, 1)
+        row_tenants += [flat[3 * number : 3 * number + size].astype(jnp.int32)] * steps
+    share = jnp.concatenate(shares, axis=0)
+    share = lax.dynamic_slice_in_dim(share, own, 1, axis=1)
+    row_tenant = jnp.concatenate(row_tenants).reshape(count * steps * size, 1)
 
     holders = own ^ jnp.arange(count, dtype=jnp.int32)
     slots = (holders[:, None] * adapted + jnp.arange(adapted, dtype=jnp.int32)).reshape(-1)
@@ -248,41 +263,45 @@
     ).reshape(-1)
     shared_tenant = jnp.repeat(shared_tenant, rank).reshape(1, -1)
 
-    gate_own, up_own = gate_up([tokens.reshape(steps * size, model_width)], shared_gate, shared_up)
-    factor_shared = shared_a.reshape(shared_count, model_width)
-    factor_store = store_a.reshape(adapted * rank, model_width)
-    results = []
-    for s in range(steps):
-        rows = gathered[s]
-        inner = exchange_all(inner_products(rows, factor_shared, factor_store))
-        gate, up = gate_up(rows, w_gate[0], w_up[0])
-        pieces = down_products(
-            gate,
-            up,
-            gate_own[s * size : (s + 1) * size],
-            up_own[s * size : (s + 1) * size],
-            inner,
-            packs,
-            row_tenant,
-            slot_tenant,
-            shared_tenant,
-            share[s],
-            routed_down_weight[0],
-            shared_down,
-            size,
+    gate_own, up_own = gate_up([rows_own], shared_gate, shared_up)
+    inner = inner_products(
+        rows,
+        shared_a.reshape(shared_count, model_width),
+        store_a.reshape(adapted * rank, model_width),
+    )
+    inners = [inner] + [swap(inner, r) for r in range(1, count)]
+    gate, up = gate_up(rows, w_gate[0], w_up[0])
+
+    order = [0]
+    bit = count // 2
+    while bit >= 1:
+        order = order + [r | bit for r in order]
+        bit //= 2
+    place = lax.axis_index("tensor").astype(jnp.int32).reshape(1)
+    columns = {}
+    group = max(1, n_tensor // 2)
+    for first in range(n_tensor - group, -1, -group):
+        keep, send = down_products(
+            gate, up, gate_own, up_own, inners, packs, row_tenant, slot_tenant, shared_tenant,
+            share, routed_down_weight[0], shared_down, place, first, group, n_tensor, order,
             shared_count,
-            n_tensor,
         )
-        held = dict(enumerate(pieces))
-        bit = 1
-        while bit < count:
-            for r in sorted([r for r in held if r & bit], reverse=True):
-                arrived = swap(held.pop(r), bit)
-                held[r ^ bit] = (held[r ^ bit].astype(F32) + arrived.astype(F32)).astype(BF16)
-            bit *= 2
-        parts = lax.all_to_all(held[0], "tensor", split_axis=0, concat_axis=0, tiled=True)
-        results.append(jnp.sum(parts.astype(F32), axis=0).astype(BF16))
-    return jnp.stack(results, axis=0)
+        for j in range(group - 1, -1, -1):
+            held, leaving = keep[j], send[j]
+            bit = 1
+            while bit < count:
+                arrived = swap(leaving, bit)
+                half = held.shape[0] // 2
+                leaving = add(held[half:], arrived[half:])
+                held = add(held[:half], arrived[:half])
+                bit *= 2
+            columns[first + j] = leaving[0]
+    bit = 1
+    while bit < n_tensor:
+        for j in sorted([j for j in columns if j & bit], reverse=True):
+            columns[j ^ bit] = add(columns[j ^ bit], swap(columns.pop(j), bit, "tensor"))
+        bit *= 2
+    return columns[0].reshape(steps, size, model_width // n_tensor)
 
 
 def solution(mesh):

time: 88.5 us -> 70 us (0.79)
  waiting for transfers between devices: 26.4 us -> 11.5 us
  local copies, waits for them, and re-layouts: 20.3 us -> 8.09 us
  Pallas kernels: 15 us -> 25.1 us
  starting transfers between devices: 19.5 us -> 17.3 us
  other arithmetic: 6.11 us -> 7.05 us
    all_to_all x2 -> x0, waiting for transfers between devices: 13.4 us -> none  [local(): lax.all_to_all(held[0], 'tensor', split_axis=0, concat_axis=0, tiled=True)]
    unnamed x37 -> x27, local copies, waits for them, and re-layouts: 14.3 us -> 1.41 us
    all_to_all x2 -> x0, starting transfers between devices: 8.25 us -> none  [local(): lax.all_to_all(held[0], 'tensor', split_axis=0, concat_axis=0, tiled=True)]
    pallas_call x3 -> x2, Pallas kernels: 6.76 us -> 14.1 us  [gate_up(): pl.pallas_call(functools.partial(gate_up_kernel, len(rows)), grid=(depth...]
    ppermute x21 -> x20, starting transfers between devices: 11.3 us -> 17.3 us  [swap(): return lax.ppermute(value, axis, [(i, i ^ bits) for i in range(count)])]
    ppermute x21 -> x20, waiting for transfers between devices: 13 us -> 11.5 us  [swap(): return lax.ppermute(value, axis, [(i, i ^ bits) for i in range(count)])]
    pallas_call x2 -> x1, Pallas kernels: 2.49 us -> 3.97 us  [inner_products(): pl.pallas_call(functools.partial(inner_kernel, len(rows)), grid=(depth //...]
    pallas_call x2, Pallas kernels: 5.76 us -> 7 us  [down_products(): pl.pallas_call(functools.partial(down_kernel, count, size, shared_count,...]
  transfers between devices with their start and end apart: 23 -> 20, of which waited for: 7 -> 7; matrix products, arithmetic and copies ran while one was open for 10% -> 16% of each run, Pallas kernels for 17% -> 25%
where the time goes in v2:
time: 70 us; the launch traced here: 69.4 us
  Pallas kernels  25.1 us (36%)
  starting transfers between devices  17.3 us (25%)
  waiting for transfers between devices  11.5 us (16%)
  local copies, waits for them, and re-layouts  8.09 us (12%)
  other arithmetic  7.05 us (10%)
    ppermute x20, starting transfers between devices, swap(): return lax.ppermute(value, axis, [(i, i ^ bits) for i in range(count)])  17.3 us
    pallas_call x2, Pallas kernels, gate_up(): pl.pallas_call(functools.partial(gate_up_kernel, len(rows)), grid=(depth...  14.1 us
    ppermute x20, waiting for transfers between devices, swap(): return lax.ppermute(value, axis, [(i, i ^ bits) for i in range(count)])  11.5 us
    pallas_call x2, Pallas kernels, down_products(): pl.pallas_call(functools.partial(down_kernel, count, size, shared_count,...  7 us
    pallas_call x1, Pallas kernels, inner_products(): pl.pallas_call(functools.partial(inner_kernel, len(rows)), grid=(depth //...  3.97 us
    convert_element_type x4, other arithmetic, add(): return (one.astype(F32) + other.astype(F32)).astype(BF16)  2.76 us
    squeeze x2, local copies, waits for them, and re-layouts, local(): held, leaving = (keep[j], send[j])  2.16 us
    slice x3, local copies, waits for them, and re-layouts, local(): three = flat[:3 * number].astype(F32).reshape(3, steps * size, experts)  1.72 us
  transfers between devices with their start and end apart: 20, of which 7 were waited for; matrix products, arithmetic and copies ran while one was open for 16% of the time, Pallas kernels for 25%

profile of v2, /device:TPU:0, one launch (start us, length us, event | category | flops | bytes accessed | tf_op | source)
XLA Modules:
  0.0 69.4 jit_solution(5739291190287293173)
XLA Ops:
  0.5 2.6 %collective-permute-start.1 = (bf16[32,7168]{1,0:T(8,128)(2,1)}, bf16[32,7168]{1,0:T(8,128)(2,1)S(1)}, u32[]{:S(2)}, u32[]{:S(2)}) collective-permute-start(bf16[32,7168]{1,0:T(8,128)(2,1)} %bitcast.77), channel_id=1, source_target_pairs={{0,8},{4,12},{8,0},{12,4},{1,9},{5,13},{9,1},{13,5},{2,10},{6,14},... | collective-permute-start | bytes 1376264 | tf_op jit(solution)/shard_map/ppermute | solution.py:27
  3.0 0.7 convert_element_type.274
  3.7 0.7 %select_reduce_fusion = f32[2,16,4]{1,2,0:T(4,128)S(1)} fusion(f32[2,16,2]{1,2,0:T(2,128)} %param.17, s32[2,16,2]{1,2,0:T(2,128)} %param.16), kind=kLoop, calls=%fused_computation.50 | loop fusion | flops 640 | bytes 1024 | tf_op jit(solution)/shard_map/reduce_sum | solution.py:232
  4.7 0.8 %pad_maximum_fusion.refs_8_ = bf16[112,256]{1,0:T(8,128)(2,1)S(1)} fusion(bf16[16,256]{1,0:T(8,128)(2,1)S(1)} %reshape.313, bf16[32,256]{1,0:T(8,128)(2,1)} %bitcast.86, bf16[64,256]{1,0:T(8,128)(2,1)} %bitcast.85), kind=kLoop, calls=%fused_computation.36 | loop fusion | flops 172032 | bytes 114688 | tf_op jit(solution)/shard_map/concatenate | solution.py:237
  6.4 0.6 reshape_reshape.6.refs_13_
  7.2 0.7 reshape_reshape.7.refs_14_
  8.0 6.7 %shard_map.146 = (f32[32,256]{1,0:T(8,128)}, f32[32,256]{1,0:T(8,128)}) custom-call(bf16[32,7168]{1,0:T(8,128)(2,1)} %bitcast.78, bf16[7168,256]{1,0:T(8,128)(2,1)} %refs_1_.1, bf16[7168,256]{1,0:T(8,128)(2,1)} %refs_2_.1), custom_call_target="tpu_custom_call" | custom-call | flops 234881024 | bytes 7340032 | tf_op jit(solution)/shard_map/pallas_call | solution.py:67
  14.7 0.9 %collective-permute-done.7.refs_10_ = bf16[112,256]{1,0:T(8,128)(2,1)S(1)} collective-permute-done((bf16[112,256]{1,0:T(8,128)(2,1)S(1)}, bf16[112,256]{1,0:T(8,128)(2,1)S(1)}, u32[]{:S(2)}, u32[]{:S(2)}) %collective-permute-start.7) | collective-permute-done | bytes 57376 | tf_op jit(solution)/shard_map/ppermute | solution.py:27
  17.0 1.2 %collective-permute-done.8.refs_11_ = bf16[112,256]{1,0:T(8,128)(2,1)S(1)} collective-permute-done((bf16[112,256]{1,0:T(8,128)(2,1)S(1)}, bf16[112,256]{1,0:T(8,128)(2,1)S(1)}, u32[]{:S(2)}, u32[]{:S(2)}) %collective-permute-start.8) | collective-permute-done | bytes 57376 | tf_op jit(solution)/shard_map/ppermute | solution.py:27
  18.3 0.7 %copy.34.refs_12_ = s32[128,1]{1,0:T(8,128)} copy(s32[128,1]{0,1:T(1,128)S(1)} %bitcast_convert_fusion) | data formatting | bytes 1024 | tf_op jit(solution)/shard_map/reshape | solution.py:251
  19.9 0.7 %dynamic-slice_maximum_fusion.refs_15_ = f32[128,1]{1,0:T(8,128)} fusion(s32[]{:T(128)S(6)} %select_n.14, f32[32,4]{1,0:T(8,128)S(1)} %slice_add_fusion, f32[32,4]{1,0:T(8,128)S(1)} %slice_add_fusion.2, f32[32,4]{1,0:T(8,128)S(1)} %slice_add_fusion.4, f32[32,4]{1,0:T(8,128)S(1)} %add.128), kind=kLoop, calls=%fused_computation.33 | loop fusion | flops 384 | bytes 2564 | tf_op jit(solution)/shard_map/concatenate | solution.py:249
  20.6 0.9 %collective-permute-done.2.refs_3_ = bf16[32,7168]{1,0:T(8,128)(2,1)S(1)} collective-permute-done((bf16[32,7168]{1,0:T(8,128)(2,1)S(1)}, bf16[32,7168]{1,0:T(8,128)(2,1)S(1)}, u32[]{:S(2)}, u32[]{:S(2)}) %collective-permute-start.2) | collective-permute-done | bytes 458784 | tf_op jit(solution)/shard_map/ppermute | solution.py:27
  21.5 0.8 %copy-done.3 = bf16[32,7168]{1,0:T(8,128)(2,1)} copy-done((bf16[32,7168]{1,0:T(8,128)(2,1)}, bf16[32,7168]{1,0:T(8,128)(2,1)S(1)}, u32[]{:S(2)}) %copy-start.3) | copy-done | bytes 458776
  22.3 4.0 %shard_map.147.refs_4_ = bf16[128,96]{1,0:T(8,128)(2,1)} custom-call(bf16[32,7168]{1,0:T(8,128)(2,1)} %bitcast.79, bf16[32,7168]{1,0:T(8,128)(2,1)} %copy-done.1, bf16[32,7168]{1,0:T(8,128)(2,1)} %copy-done.2, bf16[32,7168]{1,0:T(8,128)(2,1)} %copy-done.3, bf16[64,7168]{1,0:T(8,128)(2,1)} %bitcast.83, bf16[32,7168]{1,0:T(8,128)(2,1)} %bitcast.84), custom_call_target="tpu_custom_call" | custom-call | flops 176160768 | bytes 1376256 | tf_op jit(solution)/shard_map/pallas_call | solution.py:104
  26.4 1.8 %collective-permute-start.4 = (bf16[128,96]{1,0:T(8,128)(2,1)}, bf16[128,96]{1,0:T(8,128)(2,1)S(1)}, u32[]{:S(2)}, u32[]{:S(2)}) collective-permute-start(bf16[128,96]{1,0:T(8,128)(2,1)} %shard_map.147.refs_4_), channel_id=1, source_target_pairs={{0,8},{4,12},{8,0},{12,4},{1,9},{5,13},{9,1},{13,5},{2,10},{6,14},... | collective-permute-start | bytes 73736 | tf_op jit(solution)/shard_map/ppermute | solution.py:27
  28.2 7.3 %shard_map.145 = (f32[128,256]{1,0:T(8,128)}, f32[128,256]{1,0:T(8,128)}) custom-call(bf16[32,7168]{1,0:T(8,128)(2,1)} %bitcast.80, bf16[32,7168]{1,0:T(8,128)(2,1)} %copy-done.1, bf16[32,7168]{1,0:T(8,128)(2,1)} %copy-done.2, bf16[32,7168]{1,0:T(8,128)(2,1)} %copy-done.3, bf16[7168,256]{1,0:T(8,128)(2,1)} %bitcast.81, bf16[7168,256]{1,0:T(8,128)(2,1)} %bitcast.82), custom_call_target="tpu_custom_call" | custom-call | flops 939524096 | bytes 7340032 | tf_op jit(solution)/shard_map/pallas_call | solution.py:67
  36.2 3.5 %shard_map.149 = (bf16[2,2,32,1792]{3,2,1,0:T(8,128)(2,1)}, bf16[2,2,32,1792]{3,2,1,0:T(8,128)(2,1)}) custom-call(s32[1]{0:T(128)} %bitcast.place, f32[128,256]{1,0:T(8,128)} %get-tuple-element.13.refs_0_, f32[128,256]{1,0:T(8,128)} %get-tuple-element.14.refs_1_, f32[32,256]{1,0:T(8,128)} %get-tuple-element.15.refs_2_, f32[32,256]{1,0:T(8,128)} %get-tuple-element.16.refs_3_, ...), custom_call_target="tpu_custom_call" | custom-call | flops 293601280 | bytes 3670016 | tf_op jit(solution)/shard_map/pallas_call | solution.py:177
  39.7 1.1 %slice_bitcast_fusion.1 = (bf16[2,32,1792]{2,1,0:T(8,128)(2,1)S(1)}, bf16[2,32,1792]{2,1,0:T(8,128)(2,1)S(1)}) fusion(bf16[2,2,32,1792]{3,2,1,0:T(8,128)(2,1)} %get-tuple-element.20), kind=kLoop, calls=%fused_computation.24 | loop fusion | bytes 917504 | tf_op jit(solution)/shard_map/squeeze | solution.py:290
  41.4 3.5 %shard_map.148 = (bf16[2,2,32,1792]{3,2,1,0:T(8,128)(2,1)}, bf16[2,2,32,1792]{3,2,1,0:T(8,128)(2,1)}) custom-call(s32[1]{0:T(128)} %bitcast.place, f32[128,256]{1,0:T(8,128)} %get-tuple-element.13.refs_0_, f32[128,256]{1,0:T(8,128)} %get-tuple-element.14.refs_1_, f32[32,256]{1,0:T(8,128)} %get-tuple-element.15.refs_2_, f32[32,256]{1,0:T(8,128)} %get-tuple-element.16.refs_3_, ...), custom_call_target="tpu_custom_call" | custom-call | flops 293601280 | bytes 3670016 | tf_op jit(solution)/shard_map/pallas_call | solution.py:177
  44.9 1.1 %slice_bitcast_fusion.3 = (bf16[2,32,1792]{2,1,0:T(8,128)(2,1)S(1)}, bf16[2,32,1792]{2,1,0:T(8,128)(2,1)S(1)}) fusion(bf16[2,2,32,1792]{3,2,1,0:T(8,128)(2,1)} %get-tuple-element.18), kind=kLoop, calls=%fused_computation.28 | loop fusion | bytes 917504 | tf_op jit(solution)/shard_map/squeeze | solution.py:290
  46.6 1.8 %collective-permute-start.17 = (bf16[1,32,1792]{2,1,0:T(8,128)(2,1)S(1)}, bf16[1,32,1792]{2,1,0:T(8,128)(2,1)S(1)}, u32[]{:S(2)}, u32[]{:S(2)}) collective-permute-start(bf16[1,32,1792]{2,1,0:T(8,128)(2,1)S(1)} %get-tuple-element.26), channel_id=1, source_target_pairs={{0,8},{4,12},{8,0},{12,4},{1,9},{5,13},{9,1},{13,5},{2,10},{6,14},... | collective-permute-start | bytes 344072 | tf_op jit(solution)/shard_map/ppermute | solution.py:27
  48.7 1.0 %fusion.8 = (bf16[1,32,1792]{2,1,0:T(8,128)(2,1)S(1)}, bf16[1,32,1792]{2,1,0:T(8,128)(2,1)S(1)}) fusion(bf16[2,32,1792]{2,1,0:T(8,128)(2,1)S(1)} %collective-permute-done.9, bf16[2,2,32,1792]{3,2,1,0:T(8,128)(2,1)} %get-tuple-element.17, bf16[2,32,1792]{2,1,0:T(8,128)(2,1)S(1)} %collective-permute-done.11), kind=kLoop, calls=%fused_computation.17 | loop fusion | flops 458752 | bytes 688128 | tf_op jit(solution)/shard_map/convert_element_type | solution.py:31
  49.7 1.8 %collective-permute-start.12 = (bf16[1,32,1792]{2,1,0:T(8,128)(2,1)S(1)}, bf16[1,32,1792]{2,1,0:T(8,128)(2,1)S(1)}, u32[]{:S(2)}, u32[]{:S(2)}) collective-permute-start(bf16[1,32,1792]{2,1,0:T(8,128)(2,1)S(1)} %get-tuple-element.22), channel_id=1, source_target_pairs={{0,8},{4,12},{8,0},{12,4},{1,9},{5,13},{9,1},{13,5},{2,10},{6,14},... | collective-permute-start | bytes 344072 | tf_op jit(solution)/shard_map/ppermute | solution.py:27
  51.8 0.8 %collective-permute-done.17 = bf16[1,32,1792]{2,1,0:T(8,128)(2,1)S(1)} collective-permute-done((bf16[1,32,1792]{2,1,0:T(8,128)(2,1)S(1)}, bf16[1,32,1792]{2,1,0:T(8,128)(2,1)S(1)}, u32[]{:S(2)}, u32[]{:S(2)}) %collective-permute-start.17) | collective-permute-done | bytes 114720 | tf_op jit(solution)/shard_map/ppermute | solution.py:27
  52.7 1.8 %collective-permute-start.18 = (bf16[32,1792]{1,0:T(8,128)(2,1)S(1)}, bf16[32,1792]{1,0:T(8,128)(2,1)S(1)}, u32[]{:S(2)}, u32[]{:S(2)}) collective-permute-start(bf16[32,1792]{1,0:T(8,128)(2,1)S(1)} %fusion.13), channel_id=1, source_target_pairs={{0,1},{1,0},{2,3},{3,2},{4,5},{5,4},{6,7},{7,6},{8,9},{9,8},{10,11... | collective-permute-start | bytes 344072 | tf_op jit(solution)/shard_map/ppermute | solution.py:27
  54.5 3.0 %collective-permute-done.12 = bf16[1,32,1792]{2,1,0:T(8,128)(2,1)S(1)} collective-permute-done((bf16[1,32,1792]{2,1,0:T(8,128)(2,1)S(1)}, bf16[1,32,1792]{2,1,0:T(8,128)(2,1)S(1)}, u32[]{:S(2)}, u32[]{:S(2)}) %collective-permute-start.12) | collective-permute-done | bytes 114720 | tf_op jit(solution)/shard_map/ppermute | solution.py:27
  57.6 0.9 %fusion.11 = bf16[32,1792]{1,0:T(8,128)(2,1)S(1)} fusion(bf16[1,32,1792]{2,1,0:T(8,128)(2,1)S(1)} %collective-permute-done.12, bf16[2,32,1792]{2,1,0:T(8,128)(2,1)S(1)} %collective-permute-done.11, bf16[2,2,32,1792]{3,2,1,0:T(8,128)(2,1)} %get-tuple-element.17), kind=kLoop, calls=%fused_computation.30 | loop fusion | flops 458752 | bytes 458752 | tf_op jit(solution)/shard_map/squeeze | solution.py:298
  58.5 1.8 %collective-permute-start.13 = (bf16[32,1792]{1,0:T(8,128)(2,1)S(1)}, bf16[32,1792]{1,0:T(8,128)(2,1)S(1)}, u32[]{:S(2)}, u32[]{:S(2)}) collective-permute-start(bf16[32,1792]{1,0:T(8,128)(2,1)S(1)} %fusion.11), channel_id=1, source_target_pairs={{0,1},{1,0},{2,3},{3,2},{4,5},{5,4},{6,7},{7,6},{8,9},{9,8},{10,11... | collective-permute-start | bytes 344072 | tf_op jit(solution)/shard_map/ppermute | solution.py:27
  60.4 2.7 %collective-permute-start.19 = (bf16[32,1792]{1,0:T(8,128)(2,1)S(1)}, bf16[32,1792]{1,0:T(8,128)(2,1)S(1)}, u32[]{:S(2)}, u32[]{:S(2)}) collective-permute-start(bf16[32,1792]{1,0:T(8,128)(2,1)S(1)} %fusion.2), channel_id=1, source_target_pairs={{0,2},{1,3},{2,0},{3,1},{4,6},{5,7},{6,4},{7,5},{8,10},{9,11},{10,... | collective-permute-start | bytes 344072 | tf_op jit(solution)/shard_map/ppermute | solution.py:27
  63.1 1.3 %collective-permute-done.13 = bf16[32,1792]{1,0:T(8,128)(2,1)S(1)} collective-permute-done((bf16[32,1792]{1,0:T(8,128)(2,1)S(1)}, bf16[32,1792]{1,0:T(8,128)(2,1)S(1)}, u32[]{:S(2)}, u32[]{:S(2)}) %collective-permute-start.13) | collective-permute-done | bytes 114720 | tf_op jit(solution)/shard_map/ppermute | solution.py:27
  64.4 3.4 %collective-permute-done.19 = bf16[32,1792]{1,0:T(8,128)(2,1)S(1)} collective-permute-done((bf16[32,1792]{1,0:T(8,128)(2,1)S(1)}, bf16[32,1792]{1,0:T(8,128)(2,1)S(1)}, u32[]{:S(2)}, u32[]{:S(2)}) %collective-permute-start.19) | collective-permute-done | bytes 114720 | tf_op jit(solution)/shard_map/ppermute | solution.py:27
  67.8 1.6 %add_convert_fusion = bf16[32,1792]{1,0:T(8,128)(2,1)} fusion(bf16[32,1792]{1,0:T(8,128)(2,1)S(1)} %collective-permute-done.19, bf16[32,1792]{1,0:T(8,128)(2,1)S(1)} %collective-permute-done.13, bf16[1,32,1792]{2,1,0:T(8,128)(2,1)S(1)} %collective-permute-done.10, bf16[2,32,1792]{2,1,0:T(8,128)(2,1)S(1)} %collective-permute-done.9, ...), kind=kLoop, calls=%fused_computation.20 | loop fusion | flops 917504 | bytes 688128 | tf_op jit(solution)/shard_map/convert_element_type | solution.py:31
  (89 shorter events, 6.9 us)
Async XLA Ops:
  0.0 6.1 %copy-start = (s32[4,16]{1,0:T(4,128)S(1)}, s32[4,16]{1,0:T(4,128)}, u32[]{:S(2)}) copy-start(s32[4,16]{1,0:T(4,128)} %param.27) | copy-start | bytes 772
  0.0 20.6 %collective-permute-start = (bf16[32,7168]{1,0:T(8,128)(2,1)}, bf16[32,7168]{1,0:T(8,128)(2,1)S(1)}, u32[]{:S(2)}, u32[]{:S(2)}) collective-permute-start(bf16[32,7168]{1,0:T(8,128)(2,1)} %bitcast.76), channel_id=1, source_target_pairs={{0,4},{4,0},{8,12},{12,8},{1,5},{5,1},{9,13},{13,9},{2,6},{6,2},{1... | collective-permute-start | bytes 1376264 | tf_op jit(solution)/shard_map/ppermute | solution.py:27
  0.5 19.2 %collective-permute-start.1 = (bf16[32,7168]{1,0:T(8,128)(2,1)}, bf16[32,7168]{1,0:T(8,128)(2,1)S(1)}, u32[]{:S(2)}, u32[]{:S(2)}) collective-permute-start(bf16[32,7168]{1,0:T(8,128)(2,1)} %bitcast.77), channel_id=1, source_target_pairs={{0,8},{4,12},{8,0},{12,4},{1,9},{5,13},{9,1},{13,5},{2,10},{6,14},... | collective-permute-start | bytes 1376264 | tf_op jit(solution)/shard_map/ppermute | solution.py:27
  5.5 9.3 %copy-start.4 = (bf16[112,256]{1,0:T(8,128)(2,1)}, bf16[112,256]{1,0:T(8,128)(2,1)S(1)}, u32[]{:S(2)}) copy-start(bf16[112,256]{1,0:T(8,128)(2,1)S(1)} %pad_maximum_fusion.refs_8_) | copy-start | bytes 172036
  5.5 10.8 %collective-permute-start.6 = (bf16[112,256]{1,0:T(8,128)(2,1)S(1)}, bf16[112,256]{1,0:T(8,128)(2,1)S(1)}, u32[]{:S(2)}, u32[]{:S(2)}) collective-permute-start(bf16[112,256]{1,0:T(8,128)(2,1)S(1)} %pad_maximum_fusion.refs_8_), channel_id=1, source_target_pairs={{0,4},{4,0},{8,12},{12,8},{1,5},{5,1},{9,13},{13,9},{2,6},{6,2},{1... | collective-permute-start | bytes 172040 | tf_op jit(solution)/shard_map/ppermute | solution.py:27
  5.6 10.0 %collective-permute-start.7 = (bf16[112,256]{1,0:T(8,128)(2,1)S(1)}, bf16[112,256]{1,0:T(8,128)(2,1)S(1)}, u32[]{:S(2)}, u32[]{:S(2)}) collective-permute-start(bf16[112,256]{1,0:T(8,128)(2,1)S(1)} %pad_maximum_fusion.refs_8_), channel_id=1, source_target_pairs={{0,8},{4,12},{8,0},{12,4},{1,9},{5,13},{9,1},{13,5},{2,10},{6,14},... | collective-permute-start | bytes 172040 | tf_op jit(solution)/shard_map/ppermute | solution.py:27
  15.6 19.9 %copy-start.7 = (bf16[112,256]{1,0:T(8,128)(2,1)}, bf16[112,256]{1,0:T(8,128)(2,1)S(1)}, u32[]{:S(2)}) copy-start(bf16[112,256]{1,0:T(8,128)(2,1)S(1)} %collective-permute-done.7.refs_10_) | copy-start | bytes 172036
  16.2 19.3 %copy-start.6 = (bf16[112,256]{1,0:T(8,128)(2,1)}, bf16[112,256]{1,0:T(8,128)(2,1)S(1)}, u32[]{:S(2)}) copy-start(bf16[112,256]{1,0:T(8,128)(2,1)S(1)} %collective-permute-done.6.refs_9_) | copy-start | bytes 172036
  16.8 1.3 %collective-permute-start.8 = (bf16[112,256]{1,0:T(8,128)(2,1)S(1)}, bf16[112,256]{1,0:T(8,128)(2,1)S(1)}, u32[]{:S(2)}, u32[]{:S(2)}) collective-permute-start(bf16[112,256]{1,0:T(8,128)(2,1)S(1)} %collective-permute-done.7.refs_10_), channel_id=1, source_target_pairs={{0,4},{4,0},{8,12},{12,8},{1,5},{5,1},{9,13},{13,9},{2,6},{6,2},{1... | collective-permute-start | bytes 172040 | tf_op jit(solution)/shard_map/ppermute | solution.py:27
  18.2 17.4 %copy-start.8 = (bf16[112,256]{1,0:T(8,128)(2,1)}, bf16[112,256]{1,0:T(8,128)(2,1)S(1)}, u32[]{:S(2)}) copy-start(bf16[112,256]{1,0:T(8,128)(2,1)S(1)} %collective-permute-done.8.refs_11_) | copy-start | bytes 172036
  19.6 1.9 %copy-start.2 = (bf16[32,7168]{1,0:T(8,128)(2,1)}, bf16[32,7168]{1,0:T(8,128)(2,1)S(1)}, u32[]{:S(2)}) copy-start(bf16[32,7168]{1,0:T(8,128)(2,1)S(1)} %collective-permute-done.1.refs_2_) | copy-start | bytes 1376260
  19.6 1.9 %collective-permute-start.2 = (bf16[32,7168]{1,0:T(8,128)(2,1)S(1)}, bf16[32,7168]{1,0:T(8,128)(2,1)S(1)}, u32[]{:S(2)}, u32[]{:S(2)}) collective-permute-start(bf16[32,7168]{1,0:T(8,128)(2,1)S(1)} %collective-permute-done.1.refs_2_), channel_id=1, source_target_pairs={{0,4},{4,0},{8,12},{12,8},{1,5},{5,1},{9,13},{13,9},{2,6},{6,2},{1... | collective-permute-start | bytes 1376264 | tf_op jit(solution)/shard_map/ppermute | solution.py:27
  20.6 0.9 %copy-start.1 = (bf16[32,7168]{1,0:T(8,128)(2,1)}, bf16[32,7168]{1,0:T(8,128)(2,1)S(1)}, u32[]{:S(2)}) copy-start(bf16[32,7168]{1,0:T(8,128)(2,1)S(1)} %collective-permute-done.refs_1_) | copy-start | bytes 1376260
  21.5 0.8 %copy-start.3 = (bf16[32,7168]{1,0:T(8,128)(2,1)}, bf16[32,7168]{1,0:T(8,128)(2,1)S(1)}, u32[]{:S(2)}) copy-start(bf16[32,7168]{1,0:T(8,128)(2,1)S(1)} %collective-permute-done.2.refs_3_) | copy-start | bytes 1376260
  26.3 9.3 %collective-permute-start.3 = (bf16[128,96]{1,0:T(8,128)(2,1)}, bf16[128,96]{1,0:T(8,128)(2,1)S(1)}, u32[]{:S(2)}, u32[]{:S(2)}) collective-permute-start(bf16[128,96]{1,0:T(8,128)(2,1)} %shard_map.147.refs_4_), channel_id=1, source_target_pairs={{0,4},{4,0},{8,12},{12,8},{1,5},{5,1},{9,13},{13,9},{2,6},{6,2},{1... | collective-permute-start | bytes 73736 | tf_op jit(solution)/shard_map/ppermute | solution.py:27
  26.4 9.1 %collective-permute-start.4 = (bf16[128,96]{1,0:T(8,128)(2,1)}, bf16[128,96]{1,0:T(8,128)(2,1)S(1)}, u32[]{:S(2)}, u32[]{:S(2)}) collective-permute-start(bf16[128,96]{1,0:T(8,128)(2,1)} %shard_map.147.refs_4_), channel_id=1, source_target_pairs={{0,8},{4,12},{8,0},{12,4},{1,9},{5,13},{9,1},{13,5},{2,10},{6,14},... | collective-permute-start | bytes 73736 | tf_op jit(solution)/shard_map/ppermute | solution.py:27
  28.2 7.4 %collective-permute-start.5 = (bf16[128,96]{1,0:T(8,128)(2,1)}, bf16[128,96]{1,0:T(8,128)(2,1)S(1)}, u32[]{:S(2)}, u32[]{:S(2)}) collective-permute-start(bf16[128,96]{1,0:T(8,128)(2,1)} %shard_map.147.refs_4_), channel_id=1, source_target_pairs={{0,12},{4,8},{8,4},{12,0},{1,13},{5,9},{9,5},{13,1},{2,14},{6,10},... | collective-permute-start | bytes 73736 | tf_op jit(solution)/shard_map/ppermute | solution.py:27
  35.5 0.6 copy-start.9
  35.6 0.6 copy-start.10
  35.6 0.6 copy-start.11
  40.8 5.8 %collective-permute-start.14 = (bf16[2,32,1792]{2,1,0:T(8,128)(2,1)S(1)}, bf16[2,32,1792]{2,1,0:T(8,128)(2,1)S(1)}, u32[]{:S(2)}, u32[]{:S(2)}) collective-permute-start(bf16[2,32,1792]{2,1,0:T(8,128)(2,1)S(1)} %get-tuple-element.27), channel_id=1, source_target_pairs={{0,4},{4,0},{8,12},{12,8},{1,5},{5,1},{9,13},{13,9},{2,6},{6,2},{1... | collective-permute-start | bytes 688136 | tf_op jit(solution)/shard_map/ppermute | solution.py:27
  41.2 5.3 %copy-start.5 = (bf16[2,2,32,1792]{3,2,1,0:T(8,128)(2,1)S(1)}, bf16[2,2,32,1792]{3,2,1,0:T(8,128)(2,1)}, u32[]{:S(2)}) copy-start(bf16[2,2,32,1792]{3,2,1,0:T(8,128)(2,1)} %get-tuple-element.19) | copy-start | bytes 1376260
  41.2 5.3 %collective-permute-start.16 = (bf16[2,32,1792]{2,1,0:T(8,128)(2,1)S(1)}, bf16[2,32,1792]{2,1,0:T(8,128)(2,1)S(1)}, u32[]{:S(2)}, u32[]{:S(2)}) collective-permute-start(bf16[2,32,1792]{2,1,0:T(8,128)(2,1)S(1)} %get-tuple-element.28), channel_id=1, source_target_pairs={{0,4},{4,0},{8,12},{12,8},{1,5},{5,1},{9,13},{13,9},{2,6},{6,2},{1... | collective-permute-start | bytes 688136 | tf_op jit(solution)/shard_map/ppermute | solution.py:27
  45.9 2.8 %collective-permute-start.9 = (bf16[2,32,1792]{2,1,0:T(8,128)(2,1)S(1)}, bf16[2,32,1792]{2,1,0:T(8,128)(2,1)S(1)}, u32[]{:S(2)}, u32[]{:S(2)}) collective-permute-start(bf16[2,32,1792]{2,1,0:T(8,128)(2,1)S(1)} %get-tuple-element.23), channel_id=1, source_target_pairs={{0,4},{4,0},{8,12},{12,8},{1,5},{5,1},{9,13},{13,9},{2,6},{6,2},{1... | collective-permute-start | bytes 688136 | tf_op jit(solution)/shard_map/ppermute | solution.py:27
  46.4 2.3 %collective-permute-start.11 = (bf16[2,32,1792]{2,1,0:T(8,128)(2,1)S(1)}, bf16[2,32,1792]{2,1,0:T(8,128)(2,1)S(1)}, u32[]{:S(2)}, u32[]{:S(2)}) collective-permute-start(bf16[2,32,1792]{2,1,0:T(8,128)(2,1)S(1)} %get-tuple-element.24), channel_id=1, source_target_pairs={{0,4},{4,0},{8,12},{12,8},{1,5},{5,1},{9,13},{13,9},{2,6},{6,2},{1... | collective-permute-start | bytes 688136 | tf_op jit(solution)/shard_map/ppermute | solution.py:27
  46.6 6.0 %collective-permute-start.17 = (bf16[1,32,1792]{2,1,0:T(8,128)(2,1)S(1)}, bf16[1,32,1792]{2,1,0:T(8,128)(2,1)S(1)}, u32[]{:S(2)}, u32[]{:S(2)}) collective-permute-start(bf16[1,32,1792]{2,1,0:T(8,128)(2,1)S(1)} %get-tuple-element.26), channel_id=1, source_target_pairs={{0,8},{4,12},{8,0},{12,4},{1,9},{5,13},{9,1},{13,5},{2,10},{6,14},... | collective-permute-start | bytes 344072 | tf_op jit(solution)/shard_map/ppermute | solution.py:27
  48.4 11.9 %collective-permute-start.15 = (bf16[1,32,1792]{2,1,0:T(8,128)(2,1)S(1)}, bf16[1,32,1792]{2,1,0:T(8,128)(2,1)S(1)}, u32[]{:S(2)}, u32[]{:S(2)}) collective-permute-start(bf16[1,32,1792]{2,1,0:T(8,128)(2,1)S(1)} %get-tuple-element.25), channel_id=1, source_target_pairs={{0,8},{4,12},{8,0},{12,4},{1,9},{5,13},{9,1},{13,5},{2,10},{6,14},... | collective-permute-start | bytes 344072 | tf_op jit(solution)/shard_map/ppermute | solution.py:27
  49.7 7.8 %collective-permute-start.12 = (bf16[1,32,1792]{2,1,0:T(8,128)(2,1)S(1)}, bf16[1,32,1792]{2,1,0:T(8,128)(2,1)S(1)}, u32[]{:S(2)}, u32[]{:S(2)}) collective-permute-start(bf16[1,32,1792]{2,1,0:T(8,128)(2,1)S(1)} %get-tuple-element.22), channel_id=1, source_target_pairs={{0,8},{4,12},{8,0},{12,4},{1,9},{5,13},{9,1},{13,5},{2,10},{6,14},... | collective-permute-start | bytes 344072 | tf_op jit(solution)/shard_map/ppermute | solution.py:27
  51.5 11.5 %collective-permute-start.10 = (bf16[1,32,1792]{2,1,0:T(8,128)(2,1)S(1)}, bf16[1,32,1792]{2,1,0:T(8,128)(2,1)S(1)}, u32[]{:S(2)}, u32[]{:S(2)}) collective-permute-start(bf16[1,32,1792]{2,1,0:T(8,128)(2,1)S(1)} %get-tuple-element.21), channel_id=1, source_target_pairs={{0,8},{4,12},{8,0},{12,4},{1,9},{5,13},{9,1},{13,5},{2,10},{6,14},... | collective-permute-start | bytes 344072 | tf_op jit(solution)/shard_map/ppermute | solution.py:27
  52.7 7.6 %collective-permute-start.18 = (bf16[32,1792]{1,0:T(8,128)(2,1)S(1)}, bf16[32,1792]{1,0:T(8,128)(2,1)S(1)}, u32[]{:S(2)}, u32[]{:S(2)}) collective-permute-start(bf16[32,1792]{1,0:T(8,128)(2,1)S(1)} %fusion.13), channel_id=1, source_target_pairs={{0,1},{1,0},{2,3},{3,2},{4,5},{5,4},{6,7},{7,6},{8,9},{9,8},{10,11... | collective-permute-start | bytes 344072 | tf_op jit(solution)/shard_map/ppermute | solution.py:27
  58.5 5.9 %collective-permute-start.13 = (bf16[32,1792]{1,0:T(8,128)(2,1)S(1)}, bf16[32,1792]{1,0:T(8,128)(2,1)S(1)}, u32[]{:S(2)}, u32[]{:S(2)}) collective-permute-start(bf16[32,1792]{1,0:T(8,128)(2,1)S(1)} %fusion.11), channel_id=1, source_target_pairs={{0,1},{1,0},{2,3},{3,2},{4,5},{5,4},{6,7},{7,6},{8,9},{9,8},{10,11... | collective-permute-start | bytes 344072 | tf_op jit(solution)/shard_map/ppermute | solution.py:27
  60.4 7.4 %collective-permute-start.19 = (bf16[32,1792]{1,0:T(8,128)(2,1)S(1)}, bf16[32,1792]{1,0:T(8,128)(2,1)S(1)}, u32[]{:S(2)}, u32[]{:S(2)}) collective-permute-start(bf16[32,1792]{1,0:T(8,128)(2,1)S(1)} %fusion.2), channel_id=1, source_target_pairs={{0,2},{1,3},{2,0},{3,1},{4,6},{5,7},{6,4},{7,5},{8,10},{9,11},{10,... | collective-permute-start | bytes 344072 | tf_op jit(solution)/shard_map/ppermute | solution.py:27

commit v3 on v0

v3 whole, which is shorter than its diff:
```python
import functools

import jax
import jax.numpy as jnp
from jax import lax
from jax.experimental import pallas as pl
from jax.experimental.pallas import tpu as pltpu
from jax.sharding import PartitionSpec as P

F32 = jnp.float32
BF16 = jnp.bfloat16
MIB = 1024 * 1024


def params(mebibytes):
    return pltpu.CompilerParams(vmem_limit_bytes=mebibytes * MIB)


def cost(flops, moved):
    return pl.CostEstimate(flops=int(flops), bytes_accessed=int(moved), transcendentals=0)


def in_vmem(value):
    return pltpu.with_memory_space_constraint(value, pltpu.VMEM)


def in_hbm(value):
    return pltpu.with_memory_space_constraint(value, pltpu.HBM)


def vmem_shape(value):
    return pltpu.VMEM(value.shape, value.dtype)


VMEM_SPEC = pl.BlockSpec(memory_space=pltpu.VMEM)
HBM_SPEC = pl.BlockSpec(memory_space=pltpu.HBM)
SMEM_SPEC = pl.BlockSpec(memory_space=pltpu.SMEM)


def swap(value, bits, axis="expert"):
    count = lax.axis_size(axis)
    return lax.ppermute(value, axis, [(i, i ^ bits) for i in range(count)])


def add(one, other):
    return (one.astype(F32) + other.astype(F32)).astype(BF16)


def exchange_all(values, after):
    count = lax.axis_size("expert")
    bit = count // 2
    arrived = [swap(value, bit) for value in values]
    arrived, after = lax.optimization_barrier((arrived, after))
    pieces = {0: values, bit: arrived}
    bit //= 2
    while bit >= 1:
        for r, piece in list(pieces.items()):
            pieces[r ^ bit] = [swap(value, bit) for value in piece]
        bit //= 2
    return *zip(*[pieces[r] for r in range(count)]), after


def tile_of(width):
    return 256 if width % 256 == 0 else 128


def pack_kernel(experts, ids, values, tenants, shared_b, store_b, pack):
    shared_count, width = shared_b.shape
    store_count = store_b.shape[0]
    count, top = ids.shape
    pack[:shared_count] = shared_b[...]
    pack[shared_count : shared_count + store_count] = store_b[...]
    lane = lax.broadcasted_iota(jnp.int32, (count, width), 1)
    expert = lane % experts
    weight = jnp.zeros((count, width), F32)
    for k in range(top):
        weight = weight + jnp.where(ids[:, k : k + 1] == expert, values[:, k : k + 1], 0.0)
    first = weight.astype(BF16).astype(F32)
    second = (weight - first).astype(BF16).astype(F32)
    third = weight - first - second
    meta = jnp.where(lane < experts, first, jnp.where(lane < 2 * experts, second, third))
    meta = jnp.where(lane < 3 * experts, meta, tenants[...].astype(F32))
    pack[shared_count + store_count :] = meta.astype(BF16)


def make_pack(experts, ids, values, tenants, shared_b, store_b):
    rows = ids.shape[0] + shared_b.shape[0] + store_b.shape[0]
    return pl.pallas_call(
        functools.partial(pack_kernel, experts),
        in_specs=[VMEM_SPEC] * 5,
        out_specs=VMEM_SPEC,
        out_shape=jax.ShapeDtypeStruct((rows, shared_b.shape[1]), BF16),
        compiler_params=params(4),
        cost_estimate=cost(1e5, 2e5),
    )(ids, values, tenants, shared_b, store_b)


def first_kernel(pieces, rows, gate_weight, up_weight, *refs):
    staged = len(refs) // 2 - 3
    sources = refs[:staged]
    gate, up = refs[staged : staged + 2]
    targets = refs[staged + 2 : 2 * staged + 2]
    gate_held, up_held, sems, staged_sems = refs[2 * staged + 2 :]
    depth, width = gate_weight.shape
    chunk = depth // pieces
    copies = []
    for k in range(pieces):
        part = pl.ds(k * chunk, chunk)
        pair = [
            pltpu.make_async_copy(gate_weight.at[part], gate_held.at[part], sems.at[0, k]),
            pltpu.make_async_copy(up_weight.at[part], up_held.at[part], sems.at[1, k]),
        ]
        for copy in pair:
            copy.start()
        copies.append(pair)
    staging = []
    for n in range(staged):
        size = sources[n].shape[0] // STAGE_PIECES
        for k in range(STAGE_PIECES):
            part = pl.ds(k * size, size)
            copy = pltpu.make_async_copy(
                sources[n].at[part], targets[n].at[part], staged_sems.at[n, k]
            )
            copy.start()
            staging.append(copy)
    total_gate = jnp.zeros(gate.shape, F32)
    total_up = jnp.zeros(up.shape, F32)
    for k in range(pieces):
        part = pl.ds(k * chunk, chunk)
        for copy in copies[k]:
            copy.wait()
        block = rows[:, part]
        total_gate += jnp.dot(block, gate_held[part], preferred_element_type=F32)
        total_up += jnp.dot(block, up_held[part], preferred_element_type=F32)
    gate[...] = total_gate
    up[...] = total_up
    for copy in staging:
        copy.wait()


STAGE_PIECES = 4


def first_products(rows, gate_weight, up_weight, weights):
    depth, width = gate_weight.shape
    pieces = 7
    out = jax.ShapeDtypeStruct((rows.shape[0], width), F32)
    moved = 2 * depth * width * (2 + len(weights))
    return pl.pallas_call(
        functools.partial(first_kernel, pieces),
        in_specs=[VMEM_SPEC] + [HBM_SPEC] * (2 + len(weights)),
        out_specs=[VMEM_SPEC] * (2 + len(weights)),
        out_shape=[out, out] + [vmem_shape(w) for w in weights],
        scratch_shapes=[
            pltpu.VMEM((depth, width), BF16),
            pltpu.VMEM((depth, width), BF16),
            pltpu.SemaphoreType.DMA((2, pieces)),
            pltpu.SemaphoreType.DMA((len(weights), STAGE_PIECES)),
        ],
        compiler_params=params(12),
        cost_estimate=cost(4 * rows.shape[0] * depth * width, moved),
    )(in_vmem(rows), *[in_hbm(w) for w in (gate_weight, up_weight, *weights)])


def inner_kernel(count, chunk, *refs):
    rows, factor_shared, factor_store, inner = refs[:count], *refs[count:]
    depth = factor_shared.shape[1]
    size = rows[0].shape[0]
    split = factor_shared.shape[0]
    width = split + factor_store.shape[0]
    total = jnp.zeros((count * size, width), F32)
    for k in range(depth // chunk):
        part = pl.ds(k * chunk, chunk)
        block = jnp.concatenate([ref[:, part] for ref in rows], axis=0)
        factors = jnp.concatenate([factor_shared[:, part], factor_store[:, part]], axis=0)
        total += lax.dot_general(
            block, factors, (((1,), (1,)), ((), ())), preferred_element_type=F32
        )
    inner[...] = total.astype(BF16)


def inner_products(rows, factor_shared, factor_store):
    depth = factor_shared.shape[1]
    total = rows[0].shape[0] * len(rows)
    width = factor_shared.shape[0] + factor_store.shape[0]
    return pl.pallas_call(
        functools.partial(inner_kernel, len(rows), 1024),
        in_specs=[VMEM_SPEC] * (len(rows) + 2),
        out_specs=VMEM_SPEC,
        out_shape=jax.ShapeDtypeStruct((total, width), BF16),
        compiler_params=params(12),
        cost_estimate=cost(2 * total * depth * width, 2 * depth * width),
    )(*[in_vmem(x) for x in (*rows, factor_shared, factor_store)])


def gate_up_kernel(count, chunk, *refs):
    rows, gate_weight, up_weight, gate, up = refs[:count], *refs[count:]
    depth = gate_weight.shape[0]
    total_gate = jnp.zeros(gate.shape, F32)
    total_up = jnp.zeros(up.shape, F32)
    for k in range(depth // chunk):
        part = pl.ds(k * chunk, chunk)
        block = jnp.concatenate([ref[:, part] for ref in rows], axis=0)
        total_gate += jnp.dot(block, gate_weight[part], preferred_element_type=F32)
        total_up += jnp.dot(block, up_weight[part], preferred_element_type=F32)
    gate[...] = total_gate
    up[...] = total_up


def gate_up(rows, gate_weight, up_weight):
    depth, width = gate_weight.shape
    total = rows[0].shape[0] * len(rows)
    out = jax.ShapeDtypeStruct((total, width), F32)
    return pl.pallas_call(
        functools.partial(gate_up_kernel, len(rows), 1024),
        in_specs=[VMEM_SPEC] * (len(rows) + 2),
        out_specs=[VMEM_SPEC] * 2,
        out_shape=[out, out],
        compiler_params=params(12),
        cost_estimate=cost(4 * total * depth * width, 4 * depth * width),
    )(*[in_vmem(x) for x in (*rows, gate_weight, up_weight)])


def silu(value):
    return value / (1.0 + jnp.exp(-value))


def down_kernel(count, shared_count, store_count, experts, adapted, chunks, order, *refs):
    place, pair_slot, gate, up, gate_own, up_own = refs[:6]
    inner = refs[6 : 6 + count]
    packs = refs[6 + count : 6 + 2 * count]
    down, down_own = refs[6 + 2 * count : 8 + 2 * count]
    outs = refs[8 + 2 * count :]
    own, own_part = place[0], place[1]
    total, hid = gate.shape
    size = total // count
    half = count // 2
    width = shared_count + store_count
    tenants = pair_slot.shape[1]

    meta = jnp.concatenate([ref[width:] for ref in packs], axis=0).astype(F32)
    lane = lax.broadcasted_iota(jnp.int32, meta.shape, 1)
    mine = (lane < 3 * experts) & (lane % experts == own)
    share = jnp.sum(jnp.where(mine, meta, 0.0), axis=1, keepdims=True)
    row_tenant = jnp.sum(jnp.where(lane == 3 * experts, meta, 0.0), axis=1, keepdims=True)
    row_tenant = row_tenant.astype(jnp.int32)

    column = lax.broadcasted_iota(jnp.int32, (1, count * shared_count), 1)
    rank = store_count // adapted
    own_tenants = shared_count // rank
    shared_tenant = (own ^ (column // shared_count)) * own_tenants + (column % shared_count) // rank
    column = lax.broadcasted_iota(jnp.int32, (1, count * store_count), 1)
    slot = (own ^ (column // store_count)) * adapted + (column % store_count) // rank
    slot_tenant = jnp.full(slot.shape, -1, jnp.int32)
    for t in range(tenants):
        slot_tenant = jnp.where(slot == pair_slot[own, t], t, slot_tenant)

    parts, parts_own = [], []
    for r in range(count):
        held = inner[r][...]
        blocks = [held[(k ^ r) * size : ((k ^ r) + 1) * size] for k in range(count)]
        parts.append(jnp.concatenate(blocks, axis=0)[:, shared_count:])
        parts_own.append(blocks[0][:, :shared_count])
    lifted = jnp.concatenate(parts, axis=1)
    lifted_own = jnp.concatenate(parts_own, axis=1)
    zero = jnp.zeros((), BF16)
    lifted = jnp.where(row_tenant == slot_tenant, lifted, zero)
    lifted_own = jnp.where(row_tenant[:size] == shared_tenant, lifted_own, zero)
    factor = jnp.concatenate([ref[shared_count:width] for ref in packs], axis=0)
    factor_own = jnp.concatenate([ref[:shared_count] for ref in packs], axis=0)
    upward = up[...] + jnp.dot(lifted, factor, preferred_element_type=F32)
    hidden = (silu(gate[...]) * upward).astype(BF16)
    upward_own = up_own[...] + jnp.dot(lifted_own, factor_own, preferred_element_type=F32)
    hidden_own = (silu(gate_own[...]) * upward_own).astype(BF16)

    part = outs[0].shape[-1]
    tile = tile_of(part)
    for n, chunk in enumerate(chunks):
        keep, send = outs[2 * n : 2 * n + 2]
        for place_in, j in enumerate(chunk):
            start = (own_part ^ j) * part
            for c in range(part // tile):
                columns = pl.ds(pl.multiple_of(start + c * tile, tile), tile)
                routed = jnp.dot(hidden, down[:, columns], preferred_element_type=F32) * share
                shared = jnp.dot(hidden_own, down_own[:, columns], preferred_element_type=F32)
                for at, r in enumerate(order):
                    block = routed[r * size : (r + 1) * size]
                    if r == 0:
                        block = block + shared
                    target, row = (keep, at) if at < half else (send, at - half)
                    target[row, place_in, :, c * tile : (c + 1) * tile] = block.astype(BF16)


def down_products(
    place, pair_slot, gate, up, gate_own, up_own, inner, packs, down, down_own, experts,
    adapted, chunks, order, shared_count, store_count, parts,
):
    count = len(inner)
    total, hid = gate.shape
    size = total // count
    depth = down.shape[1]
    part = depth // parts
    whole = [gate, up, gate_own, up_own, *inner, *packs, down, down_own]
    outs = []
    for chunk in chunks:
        outs += [jax.ShapeDtypeStruct((count // 2, len(chunk), size, part), BF16)] * 2
    return pl.pallas_call(
        functools.partial(
            down_kernel, count, shared_count, store_count, experts, adapted, chunks, order
        ),
        in_specs=[SMEM_SPEC] * 2 + [VMEM_SPEC] * len(whole),
        out_specs=[VMEM_SPEC] * len(outs),
        out_shape=outs,
        compiler_params=params(16),
        cost_estimate=cost(2 * (total + size) * depth * hid, 4 * depth * hid),
    )(place, pair_slot, *[in_vmem(x) for x in whole])


def local(
    tokens,
    expert_ids,
    gate_values,
    tenant_ids,
    w_gate,
    w_up,
    routed_down_weight,
    shared_gate,
    shared_up,
    shared_down,
    store_a,
    store_b,
    pair_slot,
    shared_a,
    shared_b,
):
    experts = pair_slot.shape[0]
    adapted, rank, model_width = store_a.shape
    own_tenants = shared_a.shape[0]
    hid = store_b.shape[2]
    steps, size, top_count = expert_ids.shape
    count = lax.axis_size("expert")
    n_tensor = lax.axis_size("tensor")
    own = lax.axis_index("expert")
    shared_count, store_count = own_tenants * rank, adapted * rank

    rows_own = tokens.reshape(steps * size, model_width)
    pack = make_pack(
        experts,
        expert_ids.reshape(steps * size, top_count),
        gate_values.reshape(steps * size, top_count),
        jnp.tile(tenant_ids[:, None], (steps, 1)),
        shared_b.reshape(shared_count, hid),
        store_b.reshape(store_count, hid),
    )
    rows_first, pack = lax.optimization_barrier((rows_own, pack))
    first = first_products(
        rows_first, shared_gate, shared_up, [w_gate[0], w_up[0], routed_down_weight[0], shared_down]
    )
    rows, packs, first = exchange_all([rows_own, pack], first)
    gate_own, up_own, gate_weight, up_weight, down, down_own = first
    inner = inner_products(
        rows,
        shared_a.reshape(shared_count, model_width),
        store_a.reshape(store_count, model_width),
    )
    inners = [inner] + [swap(inner, r) for r in range(1, count)]
    gate, up = gate_up(rows, gate_weight, up_weight)

    order = [0]
    bit = count // 2
    while bit >= 1:
        order = order + [r | bit for r in order]
        bit //= 2
    chunks = [[j] for j in range(n_tensor - 1, 1, -1)] + [[1, 0]]
    place = jnp.stack([own, lax.axis_index("tensor")]).astype(jnp.int32)
    outs = down_products(
        place, pair_slot, gate, up, gate_own, up_own, inners, packs, down, down_own, experts,
        adapted, chunks, order, shared_count, store_count, n_tensor,
    )
    arrived_parts = []
    for n, chunk in enumerate(chunks):
        held, leaving = outs[2 * n : 2 * n + 2]
        bit = 1
        while bit < count:
            arrived = swap(leaving, bit)
            half = held.shape[0] // 2
            leaving = add(held[half:], arrived[half:])
            held = add(held[:half], arrived[:half])
            bit *= 2
        for place_in, j in enumerate(chunk):
            value = leaving[0, place_in]
            arrived_parts.append(swap(value, j, "tensor") if j else value)
    total = sum(value.astype(F32) for value in arrived_parts)
    return total.astype(BF16).reshape(steps, size, model_width // n_tensor)


def solution(mesh):
    return jax.shard_map(
        local,
        mesh=mesh,
        in_specs=(
            P(None, ("groups", "expert"), None),
            P(None, ("groups", "expert"), None),
            P(None, ("groups", "expert"), None),
            P(("groups", "expert")),
            P("expert", None, "tensor"),
            P("expert", None, "tensor"),
            P("expert", "tensor", None),
            P(None, "tensor"),
            P(None, "tensor"),
            P("tensor", None),
            P("expert", None, None),
            P("expert", None, "tensor"),
            P(),
            P("expert", None, None),
            P("expert", None, "tensor"),
        ),
        out_specs=P(None, ("groups", "expert"), "tensor"),
        check_vma=False,
    )
```

time: 189 us -> 58.5 us (0.31)
  matrix products: 52.6 us -> 0 us
  waiting for transfers between devices: 63.4 us -> 11.3 us
  between operations: 13.5 us -> 0.22 us
  Pallas kernels: 0 us -> 11.5 us
  starting transfers between devices: 29.1 us -> 17.7 us
  blocking collectives: 6.46 us -> 0 us
  other arithmetic: 5.88 us -> 1.09 us
    dot_general x26 -> x0, matrix products: 52.6 us -> none  [the longest x4 11.4 us: feed_forward(): return jnp.dot(hidden, down_weight, preferred_element_type=jnp.float32)]
    reduce_scatter x2 -> x0, waiting for transfers between devices: 33.8 us -> none  [local(): lax.psum_scatter(jnp.concatenate([routed_terms, shared_terms], axis=0).as...]
    all_to_all x8 -> x0, starting transfers between devices: 28.9 us -> none  [the longest x2 7.75 us: local(): lax.all_to_all(outgoing, 'expert', split_axis=0, concat_axis=0, tiled=True)]
    all_to_all x8 -> x0, waiting for transfers between devices: 28.8 us -> none  [the longest x2 17.8 us: local(): lax.all_to_all(outgoing, 'expert', split_axis=0, concat_axis=0, tiled=True)]
    ppermute x0 -> x18, starting transfers between devices: none -> 17.7 us  [swap(): return lax.ppermute(value, axis, [(i, i ^ bits) for i in range(count)])]
    pallas_call x0 -> x5, Pallas kernels: none -> 11.5 us  [the longest x1 7.69 us: first_products(): pl.pallas_call(functools.partial(first_kernel, pieces), in_specs=[VMEM_SP...]
    ppermute x0 -> x18, waiting for transfers between devices: none -> 11.3 us  [swap(): return lax.ppermute(value, axis, [(i, i ^ bits) for i in range(count)])]
    unnamed x60 -> x30, local copies, waits for them, and re-layouts: 4.08 us -> 14 us
  transfers between devices with their start and end apart: 11 -> 18, of which waited for: 7 -> 6; matrix products, arithmetic and copies ran while one was open for 32% -> 5% of each run, Pallas kernels for 0% -> 16%
where the time goes in v3:
time: 58.5 us; the launch traced here: 58.1 us
  starting transfers between devices  17.7 us (30%)
  local copies, waits for them, and re-layouts  16.3 us (28%)
  Pallas kernels  11.5 us (20%)
  waiting for transfers between devices  11.3 us (19%)
  other arithmetic  1.09 us (2%)
    ppermute x18, starting transfers between devices, swap(): return lax.ppermute(value, axis, [(i, i ^ bits) for i in range(count)])  17.7 us
    unnamed x30, local copies, waits for them, and re-layouts  14 us
    ppermute x18, waiting for transfers between devices, swap(): return lax.ppermute(value, axis, [(i, i ^ bits) for i in range(count)])  11.3 us
    pallas_call x1, Pallas kernels, first_products(): pl.pallas_call(functools.partial(first_kernel, pieces), in_specs=[VMEM_SP...  7.69 us
    pallas_call x1, Pallas kernels, down_products(): pl.pallas_call(functools.partial(down_kernel, count, shared_count, store_...  2.03 us
  transfers between devices with their start and end apart: 18, of which 6 were waited for; matrix products, arithmetic and copies ran while one was open for 5% of the time, Pallas kernels for 16%

profile of v3, /device:TPU:0, one launch (start us, length us, event | category | flops | bytes accessed | tf_op | source)
XLA Modules:
  0.0 58.1 jit_solution(4260880118568958052)
XLA Ops:
  0.0 3.0 %collective-permute-start.1 = (bf16[32,7168]{1,0:T(8,128)(2,1)}, bf16[32,7168]{1,0:T(8,128)(2,1)S(1)}, u32[]{:S(2)}, u32[]{:S(2)}) collective-permute-start(bf16[32,7168]{1,0:T(8,128)(2,1)} %bitcast.24), channel_id=1, source_target_pairs={{0,8},{4,12},{8,0},{12,4},{1,9},{5,13},{9,1},{13,5},{2,10},{6,14},... | collective-permute-start | bytes 1376264 | tf_op jit(solution)/shard_map/ppermute | solution.py:42
  3.0 0.8 %copy.21 = s32[2,16,2]{2,1,0:T(8,128)S(1)} copy(s32[2,16,2]{1,2,0:T(2,128)} %param.16) | data formatting | bytes 512 | tf_op jit(solution)/shard_map/reshape | solution.py:349
  3.7 0.8 %copy.22 = f32[2,16,2]{2,1,0:T(8,128)S(1)} copy(f32[2,16,2]{1,2,0:T(2,128)} %param.17) | data formatting | bytes 512 | tf_op jit(solution)/shard_map/reshape | solution.py:350
  4.5 0.7 %tile.8 = s32[2,16]{1,0:T(2,128)S(1)} broadcast(s32[16]{0:T(128)} %param.18), dimensions={1} | broadcast | bytes 192 | tf_op jit(solution)/shard_map/tile | solution.py:351
  5.2 0.8 %copy-done.12 = bf16[4,16,256]{2,1,0:T(8,128)(2,1)S(1)} copy-done((bf16[4,16,256]{2,1,0:T(8,128)(2,1)S(1)}, bf16[4,16,256]{2,1,0:T(8,128)(2,1)}, u32[]{:S(2)}) %copy-start.12) | copy-done | bytes 32792
  6.0 0.7 %copy-done.13 = bf16[2,16,256]{2,1,0:T(8,128)(2,1)S(1)} copy-done((bf16[2,16,256]{2,1,0:T(8,128)(2,1)S(1)}, bf16[2,16,256]{2,1,0:T(8,128)(2,1)}, u32[]{:S(2)}) %copy-start.13) | copy-done | bytes 16408
  7.0 1.0 %copy-done = bf16[2,16,7168]{2,1,0:T(8,128)(2,1)S(1)} copy-done((bf16[2,16,7168]{2,1,0:T(8,128)(2,1)S(1)}, bf16[2,16,7168]{2,1,0:T(8,128)(2,1)}, u32[]{:S(2)}) %copy-start) | copy-done | bytes 458776
  8.0 7.7 %shard_map.146 = (f32[32,256]{1,0:T(8,128)S(1)}, f32[32,256]{1,0:T(8,128)S(1)}, bf16[7168,256]{1,0:T(8,128)(2,1)S(1)}, bf16[7168,256]{1,0:T(8,128)(2,1)S(1)}, bf...) custom-call(bf16[32,7168]{1,0:T(8,128)(2,1)S(1)} %bitcast.26, bf16[7168,256]{1,0:T(8,128)(2,1)} %gate_weight.1, ...), custom_call_target="tpu_custom_call" | custom-call | flops 234881024 | bytes 22020096 | tf_op jit(solution)/shard_map/pallas_call | solution.py:149
  15.7 1.8 %copy-done.2 = bf16[256,7168]{1,0:T(8,128)(2,1)} copy-done((bf16[256,7168]{1,0:T(8,128)(2,1)}, bf16[256,7168]{1,0:T(8,128)(2,1)S(1)}, u32[]{:S(2)}) %copy-start.2) | copy-done | bytes 3670040
  17.5 1.8 %copy-done.4 = bf16[256,7168]{1,0:T(8,128)(2,1)} copy-done((bf16[256,7168]{1,0:T(8,128)(2,1)}, bf16[256,7168]{1,0:T(8,128)(2,1)S(1)}, u32[]{:S(2)}) %copy-start.4) | copy-done | bytes 3670040
  19.3 1.9 %copy-done.6 = bf16[7168,256]{1,0:T(8,128)(2,1)} copy-done((bf16[7168,256]{1,0:T(8,128)(2,1)}, bf16[7168,256]{1,0:T(8,128)(2,1)S(1)}, u32[]{:S(2)}) %copy-start.6) | copy-done | bytes 3670040
  21.2 1.9 %copy-done.8 = bf16[7168,256]{1,0:T(8,128)(2,1)} copy-done((bf16[7168,256]{1,0:T(8,128)(2,1)}, bf16[7168,256]{1,0:T(8,128)(2,1)S(1)}, u32[]{:S(2)}) %copy-start.8) | copy-done | bytes 3670040
  23.1 0.5 collective-permute-start.3
  24.2 0.9 %collective-permute-done.3.refs_3_ = bf16[32,7168]{1,0:T(8,128)(2,1)S(1)} collective-permute-done((bf16[32,7168]{1,0:T(8,128)(2,1)S(1)}, bf16[32,7168]{1,0:T(8,128)(2,1)S(1)}, u32[]{:S(2)}, u32[]{:S(2)}) %collective-permute-start.3) | collective-permute-done | bytes 458784 | tf_op jit(solution)/shard_map/ppermute | solution.py:42
  25.1 0.6 %shard_map.148.refs_6_ = bf16[128,96]{1,0:T(8,128)(2,1)S(1)} custom-call(bf16[32,7168]{1,0:T(8,128)(2,1)S(1)} %bitcast.27, bf16[32,7168]{1,0:T(8,128)(2,1)S(1)} %collective-permute-done.refs_1_, bf16[32,7168]{1,0:T(8,128)(2,1)S(1)} %collective-permute-done.1.refs_2_, bf16[32,7168]{1,0:T(8,128)(2,1)S(1)} %collective-permute-done.3.refs_3_, ...), custom_call_target="tpu_custom_call" | custom-call | flops 176160768 | bytes 1376256 | tf_op jit(solution)/shard_map/pallas_call | solution.py:186
  26.2 1.9 %collective-permute-start.5 = (bf16[128,96]{1,0:T(8,128)(2,1)S(1)}, bf16[128,96]{1,0:T(8,128)(2,1)S(1)}, u32[]{:S(2)}, u32[]{:S(2)}) collective-permute-start(bf16[128,96]{1,0:T(8,128)(2,1)S(1)} %shard_map.148.refs_6_), channel_id=1, source_target_pairs={{0,8},{4,12},{8,0},{12,4},{1,9},{5,13},{9,1},{13,5},{2,10},{6,14},... | collective-permute-start | bytes 73736 | tf_op jit(solution)/shard_map/ppermute | solution.py:42
  28.1 2.0 %copy-done.7 = bf16[7168,256]{1,0:T(8,128)(2,1)S(1)} copy-done((bf16[7168,256]{1,0:T(8,128)(2,1)S(1)}, bf16[7168,256]{1,0:T(8,128)(2,1)}, u32[]{:S(2)}) %copy-start.7) | copy-done | bytes 3670040
  30.2 2.0 %copy-done.9 = bf16[7168,256]{1,0:T(8,128)(2,1)S(1)} copy-done((bf16[7168,256]{1,0:T(8,128)(2,1)S(1)}, bf16[7168,256]{1,0:T(8,128)(2,1)}, u32[]{:S(2)}) %copy-start.9) | copy-done | bytes 3670040
  32.2 1.1 %shard_map.147 = (f32[128,256]{1,0:T(8,128)S(1)}, f32[128,256]{1,0:T(8,128)S(1)}) custom-call(bf16[32,7168]{1,0:T(8,128)(2,1)S(1)} %bitcast.28, bf16[32,7168]{1,0:T(8,128)(2,1)S(1)} %collective-permute-done.refs_1_, bf16[32,7168]{1,0:T(8,128)(2,1)S(1)} %collective-permute-done.1.refs_2_, bf16[32,7168]{1,0:T(8,128)(2,1)S(1)} %collective-permute-done.3.refs_3_, ...), custom_call_target="tpu_custom_call" | custom-call | flops 939524096 | bytes 7340032 | tf_op jit(solution)/shard_map/pallas_call | solution.py:214
  33.4 2.0 %shard_map.149 = (bf16[2,1,32,1792]{3,2,1,0:T(8,128)(2,1)S(1)}, bf16[2,1,32,1792]{3,2,1,0:T(8,128)(2,1)S(1)}, bf16[2,1,32,1792]{3,2,1,0:T(8,128)(2,1)S(1)}, bf16...) custom-call(s32[2]{0:T(128)S(1)} %pad_add_fusion.refs_0_, ...), custom_call_target="tpu_custom_call" | custom-call | flops 587202560 | bytes 7340032 | tf_op jit(solution)/shard_map/pallas_call | solution.py:307
  36.2 0.8 %collective-permute-done.12 = bf16[2,1,32,1792]{3,2,1,0:T(8,128)(2,1)S(1)} collective-permute-done((bf16[2,1,32,1792]{3,2,1,0:T(8,128)(2,1)S(1)}, bf16[2,1,32,1792]{3,2,1,0:T(8,128)(2,1)S(1)}, u32[]{:S(2)}, u32[]{:S(2)}) %collective-permute-start.12) | collective-permute-done | bytes 229408 | tf_op jit(solution)/shard_map/ppermute | solution.py:42
  37.0 1.8 %collective-permute-start.13 = (bf16[1,1,32,1792]{3,2,1,0:T(8,128)(2,1)S(1)}, bf16[1,1,32,1792]{3,2,1,0:T(8,128)(2,1)S(1)}, u32[]{:S(2)}, u32[]{:S(2)}) collective-permute-start(bf16[1,1,32,1792]{3,2,1,0:T(8,128)(2,1)S(1)} %add_convert_fusion.4), channel_id=1, source_target_pairs={{0,8},{4,12},{8,0},{12,4},{1,9},{5,13},{9,1},{13,5},{2,10},{6,14},... | collective-permute-start | bytes 344072 | tf_op jit(solution)/shard_map/ppermute | solution.py:42
  38.9 1.0 %collective-permute-start.10 = (bf16[1,1,32,1792]{3,2,1,0:T(8,128)(2,1)S(1)}, bf16[1,1,32,1792]{3,2,1,0:T(8,128)(2,1)S(1)}, u32[]{:S(2)}, u32[]{:S(2)}) collective-permute-start(bf16[1,1,32,1792]{3,2,1,0:T(8,128)(2,1)S(1)} %add_convert_fusion.7), channel_id=1, source_target_pairs={{0,8},{4,12},{8,0},{12,4},{1,9},{5,13},{9,1},{13,5},{2,10},{6,14},... | collective-permute-start | bytes 344072 | tf_op jit(solution)/shard_map/ppermute | solution.py:42
  39.9 3.2 %collective-permute-done.13 = bf16[1,1,32,1792]{3,2,1,0:T(8,128)(2,1)S(1)} collective-permute-done((bf16[1,1,32,1792]{3,2,1,0:T(8,128)(2,1)S(1)}, bf16[1,1,32,1792]{3,2,1,0:T(8,128)(2,1)S(1)}, u32[]{:S(2)}, u32[]{:S(2)}) %collective-permute-start.13) | collective-permute-done | bytes 114720 | tf_op jit(solution)/shard_map/ppermute | solution.py:42
  43.1 2.9 %collective-permute-start.14 = (bf16[32,1792]{1,0:T(8,128)(2,1)S(1)}, bf16[32,1792]{1,0:T(8,128)(2,1)S(1)}, u32[]{:S(2)}, u32[]{:S(2)}) collective-permute-start(bf16[32,1792]{1,0:T(8,128)(2,1)S(1)} %fusion.2), channel_id=1, source_target_pairs={{0,2},{1,3},{2,0},{3,1},{4,6},{5,7},{6,4},{7,5},{8,10},{9,11},{10,... | collective-permute-start | bytes 344072 | tf_op jit(solution)/shard_map/ppermute | solution.py:42
  46.1 1.6 %collective-permute-start.16 = (bf16[1,2,32,1792]{3,2,1,0:T(8,128)(2,1)S(1)}, bf16[1,2,32,1792]{3,2,1,0:T(8,128)(2,1)S(1)}, u32[]{:S(2)}, u32[]{:S(2)}) collective-permute-start(bf16[1,2,32,1792]{3,2,1,0:T(8,128)(2,1)S(1)} %add_convert_fusion.1), channel_id=1, source_target_pairs={{0,8},{4,12},{8,0},{12,4},{1,9},{5,13},{9,1},{13,5},{2,10},{6,14},... | collective-permute-start | bytes 688136 | tf_op jit(solution)/shard_map/ppermute | solution.py:42
  47.7 1.4 %collective-permute-start.11 = (bf16[32,1792]{1,0:T(8,128)(2,1)S(1)}, bf16[32,1792]{1,0:T(8,128)(2,1)S(1)}, u32[]{:S(2)}, u32[]{:S(2)}) collective-permute-start(bf16[32,1792]{1,0:T(8,128)(2,1)S(1)} %fusion.1), channel_id=1, source_target_pairs={{0,3},{1,2},{2,1},{3,0},{4,7},{5,6},{6,5},{7,4},{8,11},{9,10},{10,... | collective-permute-start | bytes 344072 | tf_op jit(solution)/shard_map/ppermute | solution.py:42
  49.1 3.2 %collective-permute-done.16 = bf16[1,2,32,1792]{3,2,1,0:T(8,128)(2,1)S(1)} collective-permute-done((bf16[1,2,32,1792]{3,2,1,0:T(8,128)(2,1)S(1)}, bf16[1,2,32,1792]{3,2,1,0:T(8,128)(2,1)S(1)}, u32[]{:S(2)}, u32[]{:S(2)}) %collective-permute-start.16) | collective-permute-done | bytes 229408 | tf_op jit(solution)/shard_map/ppermute | solution.py:42
  52.5 1.6 %collective-permute-start.17 = (bf16[32,1792]{1,0:T(8,128)(2,1)S(1)}, bf16[32,1792]{1,0:T(8,128)(2,1)S(1)}, u32[]{:S(2)}, u32[]{:S(2)}) collective-permute-start(bf16[32,1792]{1,0:T(8,128)(2,1)S(1)} %slice_bitcast_fusion.1), channel_id=1, source_target_pairs={{0,1},{1,0},{2,3},{3,2},{4,5},{5,4},{6,7},{7,6},{8,9},{9,8},{10,11... | collective-permute-start | bytes 344072 | tf_op jit(solution)/shard_map/ppermute | solution.py:42
  54.1 1.4 %collective-permute-done.11 = bf16[32,1792]{1,0:T(8,128)(2,1)S(1)} collective-permute-done((bf16[32,1792]{1,0:T(8,128)(2,1)S(1)}, bf16[32,1792]{1,0:T(8,128)(2,1)S(1)}, u32[]{:S(2)}, u32[]{:S(2)}) %collective-permute-start.11) | collective-permute-done | bytes 114720 | tf_op jit(solution)/shard_map/ppermute | solution.py:42
  55.6 1.8 %collective-permute-done.17 = bf16[32,1792]{1,0:T(8,128)(2,1)S(1)} collective-permute-done((bf16[32,1792]{1,0:T(8,128)(2,1)S(1)}, bf16[32,1792]{1,0:T(8,128)(2,1)S(1)}, u32[]{:S(2)}, u32[]{:S(2)}) %collective-permute-start.17) | collective-permute-done | bytes 114720 | tf_op jit(solution)/shard_map/ppermute | solution.py:42
  57.4 0.7 %fusion = bf16[32,1792]{1,0:T(8,128)(2,1)} fusion(bf16[32,1792]{1,0:T(8,128)(2,1)S(1)} %collective-permute-done.17, bf16[32,1792]{1,0:T(8,128)(2,1)S(1)} %collective-permute-done.14, bf16[32,1792]{1,0:T(8,128)(2,1)S(1)} %collective-permute-done.11, bf16[1,2,32,1792]{3,2,1,0:T(8,128)(2,1)S(1)} %add_convert_fusion), kind=kLoop, calls=%fused_computation.4 | loop fusion | flops 458752 | bytes 573440 | tf_op jit(solution)/shard_map/convert_element_type | solution.py:394
  (52 shorter events, 2.5 us)
Async XLA Ops:
  0.0 23.1 %collective-permute-start.1 = (bf16[32,7168]{1,0:T(8,128)(2,1)}, bf16[32,7168]{1,0:T(8,128)(2,1)S(1)}, u32[]{:S(2)}, u32[]{:S(2)}) collective-permute-start(bf16[32,7168]{1,0:T(8,128)(2,1)} %bitcast.24), channel_id=1, source_target_pairs={{0,8},{4,12},{8,0},{12,4},{1,9},{5,13},{9,1},{13,5},{2,10},{6,14},... | collective-permute-start | bytes 1376264 | tf_op jit(solution)/shard_map/ppermute | solution.py:42
  5.2 0.8 %copy-start.12 = (bf16[4,16,256]{2,1,0:T(8,128)(2,1)S(1)}, bf16[4,16,256]{2,1,0:T(8,128)(2,1)}, u32[]{:S(2)}) copy-start(bf16[4,16,256]{2,1,0:T(8,128)(2,1)} %param.29) | copy-start | bytes 98308
  6.8 16.3 %collective-permute-start.2 = (bf16[128,256]{1,0:T(8,128)(2,1)S(1)}, bf16[128,256]{1,0:T(8,128)(2,1)S(1)}, u32[]{:S(2)}, u32[]{:S(2)}) collective-permute-start(bf16[128,256]{1,0:T(8,128)(2,1)S(1)} %shard_map.145.refs_10_), channel_id=1, source_target_pairs={{0,8},{4,12},{8,0},{12,4},{1,9},{5,13},{9,1},{13,5},{2,10},{6,14},... | collective-permute-start | bytes 196616 | tf_op jit(solution)/shard_map/ppermute | solution.py:42
  6.9 17.3 %collective-permute-start = (bf16[32,7168]{1,0:T(8,128)(2,1)}, bf16[32,7168]{1,0:T(8,128)(2,1)S(1)}, u32[]{:S(2)}, u32[]{:S(2)}) collective-permute-start(bf16[32,7168]{1,0:T(8,128)(2,1)} %bitcast.25), channel_id=1, source_target_pairs={{0,4},{4,0},{8,12},{12,8},{1,5},{5,1},{9,13},{13,9},{2,6},{6,2},{1... | collective-permute-start | bytes 1376264 | tf_op jit(solution)/shard_map/ppermute | solution.py:42
  7.0 1.0 %copy-start = (bf16[2,16,7168]{2,1,0:T(8,128)(2,1)S(1)}, bf16[2,16,7168]{2,1,0:T(8,128)(2,1)}, u32[]{:S(2)}) copy-start(bf16[2,16,7168]{2,1,0:T(8,128)(2,1)} %param.15) | copy-start | bytes 1376260
  8.0 17.1 %copy-start.1 = (bf16[2,16,7168]{2,1,0:T(8,128)(2,1)S(1)}, bf16[2,16,7168]{2,1,0:T(8,128)(2,1)}, u32[]{:S(2)}) copy-start(bf16[2,16,7168]{2,1,0:T(8,128)(2,1)} %param.15) | copy-start | bytes 1376260
  8.0 17.1 %copy-start.10 = (bf16[4,16,7168]{2,1,0:T(8,128)(2,1)S(1)}, bf16[4,16,7168]{2,1,0:T(8,128)(2,1)}, u32[]{:S(2)}) copy-start(bf16[4,16,7168]{2,1,0:T(8,128)(2,1)} %param.28) | copy-start | bytes 2752516
  8.0 17.1 %copy-start.11 = (bf16[2,16,7168]{2,1,0:T(8,128)(2,1)S(1)}, bf16[2,16,7168]{2,1,0:T(8,128)(2,1)}, u32[]{:S(2)}) copy-start(bf16[2,16,7168]{2,1,0:T(8,128)(2,1)} %param.25) | copy-start | bytes 1376260
  15.7 1.8 %copy-start.2 = (bf16[256,7168]{1,0:T(8,128)(2,1)}, bf16[256,7168]{1,0:T(8,128)(2,1)S(1)}, u32[]{:S(2)}) copy-start(bf16[256,7168]{1,0:T(8,128)(2,1)S(1)} %get-tuple-element.45.refs_14_) | copy-start | bytes 11010052
  17.5 1.8 %copy-start.4 = (bf16[256,7168]{1,0:T(8,128)(2,1)}, bf16[256,7168]{1,0:T(8,128)(2,1)S(1)}, u32[]{:S(2)}) copy-start(bf16[256,7168]{1,0:T(8,128)(2,1)S(1)} %get-tuple-element.46.refs_15_) | copy-start | bytes 11010052
  19.3 1.9 %copy-start.6 = (bf16[7168,256]{1,0:T(8,128)(2,1)}, bf16[7168,256]{1,0:T(8,128)(2,1)S(1)}, u32[]{:S(2)}) copy-start(bf16[7168,256]{1,0:T(8,128)(2,1)S(1)} %get-tuple-element.38.refs_4_) | copy-start | bytes 11010052
  21.2 1.9 %copy-start.8 = (bf16[7168,256]{1,0:T(8,128)(2,1)}, bf16[7168,256]{1,0:T(8,128)(2,1)S(1)}, u32[]{:S(2)}) copy-start(bf16[7168,256]{1,0:T(8,128)(2,1)S(1)} %get-tuple-element.39.refs_5_) | copy-start | bytes 11010052
  23.1 1.9 %collective-permute-start.3 = (bf16[32,7168]{1,0:T(8,128)(2,1)S(1)}, bf16[32,7168]{1,0:T(8,128)(2,1)S(1)}, u32[]{:S(2)}, u32[]{:S(2)}) collective-permute-start(bf16[32,7168]{1,0:T(8,128)(2,1)S(1)} %collective-permute-done.1.refs_2_), channel_id=1, source_target_pairs={{0,4},{4,0},{8,12},{12,8},{1,5},{5,1},{9,13},{13,9},{2,6},{6,2},{1... | collective-permute-start | bytes 1376264 | tf_op jit(solution)/shard_map/ppermute | solution.py:42
  23.6 9.7 %collective-permute-start.7 = (bf16[128,256]{1,0:T(8,128)(2,1)S(1)}, bf16[128,256]{1,0:T(8,128)(2,1)S(1)}, u32[]{:S(2)}, u32[]{:S(2)}) collective-permute-start(bf16[128,256]{1,0:T(8,128)(2,1)S(1)} %shard_map.145.refs_10_), channel_id=1, source_target_pairs={{0,4},{4,0},{8,12},{12,8},{1,5},{5,1},{9,13},{13,9},{2,6},{6,2},{1... | collective-permute-start | bytes 196616 | tf_op jit(solution)/shard_map/ppermute | solution.py:42
  23.8 9.6 %collective-permute-start.8 = (bf16[128,256]{1,0:T(8,128)(2,1)S(1)}, bf16[128,256]{1,0:T(8,128)(2,1)S(1)}, u32[]{:S(2)}, u32[]{:S(2)}) collective-permute-start(bf16[128,256]{1,0:T(8,128)(2,1)S(1)} %collective-permute-done.2.refs_12_), channel_id=1, source_target_pairs={{0,4},{4,0},{8,12},{12,8},{1,5},{5,1},{9,13},{13,9},{2,6},{6,2},{1... | collective-permute-start | bytes 196616 | tf_op jit(solution)/shard_map/ppermute | solution.py:42
  25.1 8.3 %copy-start.14 = (s32[4,16]{1,0:T(4,128)S(1)}, s32[4,16]{1,0:T(4,128)}, u32[]{:S(2)}) copy-start(s32[4,16]{1,0:T(4,128)} %refs_1_.1) | copy-start | bytes 772
  25.7 7.7 %copy-start.3 = (bf16[256,7168]{1,0:T(8,128)(2,1)S(1)}, bf16[256,7168]{1,0:T(8,128)(2,1)}, u32[]{:S(2)}) copy-start(bf16[256,7168]{1,0:T(8,128)(2,1)} %copy-done.2) | copy-start | bytes 11010052
  25.7 7.7 %copy-start.5 = (bf16[256,7168]{1,0:T(8,128)(2,1)S(1)}, bf16[256,7168]{1,0:T(8,128)(2,1)}, u32[]{:S(2)}) copy-start(bf16[256,7168]{1,0:T(8,128)(2,1)} %copy-done.4) | copy-start | bytes 11010052
  25.7 7.6 %collective-permute-start.4 = (bf16[128,96]{1,0:T(8,128)(2,1)S(1)}, bf16[128,96]{1,0:T(8,128)(2,1)S(1)}, u32[]{:S(2)}, u32[]{:S(2)}) collective-permute-start(bf16[128,96]{1,0:T(8,128)(2,1)S(1)} %shard_map.148.refs_6_), channel_id=1, source_target_pairs={{0,4},{4,0},{8,12},{12,8},{1,5},{5,1},{9,13},{13,9},{2,6},{6,2},{1... | collective-permute-start | bytes 73736 | tf_op jit(solution)/shard_map/ppermute | solution.py:42
  26.2 7.2 %collective-permute-start.5 = (bf16[128,96]{1,0:T(8,128)(2,1)S(1)}, bf16[128,96]{1,0:T(8,128)(2,1)S(1)}, u32[]{:S(2)}, u32[]{:S(2)}) collective-permute-start(bf16[128,96]{1,0:T(8,128)(2,1)S(1)} %shard_map.148.refs_6_), channel_id=1, source_target_pairs={{0,8},{4,12},{8,0},{12,4},{1,9},{5,13},{9,1},{13,5},{2,10},{6,14},... | collective-permute-start | bytes 73736 | tf_op jit(solution)/shard_map/ppermute | solution.py:42
  28.1 5.2 %collective-permute-start.6 = (bf16[128,96]{1,0:T(8,128)(2,1)S(1)}, bf16[128,96]{1,0:T(8,128)(2,1)S(1)}, u32[]{:S(2)}, u32[]{:S(2)}) collective-permute-start(bf16[128,96]{1,0:T(8,128)(2,1)S(1)} %shard_map.148.refs_6_), channel_id=1, source_target_pairs={{0,12},{4,8},{8,4},{12,0},{1,13},{5,9},{9,5},{13,1},{2,14},{6,10},... | collective-permute-start | bytes 73736 | tf_op jit(solution)/shard_map/ppermute | solution.py:42
  28.1 2.0 %copy-start.7 = (bf16[7168,256]{1,0:T(8,128)(2,1)S(1)}, bf16[7168,256]{1,0:T(8,128)(2,1)}, u32[]{:S(2)}) copy-start(bf16[7168,256]{1,0:T(8,128)(2,1)} %copy-done.6) | copy-start | bytes 11010052
  30.2 2.0 %copy-start.9 = (bf16[7168,256]{1,0:T(8,128)(2,1)S(1)}, bf16[7168,256]{1,0:T(8,128)(2,1)}, u32[]{:S(2)}) copy-start(bf16[7168,256]{1,0:T(8,128)(2,1)} %copy-done.8) | copy-start | bytes 11010052
  35.4 1.6 %collective-permute-start.12 = (bf16[2,1,32,1792]{3,2,1,0:T(8,128)(2,1)S(1)}, bf16[2,1,32,1792]{3,2,1,0:T(8,128)(2,1)S(1)}, u32[]{:S(2)}, u32[]{:S(2)}) collective-permute-start(bf16[2,1,32,1792]{3,2,1,0:T(8,128)(2,1)S(1)} %get-tuple-element.50), channel_id=1, source_target_pairs={{0,4},{4,0},{8,12},{12,8},{1,5},{5,1},{9,13},{13,9},{2,6},{6,2},{1... | collective-permute-start | bytes 688136 | tf_op jit(solution)/shard_map/ppermute | solution.py:42
  35.7 10.3 %collective-permute-start.15 = (bf16[2,2,32,1792]{3,2,1,0:T(8,128)(2,1)S(1)}, bf16[2,2,32,1792]{3,2,1,0:T(8,128)(2,1)S(1)}, u32[]{:S(2)}, u32[]{:S(2)}) collective-permute-start(bf16[2,2,32,1792]{3,2,1,0:T(8,128)(2,1)S(1)} %get-tuple-element.52), channel_id=1, source_target_pairs={{0,4},{4,0},{8,12},{12,8},{1,5},{5,1},{9,13},{13,9},{2,6},{6,2},{1... | collective-permute-start | bytes 1376264 | tf_op jit(solution)/shard_map/ppermute | solution.py:42
  36.0 2.9 %collective-permute-start.9 = (bf16[2,1,32,1792]{3,2,1,0:T(8,128)(2,1)S(1)}, bf16[2,1,32,1792]{3,2,1,0:T(8,128)(2,1)S(1)}, u32[]{:S(2)}, u32[]{:S(2)}) collective-permute-start(bf16[2,1,32,1792]{3,2,1,0:T(8,128)(2,1)S(1)} %get-tuple-element.48), channel_id=1, source_target_pairs={{0,4},{4,0},{8,12},{12,8},{1,5},{5,1},{9,13},{13,9},{2,6},{6,2},{1... | collective-permute-start | bytes 688136 | tf_op jit(solution)/shard_map/ppermute | solution.py:42
  37.0 6.0 %collective-permute-start.13 = (bf16[1,1,32,1792]{3,2,1,0:T(8,128)(2,1)S(1)}, bf16[1,1,32,1792]{3,2,1,0:T(8,128)(2,1)S(1)}, u32[]{:S(2)}, u32[]{:S(2)}) collective-permute-start(bf16[1,1,32,1792]{3,2,1,0:T(8,128)(2,1)S(1)} %add_convert_fusion.4), channel_id=1, source_target_pairs={{0,8},{4,12},{8,0},{12,4},{1,9},{5,13},{9,1},{13,5},{2,10},{6,14},... | collective-permute-start | bytes 344072 | tf_op jit(solution)/shard_map/ppermute | solution.py:42
  38.9 8.8 %collective-permute-start.10 = (bf16[1,1,32,1792]{3,2,1,0:T(8,128)(2,1)S(1)}, bf16[1,1,32,1792]{3,2,1,0:T(8,128)(2,1)S(1)}, u32[]{:S(2)}, u32[]{:S(2)}) collective-permute-start(bf16[1,1,32,1792]{3,2,1,0:T(8,128)(2,1)S(1)} %add_convert_fusion.7), channel_id=1, source_target_pairs={{0,8},{4,12},{8,0},{12,4},{1,9},{5,13},{9,1},{13,5},{2,10},{6,14},... | collective-permute-start | bytes 344072 | tf_op jit(solution)/shard_map/ppermute | solution.py:42
  43.1 11.0 %collective-permute-start.14 = (bf16[32,1792]{1,0:T(8,128)(2,1)S(1)}, bf16[32,1792]{1,0:T(8,128)(2,1)S(1)}, u32[]{:S(2)}, u32[]{:S(2)}) collective-permute-start(bf16[32,1792]{1,0:T(8,128)(2,1)S(1)} %fusion.2), channel_id=1, source_target_pairs={{0,2},{1,3},{2,0},{3,1},{4,6},{5,7},{6,4},{7,5},{8,10},{9,11},{10,... | collective-permute-start | bytes 344072 | tf_op jit(solution)/shard_map/ppermute | solution.py:42
  46.1 6.3 %collective-permute-start.16 = (bf16[1,2,32,1792]{3,2,1,0:T(8,128)(2,1)S(1)}, bf16[1,2,32,1792]{3,2,1,0:T(8,128)(2,1)S(1)}, u32[]{:S(2)}, u32[]{:S(2)}) collective-permute-start(bf16[1,2,32,1792]{3,2,1,0:T(8,128)(2,1)S(1)} %add_convert_fusion.1), channel_id=1, source_target_pairs={{0,8},{4,12},{8,0},{12,4},{1,9},{5,13},{9,1},{13,5},{2,10},{6,14},... | collective-permute-start | bytes 688136 | tf_op jit(solution)/shard_map/ppermute | solution.py:42
  47.7 7.8 %collective-permute-start.11 = (bf16[32,1792]{1,0:T(8,128)(2,1)S(1)}, bf16[32,1792]{1,0:T(8,128)(2,1)S(1)}, u32[]{:S(2)}, u32[]{:S(2)}) collective-permute-start(bf16[32,1792]{1,0:T(8,128)(2,1)S(1)} %fusion.1), channel_id=1, source_target_pairs={{0,3},{1,2},{2,1},{3,0},{4,7},{5,6},{6,5},{7,4},{8,11},{9,10},{10,... | collective-permute-start | bytes 344072 | tf_op jit(solution)/shard_map/ppermute | solution.py:42
  52.5 4.9 %collective-permute-start.17 = (bf16[32,1792]{1,0:T(8,128)(2,1)S(1)}, bf16[32,1792]{1,0:T(8,128)(2,1)S(1)}, u32[]{:S(2)}, u32[]{:S(2)}) collective-permute-start(bf16[32,1792]{1,0:T(8,128)(2,1)S(1)} %slice_bitcast_fusion.1), channel_id=1, source_target_pairs={{0,1},{1,0},{2,3},{3,2},{4,5},{5,4},{6,7},{7,6},{8,9},{9,8},{10,11... | collective-permute-start | bytes 344072 | tf_op jit(solution)/shard_map/ppermute | solution.py:42
  (1 other events, 0.7 us)

commit v4 on v3

v4 whole, which is shorter than its diff:
```python
import functools

import jax
import jax.numpy as jnp
from jax import lax
from jax.experimental import pallas as pl
from jax.experimental.pallas import tpu as pltpu
from jax.sharding import PartitionSpec as P

F32 = jnp.float32
BF16 = jnp.bfloat16
MIB = 1024 * 1024


def params(mebibytes):
    return pltpu.CompilerParams(vmem_limit_bytes=mebibytes * MIB)


def cost(flops, moved):
    return pl.CostEstimate(flops=int(flops), bytes_accessed=int(moved), transcendentals=0)


def in_vmem(value):
    return pltpu.with_memory_space_constraint(value, pltpu.VMEM)


def in_hbm(value):
    return pltpu.with_memory_space_constraint(value, pltpu.HBM)


def vmem_shape(value):
    return pltpu.VMEM(value.shape, value.dtype)


VMEM_SPEC = pl.BlockSpec(memory_space=pltpu.VMEM)
HBM_SPEC = pl.BlockSpec(memory_space=pltpu.HBM)


def swap(value, bits, axis="expert"):
    count = lax.axis_size(axis)
    return lax.ppermute(value, axis, [(i, i ^ bits) for i in range(count)])


def add(one, other):
    return (one.astype(F32) + other.astype(F32)).astype(BF16)


def exchange_rest(value, arrived):
    count = lax.axis_size("expert")
    bit = count // 2
    pieces = {0: value, bit: arrived}
    bit //= 2
    while bit >= 1:
        pieces.update({r ^ bit: swap(piece, bit) for r, piece in list(pieces.items())})
        bit //= 2
    return [pieces[r] for r in range(count)]


def tile_of(width):
    return 256 if width % 256 == 0 else 128


def column_of(row, size):
    lane = lax.broadcasted_iota(jnp.int32, (size, row.shape[1]), 1)
    place = lax.broadcasted_iota(jnp.int32, (size, row.shape[1]), 0)
    return jnp.sum(jnp.where(lane == place, row.astype(F32), 0.0), axis=1, keepdims=True)


def first_kernel(
    experts, pieces, rows, gate_weight, up_weight, ids, values, tenants, pair_slot, shared_b,
    store_b, factor_shared, factor_store, gate_weight_routed, up_weight_routed, down, down_own,
    gate, up, pack, columns, rows_out, factor_shared_out, factor_store_out, gate_out, up_out,
    down_out, down_own_out, gate_held, up_held, ids_held, values_held, tenants_held,
    pair_slot_held, small_sems, sems, stage_sems,
):
    own, own_part = lax.axis_index("expert"), lax.axis_index("tensor")
    parts = lax.axis_size("tensor")
    depth = gate_weight.shape[0]
    shared_count, width = shared_b.shape
    store_count = store_b.shape[0]
    base = shared_count + store_count

    small = [
        (rows, rows_out),
        (ids, ids_held),
        (values, values_held),
        (tenants, tenants_held),
        (pair_slot, pair_slot_held),
        (shared_b, pack.at[pl.ds(0, shared_count)]),
        (store_b, pack.at[pl.ds(shared_count, store_count)]),
    ]
    small = [
        pltpu.make_async_copy(source, target, small_sems.at[n])
        for n, (source, target) in enumerate(small)
    ]
    for copy in small:
        copy.start()
    chunk = depth // pieces
    copies = []
    for k in range(pieces):
        part = pl.ds(k * chunk, chunk)
        pair = [
            pltpu.make_async_copy(gate_weight.at[part], gate_held.at[part], sems.at[0, k]),
            pltpu.make_async_copy(up_weight.at[part], up_held.at[part], sems.at[1, k]),
        ]
        for copy in pair:
            copy.start()
        copies.append(pair)
    staged = [(factor_shared, factor_shared_out), (factor_store, factor_store_out)]
    for source, target in ((gate_weight_routed, gate_out), (up_weight_routed, up_out)):
        piece = depth // parts
        for k in range(parts):
            part = pl.ds(k * piece, piece)
            staged.append((source.at[part], target.at[part]))
    piece = depth // parts
    for source, target in ((down, down_out), (down_own, down_own_out)):
        for j in range(parts):
            start = pl.multiple_of((own_part ^ j) * piece, piece)
            staged.append((source.at[:, pl.ds(start, piece)], target.at[:, pl.ds(j * piece, piece)]))
    staged = [
        pltpu.make_async_copy(source, target, stage_sems.at[n])
        for n, (source, target) in enumerate(staged)
    ]
    for copy in staged:
        copy.start()
    for copy in small:
        copy.wait()

    steps, top, size = ids_held.shape
    tenant = column_of(tenants_held[...], size)
    lane = lax.broadcasted_iota(jnp.int32, (size, width), 1)
    for s in range(steps):
        weight = jnp.zeros((size, width), F32)
        for k in range(top):
            expert = column_of(ids_held[s, k : k + 1], size).astype(jnp.int32)
            value = column_of(values_held[s, k : k + 1], size)
            weight = weight + jnp.where(expert == lane % experts, value, 0.0)
        high = weight.astype(BF16).astype(F32)
        middle = (weight - high).astype(BF16).astype(F32)
        low = weight - high - middle
        meta = jnp.where(lane < experts, high, jnp.where(lane < 2 * experts, middle, low))
        meta = jnp.where(lane < 3 * experts, meta, tenant)
        pack[base + s * size : base + (s + 1) * size] = meta.astype(BF16)

    tenant_count = pair_slot_held.shape[1]
    place = lax.broadcasted_iota(jnp.int32, pair_slot_held.shape, 0)
    own_row = jnp.sum(
        jnp.where(place == own, pair_slot_held[...].astype(F32), 0.0), axis=0, keepdims=True
    )
    own_slots = column_of(own_row, tenant_count).astype(jnp.int32)
    total = columns.shape[1]
    per_device = tenant_count // lax.axis_size("expert")
    rank = shared_count // per_device
    column = lax.broadcasted_iota(jnp.int32, (1, total), 1)
    shared_tenant = (own ^ (column // shared_count)) * per_device + column % shared_count // rank
    slot = (own ^ (column // store_count)) * (store_count // rank) + column % store_count // rank
    tenant_number = lax.broadcasted_iota(jnp.int32, (tenant_count, total), 0)
    slot_tenant = jnp.max(jnp.where(own_slots == slot, tenant_number, -1), axis=0, keepdims=True)
    columns[0:1] = shared_tenant
    columns[1:2] = slot_tenant
    columns[2:3] = jnp.full((1, total), own, jnp.int32)
    columns[3:8] = jnp.zeros((5, total), jnp.int32)

    total_gate = jnp.zeros(gate.shape, F32)
    total_up = jnp.zeros(up.shape, F32)
    for k in range(pieces):
        part = pl.ds(k * chunk, chunk)
        for copy in copies[k]:
            copy.wait()
        block = rows_out[:, part]
        total_gate += jnp.dot(block, gate_held[part], preferred_element_type=F32)
        total_up += jnp.dot(block, up_held[part], preferred_element_type=F32)
    gate[...] = total_gate
    up[...] = total_up
    for copy in staged:
        copy.wait()


def first_products(
    experts, rows, gate_weight, up_weight, ids, values, tenants, pair_slot, shared_b, store_b,
    staged,
):
    depth, width = gate_weight.shape
    count, parts = lax.axis_size("expert"), lax.axis_size("tensor")
    pieces = 7
    product = jax.ShapeDtypeStruct((rows.shape[0], width), F32)
    pack = jax.ShapeDtypeStruct(
        (shared_b.shape[0] + store_b.shape[0] + rows.shape[0], width), BF16
    )
    columns = count * max(shared_b.shape[0], store_b.shape[0])
    columns = jax.ShapeDtypeStruct((8, columns), jnp.int32)
    inputs = [
        rows, gate_weight, up_weight, ids, values, tenants, pair_slot, shared_b, store_b, *staged
    ]
    moved = sum(value.size * 2 for value in (rows, gate_weight, up_weight, *staged))
    outs = [product, product, pack, columns, *[vmem_shape(value) for value in (rows, *staged)]]
    return pl.pallas_call(
        functools.partial(first_kernel, experts, pieces),
        in_specs=[HBM_SPEC] * len(inputs),
        out_specs=[VMEM_SPEC] * len(outs),
        out_shape=outs,
        scratch_shapes=[
            pltpu.VMEM((depth, width), BF16),
            pltpu.VMEM((depth, width), BF16),
            pltpu.VMEM(ids.shape, jnp.int32),
            pltpu.VMEM(values.shape, F32),
            pltpu.VMEM(tenants.shape, jnp.int32),
            pltpu.VMEM(pair_slot.shape, jnp.int32),
            pltpu.SemaphoreType.DMA((7,)),
            pltpu.SemaphoreType.DMA((2, pieces)),
            pltpu.SemaphoreType.DMA((2 + 4 * parts,)),
        ],
        compiler_params=params(12),
        cost_estimate=cost(4 * rows.shape[0] * depth * width, moved),
    )(*[in_hbm(value) for value in inputs])


def inner_kernel(count, chunk, *refs):
    rows, factor_shared, factor_store, inner = refs[:count], *refs[count:]
    depth = factor_shared.shape[1]
    size = rows[0].shape[0]
    split = factor_shared.shape[0]
    width = split + factor_store.shape[0]
    total = jnp.zeros((count * size, width), F32)
    for k in range(depth // chunk):
        part = pl.ds(k * chunk, chunk)
        block = jnp.concatenate([ref[:, part] for ref in rows], axis=0)
        factors = jnp.concatenate([factor_shared[:, part], factor_store[:, part]], axis=0)
        total += lax.dot_general(
            block, factors, (((1,), (1,)), ((), ())), preferred_element_type=F32
        )
    inner[...] = total.astype(BF16)


def inner_products(rows, factor_shared, factor_store):
    depth = factor_shared.shape[1]
    total = rows[0].shape[0] * len(rows)
    width = factor_shared.shape[0] + factor_store.shape[0]
    return pl.pallas_call(
        functools.partial(inner_kernel, len(rows), 1024),
        in_specs=[VMEM_SPEC] * (len(rows) + 2),
        out_specs=VMEM_SPEC,
        out_shape=jax.ShapeDtypeStruct((total, width), BF16),
        compiler_params=params(12),
        cost_estimate=cost(2 * total * depth * width, 2 * depth * width),
    )(*[in_vmem(x) for x in (*rows, factor_shared, factor_store)])


def gate_up_kernel(count, chunk, *refs):
    rows, gate_weight, up_weight, gate, up = refs[:count], *refs[count:]
    depth = gate_weight.shape[0]
    total_gate = jnp.zeros(gate.shape, F32)
    total_up = jnp.zeros(up.shape, F32)
    for k in range(depth // chunk):
        part = pl.ds(k * chunk, chunk)
        block = jnp.concatenate([ref[:, part] for ref in rows], axis=0)
        total_gate += jnp.dot(block, gate_weight[part], preferred_element_type=F32)
        total_up += jnp.dot(block, up_weight[part], preferred_element_type=F32)
    gate[...] = total_gate
    up[...] = total_up


def gate_up(rows, gate_weight, up_weight):
    depth, width = gate_weight.shape
    total = rows[0].shape[0] * len(rows)
    out = jax.ShapeDtypeStruct((total, width), F32)
    return pl.pallas_call(
        functools.partial(gate_up_kernel, len(rows), 1024),
        in_specs=[VMEM_SPEC] * (len(rows) + 2),
        out_specs=[VMEM_SPEC] * 2,
        out_shape=[out, out],
        compiler_params=params(12),
        cost_estimate=cost(4 * total * depth * width, 4 * depth * width),
    )(*[in_vmem(x) for x in (*rows, gate_weight, up_weight)])


def silu(value):
    return value / (1.0 + jnp.exp(-value))


def down_kernel(shared_count, store_count, experts, chunks, order, *refs):
    count = len(order)
    gate, up, gate_own, up_own, columns = refs[:5]
    inner = refs[5 : 5 + count]
    packs = refs[5 + count : 5 + 2 * count]
    down, down_own = refs[5 + 2 * count : 7 + 2 * count]
    outs = refs[7 + 2 * count :]
    total, hid = gate.shape
    size = total // count
    half = count // 2
    width = shared_count + store_count

    meta = jnp.concatenate([ref[width:] for ref in packs], axis=0).astype(F32)
    lane = lax.broadcasted_iota(jnp.int32, meta.shape, 1)
    mine = (lane < 3 * experts) & (lane % experts == columns[2:3, :1])
    share = jnp.sum(jnp.where(mine, meta, 0.0), axis=1, keepdims=True)
    row_tenant = jnp.sum(jnp.where(lane == 3 * experts, meta, 0.0), axis=1, keepdims=True)
    row_tenant = row_tenant.astype(jnp.int32)

    parts, parts_own = [], []
    for r in range(count):
        held = inner[r][...]
        blocks = [held[(k ^ r) * size : ((k ^ r) + 1) * size] for k in range(count)]
        parts.append(jnp.concatenate(blocks, axis=0)[:, shared_count:])
        parts_own.append(blocks[0][:, :shared_count])
    lifted = jnp.concatenate(parts, axis=1)
    lifted_own = jnp.concatenate(parts_own, axis=1)
    zero = jnp.zeros((), BF16)
    slot_tenant = columns[1:2, : count * store_count]
    shared_tenant = columns[0:1, : count * shared_count]
    lifted = jnp.where(row_tenant == slot_tenant, lifted, zero)
    lifted_own = jnp.where(row_tenant[:size] == shared_tenant, lifted_own, zero)
    factor = jnp.concatenate([ref[shared_count:width] for ref in packs], axis=0)
    factor_own = jnp.concatenate([ref[:shared_count] for ref in packs], axis=0)
    upward = up[...] + jnp.dot(lifted, factor, preferred_element_type=F32)
    hidden = (silu(gate[...]) * upward).astype(BF16)
    upward_own = up_own[...] + jnp.dot(lifted_own, factor_own, preferred_element_type=F32)
    hidden_own = (silu(gate_own[...]) * upward_own).astype(BF16)

    part = outs[0].shape[-1]
    tile = tile_of(part)
    for n, chunk in enumerate(chunks):
        keep, send = outs[2 * n : 2 * n + 2]
        for place, j in enumerate(chunk):
            for c in range(part // tile):
                cut = slice(j * part + c * tile, j * part + (c + 1) * tile)
                routed = jnp.dot(hidden, down[:, cut], preferred_element_type=F32) * share
                shared = jnp.dot(hidden_own, down_own[:, cut], preferred_element_type=F32)
                for at, r in enumerate(order):
                    block = routed[r * size : (r + 1) * size]
                    if r == 0:
                        block = block + shared
                    target, row = (keep, at) if at < half else (send, at - half)
                    target[row, place, :, c * tile : (c + 1) * tile] = block.astype(BF16)


def down_products(
    gate, up, gate_own, up_own, columns, inner, packs, down, down_own, experts, chunks, order,
    shared_count, store_count,
):
    count = len(inner)
    total, hid = gate.shape
    size = total // count
    depth = down.shape[1]
    part = depth // lax.axis_size("tensor")
    whole = [gate, up, gate_own, up_own, columns, *inner, *packs, down, down_own]
    outs = []
    for chunk in chunks:
        outs += [jax.ShapeDtypeStruct((count // 2, len(chunk), size, part), BF16)] * 2
    return pl.pallas_call(
        functools.partial(down_kernel, shared_count, store_count, experts, chunks, order),
        in_specs=[VMEM_SPEC] * len(whole),
        out_specs=[VMEM_SPEC] * len(outs),
        out_shape=outs,
        compiler_params=params(16),
        cost_estimate=cost(2 * (total + size) * depth * hid, 4 * depth * hid),
    )(*[in_vmem(x) for x in whole])


def local(
    tokens,
    expert_ids,
    gate_values,
    tenant_ids,
    w_gate,
    w_up,
    routed_down_weight,
    shared_gate,
    shared_up,
    shared_down,
    store_a,
    store_b,
    pair_slot,
    shared_a,
    shared_b,
):
    experts = pair_slot.shape[0]
    adapted, rank, model_width = store_a.shape
    hid = store_b.shape[2]
    steps, size, _ = expert_ids.shape
    count = lax.axis_size("expert")
    n_tensor = lax.axis_size("tensor")
    shared_count, store_count = shared_a.shape[0] * rank, adapted * rank

    rows_own = tokens.reshape(steps * size, model_width)
    arrived = swap(rows_own, count // 2)
    first = first_products(
        experts,
        rows_own,
        shared_gate,
        shared_up,
        jnp.swapaxes(expert_ids, 1, 2),
        jnp.swapaxes(gate_values, 1, 2),
        tenant_ids.reshape(1, size),
        pair_slot,
        shared_b.reshape(shared_count, hid),
        store_b.reshape(store_count, hid),
        [
            shared_a.reshape(shared_count, model_width),
            store_a.reshape(store_count, model_width),
            w_gate[0],
            w_up[0],
            routed_down_weight[0],
            shared_down,
        ],
    )
    arrived, first = lax.optimization_barrier((arrived, first))
    gate_own, up_own, pack, columns, rows_held, factor_shared, factor_store = first[:7]
    gate_weight, up_weight, down, down_own = first[7:]
    rows = exchange_rest(rows_own, arrived)
    rows[0] = rows_held
    pack_arrived = swap(pack, count // 2)
    inner = inner_products(rows, factor_shared, factor_store)
    pack_arrived, inner = lax.optimization_barrier((pack_arrived, inner))
    inners = [inner] + [swap(inner, r) for r in range(1, count)]
    packs = exchange_rest(pack, pack_arrived)
    gate, up = gate_up(rows, gate_weight, up_weight)

    order = [0]
    bit = count // 2
    while bit >= 1:
        order = order + [r | bit for r in order]
        bit //= 2
    chunks = [[j] for j in range(n_tensor - 1, 1, -1)] + [[1, 0]]
    outs = down_products(
        gate, up, gate_own, up_own, columns, inners, packs, down, down_own, experts, chunks, order,
        shared_count, store_count,
    )
    held, leaving = list(outs[0::2]), list(outs[1::2])
    bit = 1
    while bit < count:
        half = count // (2 * bit) // 2
        arrived = []
        for n in range(len(chunks)):
            if bit > 1 and n > 1:
                leaving[n], arrived[n - 2] = lax.optimization_barrier((leaving[n], arrived[n - 2]))
            arrived.append(swap(leaving[n], bit))
        leaving = [add(h[half:], a[half:]) for h, a in zip(held, arrived)]
        held = [add(h[:half], a[:half]) for h, a in zip(held, arrived)]
        bit *= 2
    total = None
    for n, chunk in enumerate(chunks):
        for place, j in enumerate(chunk):
            value = leaving[n][0, place]
            value = (swap(value, j, "tensor") if j else value).astype(F32)
            total = value if total is None else total + value
    return total.astype(BF16).reshape(steps, size, model_width // n_tensor)


def solution(mesh):
    return jax.shard_map(
        local,
        mesh=mesh,
        in_specs=(
            P(None, ("groups", "expert"), None),
            P(None, ("groups", "expert"), None),
            P(None, ("groups", "expert"), None),
            P(("groups", "expert")),
            P("expert", None, "tensor"),
            P("expert", None, "tensor"),
            P("expert", "tensor", None),
            P(None, "tensor"),
            P(None, "tensor"),
            P("tensor", None),
            P("expert", None, None),
            P("expert", None, "tensor"),
            P(),
            P("expert", None, None),
            P("expert", None, "tensor"),
        ),
        out_specs=P(None, ("groups", "expert"), "tensor"),
        check_vma=False,
    )
```

time: 58.5 us -> 47.1 us (0.81)
  local copies, waits for them, and re-layouts: 16.3 us -> 0.01 us
  waiting for transfers between devices: 11.3 us -> 15.2 us
  Pallas kernels: 11.5 us -> 12.8 us
    unnamed x30 -> x0, local copies, waits for them, and re-layouts: 14 us -> none
    ppermute x18, waiting for transfers between devices: 11.3 us -> 15.2 us  [swap(): return lax.ppermute(value, axis, [(i, i ^ bits) for i in range(count)])]
    reshape x2 -> x0, local copies, waits for them, and re-layouts: 1.53 us -> none  [the longest x1 0.76 us: local(): expert_ids.reshape(steps * size, top_count)]
    pallas_call x3 -> x2, Pallas kernels: 9.81 us -> 11.1 us  [the longest x1 9.63 us: first_products(): pl.pallas_call(functools.partial(first_kernel, experts, pieces), in_specs...]
    another operation x2 -> x0, local copies, waits for them, and re-layouts: 0.74 us -> none  [local(): jnp.tile(tenant_ids[:, None], (steps, 1))]
  transfers between devices with their start and end apart: 18 -> 18, of which waited for: 6 -> 8; matrix products, arithmetic and copies ran while one was open for 5% -> 1% of each run, Pallas kernels for 16% -> 24%
where the time goes in v4:
time: 47.1 us; the launch traced here: 46.9 us
  starting transfers between devices  17.8 us (38%)
  waiting for transfers between devices  15.2 us (32%)
  Pallas kernels  12.8 us (27%)
  other arithmetic  1.02 us (2%)
    ppermute x18, starting transfers between devices, swap(): return lax.ppermute(value, axis, [(i, i ^ bits) for i in range(count)])  17.8 us
    ppermute x18, waiting for transfers between devices, swap(): return lax.ppermute(value, axis, [(i, i ^ bits) for i in range(count)])  15.2 us
    pallas_call x1, Pallas kernels, first_products(): pl.pallas_call(functools.partial(first_kernel, experts, pieces), in_specs...  9.63 us
    pallas_call x1, Pallas kernels, down_products(): pl.pallas_call(functools.partial(down_kernel, shared_count, store_count,...  1.45 us
    pallas_call x1, Pallas kernels, gate_up(): pl.pallas_call(functools.partial(gate_up_kernel, len(rows), 1024), in_spe...  1.11 us
  transfers between devices with their start and end apart: 18, of which 8 were waited for; matrix products, arithmetic and copies ran while one was open for 1% of the time, Pallas kernels for 24%

profile of v4, /device:TPU:0, one launch (start us, length us, event | category | flops | bytes accessed | tf_op | source)
XLA Modules:
  0.0 46.9 jit_solution(14603854103479708855)
XLA Ops:
  0.0 3.0 %collective-permute-start = (bf16[32,7168]{1,0:T(8,128)(2,1)}, bf16[32,7168]{1,0:T(8,128)(2,1)S(1)}, u32[]{:S(2)}, u32[]{:S(2)}) collective-permute-start(bf16[32,7168]{1,0:T(8,128)(2,1)} %bitcast.28), channel_id=1, source_target_pairs={{0,8},{4,12},{8,0},{12,4},{1,9},{5,13},{9,1},{13,5},{2,10},{6,14},... | collective-permute-start | bytes 1376264 | tf_op jit(solution)/shard_map/ppermute | solution.py:41
  3.0 9.6 %shard_map.145 = (f32[32,256]{1,0:T(8,128)S(1)}, f32[32,256]{1,0:T(8,128)S(1)}, bf16[128,256]{1,0:T(8,128)(2,1)S(1)}, s32[8,256]{1,0:T(8,128)S(1)}, bf16[32,7168...) custom-call(bf16[32,7168]{1,0:T(8,128)(2,1)} %bitcast.30, ...), custom_call_target="tpu_custom_call" | custom-call | flops 234881024 | bytes 23855104 | tf_op jit(solution)/shard_map/pallas_call | solution.py:197
  12.6 1.1 %collective-permute-done.refs_2_ = bf16[32,7168]{1,0:T(8,128)(2,1)S(1)} collective-permute-done((bf16[32,7168]{1,0:T(8,128)(2,1)}, bf16[32,7168]{1,0:T(8,128)(2,1)S(1)}, u32[]{:S(2)}, u32[]{:S(2)}) %collective-permute-start) | collective-permute-done | bytes 458784 | tf_op jit(solution)/shard_map/ppermute | solution.py:41
  13.7 1.7 %collective-permute-start.3 = (bf16[128,256]{1,0:T(8,128)(2,1)S(1)}, bf16[128,256]{1,0:T(8,128)(2,1)S(1)}, u32[]{:S(2)}, u32[]{:S(2)}) collective-permute-start(bf16[128,256]{1,0:T(8,128)(2,1)S(1)} %get-tuple-element.60.refs_9_), channel_id=1, source_target_pairs={{0,8},{4,12},{8,0},{12,4},{1,9},{5,13},{9,1},{13,5},{2,10},{6,14},... | collective-permute-start | bytes 196616 | tf_op jit(solution)/shard_map/ppermute | solution.py:41
  15.4 0.2 collective-permute-start.7
  15.7 0.6 %shard_map.147.refs_5_ = bf16[128,96]{1,0:T(8,128)(2,1)S(1)} custom-call(bf16[32,7168]{1,0:T(8,128)(2,1)S(1)} %get-tuple-element.51.refs_0_, bf16[32,7168]{1,0:T(8,128)(2,1)S(1)} %collective-permute-done.1.refs_1_, bf16[32,7168]{1,0:T(8,128)(2,1)S(1)} %collective-permute-done.refs_2_, bf16[32,7168]{1,0:T(8,128)(2,1)S(1)} %collective-permute-done.2.refs_3_, ...), custom_call_target="tpu_custom_call" | custom-call | flops 176160768 | bytes 1376256 | tf_op jit(solution)/shard_map/pallas_call | solution.py:239
  16.3 1.9 %collective-permute-done.3.refs_11_ = bf16[128,256]{1,0:T(8,128)(2,1)S(1)} collective-permute-done((bf16[128,256]{1,0:T(8,128)(2,1)S(1)}, bf16[128,256]{1,0:T(8,128)(2,1)S(1)}, u32[]{:S(2)}, u32[]{:S(2)}) %collective-permute-start.3) | collective-permute-done | bytes 65568 | tf_op jit(solution)/shard_map/ppermute | solution.py:41
  18.2 1.7 %collective-permute-start.5 = (bf16[128,96]{1,0:T(8,128)(2,1)S(1)}, bf16[128,96]{1,0:T(8,128)(2,1)S(1)}, u32[]{:S(2)}, u32[]{:S(2)}) collective-permute-start(bf16[128,96]{1,0:T(8,128)(2,1)S(1)} %shard_map.147.refs_5_), channel_id=1, source_target_pairs={{0,8},{4,12},{8,0},{12,4},{1,9},{5,13},{9,1},{13,5},{2,10},{6,14},... | collective-permute-start | bytes 73736 | tf_op jit(solution)/shard_map/ppermute | solution.py:41
  20.0 0.1 collective-permute-start.6
  20.1 0.3 collective-permute-start.8
  20.3 1.1 %shard_map.146 = (f32[128,256]{1,0:T(8,128)S(1)}, f32[128,256]{1,0:T(8,128)S(1)}) custom-call(bf16[32,7168]{1,0:T(8,128)(2,1)S(1)} %get-tuple-element.51.refs_0_, bf16[32,7168]{1,0:T(8,128)(2,1)S(1)} %collective-permute-done.1.refs_1_, bf16[32,7168]{1,0:T(8,128)(2,1)S(1)} %collective-permute-done.refs_2_, ...), custom_call_target="tpu_custom_call" | custom-call | flops 939524096 | bytes 7340032 | tf_op jit(solution)/shard_map/pallas_call | solution.py:267
  21.5 0.6 %collective-permute-done.5.refs_7_ = bf16[128,96]{1,0:T(8,128)(2,1)S(1)} collective-permute-done((bf16[128,96]{1,0:T(8,128)(2,1)S(1)}, bf16[128,96]{1,0:T(8,128)(2,1)S(1)}, u32[]{:S(2)}, u32[]{:S(2)}) %collective-permute-start.5) | collective-permute-done | bytes 24608 | tf_op jit(solution)/shard_map/ppermute | solution.py:41
  22.1 1.2 %collective-permute-done.6.refs_8_ = bf16[128,96]{1,0:T(8,128)(2,1)S(1)} collective-permute-done((bf16[128,96]{1,0:T(8,128)(2,1)S(1)}, bf16[128,96]{1,0:T(8,128)(2,1)S(1)}, u32[]{:S(2)}, u32[]{:S(2)}) %collective-permute-start.6) | collective-permute-done | bytes 24608 | tf_op jit(solution)/shard_map/ppermute | solution.py:41
  23.3 1.4 %shard_map.148 = (bf16[2,1,32,1792]{3,2,1,0:T(8,128)(2,1)S(1)}, bf16[2,1,32,1792]{3,2,1,0:T(8,128)(2,1)S(1)}, bf16[2,1,32,1792]{3,2,1,0:T(8,128)(2,1)S(1)}, bf16...) custom-call(f32[128,256]{1,0:T(8,128)S(1)} %get-tuple-element.55.refs_0_, ...), custom_call_target="tpu_custom_call" | custom-call | flops 587202560 | bytes 7340032 | tf_op jit(solution)/shard_map/pallas_call | solution.py:350
  24.8 0.3 collective-permute-start.13
  25.0 0.3 collective-permute-start.9
  25.3 0.2 collective-permute-start.10
  25.6 0.8 %collective-permute-done.13 = bf16[2,1,32,1792]{3,2,1,0:T(8,128)(2,1)S(1)} collective-permute-done((bf16[2,1,32,1792]{3,2,1,0:T(8,128)(2,1)S(1)}, bf16[2,1,32,1792]{3,2,1,0:T(8,128)(2,1)S(1)}, u32[]{:S(2)}, u32[]{:S(2)}) %collective-permute-start.13) | collective-permute-done | bytes 229408 | tf_op jit(solution)/shard_map/ppermute | solution.py:41
  26.3 0.9 %collective-permute-start.14 = (bf16[1,1,32,1792]{3,2,1,0:T(8,128)(2,1)S(1)}, bf16[1,1,32,1792]{3,2,1,0:T(8,128)(2,1)S(1)}, u32[]{:S(2)}, u32[]{:S(2)}) collective-permute-start(bf16[1,1,32,1792]{3,2,1,0:T(8,128)(2,1)S(1)} %add_convert_fusion.4), channel_id=1, source_target_pairs={{0,8},{4,12},{8,0},{12,4},{1,9},{5,13},{9,1},{13,5},{2,10},{6,14},... | collective-permute-start | bytes 344072 | tf_op jit(solution)/shard_map/ppermute | solution.py:41
  27.3 1.3 %collective-permute-start.11 = (bf16[1,1,32,1792]{3,2,1,0:T(8,128)(2,1)S(1)}, bf16[1,1,32,1792]{3,2,1,0:T(8,128)(2,1)S(1)}, u32[]{:S(2)}, u32[]{:S(2)}) collective-permute-start(bf16[1,1,32,1792]{3,2,1,0:T(8,128)(2,1)S(1)} %add_convert_fusion.7), channel_id=1, source_target_pairs={{0,8},{4,12},{8,0},{12,4},{1,9},{5,13},{9,1},{13,5},{2,10},{6,14},... | collective-permute-start | bytes 344072 | tf_op jit(solution)/shard_map/ppermute | solution.py:41
  28.5 3.8 %collective-permute-done.14 = bf16[1,1,32,1792]{3,2,1,0:T(8,128)(2,1)S(1)} collective-permute-done((bf16[1,1,32,1792]{3,2,1,0:T(8,128)(2,1)S(1)}, bf16[1,1,32,1792]{3,2,1,0:T(8,128)(2,1)S(1)}, u32[]{:S(2)}, u32[]{:S(2)}) %collective-permute-start.14) | collective-permute-done | bytes 114720 | tf_op jit(solution)/shard_map/ppermute | solution.py:41
  32.4 0.1 fusion.2
  32.4 2.7 %collective-permute-start.15 = (bf16[32,1792]{1,0:T(8,128)(2,1)S(1)}, bf16[32,1792]{1,0:T(8,128)(2,1)S(1)}, u32[]{:S(2)}, u32[]{:S(2)}) collective-permute-start(bf16[32,1792]{1,0:T(8,128)(2,1)S(1)} %fusion.2), channel_id=1, source_target_pairs={{0,2},{1,3},{2,0},{3,1},{4,6},{5,7},{6,4},{7,5},{8,10},{9,11},{10,... | collective-permute-start | bytes 344072 | tf_op jit(solution)/shard_map/ppermute | solution.py:41
  35.1 0.1 add_convert_fusion.2
  35.2 0.9 %collective-permute-start.16 = (bf16[1,2,32,1792]{3,2,1,0:T(8,128)(2,1)S(1)}, bf16[1,2,32,1792]{3,2,1,0:T(8,128)(2,1)S(1)}, u32[]{:S(2)}, u32[]{:S(2)}) collective-permute-start(bf16[1,2,32,1792]{3,2,1,0:T(8,128)(2,1)S(1)} %add_convert_fusion.2), channel_id=1, source_target_pairs={{0,8},{4,12},{8,0},{12,4},{1,9},{5,13},{9,1},{13,5},{2,10},{6,14},... | collective-permute-start | bytes 688136 | tf_op jit(solution)/shard_map/ppermute | solution.py:41
  36.2 2.5 %collective-permute-start.12 = (bf16[32,1792]{1,0:T(8,128)(2,1)S(1)}, bf16[32,1792]{1,0:T(8,128)(2,1)S(1)}, u32[]{:S(2)}, u32[]{:S(2)}) collective-permute-start(bf16[32,1792]{1,0:T(8,128)(2,1)S(1)} %fusion.1), channel_id=1, source_target_pairs={{0,3},{1,2},{2,1},{3,0},{4,7},{5,6},{6,5},{7,4},{8,11},{9,10},{10,... | collective-permute-start | bytes 344072 | tf_op jit(solution)/shard_map/ppermute | solution.py:41
  38.7 2.6 %collective-permute-done.16 = bf16[1,2,32,1792]{3,2,1,0:T(8,128)(2,1)S(1)} collective-permute-done((bf16[1,2,32,1792]{3,2,1,0:T(8,128)(2,1)S(1)}, bf16[1,2,32,1792]{3,2,1,0:T(8,128)(2,1)S(1)}, u32[]{:S(2)}, u32[]{:S(2)}) %collective-permute-start.16) | collective-permute-done | bytes 229408 | tf_op jit(solution)/shard_map/ppermute | solution.py:41
  41.3 0.1 add_convert_fusion
  41.4 1.6 %collective-permute-start.17 = (bf16[32,1792]{1,0:T(8,128)(2,1)S(1)}, bf16[32,1792]{1,0:T(8,128)(2,1)S(1)}, u32[]{:S(2)}, u32[]{:S(2)}) collective-permute-start(bf16[32,1792]{1,0:T(8,128)(2,1)S(1)} %slice_bitcast_fusion.1), channel_id=1, source_target_pairs={{0,1},{1,0},{2,3},{3,2},{4,5},{5,4},{6,7},{7,6},{8,9},{9,8},{10,11... | collective-permute-start | bytes 344072 | tf_op jit(solution)/shard_map/ppermute | solution.py:41
  43.0 0.0 collective-permute-done.12
  43.0 3.2 %collective-permute-done.17 = bf16[32,1792]{1,0:T(8,128)(2,1)S(1)} collective-permute-done((bf16[32,1792]{1,0:T(8,128)(2,1)S(1)}, bf16[32,1792]{1,0:T(8,128)(2,1)S(1)}, u32[]{:S(2)}, u32[]{:S(2)}) %collective-permute-start.17) | collective-permute-done | bytes 114720 | tf_op jit(solution)/shard_map/ppermute | solution.py:41
  46.2 0.7 %fusion = bf16[32,1792]{1,0:T(8,128)(2,1)} fusion(bf16[32,1792]{1,0:T(8,128)(2,1)S(1)} %collective-permute-done.17, bf16[32,1792]{1,0:T(8,128)(2,1)S(1)} %collective-permute-done.15, bf16[32,1792]{1,0:T(8,128)(2,1)S(1)} %collective-permute-done.12, bf16[1,2,32,1792]{3,2,1,0:T(8,128)(2,1)S(1)} %add_convert_fusion), kind=kLoop, calls=%fused_computation.4 | loop fusion | flops 458752 | bytes 573440 | tf_op jit(solution)/shard_map/convert_element_type | solution.py:447
  (16 shorter events, 0.2 us)
Async XLA Ops:
  0.0 13.7 %collective-permute-start = (bf16[32,7168]{1,0:T(8,128)(2,1)}, bf16[32,7168]{1,0:T(8,128)(2,1)S(1)}, u32[]{:S(2)}, u32[]{:S(2)}) collective-permute-start(bf16[32,7168]{1,0:T(8,128)(2,1)} %bitcast.28), channel_id=1, source_target_pairs={{0,8},{4,12},{8,0},{12,4},{1,9},{5,13},{9,1},{13,5},{2,10},{6,14},... | collective-permute-start | bytes 1376264 | tf_op jit(solution)/shard_map/ppermute | solution.py:41
  3.0 12.7 %collective-permute-start.1 = (bf16[32,7168]{1,0:T(8,128)(2,1)}, bf16[32,7168]{1,0:T(8,128)(2,1)S(1)}, u32[]{:S(2)}, u32[]{:S(2)}) collective-permute-start(bf16[32,7168]{1,0:T(8,128)(2,1)} %bitcast.29), channel_id=1, source_target_pairs={{0,4},{4,0},{8,12},{12,8},{1,5},{5,1},{9,13},{13,9},{2,6},{6,2},{1... | collective-permute-start | bytes 1376264 | tf_op jit(solution)/shard_map/ppermute | solution.py:41
  13.7 2.0 %collective-permute-start.2 = (bf16[32,7168]{1,0:T(8,128)(2,1)S(1)}, bf16[32,7168]{1,0:T(8,128)(2,1)S(1)}, u32[]{:S(2)}, u32[]{:S(2)}) collective-permute-start(bf16[32,7168]{1,0:T(8,128)(2,1)S(1)} %collective-permute-done.refs_2_), channel_id=1, source_target_pairs={{0,4},{4,0},{8,12},{12,8},{1,5},{5,1},{9,13},{13,9},{2,6},{6,2},{1... | collective-permute-start | bytes 1376264 | tf_op jit(solution)/shard_map/ppermute | solution.py:41
  13.7 4.5 %collective-permute-start.3 = (bf16[128,256]{1,0:T(8,128)(2,1)S(1)}, bf16[128,256]{1,0:T(8,128)(2,1)S(1)}, u32[]{:S(2)}, u32[]{:S(2)}) collective-permute-start(bf16[128,256]{1,0:T(8,128)(2,1)S(1)} %get-tuple-element.60.refs_9_), channel_id=1, source_target_pairs={{0,8},{4,12},{8,0},{12,4},{1,9},{5,13},{9,1},{13,5},{2,10},{6,14},... | collective-permute-start | bytes 196616 | tf_op jit(solution)/shard_map/ppermute | solution.py:41
  15.4 6.0 %collective-permute-start.7 = (bf16[128,256]{1,0:T(8,128)(2,1)S(1)}, bf16[128,256]{1,0:T(8,128)(2,1)S(1)}, u32[]{:S(2)}, u32[]{:S(2)}) collective-permute-start(bf16[128,256]{1,0:T(8,128)(2,1)S(1)} %get-tuple-element.60.refs_9_), channel_id=1, source_target_pairs={{0,4},{4,0},{8,12},{12,8},{1,5},{5,1},{9,13},{13,9},{2,6},{6,2},{1... | collective-permute-start | bytes 196616 | tf_op jit(solution)/shard_map/ppermute | solution.py:41
  18.2 3.3 %collective-permute-start.4 = (bf16[128,96]{1,0:T(8,128)(2,1)S(1)}, bf16[128,96]{1,0:T(8,128)(2,1)S(1)}, u32[]{:S(2)}, u32[]{:S(2)}) collective-permute-start(bf16[128,96]{1,0:T(8,128)(2,1)S(1)} %shard_map.147.refs_5_), channel_id=1, source_target_pairs={{0,4},{4,0},{8,12},{12,8},{1,5},{5,1},{9,13},{13,9},{2,6},{6,2},{1... | collective-permute-start | bytes 73736 | tf_op jit(solution)/shard_map/ppermute | solution.py:41
  18.2 3.9 %collective-permute-start.5 = (bf16[128,96]{1,0:T(8,128)(2,1)S(1)}, bf16[128,96]{1,0:T(8,128)(2,1)S(1)}, u32[]{:S(2)}, u32[]{:S(2)}) collective-permute-start(bf16[128,96]{1,0:T(8,128)(2,1)S(1)} %shard_map.147.refs_5_), channel_id=1, source_target_pairs={{0,8},{4,12},{8,0},{12,4},{1,9},{5,13},{9,1},{13,5},{2,10},{6,14},... | collective-permute-start | bytes 73736 | tf_op jit(solution)/shard_map/ppermute | solution.py:41
  20.0 3.3 %collective-permute-start.6 = (bf16[128,96]{1,0:T(8,128)(2,1)S(1)}, bf16[128,96]{1,0:T(8,128)(2,1)S(1)}, u32[]{:S(2)}, u32[]{:S(2)}) collective-permute-start(bf16[128,96]{1,0:T(8,128)(2,1)S(1)} %shard_map.147.refs_5_), channel_id=1, source_target_pairs={{0,12},{4,8},{8,4},{12,0},{1,13},{5,9},{9,5},{13,1},{2,14},{6,10},... | collective-permute-start | bytes 73736 | tf_op jit(solution)/shard_map/ppermute | solution.py:41
  20.1 3.2 %collective-permute-start.8 = (bf16[128,256]{1,0:T(8,128)(2,1)S(1)}, bf16[128,256]{1,0:T(8,128)(2,1)S(1)}, u32[]{:S(2)}, u32[]{:S(2)}) collective-permute-start(bf16[128,256]{1,0:T(8,128)(2,1)S(1)} %collective-permute-done.3.refs_11_), channel_id=1, source_target_pairs={{0,4},{4,0},{8,12},{12,8},{1,5},{5,1},{9,13},{13,9},{2,6},{6,2},{1... | collective-permute-start | bytes 196616 | tf_op jit(solution)/shard_map/ppermute | solution.py:41
  24.8 1.6 %collective-permute-start.13 = (bf16[2,1,32,1792]{3,2,1,0:T(8,128)(2,1)S(1)}, bf16[2,1,32,1792]{3,2,1,0:T(8,128)(2,1)S(1)}, u32[]{:S(2)}, u32[]{:S(2)}) collective-permute-start(bf16[2,1,32,1792]{3,2,1,0:T(8,128)(2,1)S(1)} %get-tuple-element.73), channel_id=1, source_target_pairs={{0,4},{4,0},{8,12},{12,8},{1,5},{5,1},{9,13},{13,9},{2,6},{6,2},{1... | collective-permute-start | bytes 688136 | tf_op jit(solution)/shard_map/ppermute | solution.py:41
  25.0 2.2 %collective-permute-start.9 = (bf16[2,1,32,1792]{3,2,1,0:T(8,128)(2,1)S(1)}, bf16[2,1,32,1792]{3,2,1,0:T(8,128)(2,1)S(1)}, u32[]{:S(2)}, u32[]{:S(2)}) collective-permute-start(bf16[2,1,32,1792]{3,2,1,0:T(8,128)(2,1)S(1)} %get-tuple-element.68), channel_id=1, source_target_pairs={{0,4},{4,0},{8,12},{12,8},{1,5},{5,1},{9,13},{13,9},{2,6},{6,2},{1... | collective-permute-start | bytes 688136 | tf_op jit(solution)/shard_map/ppermute | solution.py:41
  25.3 9.8 %collective-permute-start.10 = (bf16[2,2,32,1792]{3,2,1,0:T(8,128)(2,1)S(1)}, bf16[2,2,32,1792]{3,2,1,0:T(8,128)(2,1)S(1)}, u32[]{:S(2)}, u32[]{:S(2)}) collective-permute-start(bf16[2,2,32,1792]{3,2,1,0:T(8,128)(2,1)S(1)} %get-tuple-element.70), channel_id=1, source_target_pairs={{0,4},{4,0},{8,12},{12,8},{1,5},{5,1},{9,13},{13,9},{2,6},{6,2},{1... | collective-permute-start | bytes 1376264 | tf_op jit(solution)/shard_map/ppermute | solution.py:41
  26.3 6.0 %collective-permute-start.14 = (bf16[1,1,32,1792]{3,2,1,0:T(8,128)(2,1)S(1)}, bf16[1,1,32,1792]{3,2,1,0:T(8,128)(2,1)S(1)}, u32[]{:S(2)}, u32[]{:S(2)}) collective-permute-start(bf16[1,1,32,1792]{3,2,1,0:T(8,128)(2,1)S(1)} %add_convert_fusion.4), channel_id=1, source_target_pairs={{0,8},{4,12},{8,0},{12,4},{1,9},{5,13},{9,1},{13,5},{2,10},{6,14},... | collective-permute-start | bytes 344072 | tf_op jit(solution)/shard_map/ppermute | solution.py:41
  27.3 7.9 %collective-permute-start.11 = (bf16[1,1,32,1792]{3,2,1,0:T(8,128)(2,1)S(1)}, bf16[1,1,32,1792]{3,2,1,0:T(8,128)(2,1)S(1)}, u32[]{:S(2)}, u32[]{:S(2)}) collective-permute-start(bf16[1,1,32,1792]{3,2,1,0:T(8,128)(2,1)S(1)} %add_convert_fusion.7), channel_id=1, source_target_pairs={{0,8},{4,12},{8,0},{12,4},{1,9},{5,13},{9,1},{13,5},{2,10},{6,14},... | collective-permute-start | bytes 344072 | tf_op jit(solution)/shard_map/ppermute | solution.py:41
  32.4 10.6 %collective-permute-start.15 = (bf16[32,1792]{1,0:T(8,128)(2,1)S(1)}, bf16[32,1792]{1,0:T(8,128)(2,1)S(1)}, u32[]{:S(2)}, u32[]{:S(2)}) collective-permute-start(bf16[32,1792]{1,0:T(8,128)(2,1)S(1)} %fusion.2), channel_id=1, source_target_pairs={{0,2},{1,3},{2,0},{3,1},{4,6},{5,7},{6,4},{7,5},{8,10},{9,11},{10,... | collective-permute-start | bytes 344072 | tf_op jit(solution)/shard_map/ppermute | solution.py:41
  35.2 6.1 %collective-permute-start.16 = (bf16[1,2,32,1792]{3,2,1,0:T(8,128)(2,1)S(1)}, bf16[1,2,32,1792]{3,2,1,0:T(8,128)(2,1)S(1)}, u32[]{:S(2)}, u32[]{:S(2)}) collective-permute-start(bf16[1,2,32,1792]{3,2,1,0:T(8,128)(2,1)S(1)} %add_convert_fusion.2), channel_id=1, source_target_pairs={{0,8},{4,12},{8,0},{12,4},{1,9},{5,13},{9,1},{13,5},{2,10},{6,14},... | collective-permute-start | bytes 688136 | tf_op jit(solution)/shard_map/ppermute | solution.py:41
  36.2 6.9 %collective-permute-start.12 = (bf16[32,1792]{1,0:T(8,128)(2,1)S(1)}, bf16[32,1792]{1,0:T(8,128)(2,1)S(1)}, u32[]{:S(2)}, u32[]{:S(2)}) collective-permute-start(bf16[32,1792]{1,0:T(8,128)(2,1)S(1)} %fusion.1), channel_id=1, source_target_pairs={{0,3},{1,2},{2,1},{3,0},{4,7},{5,6},{6,5},{7,4},{8,11},{9,10},{10,... | collective-permute-start | bytes 344072 | tf_op jit(solution)/shard_map/ppermute | solution.py:41
  41.4 4.9 %collective-permute-start.17 = (bf16[32,1792]{1,0:T(8,128)(2,1)S(1)}, bf16[32,1792]{1,0:T(8,128)(2,1)S(1)}, u32[]{:S(2)}, u32[]{:S(2)}) collective-permute-start(bf16[32,1792]{1,0:T(8,128)(2,1)S(1)} %slice_bitcast_fusion.1), channel_id=1, source_target_pairs={{0,1},{1,0},{2,3},{3,2},{4,5},{5,4},{6,7},{7,6},{8,9},{9,8},{10,11... | collective-permute-start | bytes 344072 | tf_op jit(solution)/shard_map/ppermute | solution.py:41

commit v5 on v4

--- a/solution.py
+++ b/solution.py
@@ -43,6 +43,10 @@
 
 def add(one, other):
     return (one.astype(F32) + other.astype(F32)).astype(BF16)
+
+
+def total_of(values):
+    return sum(value.astype(F32) for value in values).astype(BF16)
 
 
 def exchange_rest(value, arrived):
@@ -60,6 +64,24 @@
     return 256 if width % 256 == 0 else 128
 
 
+def stage_kernel(source, target, sem):
+    copy = pltpu.make_async_copy(source, target, sem)
+    copy.start()
+    copy.wait()
+
+
+def stage(value):
+    return pl.pallas_call(
+        stage_kernel,
+        in_specs=[HBM_SPEC],
+        out_specs=VMEM_SPEC,
+        out_shape=vmem_shape(value),
+        scratch_shapes=[pltpu.SemaphoreType.DMA],
+        compiler_params=params(1),
+        cost_estimate=cost(0, 2 * value.size),
+    )(in_hbm(value))
+
+
 def column_of(row, size):
     lane = lax.broadcasted_iota(jnp.int32, (size, row.shape[1]), 1)
     place = lax.broadcasted_iota(jnp.int32, (size, row.shape[1]), 0)
@@ -69,7 +91,7 @@
 def first_kernel(
     experts, pieces, rows, gate_weight, up_weight, ids, values, tenants, pair_slot, shared_b,
     store_b, factor_shared, factor_store, gate_weight_routed, up_weight_routed, down, down_own,
-    gate, up, pack, columns, rows_out, factor_shared_out, factor_store_out, gate_out, up_out,
+    gate, up, pack, columns, factor_shared_out, factor_store_out, gate_out, up_out,
     down_out, down_own_out, gate_held, up_held, ids_held, values_held, tenants_held,
     pair_slot_held, small_sems, sems, stage_sems,
 ):
@@ -81,7 +103,6 @@
     base = shared_count + store_count
 
     small = [
-        (rows, rows_out),
         (ids, ids_held),
         (values, values_held),
         (tenants, tenants_held),
@@ -167,7 +188,7 @@
         part = pl.ds(k * chunk, chunk)
         for copy in copies[k]:
             copy.wait()
-        block = rows_out[:, part]
+        block = rows[:, part]
         total_gate += jnp.dot(block, gate_held[part], preferred_element_type=F32)
         total_up += jnp.dot(block, up_held[part], preferred_element_type=F32)
     gate[...] = total_gate
@@ -189,14 +210,12 @@
     )
     columns = count * max(shared_b.shape[0], store_b.shape[0])
     columns = jax.ShapeDtypeStruct((8, columns), jnp.int32)
-    inputs = [
-        rows, gate_weight, up_weight, ids, values, tenants, pair_slot, shared_b, store_b, *staged
-    ]
-    moved = sum(value.size * 2 for value in (rows, gate_weight, up_weight, *staged))
-    outs = [product, product, pack, columns, *[vmem_shape(value) for value in (rows, *staged)]]
+    inputs = [gate_weight, up_weight, ids, values, tenants, pair_slot, shared_b, store_b, *staged]
+    moved = sum(value.size * 2 for value in (gate_weight, up_weight, *staged))
+    outs = [product, product, pack, columns, *[vmem_shape(value) for value in staged]]
     return pl.pallas_call(
         functools.partial(first_kernel, experts, pieces),
-        in_specs=[HBM_SPEC] * len(inputs),
+        in_specs=[VMEM_SPEC] + [HBM_SPEC] * len(inputs),
         out_specs=[VMEM_SPEC] * len(outs),
         out_shape=outs,
         scratch_shapes=[
@@ -206,13 +225,13 @@
             pltpu.VMEM(values.shape, F32),
             pltpu.VMEM(tenants.shape, jnp.int32),
             pltpu.VMEM(pair_slot.shape, jnp.int32),
-            pltpu.SemaphoreType.DMA((7,)),
+            pltpu.SemaphoreType.DMA((6,)),
             pltpu.SemaphoreType.DMA((2, pieces)),
             pltpu.SemaphoreType.DMA((2 + 4 * parts,)),
         ],
         compiler_params=params(12),
         cost_estimate=cost(4 * rows.shape[0] * depth * width, moved),
-    )(*[in_hbm(value) for value in inputs])
+    )(in_vmem(rows), *[in_hbm(value) for value in inputs])
 
 
 def inner_kernel(count, chunk, *refs):
@@ -382,7 +401,7 @@
     n_tensor = lax.axis_size("tensor")
     shared_count, store_count = shared_a.shape[0] * rank, adapted * rank
 
-    rows_own = tokens.reshape(steps * size, model_width)
+    rows_own = stage(tokens.reshape(steps * size, model_width))
     arrived = swap(rows_own, count // 2)
     first = first_products(
         experts,
@@ -405,23 +424,26 @@
         ],
     )
     arrived, first = lax.optimization_barrier((arrived, first))
-    gate_own, up_own, pack, columns, rows_held, factor_shared, factor_store = first[:7]
-    gate_weight, up_weight, down, down_own = first[7:]
+    gate_own, up_own, pack, columns, factor_shared, factor_store = first[:6]
+    gate_weight, up_weight, down, down_own = first[6:]
     rows = exchange_rest(rows_own, arrived)
-    rows[0] = rows_held
     pack_arrived = swap(pack, count // 2)
     inner = inner_products(rows, factor_shared, factor_store)
-    pack_arrived, inner = lax.optimization_barrier((pack_arrived, inner))
-    inners = [inner] + [swap(inner, r) for r in range(1, count)]
+    inner_arrived = swap(inner, count // 2)
+    gate, up = gate_up(rows, gate_weight, up_weight)
+    pack_arrived, inner_arrived, gate = lax.optimization_barrier(
+        (pack_arrived, inner_arrived, gate)
+    )
+    inners = exchange_rest(inner, inner_arrived)
     packs = exchange_rest(pack, pack_arrived)
-    gate, up = gate_up(rows, gate_weight, up_weight)
 
     order = [0]
     bit = count // 2
     while bit >= 1:
         order = order + [r | bit for r in order]
         bit //= 2
-    chunks = [[j] for j in range(n_tensor - 1, 1, -1)] + [[1, 0]]
+    blocks = list(range(n_tensor - 1, -1, -1))
+    chunks = [blocks[: n_tensor // 2], blocks[n_tensor // 2 :]]
     outs = down_products(
         gate, up, gate_own, up_own, columns, inners, packs, down, down_own, experts, chunks, order,
         shared_count, store_count,
@@ -432,19 +454,23 @@
         half = count // (2 * bit) // 2
         arrived = []
         for n in range(len(chunks)):
-            if bit > 1 and n > 1:
-                leaving[n], arrived[n - 2] = lax.optimization_barrier((leaving[n], arrived[n - 2]))
+            if bit > 1 and n > 0:
+                leaving[n], arrived[n - 1] = lax.optimization_barrier((leaving[n], arrived[n - 1]))
             arrived.append(swap(leaving[n], bit))
-        leaving = [add(h[half:], a[half:]) for h, a in zip(held, arrived)]
-        held = [add(h[:half], a[:half]) for h, a in zip(held, arrived)]
+        if 2 * bit < count:
+            leaving = [add(h[half:], a[half:]) for h, a in zip(held, arrived)]
+            held = [add(h[:half], a[:half]) for h, a in zip(held, arrived)]
         bit *= 2
-    total = None
+    parts = {}
     for n, chunk in enumerate(chunks):
         for place, j in enumerate(chunk):
-            value = leaving[n][0, place]
-            value = (swap(value, j, "tensor") if j else value).astype(F32)
-            total = value if total is None else total + value
-    return total.astype(BF16).reshape(steps, size, model_width // n_tensor)
+            parts[j] = [held[n][0, place], arrived[n][0, place]]
+    bit = 1
+    while bit < n_tensor:
+        for j in sorted([j for j in parts if j & bit], reverse=True):
+            parts[j ^ bit].append(swap(total_of(parts.pop(j)), bit, "tensor"))
+        bit *= 2
+    return total_of(parts[0]).reshape(steps, size, model_width // n_tensor)
 
 
 def solution(mesh):

time: 47.1 us -> 48.1 us (1.021)
  waiting for transfers between devices: 15.2 us -> 17.2 us
  starting transfers between devices: 17.8 us -> 16.3 us
  Pallas kernels: 12.8 us -> 13.3 us
    ppermute x18 -> x16, waiting for transfers between devices: 15.2 us -> 17.2 us  [swap(): return lax.ppermute(value, axis, [(i, i ^ bits) for i in range(count)])]
    ppermute x18 -> x16, starting transfers between devices: 17.8 us -> 16.3 us  [swap(): return lax.ppermute(value, axis, [(i, i ^ bits) for i in range(count)])]
    pallas_call x0 -> x1, Pallas kernels: none -> 1.03 us  [stage(): pl.pallas_call(stage_kernel, in_specs=[HBM_SPEC], out_specs=VMEM_SPEC, ou...]
    pallas_call x1, Pallas kernels: 9.63 us -> 9.07 us  [first_products(): pl.pallas_call(functools.partial(first_kernel, experts, pieces), in_specs...]
  transfers between devices with their start and end apart: 18 -> 16, of which waited for: 8 -> 10; matrix products, arithmetic and copies ran while one was open for 1% -> 1% of each run, Pallas kernels for 24% -> 23%
where the time goes in v5:
time: 48.1 us; the launch traced here: 48 us
  waiting for transfers between devices  17.2 us (36%)
  starting transfers between devices  16.3 us (34%)
  Pallas kernels  13.3 us (28%)
  other arithmetic  1.03 us (2%)
    ppermute x16, waiting for transfers between devices, swap(): return lax.ppermute(value, axis, [(i, i ^ bits) for i in range(count)])  17.2 us
    ppermute x16, starting transfers between devices, swap(): return lax.ppermute(value, axis, [(i, i ^ bits) for i in range(count)])  16.3 us
    pallas_call x1, Pallas kernels, first_products(): pl.pallas_call(functools.partial(first_kernel, experts, pieces), in_specs...  9.07 us
    pallas_call x1, Pallas kernels, down_products(): pl.pallas_call(functools.partial(down_kernel, shared_count, store_count,...  1.45 us
    pallas_call x1, Pallas kernels, gate_up(): pl.pallas_call(functools.partial(gate_up_kernel, len(rows), 1024), in_spe...  1.14 us
    pallas_call x1, Pallas kernels, stage(): pl.pallas_call(stage_kernel, in_specs=[HBM_SPEC], out_specs=VMEM_SPEC, ou...  1.03 us
  transfers between devices with their start and end apart: 16, of which 10 were waited for; matrix products, arithmetic and copies ran while one was open for 1% of the time, Pallas kernels for 23%

profile of v5, /device:TPU:0, one launch (start us, length us, event | category | flops | bytes accessed | tf_op | source)
XLA Modules:
  0.0 48.0 jit_solution(500374509292761270)
XLA Ops:
  0.0 1.0 %shard_map.145.rows.refs_0_ = bf16[32,7168]{1,0:T(8,128)(2,1)S(1)} custom-call(bf16[32,7168]{1,0:T(8,128)(2,1)} %bitcast.30), custom_call_target="tpu_custom_call" | custom-call | bytes 458752 | tf_op jit(solution)/shard_map/pallas_call | solution.py:74
  1.0 3.0 %collective-permute-start = (bf16[32,7168]{1,0:T(8,128)(2,1)S(1)}, bf16[32,7168]{1,0:T(8,128)(2,1)S(1)}, u32[]{:S(2)}, u32[]{:S(2)}) collective-permute-start(bf16[32,7168]{1,0:T(8,128)(2,1)S(1)} %shard_map.145.rows.refs_0_), channel_id=1, source_target_pairs={{0,8},{4,12},{8,0},{12,4},{1,9},{5,13},{9,1},{13,5},{2,10},{6,14},... | collective-permute-start | bytes 1376264 | tf_op jit(solution)/shard_map/ppermute | solution.py:41
  4.1 0.0 collective-permute-start.2
  4.1 9.1 %shard_map.146 = (f32[32,256]{1,0:T(8,128)S(1)}, f32[32,256]{1,0:T(8,128)S(1)}, bf16[128,256]{1,0:T(8,128)(2,1)S(1)}, s32[8,256]{1,0:T(8,128)S(1)}, bf16[64,7168...) custom-call(bf16[32,7168]{1,0:T(8,128)(2,1)S(1)} %shard_map.145.rows, ...), custom_call_target="tpu_custom_call" | custom-call | flops 234881024 | bytes 23396352 | tf_op jit(solution)/shard_map/pallas_call | solution.py:216
  13.2 1.4 %collective-permute-done.refs_2_ = bf16[32,7168]{1,0:T(8,128)(2,1)S(1)} collective-permute-done((bf16[32,7168]{1,0:T(8,128)(2,1)S(1)}, bf16[32,7168]{1,0:T(8,128)(2,1)S(1)}, u32[]{:S(2)}, u32[]{:S(2)}) %collective-permute-start) | collective-permute-done | bytes 458784 | tf_op jit(solution)/shard_map/ppermute | solution.py:41
  14.6 1.7 %collective-permute-start.1 = (bf16[128,256]{1,0:T(8,128)(2,1)S(1)}, bf16[128,256]{1,0:T(8,128)(2,1)S(1)}, u32[]{:S(2)}, u32[]{:S(2)}) collective-permute-start(bf16[128,256]{1,0:T(8,128)(2,1)S(1)} %get-tuple-element.47.refs_9_), channel_id=1, source_target_pairs={{0,8},{4,12},{8,0},{12,4},{1,9},{5,13},{9,1},{13,5},{2,10},{6,14},... | collective-permute-start | bytes 196616 | tf_op jit(solution)/shard_map/ppermute | solution.py:41
  16.3 0.2 collective-permute-start.7
  16.6 0.6 %shard_map.147.refs_5_ = bf16[128,96]{1,0:T(8,128)(2,1)S(1)} custom-call(bf16[32,7168]{1,0:T(8,128)(2,1)S(1)} %shard_map.145.rows.refs_0_, bf16[32,7168]{1,0:T(8,128)(2,1)S(1)} %collective-permute-done.2.refs_1_, bf16[32,7168]{1,0:T(8,128)(2,1)S(1)} %collective-permute-done.refs_2_, bf16[32,7168]{1,0:T(8,128)(2,1)S(1)} %collective-permute-done.3.refs_3_, ...), custom_call_target="tpu_custom_call" | custom-call | flops 176160768 | bytes 1376256 | tf_op jit(solution)/shard_map/pallas_call | solution.py:258
  17.2 1.6 %collective-permute-start.4 = (bf16[128,96]{1,0:T(8,128)(2,1)S(1)}, bf16[128,96]{1,0:T(8,128)(2,1)S(1)}, u32[]{:S(2)}, u32[]{:S(2)}) collective-permute-start(bf16[128,96]{1,0:T(8,128)(2,1)S(1)} %shard_map.147.refs_5_), channel_id=1, source_target_pairs={{0,8},{4,12},{8,0},{12,4},{1,9},{5,13},{9,1},{13,5},{2,10},{6,14},... | collective-permute-start | bytes 73736 | tf_op jit(solution)/shard_map/ppermute | solution.py:41
  18.8 1.1 %shard_map.148 = (f32[128,256]{1,0:T(8,128)S(1)}, f32[128,256]{1,0:T(8,128)S(1)}) custom-call(bf16[32,7168]{1,0:T(8,128)(2,1)S(1)} %shard_map.145.rows.refs_0_, bf16[32,7168]{1,0:T(8,128)(2,1)S(1)} %collective-permute-done.2.refs_1_, bf16[32,7168]{1,0:T(8,128)(2,1)S(1)} %collective-permute-done.refs_2_, bf16[32,7168]{1,0:T(8,128)(2,1)S(1)} %collective-permute-done.3.refs_3_, ...), custom_call_target="tpu_custom_call" | custom-call | flops 939524096 | bytes 7340032 | tf_op jit(solution)/shard_map/pallas_call | solution.py:286
  20.0 1.2 %collective-permute-done.4.refs_7_ = bf16[128,96]{1,0:T(8,128)(2,1)S(1)} collective-permute-done((bf16[128,96]{1,0:T(8,128)(2,1)S(1)}, bf16[128,96]{1,0:T(8,128)(2,1)S(1)}, u32[]{:S(2)}, u32[]{:S(2)}) %collective-permute-start.4) | collective-permute-done | bytes 24608 | tf_op jit(solution)/shard_map/ppermute | solution.py:41
  21.2 0.5 %collective-permute-start.5 = (bf16[128,96]{1,0:T(8,128)(2,1)S(1)}, bf16[128,96]{1,0:T(8,128)(2,1)S(1)}, u32[]{:S(2)}, u32[]{:S(2)}) collective-permute-start(bf16[128,96]{1,0:T(8,128)(2,1)S(1)} %shard_map.147.refs_5_), channel_id=1, source_target_pairs={{0,4},{4,0},{8,12},{12,8},{1,5},{5,1},{9,13},{13,9},{2,6},{6,2},{1... | collective-permute-start | bytes 73736 | tf_op jit(solution)/shard_map/ppermute | solution.py:41
  21.7 0.0 collective-permute-start.6
  21.7 0.9 %collective-permute-done.5.refs_6_ = bf16[128,96]{1,0:T(8,128)(2,1)S(1)} collective-permute-done((bf16[128,96]{1,0:T(8,128)(2,1)S(1)}, bf16[128,96]{1,0:T(8,128)(2,1)S(1)}, u32[]{:S(2)}, u32[]{:S(2)}) %collective-permute-start.5) | collective-permute-done | bytes 24608 | tf_op jit(solution)/shard_map/ppermute | solution.py:41
  22.5 0.3 collective-permute-done.6.refs_8_
  22.9 1.4 %shard_map.149 = (bf16[2,2,32,1792]{3,2,1,0:T(8,128)(2,1)S(1)}, bf16[2,2,32,1792]{3,2,1,0:T(8,128)(2,1)S(1)}, bf16[2,2,32,1792]{3,2,1,0:T(8,128)(2,1)S(1)}, bf16[2,2,32,1792]{3,2,1,0:T(8,128)(2,1)S(1)}) custom-call(f32[128,256]{1,0:T(8,128)S(1)} %get-tuple-element.54.refs_0_, f32[128,256]{1,0:T(8,128)S(1)} %get-tuple-element.55.refs_1_, ...), custom_call_target="tpu_custom_call" | custom-call | flops 587202560 | bytes 7340032 | tf_op jit(solution)/shard_map/pallas_call | solution.py:369
  24.4 0.2 collective-permute-start.10
  24.6 0.3 collective-permute-start.9
  24.9 1.3 %collective-permute-done.10 = bf16[2,2,32,1792]{3,2,1,0:T(8,128)(2,1)S(1)} collective-permute-done((bf16[2,2,32,1792]{3,2,1,0:T(8,128)(2,1)S(1)}, bf16[2,2,32,1792]{3,2,1,0:T(8,128)(2,1)S(1)}, u32[]{:S(2)}, u32[]{:S(2)}) %collective-permute-start.10) | collective-permute-done | bytes 458784 | tf_op jit(solution)/shard_map/ppermute | solution.py:41
  26.2 0.1 add_convert_fusion.1
  26.3 1.6 %collective-permute-start.11 = (bf16[1,2,32,1792]{3,2,1,0:T(8,128)(2,1)S(1)}, bf16[1,2,32,1792]{3,2,1,0:T(8,128)(2,1)S(1)}, u32[]{:S(2)}, u32[]{:S(2)}) collective-permute-start(bf16[1,2,32,1792]{3,2,1,0:T(8,128)(2,1)S(1)} %get-tuple-element.71), channel_id=1, source_target_pairs={{0,8},{4,12},{8,0},{12,4},{1,9},{5,13},{9,1},{13,5},{2,10},{6,14},... | collective-permute-start | bytes 688136 | tf_op jit(solution)/shard_map/ppermute | solution.py:41
  28.0 0.1 add_convert_fusion.3
  28.1 6.0 %collective-permute-done.11 = bf16[1,2,32,1792]{3,2,1,0:T(8,128)(2,1)S(1)} collective-permute-done((bf16[1,2,32,1792]{3,2,1,0:T(8,128)(2,1)S(1)}, bf16[1,2,32,1792]{3,2,1,0:T(8,128)(2,1)S(1)}, u32[]{:S(2)}, u32[]{:S(2)}) %collective-permute-start.11) | collective-permute-done | bytes 229408 | tf_op jit(solution)/shard_map/ppermute | solution.py:41
  34.1 1.7 %collective-permute-start.14 = (bf16[32,1792]{1,0:T(8,128)(2,1)S(1)}, bf16[32,1792]{1,0:T(8,128)(2,1)S(1)}, u32[]{:S(2)}, u32[]{:S(2)}) collective-permute-start(bf16[32,1792]{1,0:T(8,128)(2,1)S(1)} %fusion.4), channel_id=1, source_target_pairs={{0,1},{1,0},{2,3},{3,2},{4,5},{5,4},{6,7},{7,6},{8,9},{9,8},{10,11... | collective-permute-start | bytes 344072 | tf_op jit(solution)/shard_map/ppermute | solution.py:41
  35.8 1.5 %collective-permute-start.12 = (bf16[1,2,32,1792]{3,2,1,0:T(8,128)(2,1)S(1)}, bf16[1,2,32,1792]{3,2,1,0:T(8,128)(2,1)S(1)}, u32[]{:S(2)}, u32[]{:S(2)}) collective-permute-start(bf16[1,2,32,1792]{3,2,1,0:T(8,128)(2,1)S(1)} %get-tuple-element.67), channel_id=1, source_target_pairs={{0,8},{4,12},{8,0},{12,4},{1,9},{5,13},{9,1},{13,5},{2,10},{6,14},... | collective-permute-start | bytes 688136 | tf_op jit(solution)/shard_map/ppermute | solution.py:41
  37.3 1.6 %collective-permute-done.14 = bf16[32,1792]{1,0:T(8,128)(2,1)S(1)} collective-permute-done((bf16[32,1792]{1,0:T(8,128)(2,1)S(1)}, bf16[32,1792]{1,0:T(8,128)(2,1)S(1)}, u32[]{:S(2)}, u32[]{:S(2)}) %collective-permute-start.14) | collective-permute-done | bytes 114720 | tf_op jit(solution)/shard_map/ppermute | solution.py:41
  39.0 2.7 %collective-permute-start.15 = (bf16[32,1792]{1,0:T(8,128)(2,1)S(1)}, bf16[32,1792]{1,0:T(8,128)(2,1)S(1)}, u32[]{:S(2)}, u32[]{:S(2)}) collective-permute-start(bf16[32,1792]{1,0:T(8,128)(2,1)S(1)} %fusion), channel_id=1, source_target_pairs={{0,2},{1,3},{2,0},{3,1},{4,6},{5,7},{6,4},{7,5},{8,10},{9,11},{10,... | collective-permute-start | bytes 344072 | tf_op jit(solution)/shard_map/ppermute | solution.py:41
  41.7 0.6 %collective-permute-done.12 = bf16[1,2,32,1792]{3,2,1,0:T(8,128)(2,1)S(1)} collective-permute-done((bf16[1,2,32,1792]{3,2,1,0:T(8,128)(2,1)S(1)}, bf16[1,2,32,1792]{3,2,1,0:T(8,128)(2,1)S(1)}, u32[]{:S(2)}, u32[]{:S(2)}) %collective-permute-start.12) | collective-permute-done | bytes 229408 | tf_op jit(solution)/shard_map/ppermute | solution.py:41
  42.4 1.0 %collective-permute-start.13 = (bf16[32,1792]{1,0:T(8,128)(2,1)S(1)}, bf16[32,1792]{1,0:T(8,128)(2,1)S(1)}, u32[]{:S(2)}, u32[]{:S(2)}) collective-permute-start(bf16[32,1792]{1,0:T(8,128)(2,1)S(1)} %fusion.3), channel_id=1, source_target_pairs={{0,1},{1,0},{2,3},{3,2},{4,5},{5,4},{6,7},{7,6},{8,9},{9,8},{10,11... | collective-permute-start | bytes 344072 | tf_op jit(solution)/shard_map/ppermute | solution.py:41
  43.4 2.1 %collective-permute-done.15 = bf16[32,1792]{1,0:T(8,128)(2,1)S(1)} collective-permute-done((bf16[32,1792]{1,0:T(8,128)(2,1)S(1)}, bf16[32,1792]{1,0:T(8,128)(2,1)S(1)}, u32[]{:S(2)}, u32[]{:S(2)}) %collective-permute-start.15) | collective-permute-done | bytes 114720 | tf_op jit(solution)/shard_map/ppermute | solution.py:41
  45.5 1.8 %collective-permute-done.13 = bf16[32,1792]{1,0:T(8,128)(2,1)S(1)} collective-permute-done((bf16[32,1792]{1,0:T(8,128)(2,1)S(1)}, bf16[32,1792]{1,0:T(8,128)(2,1)S(1)}, u32[]{:S(2)}, u32[]{:S(2)}) %collective-permute-start.13) | collective-permute-done | bytes 114720 | tf_op jit(solution)/shard_map/ppermute | solution.py:41
  47.3 0.7 %fusion.2 = bf16[32,1792]{1,0:T(8,128)(2,1)} fusion(bf16[32,1792]{1,0:T(8,128)(2,1)S(1)} %collective-permute-done.15, bf16[32,1792]{1,0:T(8,128)(2,1)S(1)} %collective-permute-done.13, bf16[1,2,32,1792]{3,2,1,0:T(8,128)(2,1)S(1)} %collective-permute-done.12, bf16[1,2,32,1792]{3,2,1,0:T(8,128)(2,1)S(1)} %get-tuple-element.69), kind=kLoop, calls=%fused_computation.8 | loop fusion | flops 458752 | bytes 573440 | tf_op jit(solution)/shard_map/convert_element_type | solution.py:49
  (11 shorter events, 0.1 us)
Async XLA Ops:
  1.0 13.6 %collective-permute-start = (bf16[32,7168]{1,0:T(8,128)(2,1)S(1)}, bf16[32,7168]{1,0:T(8,128)(2,1)S(1)}, u32[]{:S(2)}, u32[]{:S(2)}) collective-permute-start(bf16[32,7168]{1,0:T(8,128)(2,1)S(1)} %shard_map.145.rows.refs_0_), channel_id=1, source_target_pairs={{0,8},{4,12},{8,0},{12,4},{1,9},{5,13},{9,1},{13,5},{2,10},{6,14},... | collective-permute-start | bytes 1376264 | tf_op jit(solution)/shard_map/ppermute | solution.py:41
  4.1 12.5 %collective-permute-start.2 = (bf16[32,7168]{1,0:T(8,128)(2,1)S(1)}, bf16[32,7168]{1,0:T(8,128)(2,1)S(1)}, u32[]{:S(2)}, u32[]{:S(2)}) collective-permute-start(bf16[32,7168]{1,0:T(8,128)(2,1)S(1)} %shard_map.145.rows.refs_0_), channel_id=1, source_target_pairs={{0,4},{4,0},{8,12},{12,8},{1,5},{5,1},{9,13},{13,9},{2,6},{6,2},{1... | collective-permute-start | bytes 1376264 | tf_op jit(solution)/shard_map/ppermute | solution.py:41
  14.6 2.0 %collective-permute-start.3 = (bf16[32,7168]{1,0:T(8,128)(2,1)S(1)}, bf16[32,7168]{1,0:T(8,128)(2,1)S(1)}, u32[]{:S(2)}, u32[]{:S(2)}) collective-permute-start(bf16[32,7168]{1,0:T(8,128)(2,1)S(1)} %collective-permute-done.refs_2_), channel_id=1, source_target_pairs={{0,4},{4,0},{8,12},{12,8},{1,5},{5,1},{9,13},{13,9},{2,6},{6,2},{1... | collective-permute-start | bytes 1376264 | tf_op jit(solution)/shard_map/ppermute | solution.py:41
  14.6 5.4 %collective-permute-start.1 = (bf16[128,256]{1,0:T(8,128)(2,1)S(1)}, bf16[128,256]{1,0:T(8,128)(2,1)S(1)}, u32[]{:S(2)}, u32[]{:S(2)}) collective-permute-start(bf16[128,256]{1,0:T(8,128)(2,1)S(1)} %get-tuple-element.47.refs_9_), channel_id=1, source_target_pairs={{0,8},{4,12},{8,0},{12,4},{1,9},{5,13},{9,1},{13,5},{2,10},{6,14},... | collective-permute-start | bytes 196616 | tf_op jit(solution)/shard_map/ppermute | solution.py:41
  16.3 5.4 %collective-permute-start.7 = (bf16[128,256]{1,0:T(8,128)(2,1)S(1)}, bf16[128,256]{1,0:T(8,128)(2,1)S(1)}, u32[]{:S(2)}, u32[]{:S(2)}) collective-permute-start(bf16[128,256]{1,0:T(8,128)(2,1)S(1)} %get-tuple-element.47.refs_9_), channel_id=1, source_target_pairs={{0,4},{4,0},{8,12},{12,8},{1,5},{5,1},{9,13},{13,9},{2,6},{6,2},{1... | collective-permute-start | bytes 196616 | tf_op jit(solution)/shard_map/ppermute | solution.py:41
  17.2 4.0 %collective-permute-start.4 = (bf16[128,96]{1,0:T(8,128)(2,1)S(1)}, bf16[128,96]{1,0:T(8,128)(2,1)S(1)}, u32[]{:S(2)}, u32[]{:S(2)}) collective-permute-start(bf16[128,96]{1,0:T(8,128)(2,1)S(1)} %shard_map.147.refs_5_), channel_id=1, source_target_pairs={{0,8},{4,12},{8,0},{12,4},{1,9},{5,13},{9,1},{13,5},{2,10},{6,14},... | collective-permute-start | bytes 73736 | tf_op jit(solution)/shard_map/ppermute | solution.py:41
  21.2 1.7 %collective-permute-start.8 = (bf16[128,256]{1,0:T(8,128)(2,1)S(1)}, bf16[128,256]{1,0:T(8,128)(2,1)S(1)}, u32[]{:S(2)}, u32[]{:S(2)}) collective-permute-start(bf16[128,256]{1,0:T(8,128)(2,1)S(1)} %collective-permute-done.1.refs_11_), channel_id=1, source_target_pairs={{0,4},{4,0},{8,12},{12,8},{1,5},{5,1},{9,13},{13,9},{2,6},{6,2},{1... | collective-permute-start | bytes 196616 | tf_op jit(solution)/shard_map/ppermute | solution.py:41
  21.2 1.4 %collective-permute-start.5 = (bf16[128,96]{1,0:T(8,128)(2,1)S(1)}, bf16[128,96]{1,0:T(8,128)(2,1)S(1)}, u32[]{:S(2)}, u32[]{:S(2)}) collective-permute-start(bf16[128,96]{1,0:T(8,128)(2,1)S(1)} %shard_map.147.refs_5_), channel_id=1, source_target_pairs={{0,4},{4,0},{8,12},{12,8},{1,5},{5,1},{9,13},{13,9},{2,6},{6,2},{1... | collective-permute-start | bytes 73736 | tf_op jit(solution)/shard_map/ppermute | solution.py:41
  21.7 1.2 %collective-permute-start.6 = (bf16[128,96]{1,0:T(8,128)(2,1)S(1)}, bf16[128,96]{1,0:T(8,128)(2,1)S(1)}, u32[]{:S(2)}, u32[]{:S(2)}) collective-permute-start(bf16[128,96]{1,0:T(8,128)(2,1)S(1)} %collective-permute-done.4.refs_7_), channel_id=1, source_target_pairs={{0,4},{4,0},{8,12},{12,8},{1,5},{5,1},{9,13},{13,9},{2,6},{6,2},{1... | collective-permute-start | bytes 73736 | tf_op jit(solution)/shard_map/ppermute | solution.py:41
  24.4 1.9 %collective-permute-start.10 = (bf16[2,2,32,1792]{3,2,1,0:T(8,128)(2,1)S(1)}, bf16[2,2,32,1792]{3,2,1,0:T(8,128)(2,1)S(1)}, u32[]{:S(2)}, u32[]{:S(2)}) collective-permute-start(bf16[2,2,32,1792]{3,2,1,0:T(8,128)(2,1)S(1)} %get-tuple-element.66), channel_id=1, source_target_pairs={{0,4},{4,0},{8,12},{12,8},{1,5},{5,1},{9,13},{13,9},{2,6},{6,2},{1... | collective-permute-start | bytes 1376264 | tf_op jit(solution)/shard_map/ppermute | solution.py:41
  24.6 3.4 %collective-permute-start.9 = (bf16[2,2,32,1792]{3,2,1,0:T(8,128)(2,1)S(1)}, bf16[2,2,32,1792]{3,2,1,0:T(8,128)(2,1)S(1)}, u32[]{:S(2)}, u32[]{:S(2)}) collective-permute-start(bf16[2,2,32,1792]{3,2,1,0:T(8,128)(2,1)S(1)} %get-tuple-element.64), channel_id=1, source_target_pairs={{0,4},{4,0},{8,12},{12,8},{1,5},{5,1},{9,13},{13,9},{2,6},{6,2},{1... | collective-permute-start | bytes 1376264 | tf_op jit(solution)/shard_map/ppermute | solution.py:41
  26.3 7.7 %collective-permute-start.11 = (bf16[1,2,32,1792]{3,2,1,0:T(8,128)(2,1)S(1)}, bf16[1,2,32,1792]{3,2,1,0:T(8,128)(2,1)S(1)}, u32[]{:S(2)}, u32[]{:S(2)}) collective-permute-start(bf16[1,2,32,1792]{3,2,1,0:T(8,128)(2,1)S(1)} %get-tuple-element.71), channel_id=1, source_target_pairs={{0,8},{4,12},{8,0},{12,4},{1,9},{5,13},{9,1},{13,5},{2,10},{6,14},... | collective-permute-start | bytes 688136 | tf_op jit(solution)/shard_map/ppermute | solution.py:41
  34.1 4.9 %collective-permute-start.14 = (bf16[32,1792]{1,0:T(8,128)(2,1)S(1)}, bf16[32,1792]{1,0:T(8,128)(2,1)S(1)}, u32[]{:S(2)}, u32[]{:S(2)}) collective-permute-start(bf16[32,1792]{1,0:T(8,128)(2,1)S(1)} %fusion.4), channel_id=1, source_target_pairs={{0,1},{1,0},{2,3},{3,2},{4,5},{5,4},{6,7},{7,6},{8,9},{9,8},{10,11... | collective-permute-start | bytes 344072 | tf_op jit(solution)/shard_map/ppermute | solution.py:41
  35.8 6.6 %collective-permute-start.12 = (bf16[1,2,32,1792]{3,2,1,0:T(8,128)(2,1)S(1)}, bf16[1,2,32,1792]{3,2,1,0:T(8,128)(2,1)S(1)}, u32[]{:S(2)}, u32[]{:S(2)}) collective-permute-start(bf16[1,2,32,1792]{3,2,1,0:T(8,128)(2,1)S(1)} %get-tuple-element.67), channel_id=1, source_target_pairs={{0,8},{4,12},{8,0},{12,4},{1,9},{5,13},{9,1},{13,5},{2,10},{6,14},... | collective-permute-start | bytes 688136 | tf_op jit(solution)/shard_map/ppermute | solution.py:41
  39.0 6.5 %collective-permute-start.15 = (bf16[32,1792]{1,0:T(8,128)(2,1)S(1)}, bf16[32,1792]{1,0:T(8,128)(2,1)S(1)}, u32[]{:S(2)}, u32[]{:S(2)}) collective-permute-start(bf16[32,1792]{1,0:T(8,128)(2,1)S(1)} %fusion), channel_id=1, source_target_pairs={{0,2},{1,3},{2,0},{3,1},{4,6},{5,7},{6,4},{7,5},{8,10},{9,11},{10,... | collective-permute-start | bytes 344072 | tf_op jit(solution)/shard_map/ppermute | solution.py:41
  42.4 4.9 %collective-permute-start.13 = (bf16[32,1792]{1,0:T(8,128)(2,1)S(1)}, bf16[32,1792]{1,0:T(8,128)(2,1)S(1)}, u32[]{:S(2)}, u32[]{:S(2)}) collective-permute-start(bf16[32,1792]{1,0:T(8,128)(2,1)S(1)} %fusion.3), channel_id=1, source_target_pairs={{0,1},{1,0},{2,3},{3,2},{4,5},{5,4},{6,7},{7,6},{8,9},{9,8},{10,11... | collective-permute-start | bytes 344072 | tf_op jit(solution)/shard_map/ppermute | solution.py:41

commit v6 on v4

--- a/solution.py
+++ b/solution.py
@@ -43,6 +43,10 @@
 
 def add(one, other):
     return (one.astype(F32) + other.astype(F32)).astype(BF16)
+
+
+def total_of(values):
+    return sum(value.astype(F32) for value in values).astype(BF16)
 
 
 def exchange_rest(value, arrived):
@@ -216,34 +220,47 @@
 
 
 def inner_kernel(count, chunk, *refs):
-    rows, factor_shared, factor_store, inner = refs[:count], *refs[count:]
-    depth = factor_shared.shape[1]
-    size = rows[0].shape[0]
-    split = factor_shared.shape[0]
-    width = split + factor_store.shape[0]
-    total = jnp.zeros((count * size, width), F32)
+    rows, shared, stored, outs = refs[:count], refs[count : count + 2], refs[count + 2 : count + 4], refs[count + 4 :]
+    size, depth = rows[0].shape
+    columns = (((1,), (1,)), ((), ()))
+    total_shared, total_stored = 0.0, 0.0
     for k in range(depth // chunk):
         part = pl.ds(k * chunk, chunk)
-        block = jnp.concatenate([ref[:, part] for ref in rows], axis=0)
-        factors = jnp.concatenate([factor_shared[:, part], factor_store[:, part]], axis=0)
-        total += lax.dot_general(
-            block, factors, (((1,), (1,)), ((), ())), preferred_element_type=F32
+        held = [ref[:, part] for ref in rows]
+        total_stored += lax.dot_general(
+            jnp.concatenate(held, axis=0),
+            jnp.concatenate([ref[:, part] for ref in stored], axis=0),
+            columns,
+            preferred_element_type=F32,
         )
-    inner[...] = total.astype(BF16)
-
-
-def inner_products(rows, factor_shared, factor_store):
-    depth = factor_shared.shape[1]
-    total = rows[0].shape[0] * len(rows)
-    width = factor_shared.shape[0] + factor_store.shape[0]
+        total_shared += lax.dot_general(
+            jnp.concatenate(held[::2], axis=0),
+            jnp.concatenate([ref[:, part] for ref in shared], axis=0),
+            columns,
+            preferred_element_type=F32,
+        )
+    total_stored = total_stored.astype(BF16)
+    total_shared = total_shared.astype(BF16)
+    for n, out in enumerate(outs):
+        blocks = [total_shared[n * size : (n + 1) * size]]
+        blocks += [total_stored[k * size : (k + 1) * size] for k in range(count)]
+        out[...] = jnp.concatenate(blocks, axis=1)
+
+
+def inner_products(rows, shared, stored):
+    size, depth = rows[0].shape
+    count = len(rows)
+    width = 2 * shared[0].shape[0] + 2 * stored[0].shape[0] * count
+    flops = 4 * size * depth * (shared[0].shape[0] * count // 2 + stored[0].shape[0] * count)
+    inputs = [*rows, *shared, *stored]
     return pl.pallas_call(
-        functools.partial(inner_kernel, len(rows), 1024),
-        in_specs=[VMEM_SPEC] * (len(rows) + 2),
-        out_specs=VMEM_SPEC,
-        out_shape=jax.ShapeDtypeStruct((total, width), BF16),
+        functools.partial(inner_kernel, count, 1024),
+        in_specs=[VMEM_SPEC] * len(inputs),
+        out_specs=[VMEM_SPEC] * (count // 2),
+        out_shape=[jax.ShapeDtypeStruct((size, width), BF16)] * (count // 2),
         compiler_params=params(12),
-        cost_estimate=cost(2 * total * depth * width, 2 * depth * width),
-    )(*[in_vmem(x) for x in (*rows, factor_shared, factor_store)])
+        cost_estimate=cost(flops, 2 * sum(value.size for value in inputs)),
+    )(*[in_vmem(value) for value in inputs])
 
 
 def gate_up_kernel(count, chunk, *refs):
@@ -280,14 +297,14 @@
 
 def down_kernel(shared_count, store_count, experts, chunks, order, *refs):
     count = len(order)
+    half = count // 2
     gate, up, gate_own, up_own, columns = refs[:5]
-    inner = refs[5 : 5 + count]
-    packs = refs[5 + count : 5 + 2 * count]
-    down, down_own = refs[5 + 2 * count : 7 + 2 * count]
-    outs = refs[7 + 2 * count :]
+    inner = refs[5 : 5 + half]
+    packs = refs[5 + half : 5 + half + count]
+    down, down_own = refs[5 + half + count : 7 + half + count]
+    outs = refs[7 + half + count :]
     total, hid = gate.shape
     size = total // count
-    half = count // 2
     width = shared_count + store_count
 
     meta = jnp.concatenate([ref[width:] for ref in packs], axis=0).astype(F32)
@@ -297,14 +314,15 @@
     row_tenant = jnp.sum(jnp.where(lane == 3 * experts, meta, 0.0), axis=1, keepdims=True)
     row_tenant = row_tenant.astype(jnp.int32)
 
-    parts, parts_own = [], []
-    for r in range(count):
-        held = inner[r][...]
-        blocks = [held[(k ^ r) * size : ((k ^ r) + 1) * size] for k in range(count)]
-        parts.append(jnp.concatenate(blocks, axis=0)[:, shared_count:])
-        parts_own.append(blocks[0][:, :shared_count])
-    lifted = jnp.concatenate(parts, axis=1)
-    lifted_own = jnp.concatenate(parts_own, axis=1)
+    start, stored = 2 * shared_count, 2 * store_count
+    held = [ref[...] for ref in inner]
+    lifted_own = jnp.concatenate([value[:, :start] for value in held], axis=1)
+    lifted = []
+    for k in range(count):
+        places = [start + stored * (k ^ (2 * n)) for n in range(half)]
+        blocks = [value[:, place : place + stored] for value, place in zip(held, places)]
+        lifted.append(jnp.concatenate(blocks, axis=1))
+    lifted = jnp.concatenate(lifted, axis=0)
     zero = jnp.zeros((), BF16)
     slot_tenant = columns[1:2, : count * store_count]
     shared_tenant = columns[0:1, : count * shared_count]
@@ -338,7 +356,7 @@
     gate, up, gate_own, up_own, columns, inner, packs, down, down_own, experts, chunks, order,
     shared_count, store_count,
 ):
-    count = len(inner)
+    count = len(packs)
     total, hid = gate.shape
     size = total // count
     depth = down.shape[1]
@@ -384,6 +402,8 @@
 
     rows_own = tokens.reshape(steps * size, model_width)
     arrived = swap(rows_own, count // 2)
+    shared_other = swap(shared_a, 1).reshape(shared_count, model_width)
+    store_other = swap(store_a, 1).reshape(store_count, model_width)
     first = first_products(
         experts,
         rows_own,
@@ -404,16 +424,15 @@
             shared_down,
         ],
     )
-    arrived, first = lax.optimization_barrier((arrived, first))
+    arrived, first, store_other = lax.optimization_barrier((arrived, first, store_other))
     gate_own, up_own, pack, columns, rows_held, factor_shared, factor_store = first[:7]
     gate_weight, up_weight, down, down_own = first[7:]
     rows = exchange_rest(rows_own, arrived)
     rows[0] = rows_held
-    pack_arrived = swap(pack, count // 2)
-    inner = inner_products(rows, factor_shared, factor_store)
-    pack_arrived, inner = lax.optimization_barrier((pack_arrived, inner))
-    inners = [inner] + [swap(inner, r) for r in range(1, count)]
-    packs = exchange_rest(pack, pack_arrived)
+    packs = [pack] + [swap(pack, r) for r in range(1, count)]
+    inner = inner_products(rows, [factor_shared, shared_other], [factor_store, store_other])
+    rows, inner = lax.optimization_barrier((rows, inner))
+    inners = [inner[0]] + [swap(inner[n], 2 * n) for n in range(1, count // 2)]
     gate, up = gate_up(rows, gate_weight, up_weight)
 
     order = [0]
@@ -430,21 +449,23 @@
     bit = 1
     while bit < count:
         half = count // (2 * bit) // 2
-        arrived = []
-        for n in range(len(chunks)):
-            if bit > 1 and n > 1:
-                leaving[n], arrived[n - 2] = lax.optimization_barrier((leaving[n], arrived[n - 2]))
-            arrived.append(swap(leaving[n], bit))
-        leaving = [add(h[half:], a[half:]) for h, a in zip(held, arrived)]
-        held = [add(h[:half], a[:half]) for h, a in zip(held, arrived)]
+        arrived = [swap(value, bit) for value in leaving]
+        if bit > 1:
+            arrived[0], *_ = lax.optimization_barrier((arrived[0], *leaving))
+        if 2 * bit < count:
+            leaving = [add(h[half:], a[half:]) for h, a in zip(held, arrived)]
+            held = [add(h[:half], a[:half]) for h, a in zip(held, arrived)]
         bit *= 2
-    total = None
+    parts = {}
     for n, chunk in enumerate(chunks):
         for place, j in enumerate(chunk):
-            value = leaving[n][0, place]
-            value = (swap(value, j, "tensor") if j else value).astype(F32)
-            total = value if total is None else total + value
-    return total.astype(BF16).reshape(steps, size, model_width // n_tensor)
+            parts[j] = [held[n][0, place], arrived[n][0, place]]
+    bit = 1
+    while bit < n_tensor:
+        for j in sorted([j for j in parts if j & bit], reverse=True):
+            parts[j ^ bit].append(swap(total_of(parts.pop(j)), bit, "tensor"))
+        bit *= 2
+    return total_of(parts[0]).reshape(steps, size, model_width // n_tensor)
 
 
 def solution(mesh):

time: 47.1 us -> 43.6 us (0.926)
  waiting for transfers between devices: 15.2 us -> 11.4 us
  Pallas kernels: 12.8 us -> 13.4 us
    ppermute x18, waiting for transfers between devices: 15.2 us -> 11.4 us  [swap(): return lax.ppermute(value, axis, [(i, i ^ bits) for i in range(count)])]
    pallas_call x1, Pallas kernels: 0.63 us -> 1.21 us  [inner_products(): pl.pallas_call(functools.partial(inner_kernel, count, 1024), in_specs=[VM...]
  transfers between devices with their start and end apart: 18 -> 18, of which waited for: 8 -> 9; matrix products, arithmetic and copies ran while one was open for 1% -> 1% of each run, Pallas kernels for 24% -> 28%
where the time goes in v6:
time: 43.6 us; the launch traced here: 43.5 us
  starting transfers between devices  17.6 us (40%)
  Pallas kernels  13.4 us (31%)
  waiting for transfers between devices  11.4 us (26%)
  other arithmetic  1.03 us (2%)
    ppermute x18, starting transfers between devices, swap(): return lax.ppermute(value, axis, [(i, i ^ bits) for i in range(count)])  17.6 us
    ppermute x18, waiting for transfers between devices, swap(): return lax.ppermute(value, axis, [(i, i ^ bits) for i in range(count)])  11.4 us
    pallas_call x1, Pallas kernels, first_products(): pl.pallas_call(functools.partial(first_kernel, experts, pieces), in_specs...  9.63 us
    pallas_call x1, Pallas kernels, down_products(): pl.pallas_call(functools.partial(down_kernel, shared_count, store_count,...  1.38 us
    pallas_call x1, Pallas kernels, inner_products(): pl.pallas_call(functools.partial(inner_kernel, count, 1024), in_specs=[VM...  1.21 us
    pallas_call x1, Pallas kernels, gate_up(): pl.pallas_call(functools.partial(gate_up_kernel, len(rows), 1024), in_spe...  1.19 us
  transfers between devices with their start and end apart: 18, of which 9 were waited for; matrix products, arithmetic and copies ran while one was open for 1% of the time, Pallas kernels for 28%

profile of v6, /device:TPU:0, one launch (start us, length us, event | category | flops | bytes accessed | tf_op | source)
XLA Modules:
  0.0 43.5 jit_solution(6227088403904058785)
XLA Ops:
  0.0 3.0 %collective-permute-start = (bf16[32,7168]{1,0:T(8,128)(2,1)}, bf16[32,7168]{1,0:T(8,128)(2,1)S(1)}, u32[]{:S(2)}, u32[]{:S(2)}) collective-permute-start(bf16[32,7168]{1,0:T(8,128)(2,1)} %bitcast.35), channel_id=1, source_target_pairs={{0,8},{4,12},{8,0},{12,4},{1,9},{5,13},{9,1},{13,5},{2,10},{6,14},... | collective-permute-start | bytes 1376264 | tf_op jit(solution)/shard_map/ppermute | solution.py:41
  3.0 0.5 %collective-permute-start.4 = (bf16[4,16,7168]{2,1,0:T(8,128)(2,1)}, bf16[4,16,7168]{2,1,0:T(8,128)(2,1)S(1)}, u32[]{:S(2)}, u32[]{:S(2)}) collective-permute-start(bf16[4,16,7168]{2,1,0:T(8,128)(2,1)} %param.28), channel_id=1, source_target_pairs={{0,4},{4,0},{8,12},{12,8},{1,5},{5,1},{9,13},{13,9},{2,6},{6,2},{1... | collective-permute-start | bytes 2752520 | tf_op jit(solution)/shard_map/ppermute | solution.py:41
  3.5 0.0 collective-permute-start.2
  3.5 9.6 %shard_map.145 = (f32[32,256]{1,0:T(8,128)S(1)}, f32[32,256]{1,0:T(8,128)S(1)}, bf16[128,256]{1,0:T(8,128)(2,1)S(1)}, s32[8,256]{1,0:T(8,128)S(1)}, bf16[32,7168...) custom-call(bf16[32,7168]{1,0:T(8,128)(2,1)} %bitcast.37, ...), custom_call_target="tpu_custom_call" | custom-call | flops 234881024 | bytes 23855104 | tf_op jit(solution)/shard_map/pallas_call | solution.py:201
  13.1 0.6 %collective-permute-done.refs_2_ = bf16[32,7168]{1,0:T(8,128)(2,1)S(1)} collective-permute-done((bf16[32,7168]{1,0:T(8,128)(2,1)}, bf16[32,7168]{1,0:T(8,128)(2,1)S(1)}, u32[]{:S(2)}, u32[]{:S(2)}) %collective-permute-start) | collective-permute-done | bytes 458784 | tf_op jit(solution)/shard_map/ppermute | solution.py:41
  13.7 0.0 collective-permute-start.3
  13.7 0.5 %collective-permute-start.6 = (bf16[128,256]{1,0:T(8,128)(2,1)S(1)}, bf16[128,256]{1,0:T(8,128)(2,1)S(1)}, u32[]{:S(2)}, u32[]{:S(2)}) collective-permute-start(bf16[128,256]{1,0:T(8,128)(2,1)S(1)} %get-tuple-element.77.refs_7_), channel_id=1, source_target_pairs={{0,4},{4,0},{8,12},{12,8},{1,5},{5,1},{9,13},{13,9},{2,6},{6,2},{1... | collective-permute-start | bytes 196616 | tf_op jit(solution)/shard_map/ppermute | solution.py:41
  14.2 1.7 %collective-permute-start.7 = (bf16[128,256]{1,0:T(8,128)(2,1)S(1)}, bf16[128,256]{1,0:T(8,128)(2,1)S(1)}, u32[]{:S(2)}, u32[]{:S(2)}) collective-permute-start(bf16[128,256]{1,0:T(8,128)(2,1)S(1)} %get-tuple-element.77.refs_7_), channel_id=1, source_target_pairs={{0,8},{4,12},{8,0},{12,4},{1,9},{5,13},{9,1},{13,5},{2,10},{6,14},... | collective-permute-start | bytes 196616 | tf_op jit(solution)/shard_map/ppermute | solution.py:41
  16.0 1.2 %shard_map.146 = (bf16[32,384]{1,0:T(8,128)(2,1)S(1)}, bf16[32,384]{1,0:T(8,128)(2,1)S(1)}) custom-call(bf16[32,7168]{1,0:T(8,128)(2,1)S(1)} %get-tuple-element.64.refs_0_, bf16[32,7168]{1,0:T(8,128)(2,1)S(1)} %collective-permute-done.2.refs_1_, bf16[32,7168]{1,0:T(8,128)(2,1)S(1)} %collective-permute-done.refs_2_, ...), custom_call_target="tpu_custom_call" | custom-call | flops 234881024 | bytes 4587520 | tf_op jit(solution)/shard_map/pallas_call | solution.py:256
  17.2 1.5 %collective-permute-start.5 = (bf16[32,384]{1,0:T(8,128)(2,1)S(1)}, bf16[32,384]{1,0:T(8,128)(2,1)S(1)}, u32[]{:S(2)}, u32[]{:S(2)}) collective-permute-start(bf16[32,384]{1,0:T(8,128)(2,1)S(1)} %get-tuple-element.76), channel_id=1, source_target_pairs={{0,8},{4,12},{8,0},{12,4},{1,9},{5,13},{9,1},{13,5},{2,10},{6,14},... | collective-permute-start | bytes 73736 | tf_op jit(solution)/shard_map/ppermute | solution.py:41
  18.6 1.2 %shard_map.147 = (f32[128,256]{1,0:T(8,128)S(1)}, f32[128,256]{1,0:T(8,128)S(1)}) custom-call(bf16[32,7168]{1,0:T(8,128)(2,1)S(1)} %get-tuple-element.64.refs_0_, bf16[32,7168]{1,0:T(8,128)(2,1)S(1)} %collective-permute-done.2.refs_1_, bf16[32,7168]{1,0:T(8,128)(2,1)S(1)} %collective-permute-done.refs_2_, ...), custom_call_target="tpu_custom_call" | custom-call | flops 939524096 | bytes 7340032 | tf_op jit(solution)/shard_map/pallas_call | solution.py:284
  19.9 0.4 collective-permute-done.8.refs_10_
  20.3 0.8 %collective-permute-done.5.refs_6_ = bf16[32,384]{1,0:T(8,128)(2,1)S(1)} collective-permute-done((bf16[32,384]{1,0:T(8,128)(2,1)S(1)}, bf16[32,384]{1,0:T(8,128)(2,1)S(1)}, u32[]{:S(2)}, u32[]{:S(2)}) %collective-permute-start.5) | collective-permute-done | bytes 24608 | tf_op jit(solution)/shard_map/ppermute | solution.py:41
  21.1 1.4 %shard_map.148 = (bf16[2,1,32,1792]{3,2,1,0:T(8,128)(2,1)S(1)}, bf16[2,1,32,1792]{3,2,1,0:T(8,128)(2,1)S(1)}, bf16[2,1,32,1792]{3,2,1,0:T(8,128)(2,1)S(1)}, bf16...) custom-call(f32[128,256]{1,0:T(8,128)S(1)} %get-tuple-element.70.refs_0_, ...), custom_call_target="tpu_custom_call" | custom-call | flops 587202560 | bytes 7340032 | tf_op jit(solution)/shard_map/pallas_call | solution.py:368
  22.5 0.1 collective-permute-start.14
  22.6 0.5 %collective-permute-start.9 = (bf16[2,2,32,1792]{3,2,1,0:T(8,128)(2,1)S(1)}, bf16[2,2,32,1792]{3,2,1,0:T(8,128)(2,1)S(1)}, u32[]{:S(2)}, u32[]{:S(2)}) collective-permute-start(bf16[2,2,32,1792]{3,2,1,0:T(8,128)(2,1)S(1)} %get-tuple-element.81), channel_id=1, source_target_pairs={{0,4},{4,0},{8,12},{12,8},{1,5},{5,1},{9,13},{13,9},{2,6},{6,2},{1... | collective-permute-start | bytes 1376264 | tf_op jit(solution)/shard_map/ppermute | solution.py:41
  23.1 0.1 collective-permute-start.12
  23.1 0.9 %collective-permute-done.14 = bf16[2,1,32,1792]{3,2,1,0:T(8,128)(2,1)S(1)} collective-permute-done((bf16[2,1,32,1792]{3,2,1,0:T(8,128)(2,1)S(1)}, bf16[2,1,32,1792]{3,2,1,0:T(8,128)(2,1)S(1)}, u32[]{:S(2)}, u32[]{:S(2)}) %collective-permute-start.14) | collective-permute-done | bytes 229408 | tf_op jit(solution)/shard_map/ppermute | solution.py:41
  24.1 1.5 %collective-permute-start.15 = (bf16[1,1,32,1792]{3,2,1,0:T(8,128)(2,1)S(1)}, bf16[1,1,32,1792]{3,2,1,0:T(8,128)(2,1)S(1)}, u32[]{:S(2)}, u32[]{:S(2)}) collective-permute-start(bf16[1,1,32,1792]{3,2,1,0:T(8,128)(2,1)S(1)} %add_convert_fusion.3), channel_id=1, source_target_pairs={{0,8},{4,12},{8,0},{12,4},{1,9},{5,13},{9,1},{13,5},{2,10},{6,14},... | collective-permute-start | bytes 344072 | tf_op jit(solution)/shard_map/ppermute | solution.py:41
  25.6 0.9 %collective-permute-start.13 = (bf16[1,1,32,1792]{3,2,1,0:T(8,128)(2,1)S(1)}, bf16[1,1,32,1792]{3,2,1,0:T(8,128)(2,1)S(1)}, u32[]{:S(2)}, u32[]{:S(2)}) collective-permute-start(bf16[1,1,32,1792]{3,2,1,0:T(8,128)(2,1)S(1)} %add_convert_fusion.5), channel_id=1, source_target_pairs={{0,8},{4,12},{8,0},{12,4},{1,9},{5,13},{9,1},{13,5},{2,10},{6,14},... | collective-permute-start | bytes 344072 | tf_op jit(solution)/shard_map/ppermute | solution.py:41
  26.6 0.1 add_convert_fusion.1
  26.7 3.4 %collective-permute-done.15 = bf16[1,1,32,1792]{3,2,1,0:T(8,128)(2,1)S(1)} collective-permute-done((bf16[1,1,32,1792]{3,2,1,0:T(8,128)(2,1)S(1)}, bf16[1,1,32,1792]{3,2,1,0:T(8,128)(2,1)S(1)}, u32[]{:S(2)}, u32[]{:S(2)}) %collective-permute-start.15) | collective-permute-done | bytes 114720 | tf_op jit(solution)/shard_map/ppermute | solution.py:41
  30.2 1.7 %collective-permute-start.16 = (bf16[32,1792]{1,0:T(8,128)(2,1)S(1)}, bf16[32,1792]{1,0:T(8,128)(2,1)S(1)}, u32[]{:S(2)}, u32[]{:S(2)}) collective-permute-start(bf16[32,1792]{1,0:T(8,128)(2,1)S(1)} %fusion.4), channel_id=1, source_target_pairs={{0,1},{1,0},{2,3},{3,2},{4,5},{5,4},{6,7},{7,6},{8,9},{9,8},{10,11... | collective-permute-start | bytes 344072 | tf_op jit(solution)/shard_map/ppermute | solution.py:41
  31.9 1.4 %collective-permute-start.10 = (bf16[1,2,32,1792]{3,2,1,0:T(8,128)(2,1)S(1)}, bf16[1,2,32,1792]{3,2,1,0:T(8,128)(2,1)S(1)}, u32[]{:S(2)}, u32[]{:S(2)}) collective-permute-start(bf16[1,2,32,1792]{3,2,1,0:T(8,128)(2,1)S(1)} %get-tuple-element.88), channel_id=1, source_target_pairs={{0,8},{4,12},{8,0},{12,4},{1,9},{5,13},{9,1},{13,5},{2,10},{6,14},... | collective-permute-start | bytes 688136 | tf_op jit(solution)/shard_map/ppermute | solution.py:41
  33.3 1.8 %collective-permute-done.16 = bf16[32,1792]{1,0:T(8,128)(2,1)S(1)} collective-permute-done((bf16[32,1792]{1,0:T(8,128)(2,1)S(1)}, bf16[32,1792]{1,0:T(8,128)(2,1)S(1)}, u32[]{:S(2)}, u32[]{:S(2)}) %collective-permute-start.16) | collective-permute-done | bytes 114720 | tf_op jit(solution)/shard_map/ppermute | solution.py:41
  35.0 0.1 fusion
  35.1 2.7 %collective-permute-start.17 = (bf16[32,1792]{1,0:T(8,128)(2,1)S(1)}, bf16[32,1792]{1,0:T(8,128)(2,1)S(1)}, u32[]{:S(2)}, u32[]{:S(2)}) collective-permute-start(bf16[32,1792]{1,0:T(8,128)(2,1)S(1)} %fusion), channel_id=1, source_target_pairs={{0,2},{1,3},{2,0},{3,1},{4,6},{5,7},{6,4},{7,5},{8,10},{9,11},{10,... | collective-permute-start | bytes 344072 | tf_op jit(solution)/shard_map/ppermute | solution.py:41
  37.8 0.1 collective-permute-done.10
  37.9 1.5 %collective-permute-start.11 = (bf16[32,1792]{1,0:T(8,128)(2,1)S(1)}, bf16[32,1792]{1,0:T(8,128)(2,1)S(1)}, u32[]{:S(2)}, u32[]{:S(2)}) collective-permute-start(bf16[32,1792]{1,0:T(8,128)(2,1)S(1)} %fusion.3), channel_id=1, source_target_pairs={{0,1},{1,0},{2,3},{3,2},{4,5},{5,4},{6,7},{7,6},{8,9},{9,8},{10,11... | collective-permute-start | bytes 344072 | tf_op jit(solution)/shard_map/ppermute | solution.py:41
  39.4 1.7 %collective-permute-done.17 = bf16[32,1792]{1,0:T(8,128)(2,1)S(1)} collective-permute-done((bf16[32,1792]{1,0:T(8,128)(2,1)S(1)}, bf16[32,1792]{1,0:T(8,128)(2,1)S(1)}, u32[]{:S(2)}, u32[]{:S(2)}) %collective-permute-start.17) | collective-permute-done | bytes 114720 | tf_op jit(solution)/shard_map/ppermute | solution.py:41
  41.1 1.7 %collective-permute-done.11 = bf16[32,1792]{1,0:T(8,128)(2,1)S(1)} collective-permute-done((bf16[32,1792]{1,0:T(8,128)(2,1)S(1)}, bf16[32,1792]{1,0:T(8,128)(2,1)S(1)}, u32[]{:S(2)}, u32[]{:S(2)}) %collective-permute-start.11) | collective-permute-done | bytes 114720 | tf_op jit(solution)/shard_map/ppermute | solution.py:41
  42.8 0.7 %fusion.2 = bf16[32,1792]{1,0:T(8,128)(2,1)} fusion(bf16[32,1792]{1,0:T(8,128)(2,1)S(1)} %collective-permute-done.17, bf16[32,1792]{1,0:T(8,128)(2,1)S(1)} %collective-permute-done.11, bf16[1,2,32,1792]{3,2,1,0:T(8,128)(2,1)S(1)} %collective-permute-done.10, bf16[1,2,32,1792]{3,2,1,0:T(8,128)(2,1)S(1)} %get-tuple-element.87), kind=kLoop, calls=%fused_computation.6 | loop fusion | flops 458752 | bytes 573440 | tf_op jit(solution)/shard_map/convert_element_type | solution.py:49
  (15 shorter events, 0.2 us)
Async XLA Ops:
  0.0 13.7 %collective-permute-start = (bf16[32,7168]{1,0:T(8,128)(2,1)}, bf16[32,7168]{1,0:T(8,128)(2,1)S(1)}, u32[]{:S(2)}, u32[]{:S(2)}) collective-permute-start(bf16[32,7168]{1,0:T(8,128)(2,1)} %bitcast.35), channel_id=1, source_target_pairs={{0,8},{4,12},{8,0},{12,4},{1,9},{5,13},{9,1},{13,5},{2,10},{6,14},... | collective-permute-start | bytes 1376264 | tf_op jit(solution)/shard_map/ppermute | solution.py:41
  3.0 10.7 %collective-permute-start.1 = (bf16[2,16,7168]{2,1,0:T(8,128)(2,1)}, bf16[2,16,7168]{2,1,0:T(8,128)(2,1)S(1)}, u32[]{:S(2)}, u32[]{:S(2)}) collective-permute-start(bf16[2,16,7168]{2,1,0:T(8,128)(2,1)} %param.25), channel_id=1, source_target_pairs={{0,4},{4,0},{8,12},{12,8},{1,5},{5,1},{9,13},{13,9},{2,6},{6,2},{1... | collective-permute-start | bytes 1376264 | tf_op jit(solution)/shard_map/ppermute | solution.py:41
  3.0 13.0 %collective-permute-start.4 = (bf16[4,16,7168]{2,1,0:T(8,128)(2,1)}, bf16[4,16,7168]{2,1,0:T(8,128)(2,1)S(1)}, u32[]{:S(2)}, u32[]{:S(2)}) collective-permute-start(bf16[4,16,7168]{2,1,0:T(8,128)(2,1)} %param.28), channel_id=1, source_target_pairs={{0,4},{4,0},{8,12},{12,8},{1,5},{5,1},{9,13},{13,9},{2,6},{6,2},{1... | collective-permute-start | bytes 2752520 | tf_op jit(solution)/shard_map/ppermute | solution.py:41
  3.5 12.5 %collective-permute-start.2 = (bf16[32,7168]{1,0:T(8,128)(2,1)}, bf16[32,7168]{1,0:T(8,128)(2,1)S(1)}, u32[]{:S(2)}, u32[]{:S(2)}) collective-permute-start(bf16[32,7168]{1,0:T(8,128)(2,1)} %bitcast.36), channel_id=1, source_target_pairs={{0,4},{4,0},{8,12},{12,8},{1,5},{5,1},{9,13},{13,9},{2,6},{6,2},{1... | collective-permute-start | bytes 1376264 | tf_op jit(solution)/shard_map/ppermute | solution.py:41
  13.7 2.3 %collective-permute-start.3 = (bf16[32,7168]{1,0:T(8,128)(2,1)S(1)}, bf16[32,7168]{1,0:T(8,128)(2,1)S(1)}, u32[]{:S(2)}, u32[]{:S(2)}) collective-permute-start(bf16[32,7168]{1,0:T(8,128)(2,1)S(1)} %collective-permute-done.refs_2_), channel_id=1, source_target_pairs={{0,4},{4,0},{8,12},{12,8},{1,5},{5,1},{9,13},{13,9},{2,6},{6,2},{1... | collective-permute-start | bytes 1376264 | tf_op jit(solution)/shard_map/ppermute | solution.py:41
  13.7 6.1 %collective-permute-start.6 = (bf16[128,256]{1,0:T(8,128)(2,1)S(1)}, bf16[128,256]{1,0:T(8,128)(2,1)S(1)}, u32[]{:S(2)}, u32[]{:S(2)}) collective-permute-start(bf16[128,256]{1,0:T(8,128)(2,1)S(1)} %get-tuple-element.77.refs_7_), channel_id=1, source_target_pairs={{0,4},{4,0},{8,12},{12,8},{1,5},{5,1},{9,13},{13,9},{2,6},{6,2},{1... | collective-permute-start | bytes 196616 | tf_op jit(solution)/shard_map/ppermute | solution.py:41
  14.2 5.6 %collective-permute-start.7 = (bf16[128,256]{1,0:T(8,128)(2,1)S(1)}, bf16[128,256]{1,0:T(8,128)(2,1)S(1)}, u32[]{:S(2)}, u32[]{:S(2)}) collective-permute-start(bf16[128,256]{1,0:T(8,128)(2,1)S(1)} %get-tuple-element.77.refs_7_), channel_id=1, source_target_pairs={{0,8},{4,12},{8,0},{12,4},{1,9},{5,13},{9,1},{13,5},{2,10},{6,14},... | collective-permute-start | bytes 196616 | tf_op jit(solution)/shard_map/ppermute | solution.py:41
  16.0 4.3 %collective-permute-start.8 = (bf16[128,256]{1,0:T(8,128)(2,1)S(1)}, bf16[128,256]{1,0:T(8,128)(2,1)S(1)}, u32[]{:S(2)}, u32[]{:S(2)}) collective-permute-start(bf16[128,256]{1,0:T(8,128)(2,1)S(1)} %get-tuple-element.77.refs_7_), channel_id=1, source_target_pairs={{0,12},{4,8},{8,4},{12,0},{1,13},{5,9},{9,5},{13,1},{2,14},{6,10},... | collective-permute-start | bytes 196616 | tf_op jit(solution)/shard_map/ppermute | solution.py:41
  17.2 3.9 %collective-permute-start.5 = (bf16[32,384]{1,0:T(8,128)(2,1)S(1)}, bf16[32,384]{1,0:T(8,128)(2,1)S(1)}, u32[]{:S(2)}, u32[]{:S(2)}) collective-permute-start(bf16[32,384]{1,0:T(8,128)(2,1)S(1)} %get-tuple-element.76), channel_id=1, source_target_pairs={{0,8},{4,12},{8,0},{12,4},{1,9},{5,13},{9,1},{13,5},{2,10},{6,14},... | collective-permute-start | bytes 73736 | tf_op jit(solution)/shard_map/ppermute | solution.py:41
  22.5 1.6 %collective-permute-start.14 = (bf16[2,1,32,1792]{3,2,1,0:T(8,128)(2,1)S(1)}, bf16[2,1,32,1792]{3,2,1,0:T(8,128)(2,1)S(1)}, u32[]{:S(2)}, u32[]{:S(2)}) collective-permute-start(bf16[2,1,32,1792]{3,2,1,0:T(8,128)(2,1)S(1)} %get-tuple-element.85), channel_id=1, source_target_pairs={{0,4},{4,0},{8,12},{12,8},{1,5},{5,1},{9,13},{13,9},{2,6},{6,2},{1... | collective-permute-start | bytes 688136 | tf_op jit(solution)/shard_map/ppermute | solution.py:41
  22.6 4.0 %collective-permute-start.9 = (bf16[2,2,32,1792]{3,2,1,0:T(8,128)(2,1)S(1)}, bf16[2,2,32,1792]{3,2,1,0:T(8,128)(2,1)S(1)}, u32[]{:S(2)}, u32[]{:S(2)}) collective-permute-start(bf16[2,2,32,1792]{3,2,1,0:T(8,128)(2,1)S(1)} %get-tuple-element.81), channel_id=1, source_target_pairs={{0,4},{4,0},{8,12},{12,8},{1,5},{5,1},{9,13},{13,9},{2,6},{6,2},{1... | collective-permute-start | bytes 1376264 | tf_op jit(solution)/shard_map/ppermute | solution.py:41
  23.1 2.5 %collective-permute-start.12 = (bf16[2,1,32,1792]{3,2,1,0:T(8,128)(2,1)S(1)}, bf16[2,1,32,1792]{3,2,1,0:T(8,128)(2,1)S(1)}, u32[]{:S(2)}, u32[]{:S(2)}) collective-permute-start(bf16[2,1,32,1792]{3,2,1,0:T(8,128)(2,1)S(1)} %get-tuple-element.83), channel_id=1, source_target_pairs={{0,4},{4,0},{8,12},{12,8},{1,5},{5,1},{9,13},{13,9},{2,6},{6,2},{1... | collective-permute-start | bytes 688136 | tf_op jit(solution)/shard_map/ppermute | solution.py:41
  24.1 6.1 %collective-permute-start.15 = (bf16[1,1,32,1792]{3,2,1,0:T(8,128)(2,1)S(1)}, bf16[1,1,32,1792]{3,2,1,0:T(8,128)(2,1)S(1)}, u32[]{:S(2)}, u32[]{:S(2)}) collective-permute-start(bf16[1,1,32,1792]{3,2,1,0:T(8,128)(2,1)S(1)} %add_convert_fusion.3), channel_id=1, source_target_pairs={{0,8},{4,12},{8,0},{12,4},{1,9},{5,13},{9,1},{13,5},{2,10},{6,14},... | collective-permute-start | bytes 344072 | tf_op jit(solution)/shard_map/ppermute | solution.py:41
  25.6 7.6 %collective-permute-start.13 = (bf16[1,1,32,1792]{3,2,1,0:T(8,128)(2,1)S(1)}, bf16[1,1,32,1792]{3,2,1,0:T(8,128)(2,1)S(1)}, u32[]{:S(2)}, u32[]{:S(2)}) collective-permute-start(bf16[1,1,32,1792]{3,2,1,0:T(8,128)(2,1)S(1)} %add_convert_fusion.5), channel_id=1, source_target_pairs={{0,8},{4,12},{8,0},{12,4},{1,9},{5,13},{9,1},{13,5},{2,10},{6,14},... | collective-permute-start | bytes 344072 | tf_op jit(solution)/shard_map/ppermute | solution.py:41
  30.2 4.9 %collective-permute-start.16 = (bf16[32,1792]{1,0:T(8,128)(2,1)S(1)}, bf16[32,1792]{1,0:T(8,128)(2,1)S(1)}, u32[]{:S(2)}, u32[]{:S(2)}) collective-permute-start(bf16[32,1792]{1,0:T(8,128)(2,1)S(1)} %fusion.4), channel_id=1, source_target_pairs={{0,1},{1,0},{2,3},{3,2},{4,5},{5,4},{6,7},{7,6},{8,9},{9,8},{10,11... | collective-permute-start | bytes 344072 | tf_op jit(solution)/shard_map/ppermute | solution.py:41
  31.9 6.0 %collective-permute-start.10 = (bf16[1,2,32,1792]{3,2,1,0:T(8,128)(2,1)S(1)}, bf16[1,2,32,1792]{3,2,1,0:T(8,128)(2,1)S(1)}, u32[]{:S(2)}, u32[]{:S(2)}) collective-permute-start(bf16[1,2,32,1792]{3,2,1,0:T(8,128)(2,1)S(1)} %get-tuple-element.88), channel_id=1, source_target_pairs={{0,8},{4,12},{8,0},{12,4},{1,9},{5,13},{9,1},{13,5},{2,10},{6,14},... | collective-permute-start | bytes 688136 | tf_op jit(solution)/shard_map/ppermute | solution.py:41
  35.1 6.0 %collective-permute-start.17 = (bf16[32,1792]{1,0:T(8,128)(2,1)S(1)}, bf16[32,1792]{1,0:T(8,128)(2,1)S(1)}, u32[]{:S(2)}, u32[]{:S(2)}) collective-permute-start(bf16[32,1792]{1,0:T(8,128)(2,1)S(1)} %fusion), channel_id=1, source_target_pairs={{0,2},{1,3},{2,0},{3,1},{4,6},{5,7},{6,4},{7,5},{8,10},{9,11},{10,... | collective-permute-start | bytes 344072 | tf_op jit(solution)/shard_map/ppermute | solution.py:41
  37.9 4.9 %collective-permute-start.11 = (bf16[32,1792]{1,0:T(8,128)(2,1)S(1)}, bf16[32,1792]{1,0:T(8,128)(2,1)S(1)}, u32[]{:S(2)}, u32[]{:S(2)}) collective-permute-start(bf16[32,1792]{1,0:T(8,128)(2,1)S(1)} %fusion.3), channel_id=1, source_target_pairs={{0,1},{1,0},{2,3},{3,2},{4,5},{5,4},{6,7},{7,6},{8,9},{9,8},{10,11... | collective-permute-start | bytes 344072 | tf_op jit(solution)/shard_map/ppermute | solution.py:41

commit v7 on v6

--- a/solution.py
+++ b/solution.py
@@ -222,25 +222,21 @@
 def inner_kernel(count, chunk, *refs):
     rows, shared, stored, outs = refs[:count], refs[count : count + 2], refs[count + 2 : count + 4], refs[count + 4 :]
     size, depth = rows[0].shape
-    columns = (((1,), (1,)), ((), ()))
-    total_shared, total_stored = 0.0, 0.0
+    split = 2 * shared[0].shape[0]
+    total = 0.0
     for k in range(depth // chunk):
         part = pl.ds(k * chunk, chunk)
-        held = [ref[:, part] for ref in rows]
-        total_stored += lax.dot_general(
-            jnp.concatenate(held, axis=0),
-            jnp.concatenate([ref[:, part] for ref in stored], axis=0),
-            columns,
+        total += lax.dot_general(
+            jnp.concatenate([ref[:, part] for ref in rows], axis=0),
+            jnp.concatenate([ref[:, part] for ref in (*shared, *stored)], axis=0),
+            (((1,), (1,)), ((), ())),
             preferred_element_type=F32,
         )
-        total_shared += lax.dot_general(
-            jnp.concatenate(held[::2], axis=0),
-            jnp.concatenate([ref[:, part] for ref in shared], axis=0),
-            columns,
-            preferred_element_type=F32,
-        )
-    total_stored = total_stored.astype(BF16)
-    total_shared = total_shared.astype(BF16)
+    total = total.astype(BF16)
+    total_shared = jnp.concatenate(
+        [total[r * size : (r + 1) * size, :split] for r in range(0, count, 2)], axis=0
+    )
+    total_stored = total[:, split:]
     for n, out in enumerate(outs):
         blocks = [total_shared[n * size : (n + 1) * size]]
         blocks += [total_stored[k * size : (k + 1) * size] for k in range(count)]
@@ -429,9 +425,10 @@
     gate_weight, up_weight, down, down_own = first[7:]
     rows = exchange_rest(rows_own, arrived)
     rows[0] = rows_held
-    packs = [pack] + [swap(pack, r) for r in range(1, count)]
+    pack_arrived = swap(pack, count // 2)
     inner = inner_products(rows, [factor_shared, shared_other], [factor_store, store_other])
-    rows, inner = lax.optimization_barrier((rows, inner))
+    rows, inner, pack_arrived = lax.optimization_barrier((rows, inner, pack_arrived))
+    packs = exchange_rest(pack, pack_arrived)
     inners = [inner[0]] + [swap(inner[n], 2 * n) for n in range(1, count // 2)]
     gate, up = gate_up(rows, gate_weight, up_weight)
 

time: 43.6 us -> 44.8 us (1.028)
  starting transfers between devices: 17.6 us -> 18.4 us
    ppermute x18, starting transfers between devices: 17.6 us -> 18.4 us  [swap(): return lax.ppermute(value, axis, [(i, i ^ bits) for i in range(count)])]
    ppermute x18, waiting for transfers between devices: 11.4 us -> 11.8 us  [swap(): return lax.ppermute(value, axis, [(i, i ^ bits) for i in range(count)])]
  transfers between devices with their start and end apart: 18 -> 18, of which waited for: 9 -> 9; matrix products, arithmetic and copies ran while one was open for 1% -> 1% of each run, Pallas kernels for 28% -> 27%
where the time goes in v7:
time: 44.8 us; the launch traced here: 44.6 us
  starting transfers between devices  18.4 us (41%)
  Pallas kernels  13.2 us (29%)
  waiting for transfers between devices  11.8 us (26%)
  other arithmetic  1.03 us (2%)
    ppermute x18, starting transfers between devices, swap(): return lax.ppermute(value, axis, [(i, i ^ bits) for i in range(count)])  18.4 us
    ppermute x18, waiting for transfers between devices, swap(): return lax.ppermute(value, axis, [(i, i ^ bits) for i in range(count)])  11.8 us
    pallas_call x1, Pallas kernels, first_products(): pl.pallas_call(functools.partial(first_kernel, experts, pieces), in_specs...  9.63 us
    pallas_call x1, Pallas kernels, down_products(): pl.pallas_call(functools.partial(down_kernel, shared_count, store_count,...  1.38 us
    pallas_call x1, Pallas kernels, gate_up(): pl.pallas_call(functools.partial(gate_up_kernel, len(rows), 1024), in_spe...  1.19 us
    pallas_call x1, Pallas kernels, inner_products(): pl.pallas_call(functools.partial(inner_kernel, count, 1024), in_specs=[VM...  1.05 us
  transfers between devices with their start and end apart: 18, of which 9 were waited for; matrix products, arithmetic and copies ran while one was open for 1% of the time, Pallas kernels for 27%

profile of v7, /device:TPU:0, one launch (start us, length us, event | category | flops | bytes accessed | tf_op | source)
XLA Modules:
  0.0 44.6 jit_solution(9140069427756673091)
XLA Ops:
  0.0 3.0 %collective-permute-start = (bf16[32,7168]{1,0:T(8,128)(2,1)}, bf16[32,7168]{1,0:T(8,128)(2,1)S(1)}, u32[]{:S(2)}, u32[]{:S(2)}) collective-permute-start(bf16[32,7168]{1,0:T(8,128)(2,1)} %bitcast.35), channel_id=1, source_target_pairs={{0,8},{4,12},{8,0},{12,4},{1,9},{5,13},{9,1},{13,5},{2,10},{6,14},... | collective-permute-start | bytes 1376264 | tf_op jit(solution)/shard_map/ppermute | solution.py:41
  3.0 0.0 collective-permute-start.1
  3.0 0.5 %collective-permute-start.4 = (bf16[4,16,7168]{2,1,0:T(8,128)(2,1)}, bf16[4,16,7168]{2,1,0:T(8,128)(2,1)S(1)}, u32[]{:S(2)}, u32[]{:S(2)}) collective-permute-start(bf16[4,16,7168]{2,1,0:T(8,128)(2,1)} %param.28), channel_id=1, source_target_pairs={{0,4},{4,0},{8,12},{12,8},{1,5},{5,1},{9,13},{13,9},{2,6},{6,2},{1... | collective-permute-start | bytes 2752520 | tf_op jit(solution)/shard_map/ppermute | solution.py:41
  3.5 9.6 %shard_map.145 = (f32[32,256]{1,0:T(8,128)S(1)}, f32[32,256]{1,0:T(8,128)S(1)}, bf16[128,256]{1,0:T(8,128)(2,1)S(1)}, s32[8,256]{1,0:T(8,128)S(1)}, bf16[32,7168...) custom-call(bf16[32,7168]{1,0:T(8,128)(2,1)} %bitcast.37, ...), custom_call_target="tpu_custom_call" | custom-call | flops 234881024 | bytes 23855104 | tf_op jit(solution)/shard_map/pallas_call | solution.py:201
  13.1 0.6 %collective-permute-done.refs_2_ = bf16[32,7168]{1,0:T(8,128)(2,1)S(1)} collective-permute-done((bf16[32,7168]{1,0:T(8,128)(2,1)}, bf16[32,7168]{1,0:T(8,128)(2,1)S(1)}, u32[]{:S(2)}, u32[]{:S(2)}) %collective-permute-start) | collective-permute-done | bytes 458784 | tf_op jit(solution)/shard_map/ppermute | solution.py:41
  13.7 0.0 collective-permute-start.3
  13.7 1.7 %collective-permute-start.5 = (bf16[128,256]{1,0:T(8,128)(2,1)S(1)}, bf16[128,256]{1,0:T(8,128)(2,1)S(1)}, u32[]{:S(2)}, u32[]{:S(2)}) collective-permute-start(bf16[128,256]{1,0:T(8,128)(2,1)S(1)} %get-tuple-element.65.refs_7_), channel_id=1, source_target_pairs={{0,8},{4,12},{8,0},{12,4},{1,9},{5,13},{9,1},{13,5},{2,10},{6,14},... | collective-permute-start | bytes 196616 | tf_op jit(solution)/shard_map/ppermute | solution.py:41
  15.4 0.2 collective-permute-start.7
  15.7 1.0 %shard_map.146 = (bf16[32,384]{1,0:T(8,128)(2,1)S(1)}, bf16[32,384]{1,0:T(8,128)(2,1)S(1)}) custom-call(bf16[32,7168]{1,0:T(8,128)(2,1)S(1)} %get-tuple-element.66.refs_0_, bf16[32,7168]{1,0:T(8,128)(2,1)S(1)} %collective-permute-done.2.refs_1_, bf16[32,7168]{1,0:T(8,128)(2,1)S(1)} %collective-permute-done.refs_2_, ...), custom_call_target="tpu_custom_call" | custom-call | flops 234881024 | bytes 4587520 | tf_op jit(solution)/shard_map/pallas_call | solution.py:252
  16.7 1.5 %collective-permute-done.5.refs_9_ = bf16[128,256]{1,0:T(8,128)(2,1)S(1)} collective-permute-done((bf16[128,256]{1,0:T(8,128)(2,1)S(1)}, bf16[128,256]{1,0:T(8,128)(2,1)S(1)}, u32[]{:S(2)}, u32[]{:S(2)}) %collective-permute-start.5) | collective-permute-done | bytes 65568 | tf_op jit(solution)/shard_map/ppermute | solution.py:41
  18.2 1.7 %collective-permute-start.6 = (bf16[32,384]{1,0:T(8,128)(2,1)S(1)}, bf16[32,384]{1,0:T(8,128)(2,1)S(1)}, u32[]{:S(2)}, u32[]{:S(2)}) collective-permute-start(bf16[32,384]{1,0:T(8,128)(2,1)S(1)} %get-tuple-element.78), channel_id=1, source_target_pairs={{0,8},{4,12},{8,0},{12,4},{1,9},{5,13},{9,1},{13,5},{2,10},{6,14},... | collective-permute-start | bytes 73736 | tf_op jit(solution)/shard_map/ppermute | solution.py:41
  20.0 1.2 %shard_map.147 = (f32[128,256]{1,0:T(8,128)S(1)}, f32[128,256]{1,0:T(8,128)S(1)}) custom-call(bf16[32,7168]{1,0:T(8,128)(2,1)S(1)} %get-tuple-element.66.refs_0_, bf16[32,7168]{1,0:T(8,128)(2,1)S(1)} %collective-permute-done.2.refs_1_, bf16[32,7168]{1,0:T(8,128)(2,1)S(1)} %collective-permute-done.refs_2_, ...), custom_call_target="tpu_custom_call" | custom-call | flops 939524096 | bytes 7340032 | tf_op jit(solution)/shard_map/pallas_call | solution.py:280
  21.2 0.9 %collective-permute-done.6.refs_6_ = bf16[32,384]{1,0:T(8,128)(2,1)S(1)} collective-permute-done((bf16[32,384]{1,0:T(8,128)(2,1)S(1)}, bf16[32,384]{1,0:T(8,128)(2,1)S(1)}, u32[]{:S(2)}, u32[]{:S(2)}) %collective-permute-start.6) | collective-permute-done | bytes 24608 | tf_op jit(solution)/shard_map/ppermute | solution.py:41
  22.0 1.4 %shard_map.148 = (bf16[2,1,32,1792]{3,2,1,0:T(8,128)(2,1)S(1)}, bf16[2,1,32,1792]{3,2,1,0:T(8,128)(2,1)S(1)}, bf16[2,1,32,1792]{3,2,1,0:T(8,128)(2,1)S(1)}, bf16...) custom-call(f32[128,256]{1,0:T(8,128)S(1)} %get-tuple-element.72.refs_0_, ...), custom_call_target="tpu_custom_call" | custom-call | flops 587202560 | bytes 7340032 | tf_op jit(solution)/shard_map/pallas_call | solution.py:364
  23.4 0.1 collective-permute-start.14
  23.5 0.5 %collective-permute-start.9 = (bf16[2,2,32,1792]{3,2,1,0:T(8,128)(2,1)S(1)}, bf16[2,2,32,1792]{3,2,1,0:T(8,128)(2,1)S(1)}, u32[]{:S(2)}, u32[]{:S(2)}) collective-permute-start(bf16[2,2,32,1792]{3,2,1,0:T(8,128)(2,1)S(1)} %get-tuple-element.83), channel_id=1, source_target_pairs={{0,4},{4,0},{8,12},{12,8},{1,5},{5,1},{9,13},{13,9},{2,6},{6,2},{1... | collective-permute-start | bytes 1376264 | tf_op jit(solution)/shard_map/ppermute | solution.py:41
  24.0 0.1 collective-permute-start.12
  24.1 0.9 %collective-permute-done.14 = bf16[2,1,32,1792]{3,2,1,0:T(8,128)(2,1)S(1)} collective-permute-done((bf16[2,1,32,1792]{3,2,1,0:T(8,128)(2,1)S(1)}, bf16[2,1,32,1792]{3,2,1,0:T(8,128)(2,1)S(1)}, u32[]{:S(2)}, u32[]{:S(2)}) %collective-permute-start.14) | collective-permute-done | bytes 229408 | tf_op jit(solution)/shard_map/ppermute | solution.py:41
  25.0 1.8 %collective-permute-start.15 = (bf16[1,1,32,1792]{3,2,1,0:T(8,128)(2,1)S(1)}, bf16[1,1,32,1792]{3,2,1,0:T(8,128)(2,1)S(1)}, u32[]{:S(2)}, u32[]{:S(2)}) collective-permute-start(bf16[1,1,32,1792]{3,2,1,0:T(8,128)(2,1)S(1)} %add_convert_fusion.3), channel_id=1, source_target_pairs={{0,8},{4,12},{8,0},{12,4},{1,9},{5,13},{9,1},{13,5},{2,10},{6,14},... | collective-permute-start | bytes 344072 | tf_op jit(solution)/shard_map/ppermute | solution.py:41
  26.9 0.9 %collective-permute-start.13 = (bf16[1,1,32,1792]{3,2,1,0:T(8,128)(2,1)S(1)}, bf16[1,1,32,1792]{3,2,1,0:T(8,128)(2,1)S(1)}, u32[]{:S(2)}, u32[]{:S(2)}) collective-permute-start(bf16[1,1,32,1792]{3,2,1,0:T(8,128)(2,1)S(1)} %add_convert_fusion.5), channel_id=1, source_target_pairs={{0,8},{4,12},{8,0},{12,4},{1,9},{5,13},{9,1},{13,5},{2,10},{6,14},... | collective-permute-start | bytes 344072 | tf_op jit(solution)/shard_map/ppermute | solution.py:41
  27.8 0.1 add_convert_fusion.1
  27.9 3.1 %collective-permute-done.15 = bf16[1,1,32,1792]{3,2,1,0:T(8,128)(2,1)S(1)} collective-permute-done((bf16[1,1,32,1792]{3,2,1,0:T(8,128)(2,1)S(1)}, bf16[1,1,32,1792]{3,2,1,0:T(8,128)(2,1)S(1)}, u32[]{:S(2)}, u32[]{:S(2)}) %collective-permute-start.15) | collective-permute-done | bytes 114720 | tf_op jit(solution)/shard_map/ppermute | solution.py:41
  31.1 1.9 %collective-permute-start.16 = (bf16[32,1792]{1,0:T(8,128)(2,1)S(1)}, bf16[32,1792]{1,0:T(8,128)(2,1)S(1)}, u32[]{:S(2)}, u32[]{:S(2)}) collective-permute-start(bf16[32,1792]{1,0:T(8,128)(2,1)S(1)} %fusion.4), channel_id=1, source_target_pairs={{0,1},{1,0},{2,3},{3,2},{4,5},{5,4},{6,7},{7,6},{8,9},{9,8},{10,11... | collective-permute-start | bytes 344072 | tf_op jit(solution)/shard_map/ppermute | solution.py:41
  33.0 1.5 %collective-permute-start.10 = (bf16[1,2,32,1792]{3,2,1,0:T(8,128)(2,1)S(1)}, bf16[1,2,32,1792]{3,2,1,0:T(8,128)(2,1)S(1)}, u32[]{:S(2)}, u32[]{:S(2)}) collective-permute-start(bf16[1,2,32,1792]{3,2,1,0:T(8,128)(2,1)S(1)} %get-tuple-element.90), channel_id=1, source_target_pairs={{0,8},{4,12},{8,0},{12,4},{1,9},{5,13},{9,1},{13,5},{2,10},{6,14},... | collective-permute-start | bytes 688136 | tf_op jit(solution)/shard_map/ppermute | solution.py:41
  34.5 1.5 %collective-permute-done.16 = bf16[32,1792]{1,0:T(8,128)(2,1)S(1)} collective-permute-done((bf16[32,1792]{1,0:T(8,128)(2,1)S(1)}, bf16[32,1792]{1,0:T(8,128)(2,1)S(1)}, u32[]{:S(2)}, u32[]{:S(2)}) %collective-permute-start.16) | collective-permute-done | bytes 114720 | tf_op jit(solution)/shard_map/ppermute | solution.py:41
  36.0 0.1 fusion
  36.1 2.9 %collective-permute-start.17 = (bf16[32,1792]{1,0:T(8,128)(2,1)S(1)}, bf16[32,1792]{1,0:T(8,128)(2,1)S(1)}, u32[]{:S(2)}, u32[]{:S(2)}) collective-permute-start(bf16[32,1792]{1,0:T(8,128)(2,1)S(1)} %fusion), channel_id=1, source_target_pairs={{0,2},{1,3},{2,0},{3,1},{4,6},{5,7},{6,4},{7,5},{8,10},{9,11},{10,... | collective-permute-start | bytes 344072 | tf_op jit(solution)/shard_map/ppermute | solution.py:41
  38.9 0.1 collective-permute-done.10
  39.0 1.6 %collective-permute-start.11 = (bf16[32,1792]{1,0:T(8,128)(2,1)S(1)}, bf16[32,1792]{1,0:T(8,128)(2,1)S(1)}, u32[]{:S(2)}, u32[]{:S(2)}) collective-permute-start(bf16[32,1792]{1,0:T(8,128)(2,1)S(1)} %fusion.3), channel_id=1, source_target_pairs={{0,1},{1,0},{2,3},{3,2},{4,5},{5,4},{6,7},{7,6},{8,9},{9,8},{10,11... | collective-permute-start | bytes 344072 | tf_op jit(solution)/shard_map/ppermute | solution.py:41
  40.6 1.2 %collective-permute-done.17 = bf16[32,1792]{1,0:T(8,128)(2,1)S(1)} collective-permute-done((bf16[32,1792]{1,0:T(8,128)(2,1)S(1)}, bf16[32,1792]{1,0:T(8,128)(2,1)S(1)}, u32[]{:S(2)}, u32[]{:S(2)}) %collective-permute-start.17) | collective-permute-done | bytes 114720 | tf_op jit(solution)/shard_map/ppermute | solution.py:41
  41.8 2.1 %collective-permute-done.11 = bf16[32,1792]{1,0:T(8,128)(2,1)S(1)} collective-permute-done((bf16[32,1792]{1,0:T(8,128)(2,1)S(1)}, bf16[32,1792]{1,0:T(8,128)(2,1)S(1)}, u32[]{:S(2)}, u32[]{:S(2)}) %collective-permute-start.11) | collective-permute-done | bytes 114720 | tf_op jit(solution)/shard_map/ppermute | solution.py:41
  43.9 0.7 %fusion.2 = bf16[32,1792]{1,0:T(8,128)(2,1)} fusion(bf16[32,1792]{1,0:T(8,128)(2,1)S(1)} %collective-permute-done.17, bf16[32,1792]{1,0:T(8,128)(2,1)S(1)} %collective-permute-done.11, bf16[1,2,32,1792]{3,2,1,0:T(8,128)(2,1)S(1)} %collective-permute-done.10, bf16[1,2,32,1792]{3,2,1,0:T(8,128)(2,1)S(1)} %get-tuple-element.89), kind=kLoop, calls=%fused_computation.6 | loop fusion | flops 458752 | bytes 573440 | tf_op jit(solution)/shard_map/convert_element_type | solution.py:49
  (15 shorter events, 0.2 us)
Async XLA Ops:
  0.0 13.7 %collective-permute-start = (bf16[32,7168]{1,0:T(8,128)(2,1)}, bf16[32,7168]{1,0:T(8,128)(2,1)S(1)}, u32[]{:S(2)}, u32[]{:S(2)}) collective-permute-start(bf16[32,7168]{1,0:T(8,128)(2,1)} %bitcast.35), channel_id=1, source_target_pairs={{0,8},{4,12},{8,0},{12,4},{1,9},{5,13},{9,1},{13,5},{2,10},{6,14},... | collective-permute-start | bytes 1376264 | tf_op jit(solution)/shard_map/ppermute | solution.py:41
  3.0 10.7 %collective-permute-start.1 = (bf16[2,16,7168]{2,1,0:T(8,128)(2,1)}, bf16[2,16,7168]{2,1,0:T(8,128)(2,1)S(1)}, u32[]{:S(2)}, u32[]{:S(2)}) collective-permute-start(bf16[2,16,7168]{2,1,0:T(8,128)(2,1)} %param.25), channel_id=1, source_target_pairs={{0,4},{4,0},{8,12},{12,8},{1,5},{5,1},{9,13},{13,9},{2,6},{6,2},{1... | collective-permute-start | bytes 1376264 | tf_op jit(solution)/shard_map/ppermute | solution.py:41
  3.0 12.7 %collective-permute-start.4 = (bf16[4,16,7168]{2,1,0:T(8,128)(2,1)}, bf16[4,16,7168]{2,1,0:T(8,128)(2,1)S(1)}, u32[]{:S(2)}, u32[]{:S(2)}) collective-permute-start(bf16[4,16,7168]{2,1,0:T(8,128)(2,1)} %param.28), channel_id=1, source_target_pairs={{0,4},{4,0},{8,12},{12,8},{1,5},{5,1},{9,13},{13,9},{2,6},{6,2},{1... | collective-permute-start | bytes 2752520 | tf_op jit(solution)/shard_map/ppermute | solution.py:41
  3.5 12.2 %collective-permute-start.2 = (bf16[32,7168]{1,0:T(8,128)(2,1)}, bf16[32,7168]{1,0:T(8,128)(2,1)S(1)}, u32[]{:S(2)}, u32[]{:S(2)}) collective-permute-start(bf16[32,7168]{1,0:T(8,128)(2,1)} %bitcast.36), channel_id=1, source_target_pairs={{0,4},{4,0},{8,12},{12,8},{1,5},{5,1},{9,13},{13,9},{2,6},{6,2},{1... | collective-permute-start | bytes 1376264 | tf_op jit(solution)/shard_map/ppermute | solution.py:41
  13.7 2.0 %collective-permute-start.3 = (bf16[32,7168]{1,0:T(8,128)(2,1)S(1)}, bf16[32,7168]{1,0:T(8,128)(2,1)S(1)}, u32[]{:S(2)}, u32[]{:S(2)}) collective-permute-start(bf16[32,7168]{1,0:T(8,128)(2,1)S(1)} %collective-permute-done.refs_2_), channel_id=1, source_target_pairs={{0,4},{4,0},{8,12},{12,8},{1,5},{5,1},{9,13},{13,9},{2,6},{6,2},{1... | collective-permute-start | bytes 1376264 | tf_op jit(solution)/shard_map/ppermute | solution.py:41
  13.7 4.5 %collective-permute-start.5 = (bf16[128,256]{1,0:T(8,128)(2,1)S(1)}, bf16[128,256]{1,0:T(8,128)(2,1)S(1)}, u32[]{:S(2)}, u32[]{:S(2)}) collective-permute-start(bf16[128,256]{1,0:T(8,128)(2,1)S(1)} %get-tuple-element.65.refs_7_), channel_id=1, source_target_pairs={{0,8},{4,12},{8,0},{12,4},{1,9},{5,13},{9,1},{13,5},{2,10},{6,14},... | collective-permute-start | bytes 196616 | tf_op jit(solution)/shard_map/ppermute | solution.py:41
  15.4 5.7 %collective-permute-start.7 = (bf16[128,256]{1,0:T(8,128)(2,1)S(1)}, bf16[128,256]{1,0:T(8,128)(2,1)S(1)}, u32[]{:S(2)}, u32[]{:S(2)}) collective-permute-start(bf16[128,256]{1,0:T(8,128)(2,1)S(1)} %get-tuple-element.65.refs_7_), channel_id=1, source_target_pairs={{0,4},{4,0},{8,12},{12,8},{1,5},{5,1},{9,13},{13,9},{2,6},{6,2},{1... | collective-permute-start | bytes 196616 | tf_op jit(solution)/shard_map/ppermute | solution.py:41
  18.2 3.8 %collective-permute-start.8 = (bf16[128,256]{1,0:T(8,128)(2,1)S(1)}, bf16[128,256]{1,0:T(8,128)(2,1)S(1)}, u32[]{:S(2)}, u32[]{:S(2)}) collective-permute-start(bf16[128,256]{1,0:T(8,128)(2,1)S(1)} %collective-permute-done.5.refs_9_), channel_id=1, source_target_pairs={{0,4},{4,0},{8,12},{12,8},{1,5},{5,1},{9,13},{13,9},{2,6},{6,2},{1... | collective-permute-start | bytes 196616 | tf_op jit(solution)/shard_map/ppermute | solution.py:41
  18.2 3.8 %collective-permute-start.6 = (bf16[32,384]{1,0:T(8,128)(2,1)S(1)}, bf16[32,384]{1,0:T(8,128)(2,1)S(1)}, u32[]{:S(2)}, u32[]{:S(2)}) collective-permute-start(bf16[32,384]{1,0:T(8,128)(2,1)S(1)} %get-tuple-element.78), channel_id=1, source_target_pairs={{0,8},{4,12},{8,0},{12,4},{1,9},{5,13},{9,1},{13,5},{2,10},{6,14},... | collective-permute-start | bytes 73736 | tf_op jit(solution)/shard_map/ppermute | solution.py:41
  23.4 1.6 %collective-permute-start.14 = (bf16[2,1,32,1792]{3,2,1,0:T(8,128)(2,1)S(1)}, bf16[2,1,32,1792]{3,2,1,0:T(8,128)(2,1)S(1)}, u32[]{:S(2)}, u32[]{:S(2)}) collective-permute-start(bf16[2,1,32,1792]{3,2,1,0:T(8,128)(2,1)S(1)} %get-tuple-element.87), channel_id=1, source_target_pairs={{0,4},{4,0},{8,12},{12,8},{1,5},{5,1},{9,13},{13,9},{2,6},{6,2},{1... | collective-permute-start | bytes 688136 | tf_op jit(solution)/shard_map/ppermute | solution.py:41
  23.5 4.3 %collective-permute-start.9 = (bf16[2,2,32,1792]{3,2,1,0:T(8,128)(2,1)S(1)}, bf16[2,2,32,1792]{3,2,1,0:T(8,128)(2,1)S(1)}, u32[]{:S(2)}, u32[]{:S(2)}) collective-permute-start(bf16[2,2,32,1792]{3,2,1,0:T(8,128)(2,1)S(1)} %get-tuple-element.83), channel_id=1, source_target_pairs={{0,4},{4,0},{8,12},{12,8},{1,5},{5,1},{9,13},{13,9},{2,6},{6,2},{1... | collective-permute-start | bytes 1376264 | tf_op jit(solution)/shard_map/ppermute | solution.py:41
  24.0 2.8 %collective-permute-start.12 = (bf16[2,1,32,1792]{3,2,1,0:T(8,128)(2,1)S(1)}, bf16[2,1,32,1792]{3,2,1,0:T(8,128)(2,1)S(1)}, u32[]{:S(2)}, u32[]{:S(2)}) collective-permute-start(bf16[2,1,32,1792]{3,2,1,0:T(8,128)(2,1)S(1)} %get-tuple-element.85), channel_id=1, source_target_pairs={{0,4},{4,0},{8,12},{12,8},{1,5},{5,1},{9,13},{13,9},{2,6},{6,2},{1... | collective-permute-start | bytes 688136 | tf_op jit(solution)/shard_map/ppermute | solution.py:41
  25.0 6.1 %collective-permute-start.15 = (bf16[1,1,32,1792]{3,2,1,0:T(8,128)(2,1)S(1)}, bf16[1,1,32,1792]{3,2,1,0:T(8,128)(2,1)S(1)}, u32[]{:S(2)}, u32[]{:S(2)}) collective-permute-start(bf16[1,1,32,1792]{3,2,1,0:T(8,128)(2,1)S(1)} %add_convert_fusion.3), channel_id=1, source_target_pairs={{0,8},{4,12},{8,0},{12,4},{1,9},{5,13},{9,1},{13,5},{2,10},{6,14},... | collective-permute-start | bytes 344072 | tf_op jit(solution)/shard_map/ppermute | solution.py:41
  26.9 7.6 %collective-permute-start.13 = (bf16[1,1,32,1792]{3,2,1,0:T(8,128)(2,1)S(1)}, bf16[1,1,32,1792]{3,2,1,0:T(8,128)(2,1)S(1)}, u32[]{:S(2)}, u32[]{:S(2)}) collective-permute-start(bf16[1,1,32,1792]{3,2,1,0:T(8,128)(2,1)S(1)} %add_convert_fusion.5), channel_id=1, source_target_pairs={{0,8},{4,12},{8,0},{12,4},{1,9},{5,13},{9,1},{13,5},{2,10},{6,14},... | collective-permute-start | bytes 344072 | tf_op jit(solution)/shard_map/ppermute | solution.py:41
  31.1 4.9 %collective-permute-start.16 = (bf16[32,1792]{1,0:T(8,128)(2,1)S(1)}, bf16[32,1792]{1,0:T(8,128)(2,1)S(1)}, u32[]{:S(2)}, u32[]{:S(2)}) collective-permute-start(bf16[32,1792]{1,0:T(8,128)(2,1)S(1)} %fusion.4), channel_id=1, source_target_pairs={{0,1},{1,0},{2,3},{3,2},{4,5},{5,4},{6,7},{7,6},{8,9},{9,8},{10,11... | collective-permute-start | bytes 344072 | tf_op jit(solution)/shard_map/ppermute | solution.py:41
  33.0 6.0 %collective-permute-start.10 = (bf16[1,2,32,1792]{3,2,1,0:T(8,128)(2,1)S(1)}, bf16[1,2,32,1792]{3,2,1,0:T(8,128)(2,1)S(1)}, u32[]{:S(2)}, u32[]{:S(2)}) collective-permute-start(bf16[1,2,32,1792]{3,2,1,0:T(8,128)(2,1)S(1)} %get-tuple-element.90), channel_id=1, source_target_pairs={{0,8},{4,12},{8,0},{12,4},{1,9},{5,13},{9,1},{13,5},{2,10},{6,14},... | collective-permute-start | bytes 688136 | tf_op jit(solution)/shard_map/ppermute | solution.py:41
  36.1 5.8 %collective-permute-start.17 = (bf16[32,1792]{1,0:T(8,128)(2,1)S(1)}, bf16[32,1792]{1,0:T(8,128)(2,1)S(1)}, u32[]{:S(2)}, u32[]{:S(2)}) collective-permute-start(bf16[32,1792]{1,0:T(8,128)(2,1)S(1)} %fusion), channel_id=1, source_target_pairs={{0,2},{1,3},{2,0},{3,1},{4,6},{5,7},{6,4},{7,5},{8,10},{9,11},{10,... | collective-permute-start | bytes 344072 | tf_op jit(solution)/shard_map/ppermute | solution.py:41
  39.0 4.9 %collective-permute-start.11 = (bf16[32,1792]{1,0:T(8,128)(2,1)S(1)}, bf16[32,1792]{1,0:T(8,128)(2,1)S(1)}, u32[]{:S(2)}, u32[]{:S(2)}) collective-permute-start(bf16[32,1792]{1,0:T(8,128)(2,1)S(1)} %fusion.3), channel_id=1, source_target_pairs={{0,1},{1,0},{2,3},{3,2},{4,5},{5,4},{6,7},{7,6},{8,9},{9,8},{10,11... | collective-permute-start | bytes 344072 | tf_op jit(solution)/shard_map/ppermute | solution.py:41

commit v8 on v7

v8 whole, which is shorter than its diff:
```python
import functools

import jax
import jax.numpy as jnp
from jax import lax
from jax.experimental import pallas as pl
from jax.experimental.pallas import tpu as pltpu
from jax.sharding import PartitionSpec as P

F32 = jnp.float32
BF16 = jnp.bfloat16
MIB = 1024 * 1024


def params(mebibytes):
    return pltpu.CompilerParams(vmem_limit_bytes=mebibytes * MIB)


def cost(flops, moved):
    return pl.CostEstimate(flops=int(flops), bytes_accessed=int(moved), transcendentals=0)


def in_vmem(value):
    return pltpu.with_memory_space_constraint(value, pltpu.VMEM)


def in_hbm(value):
    return pltpu.with_memory_space_constraint(value, pltpu.HBM)


def vmem_shape(value):
    return pltpu.VMEM(value.shape, value.dtype)


VMEM_SPEC = pl.BlockSpec(memory_space=pltpu.VMEM)
HBM_SPEC = pl.BlockSpec(memory_space=pltpu.HBM)


def swap(value, bits, axis="expert"):
    count = lax.axis_size(axis)
    return lax.ppermute(value, axis, [(i, i ^ bits) for i in range(count)])


def add(one, other):
    return (one.astype(F32) + other.astype(F32)).astype(BF16)


def total_of(values):
    return sum(value.astype(F32) for value in values).astype(BF16)


def exchange_rest(value, arrived):
    count = lax.axis_size("expert")
    bit = count // 2
    pieces = {0: value, bit: arrived}
    bit //= 2
    while bit >= 1:
        pieces.update({r ^ bit: swap(piece, bit) for r, piece in list(pieces.items())})
        bit //= 2
    return [pieces[r] for r in range(count)]


def tile_of(width):
    return 256 if width % 256 == 0 else 128


def column_of(row, size):
    lane = lax.broadcasted_iota(jnp.int32, (size, row.shape[1]), 1)
    place = lax.broadcasted_iota(jnp.int32, (size, row.shape[1]), 0)
    return jnp.sum(jnp.where(lane == place, row.astype(F32), 0.0), axis=1, keepdims=True)


def first_kernel(
    experts, ids, values, tenants, pair_slot, rows, store_b, shared_b, factor_store, factor_shared,
    gate_weight, up_weight, gate_shared, up_shared, down, down_shared, meta, columns, *refs
):
    targets, (ids_held, values_held, tenants_held, pair_slot_held, small_sems, sems) = refs[:-6], refs[-6:]
    own, own_part = lax.axis_index("expert"), lax.axis_index("tensor")
    parts = lax.axis_size("tensor")
    small = [
        (ids, ids_held), (values, values_held), (tenants, tenants_held), (pair_slot, pair_slot_held)
    ]
    small = [
        pltpu.make_async_copy(source, target, small_sems.at[n])
        for n, (source, target) in enumerate(small)
    ]
    sources = [
        rows, store_b, shared_b, factor_store, factor_shared, gate_weight, up_weight, gate_shared,
        up_shared, down, down_shared,
    ]
    staged = list(zip(sources[:5], targets[:5]))
    piece = gate_weight.shape[0] // parts
    for source, target in zip(sources[5:9], targets[5:9]):
        for k in range(parts):
            part = pl.ds(k * piece, piece)
            staged.append((source.at[part], target.at[part]))
    for source, target in zip(sources[9:], targets[9:]):
        for j in range(parts):
            start = pl.multiple_of((own_part ^ j) * piece, piece)
            staged.append((source.at[:, pl.ds(start, piece)], target.at[:, pl.ds(j * piece, piece)]))
    staged = [
        pltpu.make_async_copy(source, target, sems.at[n])
        for n, (source, target) in enumerate(staged)
    ]
    for copy in (*small, *staged):
        copy.start()
    for copy in small:
        copy.wait()

    steps, top, size = ids_held.shape
    tenant = column_of(tenants_held[...], size)
    lane = lax.broadcasted_iota(jnp.int32, (size, meta.shape[1]), 1)
    for s in range(steps):
        weight = jnp.zeros(lane.shape, F32)
        for k in range(top):
            expert = column_of(ids_held[s, k : k + 1], size).astype(jnp.int32)
            value = column_of(values_held[s, k : k + 1], size)
            weight = weight + jnp.where(expert == lane % experts, value, 0.0)
        high = weight.astype(BF16).astype(F32)
        middle = (weight - high).astype(BF16).astype(F32)
        low = weight - high - middle
        found = jnp.where(lane < experts, high, jnp.where(lane < 2 * experts, middle, low))
        found = jnp.where(lane < 3 * experts, found, tenant)
        meta[s * size : (s + 1) * size] = found.astype(BF16)

    tenant_count = pair_slot_held.shape[1]
    place = lax.broadcasted_iota(jnp.int32, pair_slot_held.shape, 0)
    own_row = jnp.sum(
        jnp.where(place == own, pair_slot_held[...].astype(F32), 0.0), axis=0, keepdims=True
    )
    own_slots = column_of(own_row, tenant_count).astype(jnp.int32)
    total = columns.shape[1]
    per_device = tenant_count // lax.axis_size("expert")
    shared_count, store_count = shared_b.shape[0], store_b.shape[0]
    rank = shared_count // per_device
    column = lax.broadcasted_iota(jnp.int32, (1, total), 1)
    shared_tenant = own * per_device + column % shared_count // rank
    slot = (own ^ (column // store_count)) * (store_count // rank) + column % store_count // rank
    tenant_number = lax.broadcasted_iota(jnp.int32, (tenant_count, total), 0)
    slot_tenant = jnp.max(jnp.where(own_slots == slot, tenant_number, -1), axis=0, keepdims=True)
    columns[0:1] = shared_tenant
    columns[1:2] = slot_tenant
    columns[2:3] = jnp.full((1, total), own, jnp.int32)
    columns[3:8] = jnp.zeros((5, total), jnp.int32)
    for copy in staged:
        copy.wait()


def first_call(experts, ids, values, tenants, pair_slot, staged):
    parts = lax.axis_size("tensor")
    steps, _, size = ids.shape
    columns = max(lax.axis_size("expert") * staged[1].shape[0], staged[2].shape[0])
    outs = [
        jax.ShapeDtypeStruct((steps * size, META), BF16),
        jax.ShapeDtypeStruct((8, columns), jnp.int32),
        *[vmem_shape(value) for value in staged],
    ]
    inputs = [ids, values, tenants, pair_slot, *staged]
    return pl.pallas_call(
        functools.partial(first_kernel, experts),
        in_specs=[HBM_SPEC] * len(inputs),
        out_specs=[VMEM_SPEC] * len(outs),
        out_shape=outs,
        scratch_shapes=[
            pltpu.VMEM(ids.shape, jnp.int32),
            pltpu.VMEM(values.shape, F32),
            pltpu.VMEM(tenants.shape, jnp.int32),
            pltpu.VMEM(pair_slot.shape, jnp.int32),
            pltpu.SemaphoreType.DMA((4,)),
            pltpu.SemaphoreType.DMA((5 + 6 * parts,)),
        ],
        compiler_params=params(4),
        cost_estimate=cost(0, 2 * sum(value.size for value in staged)),
    )(*[in_hbm(value) for value in inputs])


META = 128


def message_layout(count, store_count):
    wide = max(128, 2 * store_count)
    per = wide // (2 * store_count)
    return wide + META, per, -(-(count // 2) // per)


def message_kernel(chunk, *refs):
    half = len(refs) - 5
    rows, (factor, factor_other, store_b, meta, out) = refs[:half], refs[half:]
    size, depth = rows[0].shape
    store_count, width = store_b.shape
    total = 0.0
    for k in range(depth // chunk):
        part = pl.ds(k * chunk, chunk)
        total += lax.dot_general(
            jnp.concatenate([ref[:, part] for ref in rows], axis=0),
            jnp.concatenate([factor[:, part], factor_other[:, part]], axis=0),
            (((1,), (1,)), ((), ())),
            preferred_element_type=F32,
        )
    total = total.astype(BF16)
    wide, per, lines = message_layout(2 * half, store_count)
    out[:store_count, :width] = store_b[...]
    if width < wide:
        out[:store_count, width:] = jnp.zeros((store_count, wide - width), BF16)
    for line in range(lines):
        blocks = [
            total[n * size : (n + 1) * size] if n < half else jnp.zeros((size, 2 * store_count), BF16)
            for n in range(line * per, (line + 1) * per)
        ]
        blocks.append(meta[...] if line == 0 else jnp.zeros(meta.shape, BF16))
        start = store_count + line * size
        out[start : start + size] = jnp.concatenate(blocks, axis=1)


def make_message(rows, factor, factor_other, store_b, meta):
    size, depth = rows[0].shape
    store_count = store_b.shape[0]
    wide, _, lines = message_layout(2 * len(rows), store_count)
    inputs = [*rows, factor, factor_other, store_b, meta]
    return pl.pallas_call(
        functools.partial(message_kernel, 1024),
        in_specs=[VMEM_SPEC] * len(inputs),
        out_specs=VMEM_SPEC,
        out_shape=jax.ShapeDtypeStruct((store_count + lines * size, wide), BF16),
        compiler_params=params(8),
        cost_estimate=cost(4 * size * len(rows) * depth * store_count, 2 * depth * store_count * 2),
    )(*[in_vmem(value) for value in inputs])


def gate_up_kernel(count, chunk, *refs):
    rows, factor, weights, inner, outs = refs[:count], refs[count], refs[count + 1 : count + 5], refs[count + 5], refs[count + 6 :]
    depth = factor.shape[1]
    pieces = [pl.ds(k * chunk, chunk) for k in range(depth // chunk)]
    for weight, out in zip(weights, outs):
        total = jnp.zeros(out.shape, F32)
        for part in pieces:
            block = jnp.concatenate([ref[:, part] for ref in rows], axis=0)
            total += jnp.dot(block, weight[part], preferred_element_type=F32)
        out[...] = total
    total = jnp.zeros(inner.shape, F32)
    for part in pieces:
        block = jnp.concatenate([ref[:, part] for ref in rows], axis=0)
        total += lax.dot_general(
            block, factor[:, part], (((1,), (1,)), ((), ())), preferred_element_type=F32
        )
    inner[...] = total.astype(BF16)


def gate_up(rows, factor, weights):
    depth, width = weights[0].shape
    total = rows[0].shape[0] * len(rows)
    inputs = [*rows, factor, *weights]
    out = jax.ShapeDtypeStruct((total, width), F32)
    return pl.pallas_call(
        functools.partial(gate_up_kernel, len(rows), 1024),
        in_specs=[VMEM_SPEC] * len(inputs),
        out_specs=[VMEM_SPEC] * (1 + len(weights)),
        out_shape=[jax.ShapeDtypeStruct((total, factor.shape[0]), BF16)] + [out] * len(weights),
        compiler_params=params(12),
        cost_estimate=cost(2 * len(weights) * total * depth * width, 2 * len(weights) * depth * width),
    )(*[in_vmem(x) for x in inputs])


def silu(value):
    return value / (1.0 + jnp.exp(-value))


def down_kernel(experts, chunks, order, *refs):
    count = len(order)
    half = count // 2
    inner_shared, gate, up, gate_shared, up_shared, columns, shared_b = refs[:7]
    messages = refs[7 : 7 + count]
    down, down_shared = refs[7 + count : 9 + count]
    outs = refs[9 + count :]
    total, width = gate.shape
    size = total // count
    shared_count = shared_b.shape[0]
    store_count = columns.shape[1] // count
    wide, per, _ = message_layout(count, store_count)
    own = columns[2:3, :1]

    meta = jnp.concatenate(
        [ref[store_count : store_count + size, wide - META :] for ref in messages], axis=0
    ).astype(F32)
    lane = lax.broadcasted_iota(jnp.int32, meta.shape, 1)
    mine = (lane < 3 * experts) & (lane % experts == own)
    share = jnp.sum(jnp.where(mine, meta, 0.0), axis=1, keepdims=True)
    row_tenant = jnp.sum(jnp.where(lane == 3 * experts, meta, 0.0), axis=1, keepdims=True)
    row_tenant = row_tenant.astype(jnp.int32)

    lifted = []
    for k in range(count):
        parts = []
        for h in range(0, count, 2):
            sender = h + k % 2
            n = (k ^ sender) // 2
            rows = slice(store_count + n // per * size, store_count + (n // per + 1) * size)
            lanes = slice(n % per * 2 * store_count, (n % per + 1) * 2 * store_count)
            block = messages[sender][rows, lanes]
            if k % 2:
                block = jnp.concatenate([block[:, store_count:], block[:, :store_count]], axis=1)
            parts.append(block)
        lifted.append(jnp.concatenate(parts, axis=1))
    lifted = jnp.concatenate(lifted, axis=0)
    zero = jnp.zeros((), BF16)
    lifted = jnp.where(row_tenant == columns[1:2], lifted, zero)
    shared_tenant = columns[0:1, :shared_count]
    lifted_shared = jnp.where(row_tenant == shared_tenant, inner_shared[...], zero)
    factor = jnp.concatenate([ref[:store_count, :width] for ref in messages], axis=0)
    upward = up[...] + jnp.dot(lifted, factor, preferred_element_type=F32)
    hidden = (silu(gate[...]) * upward).astype(BF16)
    upward = up_shared[...] + jnp.dot(lifted_shared, shared_b[...], preferred_element_type=F32)
    here = (row_tenant >= shared_tenant[:, :1]) & (row_tenant <= shared_tenant[:, shared_count - 1 :])
    hidden_shared = jnp.where(here, silu(gate_shared[...]) * upward, 0.0).astype(BF16)

    part = outs[0].shape[-1]
    tile = tile_of(part)
    for n, chunk in enumerate(chunks):
        keep, send = outs[2 * n : 2 * n + 2]
        for place, j in enumerate(chunk):
            for c in range(part // tile):
                cut = slice(j * part + c * tile, j * part + (c + 1) * tile)
                routed = jnp.dot(hidden, down[:, cut], preferred_element_type=F32) * share
                routed += jnp.dot(hidden_shared, down_shared[:, cut], preferred_element_type=F32)
                for at, r in enumerate(order):
                    block = routed[r * size : (r + 1) * size].astype(BF16)
                    target, row = (keep, at) if at < half else (send, at - half)
                    target[row, place, :, c * tile : (c + 1) * tile] = block


def down_products(gated, columns, shared_b, messages, down, down_shared, experts, chunks, order):
    count = len(messages)
    total, width = gated[1].shape
    size = total // count
    depth = down.shape[1]
    part = depth // lax.axis_size("tensor")
    whole = [*gated, columns, shared_b, *messages, down, down_shared]
    outs = []
    for chunk in chunks:
        outs += [jax.ShapeDtypeStruct((count // 2, len(chunk), size, part), BF16)] * 2
    return pl.pallas_call(
        functools.partial(down_kernel, experts, chunks, order),
        in_specs=[VMEM_SPEC] * len(whole),
        out_specs=[VMEM_SPEC] * len(outs),
        out_shape=outs,
        compiler_params=params(16),
        cost_estimate=cost(4 * total * depth * width, 4 * depth * width),
    )(*[in_vmem(x) for x in whole])


def local(
    tokens,
    expert_ids,
    gate_values,
    tenant_ids,
    w_gate,
    w_up,
    routed_down_weight,
    shared_gate,
    shared_up,
    shared_down,
    store_a,
    store_b,
    pair_slot,
    shared_a,
    shared_b,
):
    experts = pair_slot.shape[0]
    adapted, rank, model_width = store_a.shape
    hid = store_b.shape[2]
    steps, size, _ = expert_ids.shape
    count = lax.axis_size("expert")
    n_tensor = lax.axis_size("tensor")
    shared_count, store_count = shared_a.shape[0] * rank, adapted * rank

    rows_own = tokens.reshape(steps * size, model_width)
    arrived = swap(rows_own, count // 2)
    store_other = swap(store_a, 1).reshape(store_count, model_width)
    first = first_call(
        experts,
        jnp.swapaxes(expert_ids, 1, 2),
        jnp.swapaxes(gate_values, 1, 2),
        tenant_ids.reshape(1, size),
        pair_slot,
        [
            rows_own,
            store_b.reshape(store_count, hid),
            shared_b.reshape(shared_count, hid),
            store_a.reshape(store_count, model_width),
            shared_a.reshape(shared_count, model_width),
            w_gate[0],
            w_up[0],
            shared_gate,
            shared_up,
            routed_down_weight[0],
            shared_down,
        ],
    )
    arrived, first, store_other = lax.optimization_barrier((arrived, first, store_other))
    meta, columns, rows_held, store_b_held, shared_b_held, factor_store, factor_shared = first[:7]
    weights, down, down_own = first[7:11], first[11], first[12]
    rows = exchange_rest(rows_own, arrived)
    rows[0] = rows_held
    message = make_message(rows[::2], factor_store, store_other, store_b_held, meta)
    messages = [message] + [swap(message, r) for r in range(1, count)]
    rows[0], message = lax.optimization_barrier((rows[0], message))
    gated = gate_up(rows, factor_shared, weights)

    order = [0]
    bit = count // 2
    while bit >= 1:
        order = order + [r | bit for r in order]
        bit //= 2
    chunks = [[j] for j in range(n_tensor - 1, 1, -1)] + [[1, 0]]
    outs = down_products(
        gated, columns, shared_b_held, messages, down, down_own, experts, chunks, order
    )
    held, leaving = list(outs[0::2]), list(outs[1::2])
    bit = 1
    while bit < count:
        half = count // (2 * bit) // 2
        if bit > 1:
            leaving[1], *_ = lax.optimization_barrier((leaving[1], leaving[0]))
        arrived = [swap(value, bit) for value in leaving]
        if bit > 1:
            arrived[0], *_ = lax.optimization_barrier((arrived[0], *leaving))
        if 2 * bit < count:
            leaving = [add(h[half:], a[half:]) for h, a in zip(held, arrived)]
            held = [add(h[:half], a[:half]) for h, a in zip(held, arrived)]
        bit *= 2
    parts = {}
    for n, chunk in enumerate(chunks):
        for place, j in enumerate(chunk):
            parts[j] = [held[n][0, place], arrived[n][0, place]]
    bit = 1
    while bit < n_tensor:
        for j in sorted([j for j in parts if j & bit], reverse=True):
            parts[j ^ bit].append(swap(total_of(parts.pop(j)), bit, "tensor"))
        bit *= 2
    return total_of(parts[0]).reshape(steps, size, model_width // n_tensor)


def solution(mesh):
    return jax.shard_map(
        local,
        mesh=mesh,
        in_specs=(
            P(None, ("groups", "expert"), None),
            P(None, ("groups", "expert"), None),
            P(None, ("groups", "expert"), None),
            P(("groups", "expert")),
            P("expert", None, "tensor"),
            P("expert", None, "tensor"),
            P("expert", "tensor", None),
            P(None, "tensor"),
            P(None, "tensor"),
            P("tensor", None),
            P("expert", None, None),
            P("expert", None, "tensor"),
            P(),
            P("expert", None, None),
            P("expert", None, "tensor"),
        ),
        out_specs=P(None, ("groups", "expert"), "tensor"),
        check_vma=False,
    )
```

time: 44.8 us -> 42.6 us (0.951)
  starting transfers between devices: 18.4 us -> 14.9 us
  waiting for transfers between devices: 11.8 us -> 13.9 us
  Pallas kernels: 13.2 us -> 12.6 us
    ppermute x18 -> x16, starting transfers between devices: 18.4 us -> 14.9 us  [swap(): return lax.ppermute(value, axis, [(i, i ^ bits) for i in range(count)])]
    ppermute x18 -> x16, waiting for transfers between devices: 11.8 us -> 13.9 us  [swap(): return lax.ppermute(value, axis, [(i, i ^ bits) for i in range(count)])]
    pallas_call x3, Pallas kernels: 12.1 us -> 10 us  [the longest x1 8.15 us: first_call(): pl.pallas_call(functools.partial(first_kernel, experts), in_specs=[HBM_SP...]
    pallas_call x1, Pallas kernels: 1.19 us -> 2.53 us  [gate_up(): pl.pallas_call(functools.partial(gate_up_kernel, len(rows), 1024), in_spe...]
  transfers between devices with their start and end apart: 18 -> 16, of which waited for: 9 -> 9; matrix products, arithmetic and copies ran while one was open for 1% -> 1% of each run, Pallas kernels for 27% -> 26%
where the time goes in v8:
time: 42.6 us; the launch traced here: 42.5 us
  starting transfers between devices  14.9 us (35%)
  waiting for transfers between devices  13.9 us (33%)
  Pallas kernels  12.6 us (30%)
  other arithmetic  1.04 us (2%)
    ppermute x16, starting transfers between devices, swap(): return lax.ppermute(value, axis, [(i, i ^ bits) for i in range(count)])  14.9 us
    ppermute x16, waiting for transfers between devices, swap(): return lax.ppermute(value, axis, [(i, i ^ bits) for i in range(count)])  13.9 us
    pallas_call x1, Pallas kernels, first_call(): pl.pallas_call(functools.partial(first_kernel, experts), in_specs=[HBM_SP...  8.15 us
    pallas_call x1, Pallas kernels, gate_up(): pl.pallas_call(functools.partial(gate_up_kernel, len(rows), 1024), in_spe...  2.53 us
    pallas_call x1, Pallas kernels, down_products(): pl.pallas_call(functools.partial(down_kernel, experts, chunks, order), in...  1.43 us
    convert_element_type x4, other arithmetic, total_of(): return sum((value.astype(F32) for value in values)).astype(BF16)  0.85 us
  transfers between devices with their start and end apart: 16, of which 9 were waited for; matrix products, arithmetic and copies ran while one was open for 1% of the time, Pallas kernels for 26%

profile of v8, /device:TPU:0, one launch (start us, length us, event | category | flops | bytes accessed | tf_op | source)
XLA Modules:
  0.0 42.5 jit_solution(6898285300523555083)
XLA Ops:
  0.0 3.0 %collective-permute-start = (bf16[32,7168]{1,0:T(8,128)(2,1)}, bf16[32,7168]{1,0:T(8,128)(2,1)S(1)}, u32[]{:S(2)}, u32[]{:S(2)}) collective-permute-start(bf16[32,7168]{1,0:T(8,128)(2,1)} %bitcast.33), channel_id=1, source_target_pairs={{0,8},{4,12},{8,0},{12,4},{1,9},{5,13},{9,1},{13,5},{2,10},{6,14},... | collective-permute-start | bytes 1376264 | tf_op jit(solution)/shard_map/ppermute | solution.py:41
  3.0 0.0 collective-permute-start.1
  3.0 0.5 %collective-permute-start.2 = (bf16[32,7168]{1,0:T(8,128)(2,1)}, bf16[32,7168]{1,0:T(8,128)(2,1)S(1)}, u32[]{:S(2)}, u32[]{:S(2)}) collective-permute-start(bf16[32,7168]{1,0:T(8,128)(2,1)} %bitcast.34), channel_id=1, source_target_pairs={{0,4},{4,0},{8,12},{12,8},{1,5},{5,1},{9,13},{13,9},{2,6},{6,2},{1... | collective-permute-start | bytes 1376264 | tf_op jit(solution)/shard_map/ppermute | solution.py:41
  3.5 8.2 %shard_map.145 = (bf16[32,128]{1,0:T(8,128)(2,1)S(1)}, s32[8,128]{1,0:T(8,128)S(1)}, bf16[32,7168]{1,0:T(8,128)(2,1)S(1)}, bf16[32,256]{1,0:T(8,128)(2,1)S(1)}, ...) custom-call(s32[2,2,16]{2,1,0:T(2,128)} %bitcast.38, ...), custom_call_target="tpu_custom_call" | custom-call | bytes 23904256 | tf_op jit(solution)/shard_map/pallas_call | solution.py:159
  11.6 2.1 %collective-permute-done.refs_1_.refs_2_ = bf16[32,7168]{1,0:T(8,128)(2,1)S(1)} collective-permute-done((bf16[32,7168]{1,0:T(8,128)(2,1)}, bf16[32,7168]{1,0:T(8,128)(2,1)S(1)}, u32[]{:S(2)}, u32[]{:S(2)}) %collective-permute-start) | collective-permute-done | bytes 458784 | tf_op jit(solution)/shard_map/ppermute | solution.py:41
  13.7 0.0 collective-permute-done.1
  13.7 0.5 %shard_map.146.refs_7_ = bf16[64,256]{1,0:T(8,128)(2,1)S(1)} custom-call(bf16[32,7168]{1,0:T(8,128)(2,1)S(1)} %get-tuple-element.66.refs_0_, bf16[32,7168]{1,0:T(8,128)(2,1)S(1)} %collective-permute-done.refs_1_.refs_2_, bf16[32,7168]{1,0:T(8,128)(2,1)S(1)} %get-tuple-element.62.refs_2_, bf16[32,7168]{1,0:T(8,128)(2,1)S(1)} %bitcast.27, ...), custom_call_target="tpu_custom_call" | custom-call | flops 58720256 | bytes 917504 | tf_op jit(solution)/shard_map/pallas_call | solution.py:220
  14.2 0.5 %collective-permute-start.4 = (bf16[64,256]{1,0:T(8,128)(2,1)S(1)}, bf16[64,256]{1,0:T(8,128)(2,1)S(1)}, u32[]{:S(2)}, u32[]{:S(2)}) collective-permute-start(bf16[64,256]{1,0:T(8,128)(2,1)S(1)} %shard_map.146.refs_7_), channel_id=1, source_target_pairs={{0,4},{4,0},{8,12},{12,8},{1,5},{5,1},{9,13},{13,9},{2,6},{6,2},{1... | collective-permute-start | bytes 98312 | tf_op jit(solution)/shard_map/ppermute | solution.py:41
  14.7 1.7 %collective-permute-start.5 = (bf16[64,256]{1,0:T(8,128)(2,1)S(1)}, bf16[64,256]{1,0:T(8,128)(2,1)S(1)}, u32[]{:S(2)}, u32[]{:S(2)}) collective-permute-start(bf16[64,256]{1,0:T(8,128)(2,1)S(1)} %shard_map.146.refs_7_), channel_id=1, source_target_pairs={{0,8},{4,12},{8,0},{12,4},{1,9},{5,13},{9,1},{13,5},{2,10},{6,14},... | collective-permute-start | bytes 98312 | tf_op jit(solution)/shard_map/ppermute | solution.py:41
  16.4 2.5 %shard_map.147 = (bf16[128,64]{1,0:T(8,128)(2,1)S(1)}, f32[128,256]{1,0:T(8,128)S(1)}, f32[128,256]{1,0:T(8,128)S(1)}, f32[128,256]{1,0:T(8,128)S(1)}, f32[128,256]{1,0:T(8,128)S(1)}) custom-call(bf16[32,7168]{1,0:T(8,128)(2,1)S(1)} %get-tuple-element.66.refs_0_, bf16[32,7168]{1,0:T(8,128)(2,1)S(1)} %collective-permute-done.2.refs_1_, ...), custom_call_target="tpu_custom_call" | custom-call | flops 1879048192 | bytes 14680064 | tf_op jit(solution)/shard_map/pallas_call | solution.py:254
  19.0 1.1 %collective-permute-done.6.refs_10_ = bf16[64,256]{1,0:T(8,128)(2,1)S(1)} collective-permute-done((bf16[64,256]{1,0:T(8,128)(2,1)S(1)}, bf16[64,256]{1,0:T(8,128)(2,1)S(1)}, u32[]{:S(2)}, u32[]{:S(2)}) %collective-permute-start.6) | collective-permute-done | bytes 32800 | tf_op jit(solution)/shard_map/ppermute | solution.py:41
  20.1 1.4 %shard_map.148 = (bf16[2,1,32,1792]{3,2,1,0:T(8,128)(2,1)S(1)}, bf16[2,1,32,1792]{3,2,1,0:T(8,128)(2,1)S(1)}, bf16[2,1,32,1792]{3,2,1,0:T(8,128)(2,1)S(1)}, bf16...) custom-call(bf16[128,64]{1,0:T(8,128)(2,1)S(1)} %get-tuple-element.72.re, ...), custom_call_target="tpu_custom_call" | custom-call | flops 939524096 | bytes 7340032 | tf_op jit(solution)/shard_map/pallas_call | solution.py:341
  21.5 0.2 collective-permute-start.11
  21.7 0.4 collective-permute-start.7
  22.1 0.1 collective-permute-start.10
  22.2 0.9 %collective-permute-done.11 = bf16[2,1,32,1792]{3,2,1,0:T(8,128)(2,1)S(1)} collective-permute-done((bf16[2,1,32,1792]{3,2,1,0:T(8,128)(2,1)S(1)}, bf16[2,1,32,1792]{3,2,1,0:T(8,128)(2,1)S(1)}, u32[]{:S(2)}, u32[]{:S(2)}) %collective-permute-start.11) | collective-permute-done | bytes 229408 | tf_op jit(solution)/shard_map/ppermute | solution.py:41
  23.1 0.8 %collective-permute-start.13 = (bf16[1,1,32,1792]{3,2,1,0:T(8,128)(2,1)S(1)}, bf16[1,1,32,1792]{3,2,1,0:T(8,128)(2,1)S(1)}, u32[]{:S(2)}, u32[]{:S(2)}) collective-permute-start(bf16[1,1,32,1792]{3,2,1,0:T(8,128)(2,1)S(1)} %add_convert_fusion.4), channel_id=1, source_target_pairs={{0,8},{4,12},{8,0},{12,4},{1,9},{5,13},{9,1},{13,5},{2,10},{6,14},... | collective-permute-start | bytes 344072 | tf_op jit(solution)/shard_map/ppermute | solution.py:41
  23.9 0.2 collective-permute-done.10
  24.1 1.2 %collective-permute-start.12 = (bf16[1,1,32,1792]{3,2,1,0:T(8,128)(2,1)S(1)}, bf16[1,1,32,1792]{3,2,1,0:T(8,128)(2,1)S(1)}, u32[]{:S(2)}, u32[]{:S(2)}) collective-permute-start(bf16[1,1,32,1792]{3,2,1,0:T(8,128)(2,1)S(1)} %add_convert_fusion.5), channel_id=1, source_target_pairs={{0,8},{4,12},{8,0},{12,4},{1,9},{5,13},{9,1},{13,5},{2,10},{6,14},... | collective-permute-start | bytes 344072 | tf_op jit(solution)/shard_map/ppermute | solution.py:41
  25.3 0.1 add_convert_fusion.1
  25.4 3.7 %collective-permute-done.13 = bf16[1,1,32,1792]{3,2,1,0:T(8,128)(2,1)S(1)} collective-permute-done((bf16[1,1,32,1792]{3,2,1,0:T(8,128)(2,1)S(1)}, bf16[1,1,32,1792]{3,2,1,0:T(8,128)(2,1)S(1)}, u32[]{:S(2)}, u32[]{:S(2)}) %collective-permute-start.13) | collective-permute-done | bytes 114720 | tf_op jit(solution)/shard_map/ppermute | solution.py:41
  29.2 0.1 fusion.4
  29.2 1.6 %collective-permute-start.14 = (bf16[32,1792]{1,0:T(8,128)(2,1)S(1)}, bf16[32,1792]{1,0:T(8,128)(2,1)S(1)}, u32[]{:S(2)}, u32[]{:S(2)}) collective-permute-start(bf16[32,1792]{1,0:T(8,128)(2,1)S(1)} %fusion.4), channel_id=1, source_target_pairs={{0,1},{1,0},{2,3},{3,2},{4,5},{5,4},{6,7},{7,6},{8,9},{9,8},{10,11... | collective-permute-start | bytes 344072 | tf_op jit(solution)/shard_map/ppermute | solution.py:41
  30.9 0.7 %collective-permute-start.8 = (bf16[1,2,32,1792]{3,2,1,0:T(8,128)(2,1)S(1)}, bf16[1,2,32,1792]{3,2,1,0:T(8,128)(2,1)S(1)}, u32[]{:S(2)}, u32[]{:S(2)}) collective-permute-start(bf16[1,2,32,1792]{3,2,1,0:T(8,128)(2,1)S(1)} %get-tuple-element.90), channel_id=1, source_target_pairs={{0,8},{4,12},{8,0},{12,4},{1,9},{5,13},{9,1},{13,5},{2,10},{6,14},... | collective-permute-start | bytes 688136 | tf_op jit(solution)/shard_map/ppermute | solution.py:41
  31.5 2.5 %collective-permute-done.14 = bf16[32,1792]{1,0:T(8,128)(2,1)S(1)} collective-permute-done((bf16[32,1792]{1,0:T(8,128)(2,1)S(1)}, bf16[32,1792]{1,0:T(8,128)(2,1)S(1)}, u32[]{:S(2)}, u32[]{:S(2)}) %collective-permute-start.14) | collective-permute-done | bytes 114720 | tf_op jit(solution)/shard_map/ppermute | solution.py:41
  34.1 0.1 fusion
  34.1 2.7 %collective-permute-start.15 = (bf16[32,1792]{1,0:T(8,128)(2,1)S(1)}, bf16[32,1792]{1,0:T(8,128)(2,1)S(1)}, u32[]{:S(2)}, u32[]{:S(2)}) collective-permute-start(bf16[32,1792]{1,0:T(8,128)(2,1)S(1)} %fusion), channel_id=1, source_target_pairs={{0,2},{1,3},{2,0},{3,1},{4,6},{5,7},{6,4},{7,5},{8,10},{9,11},{10,... | collective-permute-start | bytes 344072 | tf_op jit(solution)/shard_map/ppermute | solution.py:41
  36.8 0.1 collective-permute-done.8
  36.9 1.6 %collective-permute-start.9 = (bf16[32,1792]{1,0:T(8,128)(2,1)S(1)}, bf16[32,1792]{1,0:T(8,128)(2,1)S(1)}, u32[]{:S(2)}, u32[]{:S(2)}) collective-permute-start(bf16[32,1792]{1,0:T(8,128)(2,1)S(1)} %fusion.3), channel_id=1, source_target_pairs={{0,1},{1,0},{2,3},{3,2},{4,5},{5,4},{6,7},{7,6},{8,9},{9,8},{10,11... | collective-permute-start | bytes 344072 | tf_op jit(solution)/shard_map/ppermute | solution.py:41
  38.5 1.7 %collective-permute-done.15 = bf16[32,1792]{1,0:T(8,128)(2,1)S(1)} collective-permute-done((bf16[32,1792]{1,0:T(8,128)(2,1)S(1)}, bf16[32,1792]{1,0:T(8,128)(2,1)S(1)}, u32[]{:S(2)}, u32[]{:S(2)}) %collective-permute-start.15) | collective-permute-done | bytes 114720 | tf_op jit(solution)/shard_map/ppermute | solution.py:41
  40.1 1.6 %collective-permute-done.9 = bf16[32,1792]{1,0:T(8,128)(2,1)S(1)} collective-permute-done((bf16[32,1792]{1,0:T(8,128)(2,1)S(1)}, bf16[32,1792]{1,0:T(8,128)(2,1)S(1)}, u32[]{:S(2)}, u32[]{:S(2)}) %collective-permute-start.9) | collective-permute-done | bytes 114720 | tf_op jit(solution)/shard_map/ppermute | solution.py:41
  41.8 0.7 %fusion.2 = bf16[32,1792]{1,0:T(8,128)(2,1)} fusion(bf16[32,1792]{1,0:T(8,128)(2,1)S(1)} %collective-permute-done.15, bf16[32,1792]{1,0:T(8,128)(2,1)S(1)} %collective-permute-done.9, bf16[1,2,32,1792]{3,2,1,0:T(8,128)(2,1)S(1)} %collective-permute-done.8, bf16[1,2,32,1792]{3,2,1,0:T(8,128)(2,1)S(1)} %get-tuple-element.89), kind=kLoop, calls=%fused_computation.6 | loop fusion | flops 458752 | bytes 573440 | tf_op jit(solution)/shard_map/convert_element_type | solution.py:49
  (11 shorter events, 0.1 us)
Async XLA Ops:
  0.0 13.7 %collective-permute-start = (bf16[32,7168]{1,0:T(8,128)(2,1)}, bf16[32,7168]{1,0:T(8,128)(2,1)S(1)}, u32[]{:S(2)}, u32[]{:S(2)}) collective-permute-start(bf16[32,7168]{1,0:T(8,128)(2,1)} %bitcast.33), channel_id=1, source_target_pairs={{0,8},{4,12},{8,0},{12,4},{1,9},{5,13},{9,1},{13,5},{2,10},{6,14},... | collective-permute-start | bytes 1376264 | tf_op jit(solution)/shard_map/ppermute | solution.py:41
  3.0 10.7 %collective-permute-start.1 = (bf16[2,16,7168]{2,1,0:T(8,128)(2,1)}, bf16[2,16,7168]{2,1,0:T(8,128)(2,1)S(1)}, u32[]{:S(2)}, u32[]{:S(2)}) collective-permute-start(bf16[2,16,7168]{2,1,0:T(8,128)(2,1)} %param.25), channel_id=1, source_target_pairs={{0,4},{4,0},{8,12},{12,8},{1,5},{5,1},{9,13},{13,9},{2,6},{6,2},{1... | collective-permute-start | bytes 1376264 | tf_op jit(solution)/shard_map/ppermute | solution.py:41
  3.0 13.4 %collective-permute-start.2 = (bf16[32,7168]{1,0:T(8,128)(2,1)}, bf16[32,7168]{1,0:T(8,128)(2,1)S(1)}, u32[]{:S(2)}, u32[]{:S(2)}) collective-permute-start(bf16[32,7168]{1,0:T(8,128)(2,1)} %bitcast.34), channel_id=1, source_target_pairs={{0,4},{4,0},{8,12},{12,8},{1,5},{5,1},{9,13},{13,9},{2,6},{6,2},{1... | collective-permute-start | bytes 1376264 | tf_op jit(solution)/shard_map/ppermute | solution.py:41
  13.7 2.7 %collective-permute-start.3 = (bf16[32,7168]{1,0:T(8,128)(2,1)S(1)}, bf16[32,7168]{1,0:T(8,128)(2,1)S(1)}, u32[]{:S(2)}, u32[]{:S(2)}) collective-permute-start(bf16[32,7168]{1,0:T(8,128)(2,1)S(1)} %collective-permute-done.refs_1_.refs_2_), channel_id=1, source_target_pairs={{0,4},{4,0},{8,12},{12,8},{1,5},{5,1},{9,13},{13,9},{2,6},{6,2},{1... | collective-permute-start | bytes 1376264 | tf_op jit(solution)/shard_map/ppermute | solution.py:41
  14.2 4.8 %collective-permute-start.4 = (bf16[64,256]{1,0:T(8,128)(2,1)S(1)}, bf16[64,256]{1,0:T(8,128)(2,1)S(1)}, u32[]{:S(2)}, u32[]{:S(2)}) collective-permute-start(bf16[64,256]{1,0:T(8,128)(2,1)S(1)} %shard_map.146.refs_7_), channel_id=1, source_target_pairs={{0,4},{4,0},{8,12},{12,8},{1,5},{5,1},{9,13},{13,9},{2,6},{6,2},{1... | collective-permute-start | bytes 98312 | tf_op jit(solution)/shard_map/ppermute | solution.py:41
  14.7 4.3 %collective-permute-start.5 = (bf16[64,256]{1,0:T(8,128)(2,1)S(1)}, bf16[64,256]{1,0:T(8,128)(2,1)S(1)}, u32[]{:S(2)}, u32[]{:S(2)}) collective-permute-start(bf16[64,256]{1,0:T(8,128)(2,1)S(1)} %shard_map.146.refs_7_), channel_id=1, source_target_pairs={{0,8},{4,12},{8,0},{12,4},{1,9},{5,13},{9,1},{13,5},{2,10},{6,14},... | collective-permute-start | bytes 98312 | tf_op jit(solution)/shard_map/ppermute | solution.py:41
  16.4 3.7 %collective-permute-start.6 = (bf16[64,256]{1,0:T(8,128)(2,1)S(1)}, bf16[64,256]{1,0:T(8,128)(2,1)S(1)}, u32[]{:S(2)}, u32[]{:S(2)}) collective-permute-start(bf16[64,256]{1,0:T(8,128)(2,1)S(1)} %shard_map.146.refs_7_), channel_id=1, source_target_pairs={{0,12},{4,8},{8,4},{12,0},{1,13},{5,9},{9,5},{13,1},{2,14},{6,10},... | collective-permute-start | bytes 98312 | tf_op jit(solution)/shard_map/ppermute | solution.py:41
  21.5 1.6 %collective-permute-start.11 = (bf16[2,1,32,1792]{3,2,1,0:T(8,128)(2,1)S(1)}, bf16[2,1,32,1792]{3,2,1,0:T(8,128)(2,1)S(1)}, u32[]{:S(2)}, u32[]{:S(2)}) collective-permute-start(bf16[2,1,32,1792]{3,2,1,0:T(8,128)(2,1)S(1)} %get-tuple-element.86), channel_id=1, source_target_pairs={{0,4},{4,0},{8,12},{12,8},{1,5},{5,1},{9,13},{13,9},{2,6},{6,2},{1... | collective-permute-start | bytes 688136 | tf_op jit(solution)/shard_map/ppermute | solution.py:41
  21.7 3.6 %collective-permute-start.7 = (bf16[2,2,32,1792]{3,2,1,0:T(8,128)(2,1)S(1)}, bf16[2,2,32,1792]{3,2,1,0:T(8,128)(2,1)S(1)}, u32[]{:S(2)}, u32[]{:S(2)}) collective-permute-start(bf16[2,2,32,1792]{3,2,1,0:T(8,128)(2,1)S(1)} %get-tuple-element.82), channel_id=1, source_target_pairs={{0,4},{4,0},{8,12},{12,8},{1,5},{5,1},{9,13},{13,9},{2,6},{6,2},{1... | collective-permute-start | bytes 1376264 | tf_op jit(solution)/shard_map/ppermute | solution.py:41
  22.1 2.0 %collective-permute-start.10 = (bf16[2,1,32,1792]{3,2,1,0:T(8,128)(2,1)S(1)}, bf16[2,1,32,1792]{3,2,1,0:T(8,128)(2,1)S(1)}, u32[]{:S(2)}, u32[]{:S(2)}) collective-permute-start(bf16[2,1,32,1792]{3,2,1,0:T(8,128)(2,1)S(1)} %get-tuple-element.84), channel_id=1, source_target_pairs={{0,4},{4,0},{8,12},{12,8},{1,5},{5,1},{9,13},{13,9},{2,6},{6,2},{1... | collective-permute-start | bytes 688136 | tf_op jit(solution)/shard_map/ppermute | solution.py:41
  23.1 6.1 %collective-permute-start.13 = (bf16[1,1,32,1792]{3,2,1,0:T(8,128)(2,1)S(1)}, bf16[1,1,32,1792]{3,2,1,0:T(8,128)(2,1)S(1)}, u32[]{:S(2)}, u32[]{:S(2)}) collective-permute-start(bf16[1,1,32,1792]{3,2,1,0:T(8,128)(2,1)S(1)} %add_convert_fusion.4), channel_id=1, source_target_pairs={{0,8},{4,12},{8,0},{12,4},{1,9},{5,13},{9,1},{13,5},{2,10},{6,14},... | collective-permute-start | bytes 344072 | tf_op jit(solution)/shard_map/ppermute | solution.py:41
  24.1 7.4 %collective-permute-start.12 = (bf16[1,1,32,1792]{3,2,1,0:T(8,128)(2,1)S(1)}, bf16[1,1,32,1792]{3,2,1,0:T(8,128)(2,1)S(1)}, u32[]{:S(2)}, u32[]{:S(2)}) collective-permute-start(bf16[1,1,32,1792]{3,2,1,0:T(8,128)(2,1)S(1)} %add_convert_fusion.5), channel_id=1, source_target_pairs={{0,8},{4,12},{8,0},{12,4},{1,9},{5,13},{9,1},{13,5},{2,10},{6,14},... | collective-permute-start | bytes 344072 | tf_op jit(solution)/shard_map/ppermute | solution.py:41
  29.2 4.9 %collective-permute-start.14 = (bf16[32,1792]{1,0:T(8,128)(2,1)S(1)}, bf16[32,1792]{1,0:T(8,128)(2,1)S(1)}, u32[]{:S(2)}, u32[]{:S(2)}) collective-permute-start(bf16[32,1792]{1,0:T(8,128)(2,1)S(1)} %fusion.4), channel_id=1, source_target_pairs={{0,1},{1,0},{2,3},{3,2},{4,5},{5,4},{6,7},{7,6},{8,9},{9,8},{10,11... | collective-permute-start | bytes 344072 | tf_op jit(solution)/shard_map/ppermute | solution.py:41
  30.9 6.0 %collective-permute-start.8 = (bf16[1,2,32,1792]{3,2,1,0:T(8,128)(2,1)S(1)}, bf16[1,2,32,1792]{3,2,1,0:T(8,128)(2,1)S(1)}, u32[]{:S(2)}, u32[]{:S(2)}) collective-permute-start(bf16[1,2,32,1792]{3,2,1,0:T(8,128)(2,1)S(1)} %get-tuple-element.90), channel_id=1, source_target_pairs={{0,8},{4,12},{8,0},{12,4},{1,9},{5,13},{9,1},{13,5},{2,10},{6,14},... | collective-permute-start | bytes 688136 | tf_op jit(solution)/shard_map/ppermute | solution.py:41
  34.1 6.0 %collective-permute-start.15 = (bf16[32,1792]{1,0:T(8,128)(2,1)S(1)}, bf16[32,1792]{1,0:T(8,128)(2,1)S(1)}, u32[]{:S(2)}, u32[]{:S(2)}) collective-permute-start(bf16[32,1792]{1,0:T(8,128)(2,1)S(1)} %fusion), channel_id=1, source_target_pairs={{0,2},{1,3},{2,0},{3,1},{4,6},{5,7},{6,4},{7,5},{8,10},{9,11},{10,... | collective-permute-start | bytes 344072 | tf_op jit(solution)/shard_map/ppermute | solution.py:41
  36.9 4.9 %collective-permute-start.9 = (bf16[32,1792]{1,0:T(8,128)(2,1)S(1)}, bf16[32,1792]{1,0:T(8,128)(2,1)S(1)}, u32[]{:S(2)}, u32[]{:S(2)}) collective-permute-start(bf16[32,1792]{1,0:T(8,128)(2,1)S(1)} %fusion.3), channel_id=1, source_target_pairs={{0,1},{1,0},{2,3},{3,2},{4,5},{5,4},{6,7},{7,6},{8,9},{9,8},{10,11... | collective-permute-start | bytes 344072 | tf_op jit(solution)/shard_map/ppermute | solution.py:41

commit v9 on v8

--- a/solution.py
+++ b/solution.py
@@ -49,15 +49,15 @@
     return sum(value.astype(F32) for value in values).astype(BF16)
 
 
-def exchange_rest(value, arrived):
+def far_rows(arrived, rows_own):
     count = lax.axis_size("expert")
     bit = count // 2
-    pieces = {0: value, bit: arrived}
+    pieces = {0: rows_own, bit: arrived}
     bit //= 2
-    while bit >= 1:
+    while bit > 1:
         pieces.update({r ^ bit: swap(piece, bit) for r, piece in list(pieces.items())})
         bit //= 2
-    return [pieces[r] for r in range(count)]
+    return [pieces[r] for r in range(2, count, 2)]
 
 
 def tile_of(width):
@@ -265,13 +265,42 @@
     return value / (1.0 + jnp.exp(-value))
 
 
+def down_blocks(hidden, hidden_shared, share, down, down_shared, outs, chunks, order):
+    size = hidden.shape[0] // len(order)
+    half = len(order) // 2
+    part = outs[0].shape[-1]
+    tile = tile_of(part)
+    for n, chunk in enumerate(chunks):
+        keep, send = outs[2 * n : 2 * n + 2]
+        for place, j in enumerate(chunk):
+            for c in range(part // tile):
+                cut = slice(j * part + c * tile, j * part + (c + 1) * tile)
+                routed = jnp.dot(hidden, down[:, cut], preferred_element_type=F32) * share
+                routed += jnp.dot(hidden_shared, down_shared[:, cut], preferred_element_type=F32)
+                for at, r in enumerate(order):
+                    block = routed[r * size : (r + 1) * size].astype(BF16)
+                    target, row = (keep, at) if at < half else (send, at - half)
+                    target[row, place, :, c * tile : (c + 1) * tile] = block
+
+
+def down_next_kernel(chunks, order, hidden, hidden_shared, share, down, down_shared, *outs):
+    down_blocks(
+        hidden[...], hidden_shared[...], share[:, :1], down, down_shared, outs, chunks, order
+    )
+
+
 def down_kernel(experts, chunks, order, *refs):
     count = len(order)
     half = count // 2
-    inner_shared, gate, up, gate_shared, up_shared, columns, shared_b = refs[:7]
-    messages = refs[7 : 7 + count]
-    down, down_shared = refs[7 + count : 9 + count]
-    outs = refs[9 + count :]
+    near, far, refs = refs[:5], refs[5:10], refs[10:]
+    columns, shared_b = refs[:2]
+    messages = refs[2 : 2 + count]
+    down, down_shared = refs[2 + count : 4 + count]
+    hidden_out, hidden_shared_out, share_out = refs[4 + count : 7 + count]
+    outs = refs[7 + count :]
+    inner_shared, gate, up, gate_shared, up_shared = [
+        jnp.concatenate([one[...], other[...]], axis=0) for one, other in zip(near, far)
+    ]
     total, width = gate.shape
     size = total // count
     shared_count = shared_b.shape[0]
@@ -305,46 +334,61 @@
     zero = jnp.zeros((), BF16)
     lifted = jnp.where(row_tenant == columns[1:2], lifted, zero)
     shared_tenant = columns[0:1, :shared_count]
-    lifted_shared = jnp.where(row_tenant == shared_tenant, inner_shared[...], zero)
+    lifted_shared = jnp.where(row_tenant == shared_tenant, inner_shared, zero)
     factor = jnp.concatenate([ref[:store_count, :width] for ref in messages], axis=0)
-    upward = up[...] + jnp.dot(lifted, factor, preferred_element_type=F32)
-    hidden = (silu(gate[...]) * upward).astype(BF16)
-    upward = up_shared[...] + jnp.dot(lifted_shared, shared_b[...], preferred_element_type=F32)
+    upward = up + jnp.dot(lifted, factor, preferred_element_type=F32)
+    hidden = (silu(gate) * upward).astype(BF16)
+    upward = up_shared + jnp.dot(lifted_shared, shared_b[...], preferred_element_type=F32)
     here = (row_tenant >= shared_tenant[:, :1]) & (row_tenant <= shared_tenant[:, shared_count - 1 :])
-    hidden_shared = jnp.where(here, silu(gate_shared[...]) * upward, 0.0).astype(BF16)
-
-    part = outs[0].shape[-1]
-    tile = tile_of(part)
-    for n, chunk in enumerate(chunks):
-        keep, send = outs[2 * n : 2 * n + 2]
-        for place, j in enumerate(chunk):
-            for c in range(part // tile):
-                cut = slice(j * part + c * tile, j * part + (c + 1) * tile)
-                routed = jnp.dot(hidden, down[:, cut], preferred_element_type=F32) * share
-                routed += jnp.dot(hidden_shared, down_shared[:, cut], preferred_element_type=F32)
-                for at, r in enumerate(order):
-                    block = routed[r * size : (r + 1) * size].astype(BF16)
-                    target, row = (keep, at) if at < half else (send, at - half)
-                    target[row, place, :, c * tile : (c + 1) * tile] = block
-
-
-def down_products(gated, columns, shared_b, messages, down, down_shared, experts, chunks, order):
-    count = len(messages)
-    total, width = gated[1].shape
-    size = total // count
-    depth = down.shape[1]
+    hidden_shared = jnp.where(here, silu(gate_shared) * upward, 0.0).astype(BF16)
+
+    hidden_out[...] = hidden
+    hidden_shared_out[...] = hidden_shared
+    share_out[...] = jnp.broadcast_to(share, share_out.shape)
+    down_blocks(hidden, hidden_shared, share, down, down_shared, outs, chunks, order)
+
+
+def down_outs(rows, depth, chunks, order):
+    size = rows // len(order)
     part = depth // lax.axis_size("tensor")
-    whole = [*gated, columns, shared_b, *messages, down, down_shared]
     outs = []
     for chunk in chunks:
-        outs += [jax.ShapeDtypeStruct((count // 2, len(chunk), size, part), BF16)] * 2
+        outs += [jax.ShapeDtypeStruct((len(order) // 2, len(chunk), size, part), BF16)] * 2
+    return outs
+
+
+def down_cost(rows, down, chunks):
+    part = sum(len(chunk) for chunk in chunks) * down.size // lax.axis_size("tensor")
+    return cost(4 * rows * part, 4 * part)
+
+
+def down_products(near, far, columns, shared_b, messages, down, down_shared, experts, chunks, order):
+    rows, width = near[1].shape[0] + far[1].shape[0], near[1].shape[1]
+    whole = [*near, *far, columns, shared_b, *messages, down, down_shared]
+    outs = [jax.ShapeDtypeStruct((rows, width), BF16)] * 2
+    outs += [jax.ShapeDtypeStruct((rows, 128), F32)]
+    outs += down_outs(rows, down.shape[1], chunks, order)
     return pl.pallas_call(
         functools.partial(down_kernel, experts, chunks, order),
         in_specs=[VMEM_SPEC] * len(whole),
         out_specs=[VMEM_SPEC] * len(outs),
         out_shape=outs,
         compiler_params=params(16),
-        cost_estimate=cost(4 * total * depth * width, 4 * depth * width),
+        cost_estimate=down_cost(rows, down, chunks),
+    )(*[in_vmem(x) for x in whole])
+
+
+def down_next(hidden, down, down_shared, chunks, order):
+    rows = hidden[0].shape[0]
+    whole = [*hidden, down, down_shared]
+    outs = down_outs(rows, down.shape[1], chunks, order)
+    return pl.pallas_call(
+        functools.partial(down_next_kernel, chunks, order),
+        in_specs=[VMEM_SPEC] * len(whole),
+        out_specs=[VMEM_SPEC] * len(outs),
+        out_shape=outs,
+        compiler_params=params(16),
+        cost_estimate=down_cost(rows, down, chunks),
     )(*[in_vmem(x) for x in whole])
 
 
@@ -396,15 +440,20 @@
             shared_down,
         ],
     )
-    arrived, first, store_other = lax.optimization_barrier((arrived, first, store_other))
     meta, columns, rows_held, store_b_held, shared_b_held, factor_store, factor_shared = first[:7]
     weights, down, down_own = first[7:11], first[11], first[12]
-    rows = exchange_rest(rows_own, arrived)
-    rows[0] = rows_held
-    message = make_message(rows[::2], factor_store, store_other, store_b_held, meta)
+    near = gate_up([rows_held, swap(rows_own, 1)], factor_shared, weights)
+    arrived, near, store_other, rows_held = lax.optimization_barrier(
+        (arrived, near, store_other, rows_held)
+    )
+    came = far_rows(arrived, rows_own)
+    message = make_message([rows_held, *came], factor_store, store_other, store_b_held, meta)
     messages = [message] + [swap(message, r) for r in range(1, count)]
-    rows[0], message = lax.optimization_barrier((rows[0], message))
-    gated = gate_up(rows, factor_shared, weights)
+    came, message = lax.optimization_barrier((came, message))
+    rows = []
+    for value in came:
+        rows += [value, swap(value, 1)]
+    far = gate_up(rows, factor_shared, weights)
 
     order = [0]
     bit = count // 2
@@ -412,9 +461,11 @@
         order = order + [r | bit for r in order]
         bit //= 2
     chunks = [[j] for j in range(n_tensor - 1, 1, -1)] + [[1, 0]]
-    outs = down_products(
-        gated, columns, shared_b_held, messages, down, down_own, experts, chunks, order
+    hidden = down_products(
+        near, far, columns, shared_b_held, messages, down, down_own, experts, chunks[:-1], order
     )
+    hidden, outs = hidden[:3], list(hidden[3:])
+    outs += down_next(hidden, down, down_own, chunks[-1:], order)
     held, leaving = list(outs[0::2]), list(outs[1::2])
     bit = 1
     while bit < count:

time: 42.6 us -> 42.8 us (level)
  waiting for transfers between devices: 13.9 us -> 10.2 us
  Pallas kernels: 12.6 us -> 16 us
  starting transfers between devices: 14.9 us -> 15.4 us
    ppermute x16, waiting for transfers between devices: 13.9 us -> 10.2 us  [swap(): return lax.ppermute(value, axis, [(i, i ^ bits) for i in range(count)])]
    pallas_call x1 -> x2, Pallas kernels: 2.53 us -> 5.77 us  [gate_up(): pl.pallas_call(functools.partial(gate_up_kernel, len(rows), 1024), in_spe...]
    pallas_call x0 -> x1, Pallas kernels: none -> 0.67 us  [down_next(): pl.pallas_call(functools.partial(down_next_kernel, chunks, order), in_spe...]
    pallas_call x1, Pallas kernels: 1.43 us -> 0.95 us  [down_products(): pl.pallas_call(functools.partial(down_kernel, experts, chunks, order), in...]
    ppermute x16, starting transfers between devices: 14.9 us -> 15.4 us  [swap(): return lax.ppermute(value, axis, [(i, i ^ bits) for i in range(count)])]
  transfers between devices with their start and end apart: 16 -> 16, of which waited for: 9 -> 8; matrix products, arithmetic and copies ran while one was open for 1% -> 1% of each run, Pallas kernels for 26% -> 34%
where the time goes in v9:
time: 42.8 us; the launch traced here: 42.7 us
  Pallas kernels  16 us (37%)
  starting transfers between devices  15.4 us (36%)
  waiting for transfers between devices  10.2 us (24%)
  other arithmetic  1.02 us (2%)
    ppermute x16, starting transfers between devices, swap(): return lax.ppermute(value, axis, [(i, i ^ bits) for i in range(count)])  15.4 us
    ppermute x16, waiting for transfers between devices, swap(): return lax.ppermute(value, axis, [(i, i ^ bits) for i in range(count)])  10.2 us
    pallas_call x1, Pallas kernels, first_call(): pl.pallas_call(functools.partial(first_kernel, experts), in_specs=[HBM_SP...  8.15 us
    pallas_call x2, Pallas kernels, gate_up(): pl.pallas_call(functools.partial(gate_up_kernel, len(rows), 1024), in_spe...  5.77 us
    pallas_call x1, Pallas kernels, down_products(): pl.pallas_call(functools.partial(down_kernel, experts, chunks, order), in...  0.95 us
  transfers between devices with their start and end apart: 16, of which 8 were waited for; matrix products, arithmetic and copies ran while one was open for 1% of the time, Pallas kernels for 34%

profile of v9, /device:TPU:0, one launch (start us, length us, event | category | flops | bytes accessed | tf_op | source)
XLA Modules:
  0.0 42.7 jit_solution(18370610190004337926)
XLA Ops:
  0.0 0.5 %collective-permute-start.1 = (bf16[32,7168]{1,0:T(8,128)(2,1)}, bf16[32,7168]{1,0:T(8,128)(2,1)S(1)}, u32[]{:S(2)}, u32[]{:S(2)}) collective-permute-start(bf16[32,7168]{1,0:T(8,128)(2,1)} %bitcast.32), channel_id=1, source_target_pairs={{0,4},{4,0},{8,12},{12,8},{1,5},{5,1},{9,13},{13,9},{2,6},{6,2},{1... | collective-permute-start | bytes 1376264 | tf_op jit(solution)/shard_map/ppermute | solution.py:41
  0.5 2.5 %collective-permute-start = (bf16[32,7168]{1,0:T(8,128)(2,1)}, bf16[32,7168]{1,0:T(8,128)(2,1)S(1)}, u32[]{:S(2)}, u32[]{:S(2)}) collective-permute-start(bf16[32,7168]{1,0:T(8,128)(2,1)} %bitcast.33), channel_id=1, source_target_pairs={{0,8},{4,12},{8,0},{12,4},{1,9},{5,13},{9,1},{13,5},{2,10},{6,14},... | collective-permute-start | bytes 1376264 | tf_op jit(solution)/shard_map/ppermute | solution.py:41
  3.0 0.2 collective-permute-start.2
  3.2 8.2 %shard_map.145 = (bf16[32,128]{1,0:T(8,128)(2,1)S(1)}, s32[8,128]{1,0:T(8,128)S(1)}, bf16[32,7168]{1,0:T(8,128)(2,1)S(1)}, bf16[32,256]{1,0:T(8,128)(2,1)S(1)}, ...) custom-call(s32[2,2,16]{2,1,0:T(2,128)} %bitcast.38, ...), custom_call_target="tpu_custom_call" | custom-call | bytes 23904256 | tf_op jit(solution)/shard_map/pallas_call | solution.py:159
  11.4 2.9 %shard_map.146 = (bf16[64,64]{1,0:T(8,128)(2,1)S(1)}, f32[64,256]{1,0:T(8,128)S(1)}, f32[64,256]{1,0:T(8,128)S(1)}, f32[64,256]{1,0:T(8,128)S(1)}, f32[64,256]{1,0:T(8,128)S(1)}) custom-call(bf16[32,7168]{1,0:T(8,128)(2,1)S(1)} %get-tuple-element.65.refs_0_, bf16[32,7168]{1,0:T(8,128)(2,1)S(1)} %collective-permute-done.1.refs_1_, ...), custom_call_target="tpu_custom_call" | custom-call | flops 939524096 | bytes 14680064 | tf_op jit(solution)/shard_map/pallas_call | solution.py:254
  14.3 0.1 collective-permute-done.refs_1_.refs_0_
  14.4 0.5 %shard_map.147.refs_12_ = bf16[64,256]{1,0:T(8,128)(2,1)S(1)} custom-call(bf16[32,7168]{1,0:T(8,128)(2,1)S(1)} %get-tuple-element.65.refs_0_, bf16[32,7168]{1,0:T(8,128)(2,1)S(1)} %collective-permute-done.refs_1_.refs_0_, bf16[32,7168]{1,0:T(8,128)(2,1)S(1)} %get-tuple-element.66.refs_2_, bf16[32,7168]{1,0:T(8,128)(2,1)S(1)} %bitcast.27, ...), custom_call_target="tpu_custom_call" | custom-call | flops 58720256 | bytes 917504 | tf_op jit(solution)/shard_map/pallas_call | solution.py:220
  14.8 0.2 collective-permute-start.3
  15.0 0.3 collective-permute-start.4
  15.4 1.7 %collective-permute-start.5 = (bf16[64,256]{1,0:T(8,128)(2,1)S(1)}, bf16[64,256]{1,0:T(8,128)(2,1)S(1)}, u32[]{:S(2)}, u32[]{:S(2)}) collective-permute-start(bf16[64,256]{1,0:T(8,128)(2,1)S(1)} %shard_map.147.refs_12_), channel_id=1, source_target_pairs={{0,8},{4,12},{8,0},{12,4},{1,9},{5,13},{9,1},{13,5},{2,10},{6,14},... | collective-permute-start | bytes 98312 | tf_op jit(solution)/shard_map/ppermute | solution.py:41
  17.1 2.9 %shard_map.148 = (bf16[64,64]{1,0:T(8,128)(2,1)S(1)}, f32[64,256]{1,0:T(8,128)S(1)}, f32[64,256]{1,0:T(8,128)S(1)}, f32[64,256]{1,0:T(8,128)S(1)}, f32[64,256]{1,0:T(8,128)S(1)}) custom-call(bf16[32,7168]{1,0:T(8,128)(2,1)S(1)} %collective-permute-done.refs_1_.refs_0_, bf16[32,7168]{1,0:T(8,128)(2,1)S(1)} %collective-permute-done.3.refs_1_, ...), custom_call_target="tpu_custom_call" | custom-call | flops 939524096 | bytes 14680064 | tf_op jit(solution)/shard_map/pallas_call | solution.py:254
  20.0 0.7 %collective-permute-done.6.refs_15_ = bf16[64,256]{1,0:T(8,128)(2,1)S(1)} collective-permute-done((bf16[64,256]{1,0:T(8,128)(2,1)S(1)}, bf16[64,256]{1,0:T(8,128)(2,1)S(1)}, u32[]{:S(2)}, u32[]{:S(2)}) %collective-permute-start.6) | collective-permute-done | bytes 32800 | tf_op jit(solution)/shard_map/ppermute | solution.py:41
  20.8 0.9 %shard_map.149 = (bf16[128,256]{1,0:T(8,128)(2,1)S(1)}, bf16[128,256]{1,0:T(8,128)(2,1)S(1)}, f32[128,128]{1,0:T(8,128)S(1)}, bf16[2,1,32,1792]{3,2,1,0:T(8,128)...) custom-call(bf16[64,64]{1,0:T(8,128)(2,1)S(1)} %get-tuple-element.59, ...), custom_call_target="tpu_custom_call" | custom-call | flops 469762048 | bytes 3670016 | tf_op jit(solution)/shard_map/pallas_call | solution.py:371
  21.7 0.2 collective-permute-start.11
  21.9 0.4 collective-permute-start.10
  22.3 0.7 %shard_map.150 = (bf16[2,2,32,1792]{3,2,1,0:T(8,128)(2,1)S(1)}, bf16[2,2,32,1792]{3,2,1,0:T(8,128)(2,1)S(1)}) custom-call(bf16[128,256]{1,0:T(8,128)(2,1)S(1)} %get-tuple-element.80.hidden, bf16[128,256]{1,0:T(8,128)(2,1)S(1)} %get-tuple-element.81.hidden_shared, f32[128,128]{1,0:T(8,128)S(1)} %get-tuple-element.82.share, ...), custom_call_target="tpu_custom_call" | custom-call | flops 469762048 | bytes 3670016 | tf_op jit(solution)/shard_map/pallas_call | solution.py:385
  23.0 0.2 collective-permute-start.7
  23.1 0.1 collective-permute-done.11
  23.3 1.2 %collective-permute-start.13 = (bf16[1,1,32,1792]{3,2,1,0:T(8,128)(2,1)S(1)}, bf16[1,1,32,1792]{3,2,1,0:T(8,128)(2,1)S(1)}, u32[]{:S(2)}, u32[]{:S(2)}) collective-permute-start(bf16[1,1,32,1792]{3,2,1,0:T(8,128)(2,1)S(1)} %add_convert_fusion.4), channel_id=1, source_target_pairs={{0,8},{4,12},{8,0},{12,4},{1,9},{5,13},{9,1},{13,5},{2,10},{6,14},... | collective-permute-start | bytes 344072 | tf_op jit(solution)/shard_map/ppermute | solution.py:41
  24.6 0.9 %collective-permute-start.12 = (bf16[1,1,32,1792]{3,2,1,0:T(8,128)(2,1)S(1)}, bf16[1,1,32,1792]{3,2,1,0:T(8,128)(2,1)S(1)}, u32[]{:S(2)}, u32[]{:S(2)}) collective-permute-start(bf16[1,1,32,1792]{3,2,1,0:T(8,128)(2,1)S(1)} %add_convert_fusion.5), channel_id=1, source_target_pairs={{0,8},{4,12},{8,0},{12,4},{1,9},{5,13},{9,1},{13,5},{2,10},{6,14},... | collective-permute-start | bytes 344072 | tf_op jit(solution)/shard_map/ppermute | solution.py:41
  25.5 0.1 add_convert_fusion.1
  25.6 3.7 %collective-permute-done.13 = bf16[1,1,32,1792]{3,2,1,0:T(8,128)(2,1)S(1)} collective-permute-done((bf16[1,1,32,1792]{3,2,1,0:T(8,128)(2,1)S(1)}, bf16[1,1,32,1792]{3,2,1,0:T(8,128)(2,1)S(1)}, u32[]{:S(2)}, u32[]{:S(2)}) %collective-permute-start.13) | collective-permute-done | bytes 114720 | tf_op jit(solution)/shard_map/ppermute | solution.py:41
  29.4 1.6 %collective-permute-start.14 = (bf16[32,1792]{1,0:T(8,128)(2,1)S(1)}, bf16[32,1792]{1,0:T(8,128)(2,1)S(1)}, u32[]{:S(2)}, u32[]{:S(2)}) collective-permute-start(bf16[32,1792]{1,0:T(8,128)(2,1)S(1)} %fusion.4), channel_id=1, source_target_pairs={{0,1},{1,0},{2,3},{3,2},{4,5},{5,4},{6,7},{7,6},{8,9},{9,8},{10,11... | collective-permute-start | bytes 344072 | tf_op jit(solution)/shard_map/ppermute | solution.py:41
  31.0 1.2 %collective-permute-start.8 = (bf16[1,2,32,1792]{3,2,1,0:T(8,128)(2,1)S(1)}, bf16[1,2,32,1792]{3,2,1,0:T(8,128)(2,1)S(1)}, u32[]{:S(2)}, u32[]{:S(2)}) collective-permute-start(bf16[1,2,32,1792]{3,2,1,0:T(8,128)(2,1)S(1)} %get-tuple-element.92), channel_id=1, source_target_pairs={{0,8},{4,12},{8,0},{12,4},{1,9},{5,13},{9,1},{13,5},{2,10},{6,14},... | collective-permute-start | bytes 688136 | tf_op jit(solution)/shard_map/ppermute | solution.py:41
  32.2 2.0 %collective-permute-done.14 = bf16[32,1792]{1,0:T(8,128)(2,1)S(1)} collective-permute-done((bf16[32,1792]{1,0:T(8,128)(2,1)S(1)}, bf16[32,1792]{1,0:T(8,128)(2,1)S(1)}, u32[]{:S(2)}, u32[]{:S(2)}) %collective-permute-start.14) | collective-permute-done | bytes 114720 | tf_op jit(solution)/shard_map/ppermute | solution.py:41
  34.2 0.1 fusion
  34.3 2.7 %collective-permute-start.15 = (bf16[32,1792]{1,0:T(8,128)(2,1)S(1)}, bf16[32,1792]{1,0:T(8,128)(2,1)S(1)}, u32[]{:S(2)}, u32[]{:S(2)}) collective-permute-start(bf16[32,1792]{1,0:T(8,128)(2,1)S(1)} %fusion), channel_id=1, source_target_pairs={{0,2},{1,3},{2,0},{3,1},{4,6},{5,7},{6,4},{7,5},{8,10},{9,11},{10,... | collective-permute-start | bytes 344072 | tf_op jit(solution)/shard_map/ppermute | solution.py:41
  37.0 0.1 collective-permute-done.8
  37.1 1.5 %collective-permute-start.9 = (bf16[32,1792]{1,0:T(8,128)(2,1)S(1)}, bf16[32,1792]{1,0:T(8,128)(2,1)S(1)}, u32[]{:S(2)}, u32[]{:S(2)}) collective-permute-start(bf16[32,1792]{1,0:T(8,128)(2,1)S(1)} %fusion.3), channel_id=1, source_target_pairs={{0,1},{1,0},{2,3},{3,2},{4,5},{5,4},{6,7},{7,6},{8,9},{9,8},{10,11... | collective-permute-start | bytes 344072 | tf_op jit(solution)/shard_map/ppermute | solution.py:41
  38.6 1.7 %collective-permute-done.15 = bf16[32,1792]{1,0:T(8,128)(2,1)S(1)} collective-permute-done((bf16[32,1792]{1,0:T(8,128)(2,1)S(1)}, bf16[32,1792]{1,0:T(8,128)(2,1)S(1)}, u32[]{:S(2)}, u32[]{:S(2)}) %collective-permute-start.15) | collective-permute-done | bytes 114720 | tf_op jit(solution)/shard_map/ppermute | solution.py:41
  40.3 1.6 %collective-permute-done.9 = bf16[32,1792]{1,0:T(8,128)(2,1)S(1)} collective-permute-done((bf16[32,1792]{1,0:T(8,128)(2,1)S(1)}, bf16[32,1792]{1,0:T(8,128)(2,1)S(1)}, u32[]{:S(2)}, u32[]{:S(2)}) %collective-permute-start.9) | collective-permute-done | bytes 114720 | tf_op jit(solution)/shard_map/ppermute | solution.py:41
  42.0 0.7 %fusion.2 = bf16[32,1792]{1,0:T(8,128)(2,1)} fusion(bf16[32,1792]{1,0:T(8,128)(2,1)S(1)} %collective-permute-done.15, bf16[32,1792]{1,0:T(8,128)(2,1)S(1)} %collective-permute-done.9, bf16[1,2,32,1792]{3,2,1,0:T(8,128)(2,1)S(1)} %collective-permute-done.8, bf16[1,2,32,1792]{3,2,1,0:T(8,128)(2,1)S(1)} %get-tuple-element.91), kind=kLoop, calls=%fused_computation.6 | loop fusion | flops 458752 | bytes 573440 | tf_op jit(solution)/shard_map/convert_element_type | solution.py:49
  (13 shorter events, 0.2 us)
Async XLA Ops:
  0.0 11.4 %collective-permute-start.1 = (bf16[32,7168]{1,0:T(8,128)(2,1)}, bf16[32,7168]{1,0:T(8,128)(2,1)S(1)}, u32[]{:S(2)}, u32[]{:S(2)}) collective-permute-start(bf16[32,7168]{1,0:T(8,128)(2,1)} %bitcast.32), channel_id=1, source_target_pairs={{0,4},{4,0},{8,12},{12,8},{1,5},{5,1},{9,13},{13,9},{2,6},{6,2},{1... | collective-permute-start | bytes 1376264 | tf_op jit(solution)/shard_map/ppermute | solution.py:41
  0.5 13.9 %collective-permute-start = (bf16[32,7168]{1,0:T(8,128)(2,1)}, bf16[32,7168]{1,0:T(8,128)(2,1)S(1)}, u32[]{:S(2)}, u32[]{:S(2)}) collective-permute-start(bf16[32,7168]{1,0:T(8,128)(2,1)} %bitcast.33), channel_id=1, source_target_pairs={{0,8},{4,12},{8,0},{12,4},{1,9},{5,13},{9,1},{13,5},{2,10},{6,14},... | collective-permute-start | bytes 1376264 | tf_op jit(solution)/shard_map/ppermute | solution.py:41
  3.0 11.4 %collective-permute-start.2 = (bf16[2,16,7168]{2,1,0:T(8,128)(2,1)}, bf16[2,16,7168]{2,1,0:T(8,128)(2,1)S(1)}, u32[]{:S(2)}, u32[]{:S(2)}) collective-permute-start(bf16[2,16,7168]{2,1,0:T(8,128)(2,1)} %param.25), channel_id=1, source_target_pairs={{0,4},{4,0},{8,12},{12,8},{1,5},{5,1},{9,13},{13,9},{2,6},{6,2},{1... | collective-permute-start | bytes 1376264 | tf_op jit(solution)/shard_map/ppermute | solution.py:41
  14.8 2.3 %collective-permute-start.3 = (bf16[32,7168]{1,0:T(8,128)(2,1)S(1)}, bf16[32,7168]{1,0:T(8,128)(2,1)S(1)}, u32[]{:S(2)}, u32[]{:S(2)}) collective-permute-start(bf16[32,7168]{1,0:T(8,128)(2,1)S(1)} %collective-permute-done.refs_1_.refs_0_), channel_id=1, source_target_pairs={{0,4},{4,0},{8,12},{12,8},{1,5},{5,1},{9,13},{13,9},{2,6},{6,2},{1... | collective-permute-start | bytes 1376264 | tf_op jit(solution)/shard_map/ppermute | solution.py:41
  15.0 5.0 %collective-permute-start.4 = (bf16[64,256]{1,0:T(8,128)(2,1)S(1)}, bf16[64,256]{1,0:T(8,128)(2,1)S(1)}, u32[]{:S(2)}, u32[]{:S(2)}) collective-permute-start(bf16[64,256]{1,0:T(8,128)(2,1)S(1)} %shard_map.147.refs_12_), channel_id=1, source_target_pairs={{0,4},{4,0},{8,12},{12,8},{1,5},{5,1},{9,13},{13,9},{2,6},{6,2},{1... | collective-permute-start | bytes 98312 | tf_op jit(solution)/shard_map/ppermute | solution.py:41
  15.4 4.6 %collective-permute-start.5 = (bf16[64,256]{1,0:T(8,128)(2,1)S(1)}, bf16[64,256]{1,0:T(8,128)(2,1)S(1)}, u32[]{:S(2)}, u32[]{:S(2)}) collective-permute-start(bf16[64,256]{1,0:T(8,128)(2,1)S(1)} %shard_map.147.refs_12_), channel_id=1, source_target_pairs={{0,8},{4,12},{8,0},{12,4},{1,9},{5,13},{9,1},{13,5},{2,10},{6,14},... | collective-permute-start | bytes 98312 | tf_op jit(solution)/shard_map/ppermute | solution.py:41
  17.1 3.7 %collective-permute-start.6 = (bf16[64,256]{1,0:T(8,128)(2,1)S(1)}, bf16[64,256]{1,0:T(8,128)(2,1)S(1)}, u32[]{:S(2)}, u32[]{:S(2)}) collective-permute-start(bf16[64,256]{1,0:T(8,128)(2,1)S(1)} %shard_map.147.refs_12_), channel_id=1, source_target_pairs={{0,12},{4,8},{8,4},{12,0},{1,13},{5,9},{9,5},{13,1},{2,14},{6,10},... | collective-permute-start | bytes 98312 | tf_op jit(solution)/shard_map/ppermute | solution.py:41
  21.7 1.6 %collective-permute-start.11 = (bf16[2,1,32,1792]{3,2,1,0:T(8,128)(2,1)S(1)}, bf16[2,1,32,1792]{3,2,1,0:T(8,128)(2,1)S(1)}, u32[]{:S(2)}, u32[]{:S(2)}) collective-permute-start(bf16[2,1,32,1792]{3,2,1,0:T(8,128)(2,1)S(1)} %get-tuple-element.88), channel_id=1, source_target_pairs={{0,4},{4,0},{8,12},{12,8},{1,5},{5,1},{9,13},{13,9},{2,6},{6,2},{1... | collective-permute-start | bytes 688136 | tf_op jit(solution)/shard_map/ppermute | solution.py:41
  21.9 2.7 %collective-permute-start.10 = (bf16[2,1,32,1792]{3,2,1,0:T(8,128)(2,1)S(1)}, bf16[2,1,32,1792]{3,2,1,0:T(8,128)(2,1)S(1)}, u32[]{:S(2)}, u32[]{:S(2)}) collective-permute-start(bf16[2,1,32,1792]{3,2,1,0:T(8,128)(2,1)S(1)} %get-tuple-element.86), channel_id=1, source_target_pairs={{0,4},{4,0},{8,12},{12,8},{1,5},{5,1},{9,13},{13,9},{2,6},{6,2},{1... | collective-permute-start | bytes 688136 | tf_op jit(solution)/shard_map/ppermute | solution.py:41
  23.0 2.5 %collective-permute-start.7 = (bf16[2,2,32,1792]{3,2,1,0:T(8,128)(2,1)S(1)}, bf16[2,2,32,1792]{3,2,1,0:T(8,128)(2,1)S(1)}, u32[]{:S(2)}, u32[]{:S(2)}) collective-permute-start(bf16[2,2,32,1792]{3,2,1,0:T(8,128)(2,1)S(1)} %get-tuple-element.84), channel_id=1, source_target_pairs={{0,4},{4,0},{8,12},{12,8},{1,5},{5,1},{9,13},{13,9},{2,6},{6,2},{1... | collective-permute-start | bytes 1376264 | tf_op jit(solution)/shard_map/ppermute | solution.py:41
  23.3 6.0 %collective-permute-start.13 = (bf16[1,1,32,1792]{3,2,1,0:T(8,128)(2,1)S(1)}, bf16[1,1,32,1792]{3,2,1,0:T(8,128)(2,1)S(1)}, u32[]{:S(2)}, u32[]{:S(2)}) collective-permute-start(bf16[1,1,32,1792]{3,2,1,0:T(8,128)(2,1)S(1)} %add_convert_fusion.4), channel_id=1, source_target_pairs={{0,8},{4,12},{8,0},{12,4},{1,9},{5,13},{9,1},{13,5},{2,10},{6,14},... | collective-permute-start | bytes 344072 | tf_op jit(solution)/shard_map/ppermute | solution.py:41
  24.6 7.6 %collective-permute-start.12 = (bf16[1,1,32,1792]{3,2,1,0:T(8,128)(2,1)S(1)}, bf16[1,1,32,1792]{3,2,1,0:T(8,128)(2,1)S(1)}, u32[]{:S(2)}, u32[]{:S(2)}) collective-permute-start(bf16[1,1,32,1792]{3,2,1,0:T(8,128)(2,1)S(1)} %add_convert_fusion.5), channel_id=1, source_target_pairs={{0,8},{4,12},{8,0},{12,4},{1,9},{5,13},{9,1},{13,5},{2,10},{6,14},... | collective-permute-start | bytes 344072 | tf_op jit(solution)/shard_map/ppermute | solution.py:41
  29.4 4.9 %collective-permute-start.14 = (bf16[32,1792]{1,0:T(8,128)(2,1)S(1)}, bf16[32,1792]{1,0:T(8,128)(2,1)S(1)}, u32[]{:S(2)}, u32[]{:S(2)}) collective-permute-start(bf16[32,1792]{1,0:T(8,128)(2,1)S(1)} %fusion.4), channel_id=1, source_target_pairs={{0,1},{1,0},{2,3},{3,2},{4,5},{5,4},{6,7},{7,6},{8,9},{9,8},{10,11... | collective-permute-start | bytes 344072 | tf_op jit(solution)/shard_map/ppermute | solution.py:41
  31.0 6.0 %collective-permute-start.8 = (bf16[1,2,32,1792]{3,2,1,0:T(8,128)(2,1)S(1)}, bf16[1,2,32,1792]{3,2,1,0:T(8,128)(2,1)S(1)}, u32[]{:S(2)}, u32[]{:S(2)}) collective-permute-start(bf16[1,2,32,1792]{3,2,1,0:T(8,128)(2,1)S(1)} %get-tuple-element.92), channel_id=1, source_target_pairs={{0,8},{4,12},{8,0},{12,4},{1,9},{5,13},{9,1},{13,5},{2,10},{6,14},... | collective-permute-start | bytes 688136 | tf_op jit(solution)/shard_map/ppermute | solution.py:41
  34.3 6.0 %collective-permute-start.15 = (bf16[32,1792]{1,0:T(8,128)(2,1)S(1)}, bf16[32,1792]{1,0:T(8,128)(2,1)S(1)}, u32[]{:S(2)}, u32[]{:S(2)}) collective-permute-start(bf16[32,1792]{1,0:T(8,128)(2,1)S(1)} %fusion), channel_id=1, source_target_pairs={{0,2},{1,3},{2,0},{3,1},{4,6},{5,7},{6,4},{7,5},{8,10},{9,11},{10,... | collective-permute-start | bytes 344072 | tf_op jit(solution)/shard_map/ppermute | solution.py:41
  37.1 4.9 %collective-permute-start.9 = (bf16[32,1792]{1,0:T(8,128)(2,1)S(1)}, bf16[32,1792]{1,0:T(8,128)(2,1)S(1)}, u32[]{:S(2)}, u32[]{:S(2)}) collective-permute-start(bf16[32,1792]{1,0:T(8,128)(2,1)S(1)} %fusion.3), channel_id=1, source_target_pairs={{0,1},{1,0},{2,3},{3,2},{4,5},{5,4},{6,7},{7,6},{8,9},{9,8},{10,11... | collective-permute-start | bytes 344072 | tf_op jit(solution)/shard_map/ppermute | solution.py:41

commit v10 on v9

--- a/solution.py
+++ b/solution.py
@@ -292,15 +292,13 @@
 def down_kernel(experts, chunks, order, *refs):
     count = len(order)
     half = count // 2
-    near, far, refs = refs[:5], refs[5:10], refs[10:]
+    inner_shared, gate, up, gate_shared, up_shared = [ref[...] for ref in refs[:5]]
+    refs = refs[5:]
     columns, shared_b = refs[:2]
     messages = refs[2 : 2 + count]
     down, down_shared = refs[2 + count : 4 + count]
     hidden_out, hidden_shared_out, share_out = refs[4 + count : 7 + count]
     outs = refs[7 + count :]
-    inner_shared, gate, up, gate_shared, up_shared = [
-        jnp.concatenate([one[...], other[...]], axis=0) for one, other in zip(near, far)
-    ]
     total, width = gate.shape
     size = total // count
     shared_count = shared_b.shape[0]
@@ -359,12 +357,12 @@
 
 def down_cost(rows, down, chunks):
     part = sum(len(chunk) for chunk in chunks) * down.size // lax.axis_size("tensor")
-    return cost(4 * rows * part, 4 * part)
-
-
-def down_products(near, far, columns, shared_b, messages, down, down_shared, experts, chunks, order):
-    rows, width = near[1].shape[0] + far[1].shape[0], near[1].shape[1]
-    whole = [*near, *far, columns, shared_b, *messages, down, down_shared]
+    return cost(4 * rows * part, 0)
+
+
+def down_products(gated, columns, shared_b, messages, down, down_shared, experts, chunks, order):
+    rows, width = gated[1].shape
+    whole = [*gated, columns, shared_b, *messages, down, down_shared]
     outs = [jax.ShapeDtypeStruct((rows, width), BF16)] * 2
     outs += [jax.ShapeDtypeStruct((rows, 128), F32)]
     outs += down_outs(rows, down.shape[1], chunks, order)
@@ -442,39 +440,41 @@
     )
     meta, columns, rows_held, store_b_held, shared_b_held, factor_store, factor_shared = first[:7]
     weights, down, down_own = first[7:11], first[11], first[12]
-    near = gate_up([rows_held, swap(rows_own, 1)], factor_shared, weights)
-    arrived, near, store_other, rows_held = lax.optimization_barrier(
-        (arrived, near, store_other, rows_held)
-    )
+    arrived, rows_held, store_other = lax.optimization_barrier((arrived, rows_held, store_other))
     came = far_rows(arrived, rows_own)
     message = make_message([rows_held, *came], factor_store, store_other, store_b_held, meta)
     messages = [message] + [swap(message, r) for r in range(1, count)]
     came, message = lax.optimization_barrier((came, message))
-    rows = []
+    rows = [rows_held, swap(rows_own, 1)]
     for value in came:
         rows += [value, swap(value, 1)]
-    far = gate_up(rows, factor_shared, weights)
+    gated = gate_up(rows, factor_shared, weights)
 
     order = [0]
     bit = count // 2
     while bit >= 1:
         order = order + [r | bit for r in order]
         bit //= 2
-    chunks = [[j] for j in range(n_tensor - 1, 1, -1)] + [[1, 0]]
+    chunks = [[j] for j in range(n_tensor - 1, -1, -1)]
     hidden = down_products(
-        near, far, columns, shared_b_held, messages, down, down_own, experts, chunks[:-1], order
+        gated, columns, shared_b_held, messages, down, down_own, experts, chunks[:-2], order
     )
-    hidden, outs = hidden[:3], list(hidden[3:])
-    outs += down_next(hidden, down, down_own, chunks[-1:], order)
-    held, leaving = list(outs[0::2]), list(outs[1::2])
+    hidden, held, leaving = hidden[:3], list(hidden[3::2]), list(hidden[4::2])
     bit = 1
     while bit < count:
         half = count // (2 * bit) // 2
         if bit > 1:
             leaving[1], *_ = lax.optimization_barrier((leaving[1], leaving[0]))
-        arrived = [swap(value, bit) for value in leaving]
-        if bit > 1:
-            arrived[0], *_ = lax.optimization_barrier((arrived[0], *leaving))
+        arrived = [swap(value, bit) for value in (leaving if bit == 1 else leaving[:-1])]
+        if bit == 1:
+            ready = add(held[0][half:], arrived[0][half:])
+            hidden, ready = lax.optimization_barrier((hidden, ready))
+            rest = down_next(hidden, down, down_own, chunks[len(held) :], order)
+            held += rest[0::2]
+            arrived += [swap(value, bit) for value in rest[1::2]]
+        else:
+            arrived[0], *leaving = lax.optimization_barrier((arrived[0], *leaving))
+            arrived.append(swap(leaving[-1], bit))
         if 2 * bit < count:
             leaving = [add(h[half:], a[half:]) for h, a in zip(held, arrived)]
             held = [add(h[:half], a[:half]) for h, a in zip(held, arrived)]

time: 42.8 us -> 43.2 us (level)
  Pallas kernels: 16 us -> 12.9 us
  waiting for transfers between devices: 10.2 us -> 12.5 us
  starting transfers between devices: 15.4 us -> 16.6 us
    pallas_call x2 -> x1, Pallas kernels: 5.77 us -> 2.62 us  [gate_up(): pl.pallas_call(functools.partial(gate_up_kernel, len(rows), 1024), in_spe...]
    ppermute x16 -> x18, waiting for transfers between devices: 10.2 us -> 12.5 us  [swap(): return lax.ppermute(value, axis, [(i, i ^ bits) for i in range(count)])]
    ppermute x16 -> x18, starting transfers between devices: 15.4 us -> 16.6 us  [swap(): return lax.ppermute(value, axis, [(i, i ^ bits) for i in range(count)])]
  transfers between devices with their start and end apart: 16 -> 18, of which waited for: 8 -> 7; matrix products, arithmetic and copies ran while one was open for 1% -> 1% of each run, Pallas kernels for 34% -> 28%
where the time goes in v10:
time: 43.2 us; the launch traced here: 43.1 us
  starting transfers between devices  16.6 us (38%)
  Pallas kernels  12.9 us (30%)
  waiting for transfers between devices  12.5 us (29%)
  other arithmetic  1.01 us (2%)
    ppermute x18, starting transfers between devices, swap(): return lax.ppermute(value, axis, [(i, i ^ bits) for i in range(count)])  16.6 us
    ppermute x18, waiting for transfers between devices, swap(): return lax.ppermute(value, axis, [(i, i ^ bits) for i in range(count)])  12.5 us
    pallas_call x1, Pallas kernels, first_call(): pl.pallas_call(functools.partial(first_kernel, experts), in_specs=[HBM_SP...  8.15 us
    pallas_call x1, Pallas kernels, gate_up(): pl.pallas_call(functools.partial(gate_up_kernel, len(rows), 1024), in_spe...  2.62 us
    pallas_call x1, Pallas kernels, down_products(): pl.pallas_call(functools.partial(down_kernel, experts, chunks, order), in...  0.95 us
    convert_element_type x4, other arithmetic, total_of(): return sum((value.astype(F32) for value in values)).astype(BF16)  0.89 us
  transfers between devices with their start and end apart: 18, of which 7 were waited for; matrix products, arithmetic and copies ran while one was open for 1% of the time, Pallas kernels for 28%

profile of v10, /device:TPU:0, one launch (start us, length us, event | category | flops | bytes accessed | tf_op | source)
XLA Modules:
  0.0 43.1 jit_solution(7506971408939761032)
XLA Ops:
  0.0 3.0 %collective-permute-start = (bf16[32,7168]{1,0:T(8,128)(2,1)}, bf16[32,7168]{1,0:T(8,128)(2,1)S(1)}, u32[]{:S(2)}, u32[]{:S(2)}) collective-permute-start(bf16[32,7168]{1,0:T(8,128)(2,1)} %bitcast.33), channel_id=1, source_target_pairs={{0,8},{4,12},{8,0},{12,4},{1,9},{5,13},{9,1},{13,5},{2,10},{6,14},... | collective-permute-start | bytes 1376264 | tf_op jit(solution)/shard_map/ppermute | solution.py:41
  3.0 0.5 %collective-permute-start.2 = (bf16[32,7168]{1,0:T(8,128)(2,1)}, bf16[32,7168]{1,0:T(8,128)(2,1)S(1)}, u32[]{:S(2)}, u32[]{:S(2)}) collective-permute-start(bf16[32,7168]{1,0:T(8,128)(2,1)} %bitcast.34), channel_id=1, source_target_pairs={{0,4},{4,0},{8,12},{12,8},{1,5},{5,1},{9,13},{13,9},{2,6},{6,2},{1... | collective-permute-start | bytes 1376264 | tf_op jit(solution)/shard_map/ppermute | solution.py:41
  3.5 8.2 %shard_map.145 = (bf16[32,128]{1,0:T(8,128)(2,1)S(1)}, s32[8,128]{1,0:T(8,128)S(1)}, bf16[32,7168]{1,0:T(8,128)(2,1)S(1)}, bf16[32,256]{1,0:T(8,128)(2,1)S(1)}, ...) custom-call(s32[2,2,16]{2,1,0:T(2,128)} %bitcast.38, ...), custom_call_target="tpu_custom_call" | custom-call | bytes 23904256 | tf_op jit(solution)/shard_map/pallas_call | solution.py:159
  11.6 2.1 %collective-permute-done.refs_1_.refs_2_ = bf16[32,7168]{1,0:T(8,128)(2,1)S(1)} collective-permute-done((bf16[32,7168]{1,0:T(8,128)(2,1)}, bf16[32,7168]{1,0:T(8,128)(2,1)S(1)}, u32[]{:S(2)}, u32[]{:S(2)}) %collective-permute-start) | collective-permute-done | bytes 458784 | tf_op jit(solution)/shard_map/ppermute | solution.py:41
  13.7 0.5 %shard_map.146.refs_7_ = bf16[64,256]{1,0:T(8,128)(2,1)S(1)} custom-call(bf16[32,7168]{1,0:T(8,128)(2,1)S(1)} %get-tuple-element.45.refs_0_, bf16[32,7168]{1,0:T(8,128)(2,1)S(1)} %collective-permute-done.refs_1_.refs_2_, bf16[32,7168]{1,0:T(8,128)(2,1)S(1)} %get-tuple-element.47.refs_2_, bf16[32,7168]{1,0:T(8,128)(2,1)S(1)} %bitcast.27, ...), custom_call_target="tpu_custom_call" | custom-call | flops 58720256 | bytes 917504 | tf_op jit(solution)/shard_map/pallas_call | solution.py:220
  14.2 0.0 collective-permute-start.3
  14.2 0.5 %collective-permute-start.4 = (bf16[64,256]{1,0:T(8,128)(2,1)S(1)}, bf16[64,256]{1,0:T(8,128)(2,1)S(1)}, u32[]{:S(2)}, u32[]{:S(2)}) collective-permute-start(bf16[64,256]{1,0:T(8,128)(2,1)S(1)} %shard_map.146.refs_7_), channel_id=1, source_target_pairs={{0,4},{4,0},{8,12},{12,8},{1,5},{5,1},{9,13},{13,9},{2,6},{6,2},{1... | collective-permute-start | bytes 98312 | tf_op jit(solution)/shard_map/ppermute | solution.py:41
  14.7 1.7 %collective-permute-start.5 = (bf16[64,256]{1,0:T(8,128)(2,1)S(1)}, bf16[64,256]{1,0:T(8,128)(2,1)S(1)}, u32[]{:S(2)}, u32[]{:S(2)}) collective-permute-start(bf16[64,256]{1,0:T(8,128)(2,1)S(1)} %shard_map.146.refs_7_), channel_id=1, source_target_pairs={{0,8},{4,12},{8,0},{12,4},{1,9},{5,13},{9,1},{13,5},{2,10},{6,14},... | collective-permute-start | bytes 98312 | tf_op jit(solution)/shard_map/ppermute | solution.py:41
  16.4 0.0 collective-permute-start.6
  16.4 0.0 collective-permute-done.2.refs_1_
  16.4 2.6 %shard_map.147 = (bf16[128,64]{1,0:T(8,128)(2,1)S(1)}, f32[128,256]{1,0:T(8,128)S(1)}, f32[128,256]{1,0:T(8,128)S(1)}, f32[128,256]{1,0:T(8,128)S(1)}, f32[128,256]{1,0:T(8,128)S(1)}) custom-call(bf16[32,7168]{1,0:T(8,128)(2,1)S(1)} %get-tuple-element.45.refs_0_, bf16[32,7168]{1,0:T(8,128)(2,1)S(1)} %collective-permute-done.2.refs_1_, ...), custom_call_target="tpu_custom_call" | custom-call | flops 1879048192 | bytes 14680064 | tf_op jit(solution)/shard_map/pallas_call | solution.py:254
  19.1 1.0 %collective-permute-done.6.refs_10_ = bf16[64,256]{1,0:T(8,128)(2,1)S(1)} collective-permute-done((bf16[64,256]{1,0:T(8,128)(2,1)S(1)}, bf16[64,256]{1,0:T(8,128)(2,1)S(1)}, u32[]{:S(2)}, u32[]{:S(2)}) %collective-permute-start.6) | collective-permute-done | bytes 32800 | tf_op jit(solution)/shard_map/ppermute | solution.py:41
  20.1 0.9 %shard_map.148 = (bf16[128,256]{1,0:T(8,128)(2,1)S(1)}, bf16[128,256]{1,0:T(8,128)(2,1)S(1)}, f32[128,128]{1,0:T(8,128)S(1)}, bf16[2,1,32,1792]{3,2,1,0:T(8,128)...) custom-call(bf16[128,64]{1,0:T(8,128)(2,1)S(1)} %get-tuple-element.5, ...), custom_call_target="tpu_custom_call" | custom-call | flops 469762048 | tf_op jit(solution)/shard_map/pallas_call | solution.py:369
  21.0 0.2 collective-permute-start.7
  21.2 0.4 collective-permute-start.10
  21.6 1.0 %collective-permute-done.7 = bf16[2,1,32,1792]{3,2,1,0:T(8,128)(2,1)S(1)} collective-permute-done((bf16[2,1,32,1792]{3,2,1,0:T(8,128)(2,1)S(1)}, bf16[2,1,32,1792]{3,2,1,0:T(8,128)(2,1)S(1)}, u32[]{:S(2)}, u32[]{:S(2)}) %collective-permute-start.7) | collective-permute-done | bytes 229408 | tf_op jit(solution)/shard_map/ppermute | solution.py:41
  22.6 0.8 %collective-permute-start.9 = (bf16[1,1,32,1792]{3,2,1,0:T(8,128)(2,1)S(1)}, bf16[1,1,32,1792]{3,2,1,0:T(8,128)(2,1)S(1)}, u32[]{:S(2)}, u32[]{:S(2)}) collective-permute-start(bf16[1,1,32,1792]{3,2,1,0:T(8,128)(2,1)S(1)} %add_convert_fusion.9), channel_id=1, source_target_pairs={{0,8},{4,12},{8,0},{12,4},{1,9},{5,13},{9,1},{13,5},{2,10},{6,14},... | collective-permute-start | bytes 344072 | tf_op jit(solution)/shard_map/ppermute | solution.py:41
  23.5 0.7 %shard_map.149 = (bf16[2,1,32,1792]{3,2,1,0:T(8,128)(2,1)S(1)}, bf16[2,1,32,1792]{3,2,1,0:T(8,128)(2,1)S(1)}, bf16[2,1,32,1792]{3,2,1,0:T(8,128)(2,1)S(1)}, bf16[2,1,32,1792]{3,2,1,0:T(8,128)(2,1)S(1)}) custom-call(bf16[128,256]{1,0:T(8,128)(2,1)S(1)} %get-tuple-element.71.hidden, bf16[128,256]{1,0:T(8,128)(2,1)S(1)} %get-tuple-element.72.hidden_shared, ...), custom_call_target="tpu_custom_call" | custom-call | flops 469762048 | tf_op jit(solution)/shard_map/pallas_call | solution.py:383
  24.2 0.1 collective-permute-start.11
  24.3 0.4 collective-permute-start.8
  24.8 1.3 %collective-permute-start.15 = (bf16[1,1,32,1792]{3,2,1,0:T(8,128)(2,1)S(1)}, bf16[1,1,32,1792]{3,2,1,0:T(8,128)(2,1)S(1)}, u32[]{:S(2)}, u32[]{:S(2)}) collective-permute-start(bf16[1,1,32,1792]{3,2,1,0:T(8,128)(2,1)S(1)} %add_convert_fusion.7), channel_id=1, source_target_pairs={{0,8},{4,12},{8,0},{12,4},{1,9},{5,13},{9,1},{13,5},{2,10},{6,14},... | collective-permute-start | bytes 344072 | tf_op jit(solution)/shard_map/ppermute | solution.py:41
  26.1 0.9 %collective-permute-start.13 = (bf16[1,1,32,1792]{3,2,1,0:T(8,128)(2,1)S(1)}, bf16[1,1,32,1792]{3,2,1,0:T(8,128)(2,1)S(1)}, u32[]{:S(2)}, u32[]{:S(2)}) collective-permute-start(bf16[1,1,32,1792]{3,2,1,0:T(8,128)(2,1)S(1)} %add_convert_fusion.6), channel_id=1, source_target_pairs={{0,8},{4,12},{8,0},{12,4},{1,9},{5,13},{9,1},{13,5},{2,10},{6,14},... | collective-permute-start | bytes 344072 | tf_op jit(solution)/shard_map/ppermute | solution.py:41
  27.1 1.1 %collective-permute-done.9 = bf16[1,1,32,1792]{3,2,1,0:T(8,128)(2,1)S(1)} collective-permute-done((bf16[1,1,32,1792]{3,2,1,0:T(8,128)(2,1)S(1)}, bf16[1,1,32,1792]{3,2,1,0:T(8,128)(2,1)S(1)}, u32[]{:S(2)}, u32[]{:S(2)}) %collective-permute-start.9) | collective-permute-done | bytes 114720 | tf_op jit(solution)/shard_map/ppermute | solution.py:41
  28.3 1.6 %collective-permute-start.16 = (bf16[32,1792]{1,0:T(8,128)(2,1)S(1)}, bf16[32,1792]{1,0:T(8,128)(2,1)S(1)}, u32[]{:S(2)}, u32[]{:S(2)}) collective-permute-start(bf16[32,1792]{1,0:T(8,128)(2,1)S(1)} %fusion.4), channel_id=1, source_target_pairs={{0,1},{1,0},{2,3},{3,2},{4,5},{5,4},{6,7},{7,6},{8,9},{9,8},{10,11... | collective-permute-start | bytes 344072 | tf_op jit(solution)/shard_map/ppermute | solution.py:41
  29.9 0.7 %collective-permute-start.12 = (bf16[1,1,32,1792]{3,2,1,0:T(8,128)(2,1)S(1)}, bf16[1,1,32,1792]{3,2,1,0:T(8,128)(2,1)S(1)}, u32[]{:S(2)}, u32[]{:S(2)}) collective-permute-start(bf16[1,1,32,1792]{3,2,1,0:T(8,128)(2,1)S(1)} %add_convert_fusion.5), channel_id=1, source_target_pairs={{0,8},{4,12},{8,0},{12,4},{1,9},{5,13},{9,1},{13,5},{2,10},{6,14},... | collective-permute-start | bytes 344072 | tf_op jit(solution)/shard_map/ppermute | solution.py:41
  30.6 2.7 %collective-permute-done.13 = bf16[1,1,32,1792]{3,2,1,0:T(8,128)(2,1)S(1)} collective-permute-done((bf16[1,1,32,1792]{3,2,1,0:T(8,128)(2,1)S(1)}, bf16[1,1,32,1792]{3,2,1,0:T(8,128)(2,1)S(1)}, u32[]{:S(2)}, u32[]{:S(2)}) %collective-permute-start.13) | collective-permute-done | bytes 114720 | tf_op jit(solution)/shard_map/ppermute | solution.py:41
  33.4 1.6 %collective-permute-start.14 = (bf16[32,1792]{1,0:T(8,128)(2,1)S(1)}, bf16[32,1792]{1,0:T(8,128)(2,1)S(1)}, u32[]{:S(2)}, u32[]{:S(2)}) collective-permute-start(bf16[32,1792]{1,0:T(8,128)(2,1)S(1)} %fusion.3), channel_id=1, source_target_pairs={{0,1},{1,0},{2,3},{3,2},{4,5},{5,4},{6,7},{7,6},{8,9},{9,8},{10,11... | collective-permute-start | bytes 344072 | tf_op jit(solution)/shard_map/ppermute | solution.py:41
  35.0 0.1 fusion
  35.1 2.7 %collective-permute-start.17 = (bf16[32,1792]{1,0:T(8,128)(2,1)S(1)}, bf16[32,1792]{1,0:T(8,128)(2,1)S(1)}, u32[]{:S(2)}, u32[]{:S(2)}) collective-permute-start(bf16[32,1792]{1,0:T(8,128)(2,1)S(1)} %fusion), channel_id=1, source_target_pairs={{0,2},{1,3},{2,0},{3,1},{4,6},{5,7},{6,4},{7,5},{8,10},{9,11},{10,... | collective-permute-start | bytes 344072 | tf_op jit(solution)/shard_map/ppermute | solution.py:41
  37.7 1.5 %collective-permute-done.14 = bf16[32,1792]{1,0:T(8,128)(2,1)S(1)} collective-permute-done((bf16[32,1792]{1,0:T(8,128)(2,1)S(1)}, bf16[32,1792]{1,0:T(8,128)(2,1)S(1)}, u32[]{:S(2)}, u32[]{:S(2)}) %collective-permute-start.14) | collective-permute-done | bytes 114720 | tf_op jit(solution)/shard_map/ppermute | solution.py:41
  39.2 3.2 %collective-permute-done.17 = bf16[32,1792]{1,0:T(8,128)(2,1)S(1)} collective-permute-done((bf16[32,1792]{1,0:T(8,128)(2,1)S(1)}, bf16[32,1792]{1,0:T(8,128)(2,1)S(1)}, u32[]{:S(2)}, u32[]{:S(2)}) %collective-permute-start.17) | collective-permute-done | bytes 114720 | tf_op jit(solution)/shard_map/ppermute | solution.py:41
  42.4 0.7 %fusion.2 = bf16[32,1792]{1,0:T(8,128)(2,1)} fusion(bf16[32,1792]{1,0:T(8,128)(2,1)S(1)} %collective-permute-done.17, bf16[32,1792]{1,0:T(8,128)(2,1)S(1)} %collective-permute-done.14, bf16[1,1,32,1792]{3,2,1,0:T(8,128)(2,1)S(1)} %collective-permute-done.12, bf16[2,1,32,1792]{3,2,1,0:T(8,128)(2,1)S(1)} %collective-permute-done.8, ...), kind=kLoop, calls=%fused_computation.4 | loop fusion | flops 688128 | bytes 688128 | tf_op jit(solution)/shard_map/convert_element_type | solution.py:49
  (17 shorter events, 0.2 us)
Async XLA Ops:
  0.0 13.7 %collective-permute-start = (bf16[32,7168]{1,0:T(8,128)(2,1)}, bf16[32,7168]{1,0:T(8,128)(2,1)S(1)}, u32[]{:S(2)}, u32[]{:S(2)}) collective-permute-start(bf16[32,7168]{1,0:T(8,128)(2,1)} %bitcast.33), channel_id=1, source_target_pairs={{0,8},{4,12},{8,0},{12,4},{1,9},{5,13},{9,1},{13,5},{2,10},{6,14},... | collective-permute-start | bytes 1376264 | tf_op jit(solution)/shard_map/ppermute | solution.py:41
  3.0 10.7 %collective-permute-start.1 = (bf16[2,16,7168]{2,1,0:T(8,128)(2,1)}, bf16[2,16,7168]{2,1,0:T(8,128)(2,1)S(1)}, u32[]{:S(2)}, u32[]{:S(2)}) collective-permute-start(bf16[2,16,7168]{2,1,0:T(8,128)(2,1)} %param.25), channel_id=1, source_target_pairs={{0,4},{4,0},{8,12},{12,8},{1,5},{5,1},{9,13},{13,9},{2,6},{6,2},{1... | collective-permute-start | bytes 1376264 | tf_op jit(solution)/shard_map/ppermute | solution.py:41
  3.0 13.5 %collective-permute-start.2 = (bf16[32,7168]{1,0:T(8,128)(2,1)}, bf16[32,7168]{1,0:T(8,128)(2,1)S(1)}, u32[]{:S(2)}, u32[]{:S(2)}) collective-permute-start(bf16[32,7168]{1,0:T(8,128)(2,1)} %bitcast.34), channel_id=1, source_target_pairs={{0,4},{4,0},{8,12},{12,8},{1,5},{5,1},{9,13},{13,9},{2,6},{6,2},{1... | collective-permute-start | bytes 1376264 | tf_op jit(solution)/shard_map/ppermute | solution.py:41
  14.2 2.3 %collective-permute-start.3 = (bf16[32,7168]{1,0:T(8,128)(2,1)S(1)}, bf16[32,7168]{1,0:T(8,128)(2,1)S(1)}, u32[]{:S(2)}, u32[]{:S(2)}) collective-permute-start(bf16[32,7168]{1,0:T(8,128)(2,1)S(1)} %collective-permute-done.refs_1_.refs_2_), channel_id=1, source_target_pairs={{0,4},{4,0},{8,12},{12,8},{1,5},{5,1},{9,13},{13,9},{2,6},{6,2},{1... | collective-permute-start | bytes 1376264 | tf_op jit(solution)/shard_map/ppermute | solution.py:41
  14.2 4.9 %collective-permute-start.4 = (bf16[64,256]{1,0:T(8,128)(2,1)S(1)}, bf16[64,256]{1,0:T(8,128)(2,1)S(1)}, u32[]{:S(2)}, u32[]{:S(2)}) collective-permute-start(bf16[64,256]{1,0:T(8,128)(2,1)S(1)} %shard_map.146.refs_7_), channel_id=1, source_target_pairs={{0,4},{4,0},{8,12},{12,8},{1,5},{5,1},{9,13},{13,9},{2,6},{6,2},{1... | collective-permute-start | bytes 98312 | tf_op jit(solution)/shard_map/ppermute | solution.py:41
  14.7 4.4 %collective-permute-start.5 = (bf16[64,256]{1,0:T(8,128)(2,1)S(1)}, bf16[64,256]{1,0:T(8,128)(2,1)S(1)}, u32[]{:S(2)}, u32[]{:S(2)}) collective-permute-start(bf16[64,256]{1,0:T(8,128)(2,1)S(1)} %shard_map.146.refs_7_), channel_id=1, source_target_pairs={{0,8},{4,12},{8,0},{12,4},{1,9},{5,13},{9,1},{13,5},{2,10},{6,14},... | collective-permute-start | bytes 98312 | tf_op jit(solution)/shard_map/ppermute | solution.py:41
  16.4 3.7 %collective-permute-start.6 = (bf16[64,256]{1,0:T(8,128)(2,1)S(1)}, bf16[64,256]{1,0:T(8,128)(2,1)S(1)}, u32[]{:S(2)}, u32[]{:S(2)}) collective-permute-start(bf16[64,256]{1,0:T(8,128)(2,1)S(1)} %shard_map.146.refs_7_), channel_id=1, source_target_pairs={{0,12},{4,8},{8,4},{12,0},{1,13},{5,9},{9,5},{13,1},{2,14},{6,10},... | collective-permute-start | bytes 98312 | tf_op jit(solution)/shard_map/ppermute | solution.py:41
  21.0 1.6 %collective-permute-start.7 = (bf16[2,1,32,1792]{3,2,1,0:T(8,128)(2,1)S(1)}, bf16[2,1,32,1792]{3,2,1,0:T(8,128)(2,1)S(1)}, u32[]{:S(2)}, u32[]{:S(2)}) collective-permute-start(bf16[2,1,32,1792]{3,2,1,0:T(8,128)(2,1)S(1)} %get-tuple-element.70), channel_id=1, source_target_pairs={{0,4},{4,0},{8,12},{12,8},{1,5},{5,1},{9,13},{13,9},{2,6},{6,2},{1... | collective-permute-start | bytes 688136 | tf_op jit(solution)/shard_map/ppermute | solution.py:41
  21.2 3.5 %collective-permute-start.10 = (bf16[2,1,32,1792]{3,2,1,0:T(8,128)(2,1)S(1)}, bf16[2,1,32,1792]{3,2,1,0:T(8,128)(2,1)S(1)}, u32[]{:S(2)}, u32[]{:S(2)}) collective-permute-start(bf16[2,1,32,1792]{3,2,1,0:T(8,128)(2,1)S(1)} %get-tuple-element.77), channel_id=1, source_target_pairs={{0,4},{4,0},{8,12},{12,8},{1,5},{5,1},{9,13},{13,9},{2,6},{6,2},{1... | collective-permute-start | bytes 688136 | tf_op jit(solution)/shard_map/ppermute | solution.py:41
  22.6 5.6 %collective-permute-start.9 = (bf16[1,1,32,1792]{3,2,1,0:T(8,128)(2,1)S(1)}, bf16[1,1,32,1792]{3,2,1,0:T(8,128)(2,1)S(1)}, u32[]{:S(2)}, u32[]{:S(2)}) collective-permute-start(bf16[1,1,32,1792]{3,2,1,0:T(8,128)(2,1)S(1)} %add_convert_fusion.9), channel_id=1, source_target_pairs={{0,8},{4,12},{8,0},{12,4},{1,9},{5,13},{9,1},{13,5},{2,10},{6,14},... | collective-permute-start | bytes 344072 | tf_op jit(solution)/shard_map/ppermute | solution.py:41
  24.2 1.9 %collective-permute-start.11 = (bf16[2,1,32,1792]{3,2,1,0:T(8,128)(2,1)S(1)}, bf16[2,1,32,1792]{3,2,1,0:T(8,128)(2,1)S(1)}, u32[]{:S(2)}, u32[]{:S(2)}) collective-permute-start(bf16[2,1,32,1792]{3,2,1,0:T(8,128)(2,1)S(1)} %get-tuple-element.80), channel_id=1, source_target_pairs={{0,4},{4,0},{8,12},{12,8},{1,5},{5,1},{9,13},{13,9},{2,6},{6,2},{1... | collective-permute-start | bytes 688136 | tf_op jit(solution)/shard_map/ppermute | solution.py:41
  24.3 2.8 %collective-permute-start.8 = (bf16[2,1,32,1792]{3,2,1,0:T(8,128)(2,1)S(1)}, bf16[2,1,32,1792]{3,2,1,0:T(8,128)(2,1)S(1)}, u32[]{:S(2)}, u32[]{:S(2)}) collective-permute-start(bf16[2,1,32,1792]{3,2,1,0:T(8,128)(2,1)S(1)} %get-tuple-element.75), channel_id=1, source_target_pairs={{0,4},{4,0},{8,12},{12,8},{1,5},{5,1},{9,13},{13,9},{2,6},{6,2},{1... | collective-permute-start | bytes 688136 | tf_op jit(solution)/shard_map/ppermute | solution.py:41
  24.8 10.2 %collective-permute-start.15 = (bf16[1,1,32,1792]{3,2,1,0:T(8,128)(2,1)S(1)}, bf16[1,1,32,1792]{3,2,1,0:T(8,128)(2,1)S(1)}, u32[]{:S(2)}, u32[]{:S(2)}) collective-permute-start(bf16[1,1,32,1792]{3,2,1,0:T(8,128)(2,1)S(1)} %add_convert_fusion.7), channel_id=1, source_target_pairs={{0,8},{4,12},{8,0},{12,4},{1,9},{5,13},{9,1},{13,5},{2,10},{6,14},... | collective-permute-start | bytes 344072 | tf_op jit(solution)/shard_map/ppermute | solution.py:41
  26.1 7.2 %collective-permute-start.13 = (bf16[1,1,32,1792]{3,2,1,0:T(8,128)(2,1)S(1)}, bf16[1,1,32,1792]{3,2,1,0:T(8,128)(2,1)S(1)}, u32[]{:S(2)}, u32[]{:S(2)}) collective-permute-start(bf16[1,1,32,1792]{3,2,1,0:T(8,128)(2,1)S(1)} %add_convert_fusion.6), channel_id=1, source_target_pairs={{0,8},{4,12},{8,0},{12,4},{1,9},{5,13},{9,1},{13,5},{2,10},{6,14},... | collective-permute-start | bytes 344072 | tf_op jit(solution)/shard_map/ppermute | solution.py:41
  28.3 6.7 %collective-permute-start.16 = (bf16[32,1792]{1,0:T(8,128)(2,1)S(1)}, bf16[32,1792]{1,0:T(8,128)(2,1)S(1)}, u32[]{:S(2)}, u32[]{:S(2)}) collective-permute-start(bf16[32,1792]{1,0:T(8,128)(2,1)S(1)} %fusion.4), channel_id=1, source_target_pairs={{0,1},{1,0},{2,3},{3,2},{4,5},{5,4},{6,7},{7,6},{8,9},{9,8},{10,11... | collective-permute-start | bytes 344072 | tf_op jit(solution)/shard_map/ppermute | solution.py:41
  29.9 7.8 %collective-permute-start.12 = (bf16[1,1,32,1792]{3,2,1,0:T(8,128)(2,1)S(1)}, bf16[1,1,32,1792]{3,2,1,0:T(8,128)(2,1)S(1)}, u32[]{:S(2)}, u32[]{:S(2)}) collective-permute-start(bf16[1,1,32,1792]{3,2,1,0:T(8,128)(2,1)S(1)} %add_convert_fusion.5), channel_id=1, source_target_pairs={{0,8},{4,12},{8,0},{12,4},{1,9},{5,13},{9,1},{13,5},{2,10},{6,14},... | collective-permute-start | bytes 344072 | tf_op jit(solution)/shard_map/ppermute | solution.py:41
  33.4 5.9 %collective-permute-start.14 = (bf16[32,1792]{1,0:T(8,128)(2,1)S(1)}, bf16[32,1792]{1,0:T(8,128)(2,1)S(1)}, u32[]{:S(2)}, u32[]{:S(2)}) collective-permute-start(bf16[32,1792]{1,0:T(8,128)(2,1)S(1)} %fusion.3), channel_id=1, source_target_pairs={{0,1},{1,0},{2,3},{3,2},{4,5},{5,4},{6,7},{7,6},{8,9},{9,8},{10,11... | collective-permute-start | bytes 344072 | tf_op jit(solution)/shard_map/ppermute | solution.py:41
  35.1 7.3 %collective-permute-start.17 = (bf16[32,1792]{1,0:T(8,128)(2,1)S(1)}, bf16[32,1792]{1,0:T(8,128)(2,1)S(1)}, u32[]{:S(2)}, u32[]{:S(2)}) collective-permute-start(bf16[32,1792]{1,0:T(8,128)(2,1)S(1)} %fusion), channel_id=1, source_target_pairs={{0,2},{1,3},{2,0},{3,1},{4,6},{5,7},{6,4},{7,5},{8,10},{9,11},{10,... | collective-permute-start | bytes 344072 | tf_op jit(solution)/shard_map/ppermute | solution.py:41

commit v11 on v10

--- a/solution.py
+++ b/solution.py
@@ -455,9 +455,9 @@
     while bit >= 1:
         order = order + [r | bit for r in order]
         bit //= 2
-    chunks = [[j] for j in range(n_tensor - 1, -1, -1)]
+    chunks = [[j] for j in range(n_tensor - 1, 1, -1)] + [[1, 0]]
     hidden = down_products(
-        gated, columns, shared_b_held, messages, down, down_own, experts, chunks[:-2], order
+        gated, columns, shared_b_held, messages, down, down_own, experts, chunks[:-1], order
     )
     hidden, held, leaving = hidden[:3], list(hidden[3::2]), list(hidden[4::2])
     bit = 1
@@ -465,16 +465,13 @@
         half = count // (2 * bit) // 2
         if bit > 1:
             leaving[1], *_ = lax.optimization_barrier((leaving[1], leaving[0]))
-        arrived = [swap(value, bit) for value in (leaving if bit == 1 else leaving[:-1])]
+        arrived = [swap(value, bit) for value in leaving]
         if bit == 1:
             ready = add(held[0][half:], arrived[0][half:])
             hidden, ready = lax.optimization_barrier((hidden, ready))
             rest = down_next(hidden, down, down_own, chunks[len(held) :], order)
             held += rest[0::2]
             arrived += [swap(value, bit) for value in rest[1::2]]
-        else:
-            arrived[0], *leaving = lax.optimization_barrier((arrived[0], *leaving))
-            arrived.append(swap(leaving[-1], bit))
         if 2 * bit < count:
             leaving = [add(h[half:], a[half:]) for h, a in zip(held, arrived)]
             held = [add(h[:half], a[:half]) for h, a in zip(held, arrived)]

time: 43.2 us -> 42 us (0.972)
  starting transfers between devices: 16.6 us -> 14.9 us
  waiting for transfers between devices: 12.5 us -> 13 us
    ppermute x18 -> x16, starting transfers between devices: 16.6 us -> 14.9 us  [swap(): return lax.ppermute(value, axis, [(i, i ^ bits) for i in range(count)])]
    ppermute x18 -> x16, waiting for transfers between devices: 12.5 us -> 13 us  [swap(): return lax.ppermute(value, axis, [(i, i ^ bits) for i in range(count)])]
  transfers between devices with their start and end apart: 18 -> 16, of which waited for: 7 -> 8; matrix products, arithmetic and copies ran while one was open for 1% -> 1% of each run, Pallas kernels for 28% -> 28%
where the time goes in v11:
time: 42 us; the launch traced here: 41.9 us
  starting transfers between devices  14.9 us (35%)
  waiting for transfers between devices  13 us (31%)
  Pallas kernels  12.9 us (31%)
  other arithmetic  1.02 us (2%)
    ppermute x16, starting transfers between devices, swap(): return lax.ppermute(value, axis, [(i, i ^ bits) for i in range(count)])  14.9 us
    ppermute x16, waiting for transfers between devices, swap(): return lax.ppermute(value, axis, [(i, i ^ bits) for i in range(count)])  13 us
    pallas_call x1, Pallas kernels, first_call(): pl.pallas_call(functools.partial(first_kernel, experts), in_specs=[HBM_SP...  8.15 us
    pallas_call x1, Pallas kernels, gate_up(): pl.pallas_call(functools.partial(gate_up_kernel, len(rows), 1024), in_spe...  2.62 us
    pallas_call x1, Pallas kernels, down_products(): pl.pallas_call(functools.partial(down_kernel, experts, chunks, order), in...  0.95 us
    convert_element_type x4, other arithmetic, total_of(): return sum((value.astype(F32) for value in values)).astype(BF16)  0.85 us
  transfers between devices with their start and end apart: 16, of which 8 were waited for; matrix products, arithmetic and copies ran while one was open for 1% of the time, Pallas kernels for 28%

profile of v11, /device:TPU:0, one launch (start us, length us, event | category | flops | bytes accessed | tf_op | source)
XLA Modules:
  0.0 41.9 jit_solution(4657530707367330292)
XLA Ops:
  0.0 3.0 %collective-permute-start = (bf16[32,7168]{1,0:T(8,128)(2,1)}, bf16[32,7168]{1,0:T(8,128)(2,1)S(1)}, u32[]{:S(2)}, u32[]{:S(2)}) collective-permute-start(bf16[32,7168]{1,0:T(8,128)(2,1)} %bitcast.33), channel_id=1, source_target_pairs={{0,8},{4,12},{8,0},{12,4},{1,9},{5,13},{9,1},{13,5},{2,10},{6,14},... | collective-permute-start | bytes 1376264 | tf_op jit(solution)/shard_map/ppermute | solution.py:41
  3.0 0.0 collective-permute-start.1
  3.0 0.5 %collective-permute-start.2 = (bf16[32,7168]{1,0:T(8,128)(2,1)}, bf16[32,7168]{1,0:T(8,128)(2,1)S(1)}, u32[]{:S(2)}, u32[]{:S(2)}) collective-permute-start(bf16[32,7168]{1,0:T(8,128)(2,1)} %bitcast.34), channel_id=1, source_target_pairs={{0,4},{4,0},{8,12},{12,8},{1,5},{5,1},{9,13},{13,9},{2,6},{6,2},{1... | collective-permute-start | bytes 1376264 | tf_op jit(solution)/shard_map/ppermute | solution.py:41
  3.5 8.2 %shard_map.145 = (bf16[32,128]{1,0:T(8,128)(2,1)S(1)}, s32[8,128]{1,0:T(8,128)S(1)}, bf16[32,7168]{1,0:T(8,128)(2,1)S(1)}, bf16[32,256]{1,0:T(8,128)(2,1)S(1)}, ...) custom-call(s32[2,2,16]{2,1,0:T(2,128)} %bitcast.38, ...), custom_call_target="tpu_custom_call" | custom-call | bytes 23904256 | tf_op jit(solution)/shard_map/pallas_call | solution.py:159
  11.6 2.1 %collective-permute-done.refs_1_.refs_2_ = bf16[32,7168]{1,0:T(8,128)(2,1)S(1)} collective-permute-done((bf16[32,7168]{1,0:T(8,128)(2,1)}, bf16[32,7168]{1,0:T(8,128)(2,1)S(1)}, u32[]{:S(2)}, u32[]{:S(2)}) %collective-permute-start) | collective-permute-done | bytes 458784 | tf_op jit(solution)/shard_map/ppermute | solution.py:41
  13.7 0.5 %shard_map.146.refs_7_ = bf16[64,256]{1,0:T(8,128)(2,1)S(1)} custom-call(bf16[32,7168]{1,0:T(8,128)(2,1)S(1)} %get-tuple-element.41.refs_0_, bf16[32,7168]{1,0:T(8,128)(2,1)S(1)} %collective-permute-done.refs_1_.refs_2_, bf16[32,7168]{1,0:T(8,128)(2,1)S(1)} %get-tuple-element.43.refs_2_, bf16[32,7168]{1,0:T(8,128)(2,1)S(1)} %bitcast.27, ...), custom_call_target="tpu_custom_call" | custom-call | flops 58720256 | bytes 917504 | tf_op jit(solution)/shard_map/pallas_call | solution.py:220
  14.2 0.0 collective-permute-start.3
  14.2 0.5 %collective-permute-start.4 = (bf16[64,256]{1,0:T(8,128)(2,1)S(1)}, bf16[64,256]{1,0:T(8,128)(2,1)S(1)}, u32[]{:S(2)}, u32[]{:S(2)}) collective-permute-start(bf16[64,256]{1,0:T(8,128)(2,1)S(1)} %shard_map.146.refs_7_), channel_id=1, source_target_pairs={{0,4},{4,0},{8,12},{12,8},{1,5},{5,1},{9,13},{13,9},{2,6},{6,2},{1... | collective-permute-start | bytes 98312 | tf_op jit(solution)/shard_map/ppermute | solution.py:41
  14.7 1.7 %collective-permute-start.5 = (bf16[64,256]{1,0:T(8,128)(2,1)S(1)}, bf16[64,256]{1,0:T(8,128)(2,1)S(1)}, u32[]{:S(2)}, u32[]{:S(2)}) collective-permute-start(bf16[64,256]{1,0:T(8,128)(2,1)S(1)} %shard_map.146.refs_7_), channel_id=1, source_target_pairs={{0,8},{4,12},{8,0},{12,4},{1,9},{5,13},{9,1},{13,5},{2,10},{6,14},... | collective-permute-start | bytes 98312 | tf_op jit(solution)/shard_map/ppermute | solution.py:41
  16.4 0.0 collective-permute-done.2.refs_1_
  16.4 2.6 %shard_map.147 = (bf16[128,64]{1,0:T(8,128)(2,1)S(1)}, f32[128,256]{1,0:T(8,128)S(1)}, f32[128,256]{1,0:T(8,128)S(1)}, f32[128,256]{1,0:T(8,128)S(1)}, f32[128,256]{1,0:T(8,128)S(1)}) custom-call(bf16[32,7168]{1,0:T(8,128)(2,1)S(1)} %get-tuple-element.41.refs_0_, bf16[32,7168]{1,0:T(8,128)(2,1)S(1)} %collective-permute-done.2.refs_1_, ...), custom_call_target="tpu_custom_call" | custom-call | flops 1879048192 | bytes 14680064 | tf_op jit(solution)/shard_map/pallas_call | solution.py:254
  19.1 1.0 %collective-permute-done.6.refs_10_ = bf16[64,256]{1,0:T(8,128)(2,1)S(1)} collective-permute-done((bf16[64,256]{1,0:T(8,128)(2,1)S(1)}, bf16[64,256]{1,0:T(8,128)(2,1)S(1)}, u32[]{:S(2)}, u32[]{:S(2)}) %collective-permute-start.6) | collective-permute-done | bytes 32800 | tf_op jit(solution)/shard_map/ppermute | solution.py:41
  20.1 0.9 %shard_map.148 = (bf16[128,256]{1,0:T(8,128)(2,1)S(1)}, bf16[128,256]{1,0:T(8,128)(2,1)S(1)}, f32[128,128]{1,0:T(8,128)S(1)}, bf16[2,1,32,1792]{3,2,1,0:T(8,128)...) custom-call(bf16[128,64]{1,0:T(8,128)(2,1)S(1)} %get-tuple-element.5, ...), custom_call_target="tpu_custom_call" | custom-call | flops 469762048 | tf_op jit(solution)/shard_map/pallas_call | solution.py:369
  21.0 0.2 collective-permute-start.7
  21.2 0.4 %collective-permute-start.11 = (bf16[2,1,32,1792]{3,2,1,0:T(8,128)(2,1)S(1)}, bf16[2,1,32,1792]{3,2,1,0:T(8,128)(2,1)S(1)}, u32[]{:S(2)}, u32[]{:S(2)}) collective-permute-start(bf16[2,1,32,1792]{3,2,1,0:T(8,128)(2,1)S(1)} %get-tuple-element.73), channel_id=1, source_target_pairs={{0,4},{4,0},{8,12},{12,8},{1,5},{5,1},{9,13},{13,9},{2,6},{6,2},{1... | collective-permute-start | bytes 688136 | tf_op jit(solution)/shard_map/ppermute | solution.py:41
  21.6 1.0 %collective-permute-done.7 = bf16[2,1,32,1792]{3,2,1,0:T(8,128)(2,1)S(1)} collective-permute-done((bf16[2,1,32,1792]{3,2,1,0:T(8,128)(2,1)S(1)}, bf16[2,1,32,1792]{3,2,1,0:T(8,128)(2,1)S(1)}, u32[]{:S(2)}, u32[]{:S(2)}) %collective-permute-start.7) | collective-permute-done | bytes 229408 | tf_op jit(solution)/shard_map/ppermute | solution.py:41
  22.6 0.8 %collective-permute-start.13 = (bf16[1,1,32,1792]{3,2,1,0:T(8,128)(2,1)S(1)}, bf16[1,1,32,1792]{3,2,1,0:T(8,128)(2,1)S(1)}, u32[]{:S(2)}, u32[]{:S(2)}) collective-permute-start(bf16[1,1,32,1792]{3,2,1,0:T(8,128)(2,1)S(1)} %add_convert_fusion.7), channel_id=1, source_target_pairs={{0,8},{4,12},{8,0},{12,4},{1,9},{5,13},{9,1},{13,5},{2,10},{6,14},... | collective-permute-start | bytes 344072 | tf_op jit(solution)/shard_map/ppermute | solution.py:41
  23.5 0.7 %shard_map.149 = (bf16[2,2,32,1792]{3,2,1,0:T(8,128)(2,1)S(1)}, bf16[2,2,32,1792]{3,2,1,0:T(8,128)(2,1)S(1)}) custom-call(bf16[128,256]{1,0:T(8,128)(2,1)S(1)} %get-tuple-element.67.hidden, bf16[128,256]{1,0:T(8,128)(2,1)S(1)} %get-tuple-element.68.hidden_shared, f32[128,128]{1,0:T(8,128)S(1)} %get-tuple-element.69.share, ...), custom_call_target="tpu_custom_call" | custom-call | flops 469762048 | tf_op jit(solution)/shard_map/pallas_call | solution.py:383
  24.2 0.1 collective-permute-start.8
  24.4 1.3 %collective-permute-start.12 = (bf16[1,1,32,1792]{3,2,1,0:T(8,128)(2,1)S(1)}, bf16[1,1,32,1792]{3,2,1,0:T(8,128)(2,1)S(1)}, u32[]{:S(2)}, u32[]{:S(2)}) collective-permute-start(bf16[1,1,32,1792]{3,2,1,0:T(8,128)(2,1)S(1)} %add_convert_fusion.4), channel_id=1, source_target_pairs={{0,8},{4,12},{8,0},{12,4},{1,9},{5,13},{9,1},{13,5},{2,10},{6,14},... | collective-permute-start | bytes 344072 | tf_op jit(solution)/shard_map/ppermute | solution.py:41
  25.6 2.7 %collective-permute-done.13 = bf16[1,1,32,1792]{3,2,1,0:T(8,128)(2,1)S(1)} collective-permute-done((bf16[1,1,32,1792]{3,2,1,0:T(8,128)(2,1)S(1)}, bf16[1,1,32,1792]{3,2,1,0:T(8,128)(2,1)S(1)}, u32[]{:S(2)}, u32[]{:S(2)}) %collective-permute-start.13) | collective-permute-done | bytes 114720 | tf_op jit(solution)/shard_map/ppermute | solution.py:41
  28.4 1.6 %collective-permute-start.14 = (bf16[32,1792]{1,0:T(8,128)(2,1)S(1)}, bf16[32,1792]{1,0:T(8,128)(2,1)S(1)}, u32[]{:S(2)}, u32[]{:S(2)}) collective-permute-start(bf16[32,1792]{1,0:T(8,128)(2,1)S(1)} %fusion.4), channel_id=1, source_target_pairs={{0,1},{1,0},{2,3},{3,2},{4,5},{5,4},{6,7},{7,6},{8,9},{9,8},{10,11... | collective-permute-start | bytes 344072 | tf_op jit(solution)/shard_map/ppermute | solution.py:41
  30.0 0.1 add_convert_fusion.1
  30.1 0.8 %collective-permute-start.9 = (bf16[1,2,32,1792]{3,2,1,0:T(8,128)(2,1)S(1)}, bf16[1,2,32,1792]{3,2,1,0:T(8,128)(2,1)S(1)}, u32[]{:S(2)}, u32[]{:S(2)}) collective-permute-start(bf16[1,2,32,1792]{3,2,1,0:T(8,128)(2,1)S(1)} %get-tuple-element.76), channel_id=1, source_target_pairs={{0,8},{4,12},{8,0},{12,4},{1,9},{5,13},{9,1},{13,5},{2,10},{6,14},... | collective-permute-start | bytes 688136 | tf_op jit(solution)/shard_map/ppermute | solution.py:41
  30.9 2.3 %collective-permute-done.14 = bf16[32,1792]{1,0:T(8,128)(2,1)S(1)} collective-permute-done((bf16[32,1792]{1,0:T(8,128)(2,1)S(1)}, bf16[32,1792]{1,0:T(8,128)(2,1)S(1)}, u32[]{:S(2)}, u32[]{:S(2)}) %collective-permute-start.14) | collective-permute-done | bytes 114720 | tf_op jit(solution)/shard_map/ppermute | solution.py:41
  33.2 0.1 fusion
  33.3 2.7 %collective-permute-start.15 = (bf16[32,1792]{1,0:T(8,128)(2,1)S(1)}, bf16[32,1792]{1,0:T(8,128)(2,1)S(1)}, u32[]{:S(2)}, u32[]{:S(2)}) collective-permute-start(bf16[32,1792]{1,0:T(8,128)(2,1)S(1)} %fusion), channel_id=1, source_target_pairs={{0,2},{1,3},{2,0},{3,1},{4,6},{5,7},{6,4},{7,5},{8,10},{9,11},{10,... | collective-permute-start | bytes 344072 | tf_op jit(solution)/shard_map/ppermute | solution.py:41
  35.9 0.4 collective-permute-done.9
  36.3 1.3 %collective-permute-start.10 = (bf16[32,1792]{1,0:T(8,128)(2,1)S(1)}, bf16[32,1792]{1,0:T(8,128)(2,1)S(1)}, u32[]{:S(2)}, u32[]{:S(2)}) collective-permute-start(bf16[32,1792]{1,0:T(8,128)(2,1)S(1)} %fusion.3), channel_id=1, source_target_pairs={{0,1},{1,0},{2,3},{3,2},{4,5},{5,4},{6,7},{7,6},{8,9},{9,8},{10,11... | collective-permute-start | bytes 344072 | tf_op jit(solution)/shard_map/ppermute | solution.py:41
  37.6 1.7 %collective-permute-done.15 = bf16[32,1792]{1,0:T(8,128)(2,1)S(1)} collective-permute-done((bf16[32,1792]{1,0:T(8,128)(2,1)S(1)}, bf16[32,1792]{1,0:T(8,128)(2,1)S(1)}, u32[]{:S(2)}, u32[]{:S(2)}) %collective-permute-start.15) | collective-permute-done | bytes 114720 | tf_op jit(solution)/shard_map/ppermute | solution.py:41
  39.3 1.9 %collective-permute-done.10 = bf16[32,1792]{1,0:T(8,128)(2,1)S(1)} collective-permute-done((bf16[32,1792]{1,0:T(8,128)(2,1)S(1)}, bf16[32,1792]{1,0:T(8,128)(2,1)S(1)}, u32[]{:S(2)}, u32[]{:S(2)}) %collective-permute-start.10) | collective-permute-done | bytes 114720 | tf_op jit(solution)/shard_map/ppermute | solution.py:41
  41.2 0.7 %fusion.2 = bf16[32,1792]{1,0:T(8,128)(2,1)} fusion(bf16[32,1792]{1,0:T(8,128)(2,1)S(1)} %collective-permute-done.15, bf16[32,1792]{1,0:T(8,128)(2,1)S(1)} %collective-permute-done.10, bf16[1,2,32,1792]{3,2,1,0:T(8,128)(2,1)S(1)} %collective-permute-done.9, bf16[1,2,32,1792]{3,2,1,0:T(8,128)(2,1)S(1)} %get-tuple-element.75), kind=kLoop, calls=%fused_computation.6 | loop fusion | flops 458752 | bytes 573440 | tf_op jit(solution)/shard_map/convert_element_type | solution.py:49
  (12 shorter events, 0.2 us)
Async XLA Ops:
  0.0 13.7 %collective-permute-start = (bf16[32,7168]{1,0:T(8,128)(2,1)}, bf16[32,7168]{1,0:T(8,128)(2,1)S(1)}, u32[]{:S(2)}, u32[]{:S(2)}) collective-permute-start(bf16[32,7168]{1,0:T(8,128)(2,1)} %bitcast.33), channel_id=1, source_target_pairs={{0,8},{4,12},{8,0},{12,4},{1,9},{5,13},{9,1},{13,5},{2,10},{6,14},... | collective-permute-start | bytes 1376264 | tf_op jit(solution)/shard_map/ppermute | solution.py:41
  3.0 10.7 %collective-permute-start.1 = (bf16[2,16,7168]{2,1,0:T(8,128)(2,1)}, bf16[2,16,7168]{2,1,0:T(8,128)(2,1)S(1)}, u32[]{:S(2)}, u32[]{:S(2)}) collective-permute-start(bf16[2,16,7168]{2,1,0:T(8,128)(2,1)} %param.25), channel_id=1, source_target_pairs={{0,4},{4,0},{8,12},{12,8},{1,5},{5,1},{9,13},{13,9},{2,6},{6,2},{1... | collective-permute-start | bytes 1376264 | tf_op jit(solution)/shard_map/ppermute | solution.py:41
  3.0 13.5 %collective-permute-start.2 = (bf16[32,7168]{1,0:T(8,128)(2,1)}, bf16[32,7168]{1,0:T(8,128)(2,1)S(1)}, u32[]{:S(2)}, u32[]{:S(2)}) collective-permute-start(bf16[32,7168]{1,0:T(8,128)(2,1)} %bitcast.34), channel_id=1, source_target_pairs={{0,4},{4,0},{8,12},{12,8},{1,5},{5,1},{9,13},{13,9},{2,6},{6,2},{1... | collective-permute-start | bytes 1376264 | tf_op jit(solution)/shard_map/ppermute | solution.py:41
  14.2 2.3 %collective-permute-start.3 = (bf16[32,7168]{1,0:T(8,128)(2,1)S(1)}, bf16[32,7168]{1,0:T(8,128)(2,1)S(1)}, u32[]{:S(2)}, u32[]{:S(2)}) collective-permute-start(bf16[32,7168]{1,0:T(8,128)(2,1)S(1)} %collective-permute-done.refs_1_.refs_2_), channel_id=1, source_target_pairs={{0,4},{4,0},{8,12},{12,8},{1,5},{5,1},{9,13},{13,9},{2,6},{6,2},{1... | collective-permute-start | bytes 1376264 | tf_op jit(solution)/shard_map/ppermute | solution.py:41
  14.2 4.9 %collective-permute-start.4 = (bf16[64,256]{1,0:T(8,128)(2,1)S(1)}, bf16[64,256]{1,0:T(8,128)(2,1)S(1)}, u32[]{:S(2)}, u32[]{:S(2)}) collective-permute-start(bf16[64,256]{1,0:T(8,128)(2,1)S(1)} %shard_map.146.refs_7_), channel_id=1, source_target_pairs={{0,4},{4,0},{8,12},{12,8},{1,5},{5,1},{9,13},{13,9},{2,6},{6,2},{1... | collective-permute-start | bytes 98312 | tf_op jit(solution)/shard_map/ppermute | solution.py:41
  14.7 4.4 %collective-permute-start.5 = (bf16[64,256]{1,0:T(8,128)(2,1)S(1)}, bf16[64,256]{1,0:T(8,128)(2,1)S(1)}, u32[]{:S(2)}, u32[]{:S(2)}) collective-permute-start(bf16[64,256]{1,0:T(8,128)(2,1)S(1)} %shard_map.146.refs_7_), channel_id=1, source_target_pairs={{0,8},{4,12},{8,0},{12,4},{1,9},{5,13},{9,1},{13,5},{2,10},{6,14},... | collective-permute-start | bytes 98312 | tf_op jit(solution)/shard_map/ppermute | solution.py:41
  16.4 3.7 %collective-permute-start.6 = (bf16[64,256]{1,0:T(8,128)(2,1)S(1)}, bf16[64,256]{1,0:T(8,128)(2,1)S(1)}, u32[]{:S(2)}, u32[]{:S(2)}) collective-permute-start(bf16[64,256]{1,0:T(8,128)(2,1)S(1)} %shard_map.146.refs_7_), channel_id=1, source_target_pairs={{0,12},{4,8},{8,4},{12,0},{1,13},{5,9},{9,5},{13,1},{2,14},{6,10},... | collective-permute-start | bytes 98312 | tf_op jit(solution)/shard_map/ppermute | solution.py:41
  21.0 1.6 %collective-permute-start.7 = (bf16[2,1,32,1792]{3,2,1,0:T(8,128)(2,1)S(1)}, bf16[2,1,32,1792]{3,2,1,0:T(8,128)(2,1)S(1)}, u32[]{:S(2)}, u32[]{:S(2)}) collective-permute-start(bf16[2,1,32,1792]{3,2,1,0:T(8,128)(2,1)S(1)} %get-tuple-element.66), channel_id=1, source_target_pairs={{0,4},{4,0},{8,12},{12,8},{1,5},{5,1},{9,13},{13,9},{2,6},{6,2},{1... | collective-permute-start | bytes 688136 | tf_op jit(solution)/shard_map/ppermute | solution.py:41
  21.2 3.1 %collective-permute-start.11 = (bf16[2,1,32,1792]{3,2,1,0:T(8,128)(2,1)S(1)}, bf16[2,1,32,1792]{3,2,1,0:T(8,128)(2,1)S(1)}, u32[]{:S(2)}, u32[]{:S(2)}) collective-permute-start(bf16[2,1,32,1792]{3,2,1,0:T(8,128)(2,1)S(1)} %get-tuple-element.73), channel_id=1, source_target_pairs={{0,4},{4,0},{8,12},{12,8},{1,5},{5,1},{9,13},{13,9},{2,6},{6,2},{1... | collective-permute-start | bytes 688136 | tf_op jit(solution)/shard_map/ppermute | solution.py:41
  22.6 5.7 %collective-permute-start.13 = (bf16[1,1,32,1792]{3,2,1,0:T(8,128)(2,1)S(1)}, bf16[1,1,32,1792]{3,2,1,0:T(8,128)(2,1)S(1)}, u32[]{:S(2)}, u32[]{:S(2)}) collective-permute-start(bf16[1,1,32,1792]{3,2,1,0:T(8,128)(2,1)S(1)} %add_convert_fusion.7), channel_id=1, source_target_pairs={{0,8},{4,12},{8,0},{12,4},{1,9},{5,13},{9,1},{13,5},{2,10},{6,14},... | collective-permute-start | bytes 344072 | tf_op jit(solution)/shard_map/ppermute | solution.py:41
  24.2 5.8 %collective-permute-start.8 = (bf16[2,2,32,1792]{3,2,1,0:T(8,128)(2,1)S(1)}, bf16[2,2,32,1792]{3,2,1,0:T(8,128)(2,1)S(1)}, u32[]{:S(2)}, u32[]{:S(2)}) collective-permute-start(bf16[2,2,32,1792]{3,2,1,0:T(8,128)(2,1)S(1)} %get-tuple-element.71), channel_id=1, source_target_pairs={{0,4},{4,0},{8,12},{12,8},{1,5},{5,1},{9,13},{13,9},{2,6},{6,2},{1... | collective-permute-start | bytes 1376264 | tf_op jit(solution)/shard_map/ppermute | solution.py:41
  24.4 6.5 %collective-permute-start.12 = (bf16[1,1,32,1792]{3,2,1,0:T(8,128)(2,1)S(1)}, bf16[1,1,32,1792]{3,2,1,0:T(8,128)(2,1)S(1)}, u32[]{:S(2)}, u32[]{:S(2)}) collective-permute-start(bf16[1,1,32,1792]{3,2,1,0:T(8,128)(2,1)S(1)} %add_convert_fusion.4), channel_id=1, source_target_pairs={{0,8},{4,12},{8,0},{12,4},{1,9},{5,13},{9,1},{13,5},{2,10},{6,14},... | collective-permute-start | bytes 344072 | tf_op jit(solution)/shard_map/ppermute | solution.py:41
  28.4 4.9 %collective-permute-start.14 = (bf16[32,1792]{1,0:T(8,128)(2,1)S(1)}, bf16[32,1792]{1,0:T(8,128)(2,1)S(1)}, u32[]{:S(2)}, u32[]{:S(2)}) collective-permute-start(bf16[32,1792]{1,0:T(8,128)(2,1)S(1)} %fusion.4), channel_id=1, source_target_pairs={{0,1},{1,0},{2,3},{3,2},{4,5},{5,4},{6,7},{7,6},{8,9},{9,8},{10,11... | collective-permute-start | bytes 344072 | tf_op jit(solution)/shard_map/ppermute | solution.py:41
  30.1 6.2 %collective-permute-start.9 = (bf16[1,2,32,1792]{3,2,1,0:T(8,128)(2,1)S(1)}, bf16[1,2,32,1792]{3,2,1,0:T(8,128)(2,1)S(1)}, u32[]{:S(2)}, u32[]{:S(2)}) collective-permute-start(bf16[1,2,32,1792]{3,2,1,0:T(8,128)(2,1)S(1)} %get-tuple-element.76), channel_id=1, source_target_pairs={{0,8},{4,12},{8,0},{12,4},{1,9},{5,13},{9,1},{13,5},{2,10},{6,14},... | collective-permute-start | bytes 688136 | tf_op jit(solution)/shard_map/ppermute | solution.py:41
  33.3 6.1 %collective-permute-start.15 = (bf16[32,1792]{1,0:T(8,128)(2,1)S(1)}, bf16[32,1792]{1,0:T(8,128)(2,1)S(1)}, u32[]{:S(2)}, u32[]{:S(2)}) collective-permute-start(bf16[32,1792]{1,0:T(8,128)(2,1)S(1)} %fusion), channel_id=1, source_target_pairs={{0,2},{1,3},{2,0},{3,1},{4,6},{5,7},{6,4},{7,5},{8,10},{9,11},{10,... | collective-permute-start | bytes 344072 | tf_op jit(solution)/shard_map/ppermute | solution.py:41
  36.3 4.9 %collective-permute-start.10 = (bf16[32,1792]{1,0:T(8,128)(2,1)S(1)}, bf16[32,1792]{1,0:T(8,128)(2,1)S(1)}, u32[]{:S(2)}, u32[]{:S(2)}) collective-permute-start(bf16[32,1792]{1,0:T(8,128)(2,1)S(1)} %fusion.3), channel_id=1, source_target_pairs={{0,1},{1,0},{2,3},{3,2},{4,5},{5,4},{6,7},{7,6},{8,9},{9,8},{10,11... | collective-permute-start | bytes 344072 | tf_op jit(solution)/shard_map/ppermute | solution.py:41

commit v12 on v11

--- a/solution.py
+++ b/solution.py
@@ -443,7 +443,8 @@
     arrived, rows_held, store_other = lax.optimization_barrier((arrived, rows_held, store_other))
     came = far_rows(arrived, rows_own)
     message = make_message([rows_held, *came], factor_store, store_other, store_b_held, meta)
-    messages = [message] + [swap(message, r) for r in range(1, count)]
+    messages = {r: swap(message, r) for r in [*range(2, count), 1]}
+    messages = [message] + [messages[r] for r in range(1, count)]
     came, message = lax.optimization_barrier((came, message))
     rows = [rows_held, swap(rows_own, 1)]
     for value in came:
@@ -455,16 +456,17 @@
     while bit >= 1:
         order = order + [r | bit for r in order]
         bit //= 2
-    chunks = [[j] for j in range(n_tensor - 1, 1, -1)] + [[1, 0]]
+    chunks = [[j] for j in range(n_tensor - 1, -1, -1)]
     hidden = down_products(
-        gated, columns, shared_b_held, messages, down, down_own, experts, chunks[:-1], order
+        gated, columns, shared_b_held, messages, down, down_own, experts, chunks[:-2], order
     )
     hidden, held, leaving = hidden[:3], list(hidden[3::2]), list(hidden[4::2])
     bit = 1
     while bit < count:
         half = count // (2 * bit) // 2
         if bit > 1:
-            leaving[1], *_ = lax.optimization_barrier((leaving[1], leaving[0]))
+            for n in range(1, len(leaving)):
+                leaving[n], *_ = lax.optimization_barrier((leaving[n], leaving[n - 1]))
         arrived = [swap(value, bit) for value in leaving]
         if bit == 1:
             ready = add(held[0][half:], arrived[0][half:])

time: 42 us -> 41.7 us (level)
  waiting for transfers between devices: 13 us -> 10.5 us
  starting transfers between devices: 14.9 us -> 17.1 us
    ppermute x16 -> x18, waiting for transfers between devices: 13 us -> 10.5 us  [swap(): return lax.ppermute(value, axis, [(i, i ^ bits) for i in range(count)])]
    ppermute x16 -> x18, starting transfers between devices: 14.9 us -> 17.1 us  [swap(): return lax.ppermute(value, axis, [(i, i ^ bits) for i in range(count)])]
  transfers between devices with their start and end apart: 16 -> 18, of which waited for: 8 -> 7; matrix products, arithmetic and copies ran while one was open for 1% -> 1% of each run, Pallas kernels for 28% -> 29%
where the time goes in v12:
time: 41.7 us; the launch traced here: 41.6 us
  starting transfers between devices  17.1 us (41%)
  Pallas kernels  12.9 us (31%)
  waiting for transfers between devices  10.5 us (25%)
  other arithmetic  1 us (2%)
    ppermute x18, starting transfers between devices, swap(): return lax.ppermute(value, axis, [(i, i ^ bits) for i in range(count)])  17.1 us
    ppermute x18, waiting for transfers between devices, swap(): return lax.ppermute(value, axis, [(i, i ^ bits) for i in range(count)])  10.5 us
    pallas_call x1, Pallas kernels, first_call(): pl.pallas_call(functools.partial(first_kernel, experts), in_specs=[HBM_SP...  8.15 us
    pallas_call x1, Pallas kernels, gate_up(): pl.pallas_call(functools.partial(gate_up_kernel, len(rows), 1024), in_spe...  2.62 us
    pallas_call x1, Pallas kernels, down_products(): pl.pallas_call(functools.partial(down_kernel, experts, chunks, order), in...  0.95 us
    convert_element_type x4, other arithmetic, total_of(): return sum((value.astype(F32) for value in values)).astype(BF16)  0.88 us
  transfers between devices with their start and end apart: 18, of which 7 were waited for; matrix products, arithmetic and copies ran while one was open for 1% of the time, Pallas kernels for 29%

profile of v12, /device:TPU:0, one launch (start us, length us, event | category | flops | bytes accessed | tf_op | source)
XLA Modules:
  0.0 41.6 jit_solution(149180017236651871)
XLA Ops:
  0.0 3.0 %collective-permute-start = (bf16[32,7168]{1,0:T(8,128)(2,1)}, bf16[32,7168]{1,0:T(8,128)(2,1)S(1)}, u32[]{:S(2)}, u32[]{:S(2)}) collective-permute-start(bf16[32,7168]{1,0:T(8,128)(2,1)} %bitcast.33), channel_id=1, source_target_pairs={{0,8},{4,12},{8,0},{12,4},{1,9},{5,13},{9,1},{13,5},{2,10},{6,14},... | collective-permute-start | bytes 1376264 | tf_op jit(solution)/shard_map/ppermute | solution.py:41
  3.0 0.5 %collective-permute-start.2 = (bf16[32,7168]{1,0:T(8,128)(2,1)}, bf16[32,7168]{1,0:T(8,128)(2,1)S(1)}, u32[]{:S(2)}, u32[]{:S(2)}) collective-permute-start(bf16[32,7168]{1,0:T(8,128)(2,1)} %bitcast.34), channel_id=1, source_target_pairs={{0,4},{4,0},{8,12},{12,8},{1,5},{5,1},{9,13},{13,9},{2,6},{6,2},{1... | collective-permute-start | bytes 1376264 | tf_op jit(solution)/shard_map/ppermute | solution.py:41
  3.5 8.2 %shard_map.145 = (bf16[32,128]{1,0:T(8,128)(2,1)S(1)}, s32[8,128]{1,0:T(8,128)S(1)}, bf16[32,7168]{1,0:T(8,128)(2,1)S(1)}, bf16[32,256]{1,0:T(8,128)(2,1)S(1)}, ...) custom-call(s32[2,2,16]{2,1,0:T(2,128)} %bitcast.38, ...), custom_call_target="tpu_custom_call" | custom-call | bytes 23904256 | tf_op jit(solution)/shard_map/pallas_call | solution.py:159
  11.6 2.1 %collective-permute-done.refs_1_.refs_2_ = bf16[32,7168]{1,0:T(8,128)(2,1)S(1)} collective-permute-done((bf16[32,7168]{1,0:T(8,128)(2,1)}, bf16[32,7168]{1,0:T(8,128)(2,1)S(1)}, u32[]{:S(2)}, u32[]{:S(2)}) %collective-permute-start) | collective-permute-done | bytes 458784 | tf_op jit(solution)/shard_map/ppermute | solution.py:41
  13.7 0.5 %shard_map.146.refs_7_ = bf16[64,256]{1,0:T(8,128)(2,1)S(1)} custom-call(bf16[32,7168]{1,0:T(8,128)(2,1)S(1)} %get-tuple-element.45.refs_0_, bf16[32,7168]{1,0:T(8,128)(2,1)S(1)} %collective-permute-done.refs_1_.refs_2_, bf16[32,7168]{1,0:T(8,128)(2,1)S(1)} %get-tuple-element.47.refs_2_, bf16[32,7168]{1,0:T(8,128)(2,1)S(1)} %bitcast.27, ...), custom_call_target="tpu_custom_call" | custom-call | flops 58720256 | bytes 917504 | tf_op jit(solution)/shard_map/pallas_call | solution.py:220
  14.2 0.0 collective-permute-start.3
  14.2 0.5 %collective-permute-start.4 = (bf16[64,256]{1,0:T(8,128)(2,1)S(1)}, bf16[64,256]{1,0:T(8,128)(2,1)S(1)}, u32[]{:S(2)}, u32[]{:S(2)}) collective-permute-start(bf16[64,256]{1,0:T(8,128)(2,1)S(1)} %shard_map.146.refs_7_), channel_id=1, source_target_pairs={{0,4},{4,0},{8,12},{12,8},{1,5},{5,1},{9,13},{13,9},{2,6},{6,2},{1... | collective-permute-start | bytes 98312 | tf_op jit(solution)/shard_map/ppermute | solution.py:41
  14.7 1.7 %collective-permute-start.5 = (bf16[64,256]{1,0:T(8,128)(2,1)S(1)}, bf16[64,256]{1,0:T(8,128)(2,1)S(1)}, u32[]{:S(2)}, u32[]{:S(2)}) collective-permute-start(bf16[64,256]{1,0:T(8,128)(2,1)S(1)} %shard_map.146.refs_7_), channel_id=1, source_target_pairs={{0,8},{4,12},{8,0},{12,4},{1,9},{5,13},{9,1},{13,5},{2,10},{6,14},... | collective-permute-start | bytes 98312 | tf_op jit(solution)/shard_map/ppermute | solution.py:41
  16.4 0.0 collective-permute-start.6
  16.4 0.0 collective-permute-done.2.refs_1_
  16.4 2.6 %shard_map.147 = (bf16[128,64]{1,0:T(8,128)(2,1)S(1)}, f32[128,256]{1,0:T(8,128)S(1)}, f32[128,256]{1,0:T(8,128)S(1)}, f32[128,256]{1,0:T(8,128)S(1)}, f32[128,256]{1,0:T(8,128)S(1)}) custom-call(bf16[32,7168]{1,0:T(8,128)(2,1)S(1)} %get-tuple-element.45.refs_0_, bf16[32,7168]{1,0:T(8,128)(2,1)S(1)} %collective-permute-done.2.refs_1_, ...), custom_call_target="tpu_custom_call" | custom-call | flops 1879048192 | bytes 14680064 | tf_op jit(solution)/shard_map/pallas_call | solution.py:254
  19.1 1.0 %collective-permute-done.6.refs_10_ = bf16[64,256]{1,0:T(8,128)(2,1)S(1)} collective-permute-done((bf16[64,256]{1,0:T(8,128)(2,1)S(1)}, bf16[64,256]{1,0:T(8,128)(2,1)S(1)}, u32[]{:S(2)}, u32[]{:S(2)}) %collective-permute-start.6) | collective-permute-done | bytes 32800 | tf_op jit(solution)/shard_map/ppermute | solution.py:41
  20.1 0.9 %shard_map.148 = (bf16[128,256]{1,0:T(8,128)(2,1)S(1)}, bf16[128,256]{1,0:T(8,128)(2,1)S(1)}, f32[128,128]{1,0:T(8,128)S(1)}, bf16[2,1,32,1792]{3,2,1,0:T(8,128)...) custom-call(bf16[128,64]{1,0:T(8,128)(2,1)S(1)} %get-tuple-element.5, ...), custom_call_target="tpu_custom_call" | custom-call | flops 469762048 | tf_op jit(solution)/shard_map/pallas_call | solution.py:369
  21.0 0.2 collective-permute-start.7
  21.2 0.4 %collective-permute-start.10 = (bf16[2,1,32,1792]{3,2,1,0:T(8,128)(2,1)S(1)}, bf16[2,1,32,1792]{3,2,1,0:T(8,128)(2,1)S(1)}, u32[]{:S(2)}, u32[]{:S(2)}) collective-permute-start(bf16[2,1,32,1792]{3,2,1,0:T(8,128)(2,1)S(1)} %get-tuple-element.79), channel_id=1, source_target_pairs={{0,4},{4,0},{8,12},{12,8},{1,5},{5,1},{9,13},{13,9},{2,6},{6,2},{1... | collective-permute-start | bytes 688136 | tf_op jit(solution)/shard_map/ppermute | solution.py:41
  21.6 1.0 %collective-permute-done.7 = bf16[2,1,32,1792]{3,2,1,0:T(8,128)(2,1)S(1)} collective-permute-done((bf16[2,1,32,1792]{3,2,1,0:T(8,128)(2,1)S(1)}, bf16[2,1,32,1792]{3,2,1,0:T(8,128)(2,1)S(1)}, u32[]{:S(2)}, u32[]{:S(2)}) %collective-permute-start.7) | collective-permute-done | bytes 229408 | tf_op jit(solution)/shard_map/ppermute | solution.py:41
  22.6 0.8 %collective-permute-start.15 = (bf16[1,1,32,1792]{3,2,1,0:T(8,128)(2,1)S(1)}, bf16[1,1,32,1792]{3,2,1,0:T(8,128)(2,1)S(1)}, u32[]{:S(2)}, u32[]{:S(2)}) collective-permute-start(bf16[1,1,32,1792]{3,2,1,0:T(8,128)(2,1)S(1)} %add_convert_fusion.9), channel_id=1, source_target_pairs={{0,8},{4,12},{8,0},{12,4},{1,9},{5,13},{9,1},{13,5},{2,10},{6,14},... | collective-permute-start | bytes 344072 | tf_op jit(solution)/shard_map/ppermute | solution.py:41
  23.5 0.7 %shard_map.149 = (bf16[2,1,32,1792]{3,2,1,0:T(8,128)(2,1)S(1)}, bf16[2,1,32,1792]{3,2,1,0:T(8,128)(2,1)S(1)}, bf16[2,1,32,1792]{3,2,1,0:T(8,128)(2,1)S(1)}, bf16[2,1,32,1792]{3,2,1,0:T(8,128)(2,1)S(1)}) custom-call(bf16[128,256]{1,0:T(8,128)(2,1)S(1)} %get-tuple-element.71.hidden, bf16[128,256]{1,0:T(8,128)(2,1)S(1)} %get-tuple-element.72.hidden_shared, ...), custom_call_target="tpu_custom_call" | custom-call | flops 469762048 | tf_op jit(solution)/shard_map/pallas_call | solution.py:383
  24.2 0.1 collective-permute-start.8
  24.3 0.4 %collective-permute-start.9 = (bf16[2,1,32,1792]{3,2,1,0:T(8,128)(2,1)S(1)}, bf16[2,1,32,1792]{3,2,1,0:T(8,128)(2,1)S(1)}, u32[]{:S(2)}, u32[]{:S(2)}) collective-permute-start(bf16[2,1,32,1792]{3,2,1,0:T(8,128)(2,1)S(1)} %get-tuple-element.77), channel_id=1, source_target_pairs={{0,4},{4,0},{8,12},{12,8},{1,5},{5,1},{9,13},{13,9},{2,6},{6,2},{1... | collective-permute-start | bytes 688136 | tf_op jit(solution)/shard_map/ppermute | solution.py:41
  24.8 1.3 %collective-permute-start.14 = (bf16[1,1,32,1792]{3,2,1,0:T(8,128)(2,1)S(1)}, bf16[1,1,32,1792]{3,2,1,0:T(8,128)(2,1)S(1)}, u32[]{:S(2)}, u32[]{:S(2)}) collective-permute-start(bf16[1,1,32,1792]{3,2,1,0:T(8,128)(2,1)S(1)} %add_convert_fusion.5), channel_id=1, source_target_pairs={{0,8},{4,12},{8,0},{12,4},{1,9},{5,13},{9,1},{13,5},{2,10},{6,14},... | collective-permute-start | bytes 344072 | tf_op jit(solution)/shard_map/ppermute | solution.py:41
  26.1 2.1 %collective-permute-done.15 = bf16[1,1,32,1792]{3,2,1,0:T(8,128)(2,1)S(1)} collective-permute-done((bf16[1,1,32,1792]{3,2,1,0:T(8,128)(2,1)S(1)}, bf16[1,1,32,1792]{3,2,1,0:T(8,128)(2,1)S(1)}, u32[]{:S(2)}, u32[]{:S(2)}) %collective-permute-start.15) | collective-permute-done | bytes 114720 | tf_op jit(solution)/shard_map/ppermute | solution.py:41
  28.3 1.6 %collective-permute-start.16 = (bf16[32,1792]{1,0:T(8,128)(2,1)S(1)}, bf16[32,1792]{1,0:T(8,128)(2,1)S(1)}, u32[]{:S(2)}, u32[]{:S(2)}) collective-permute-start(bf16[32,1792]{1,0:T(8,128)(2,1)S(1)} %fusion.4), channel_id=1, source_target_pairs={{0,1},{1,0},{2,3},{3,2},{4,5},{5,4},{6,7},{7,6},{8,9},{9,8},{10,11... | collective-permute-start | bytes 344072 | tf_op jit(solution)/shard_map/ppermute | solution.py:41
  30.0 0.8 %collective-permute-start.12 = (bf16[1,1,32,1792]{3,2,1,0:T(8,128)(2,1)S(1)}, bf16[1,1,32,1792]{3,2,1,0:T(8,128)(2,1)S(1)}, u32[]{:S(2)}, u32[]{:S(2)}) collective-permute-start(bf16[1,1,32,1792]{3,2,1,0:T(8,128)(2,1)S(1)} %add_convert_fusion.6), channel_id=1, source_target_pairs={{0,8},{4,12},{8,0},{12,4},{1,9},{5,13},{9,1},{13,5},{2,10},{6,14},... | collective-permute-start | bytes 344072 | tf_op jit(solution)/shard_map/ppermute | solution.py:41
  30.8 1.4 %collective-permute-start.11 = (bf16[1,1,32,1792]{3,2,1,0:T(8,128)(2,1)S(1)}, bf16[1,1,32,1792]{3,2,1,0:T(8,128)(2,1)S(1)}, u32[]{:S(2)}, u32[]{:S(2)}) collective-permute-start(bf16[1,1,32,1792]{3,2,1,0:T(8,128)(2,1)S(1)} %add_convert_fusion.7), channel_id=1, source_target_pairs={{0,8},{4,12},{8,0},{12,4},{1,9},{5,13},{9,1},{13,5},{2,10},{6,14},... | collective-permute-start | bytes 344072 | tf_op jit(solution)/shard_map/ppermute | solution.py:41
  32.2 1.0 %collective-permute-done.16 = bf16[32,1792]{1,0:T(8,128)(2,1)S(1)} collective-permute-done((bf16[32,1792]{1,0:T(8,128)(2,1)S(1)}, bf16[32,1792]{1,0:T(8,128)(2,1)S(1)}, u32[]{:S(2)}, u32[]{:S(2)}) %collective-permute-start.16) | collective-permute-done | bytes 114720 | tf_op jit(solution)/shard_map/ppermute | solution.py:41
  33.1 0.1 fusion
  33.2 2.7 %collective-permute-start.17 = (bf16[32,1792]{1,0:T(8,128)(2,1)S(1)}, bf16[32,1792]{1,0:T(8,128)(2,1)S(1)}, u32[]{:S(2)}, u32[]{:S(2)}) collective-permute-start(bf16[32,1792]{1,0:T(8,128)(2,1)S(1)} %fusion), channel_id=1, source_target_pairs={{0,2},{1,3},{2,0},{3,1},{4,6},{5,7},{6,4},{7,5},{8,10},{9,11},{10,... | collective-permute-start | bytes 344072 | tf_op jit(solution)/shard_map/ppermute | solution.py:41
  35.9 1.6 %collective-permute-start.13 = (bf16[32,1792]{1,0:T(8,128)(2,1)S(1)}, bf16[32,1792]{1,0:T(8,128)(2,1)S(1)}, u32[]{:S(2)}, u32[]{:S(2)}) collective-permute-start(bf16[32,1792]{1,0:T(8,128)(2,1)S(1)} %fusion.3), channel_id=1, source_target_pairs={{0,1},{1,0},{2,3},{3,2},{4,5},{5,4},{6,7},{7,6},{8,9},{9,8},{10,11... | collective-permute-start | bytes 344072 | tf_op jit(solution)/shard_map/ppermute | solution.py:41
  37.5 2.7 %collective-permute-done.17 = bf16[32,1792]{1,0:T(8,128)(2,1)S(1)} collective-permute-done((bf16[32,1792]{1,0:T(8,128)(2,1)S(1)}, bf16[32,1792]{1,0:T(8,128)(2,1)S(1)}, u32[]{:S(2)}, u32[]{:S(2)}) %collective-permute-start.17) | collective-permute-done | bytes 114720 | tf_op jit(solution)/shard_map/ppermute | solution.py:41
  40.3 0.6 %collective-permute-done.13 = bf16[32,1792]{1,0:T(8,128)(2,1)S(1)} collective-permute-done((bf16[32,1792]{1,0:T(8,128)(2,1)S(1)}, bf16[32,1792]{1,0:T(8,128)(2,1)S(1)}, u32[]{:S(2)}, u32[]{:S(2)}) %collective-permute-start.13) | collective-permute-done | bytes 114720 | tf_op jit(solution)/shard_map/ppermute | solution.py:41
  40.9 0.7 %fusion.2 = bf16[32,1792]{1,0:T(8,128)(2,1)} fusion(bf16[32,1792]{1,0:T(8,128)(2,1)S(1)} %collective-permute-done.17, bf16[32,1792]{1,0:T(8,128)(2,1)S(1)} %collective-permute-done.13, bf16[1,1,32,1792]{3,2,1,0:T(8,128)(2,1)S(1)} %collective-permute-done.11, bf16[2,1,32,1792]{3,2,1,0:T(8,128)(2,1)S(1)} %collective-permute-done.8, ...), kind=kLoop, calls=%fused_computation.4 | loop fusion | flops 688128 | bytes 688128 | tf_op jit(solution)/shard_map/convert_element_type | solution.py:49
  (17 shorter events, 0.2 us)
Async XLA Ops:
  0.0 13.7 %collective-permute-start = (bf16[32,7168]{1,0:T(8,128)(2,1)}, bf16[32,7168]{1,0:T(8,128)(2,1)S(1)}, u32[]{:S(2)}, u32[]{:S(2)}) collective-permute-start(bf16[32,7168]{1,0:T(8,128)(2,1)} %bitcast.33), channel_id=1, source_target_pairs={{0,8},{4,12},{8,0},{12,4},{1,9},{5,13},{9,1},{13,5},{2,10},{6,14},... | collective-permute-start | bytes 1376264 | tf_op jit(solution)/shard_map/ppermute | solution.py:41
  3.0 10.7 %collective-permute-start.1 = (bf16[2,16,7168]{2,1,0:T(8,128)(2,1)}, bf16[2,16,7168]{2,1,0:T(8,128)(2,1)S(1)}, u32[]{:S(2)}, u32[]{:S(2)}) collective-permute-start(bf16[2,16,7168]{2,1,0:T(8,128)(2,1)} %param.25), channel_id=1, source_target_pairs={{0,4},{4,0},{8,12},{12,8},{1,5},{5,1},{9,13},{13,9},{2,6},{6,2},{1... | collective-permute-start | bytes 1376264 | tf_op jit(solution)/shard_map/ppermute | solution.py:41
  3.0 13.5 %collective-permute-start.2 = (bf16[32,7168]{1,0:T(8,128)(2,1)}, bf16[32,7168]{1,0:T(8,128)(2,1)S(1)}, u32[]{:S(2)}, u32[]{:S(2)}) collective-permute-start(bf16[32,7168]{1,0:T(8,128)(2,1)} %bitcast.34), channel_id=1, source_target_pairs={{0,4},{4,0},{8,12},{12,8},{1,5},{5,1},{9,13},{13,9},{2,6},{6,2},{1... | collective-permute-start | bytes 1376264 | tf_op jit(solution)/shard_map/ppermute | solution.py:41
  14.2 2.3 %collective-permute-start.3 = (bf16[32,7168]{1,0:T(8,128)(2,1)S(1)}, bf16[32,7168]{1,0:T(8,128)(2,1)S(1)}, u32[]{:S(2)}, u32[]{:S(2)}) collective-permute-start(bf16[32,7168]{1,0:T(8,128)(2,1)S(1)} %collective-permute-done.refs_1_.refs_2_), channel_id=1, source_target_pairs={{0,4},{4,0},{8,12},{12,8},{1,5},{5,1},{9,13},{13,9},{2,6},{6,2},{1... | collective-permute-start | bytes 1376264 | tf_op jit(solution)/shard_map/ppermute | solution.py:41
  14.2 4.9 %collective-permute-start.4 = (bf16[64,256]{1,0:T(8,128)(2,1)S(1)}, bf16[64,256]{1,0:T(8,128)(2,1)S(1)}, u32[]{:S(2)}, u32[]{:S(2)}) collective-permute-start(bf16[64,256]{1,0:T(8,128)(2,1)S(1)} %shard_map.146.refs_7_), channel_id=1, source_target_pairs={{0,4},{4,0},{8,12},{12,8},{1,5},{5,1},{9,13},{13,9},{2,6},{6,2},{1... | collective-permute-start | bytes 98312 | tf_op jit(solution)/shard_map/ppermute | solution.py:41
  14.7 4.4 %collective-permute-start.5 = (bf16[64,256]{1,0:T(8,128)(2,1)S(1)}, bf16[64,256]{1,0:T(8,128)(2,1)S(1)}, u32[]{:S(2)}, u32[]{:S(2)}) collective-permute-start(bf16[64,256]{1,0:T(8,128)(2,1)S(1)} %shard_map.146.refs_7_), channel_id=1, source_target_pairs={{0,8},{4,12},{8,0},{12,4},{1,9},{5,13},{9,1},{13,5},{2,10},{6,14},... | collective-permute-start | bytes 98312 | tf_op jit(solution)/shard_map/ppermute | solution.py:41
  16.4 3.7 %collective-permute-start.6 = (bf16[64,256]{1,0:T(8,128)(2,1)S(1)}, bf16[64,256]{1,0:T(8,128)(2,1)S(1)}, u32[]{:S(2)}, u32[]{:S(2)}) collective-permute-start(bf16[64,256]{1,0:T(8,128)(2,1)S(1)} %shard_map.146.refs_7_), channel_id=1, source_target_pairs={{0,12},{4,8},{8,4},{12,0},{1,13},{5,9},{9,5},{13,1},{2,14},{6,10},... | collective-permute-start | bytes 98312 | tf_op jit(solution)/shard_map/ppermute | solution.py:41
  21.0 1.6 %collective-permute-start.7 = (bf16[2,1,32,1792]{3,2,1,0:T(8,128)(2,1)S(1)}, bf16[2,1,32,1792]{3,2,1,0:T(8,128)(2,1)S(1)}, u32[]{:S(2)}, u32[]{:S(2)}) collective-permute-start(bf16[2,1,32,1792]{3,2,1,0:T(8,128)(2,1)S(1)} %get-tuple-element.70), channel_id=1, source_target_pairs={{0,4},{4,0},{8,12},{12,8},{1,5},{5,1},{9,13},{13,9},{2,6},{6,2},{1... | collective-permute-start | bytes 688136 | tf_op jit(solution)/shard_map/ppermute | solution.py:41
  21.2 3.5 %collective-permute-start.10 = (bf16[2,1,32,1792]{3,2,1,0:T(8,128)(2,1)S(1)}, bf16[2,1,32,1792]{3,2,1,0:T(8,128)(2,1)S(1)}, u32[]{:S(2)}, u32[]{:S(2)}) collective-permute-start(bf16[2,1,32,1792]{3,2,1,0:T(8,128)(2,1)S(1)} %get-tuple-element.79), channel_id=1, source_target_pairs={{0,4},{4,0},{8,12},{12,8},{1,5},{5,1},{9,13},{13,9},{2,6},{6,2},{1... | collective-permute-start | bytes 688136 | tf_op jit(solution)/shard_map/ppermute | solution.py:41
  22.6 5.6 %collective-permute-start.15 = (bf16[1,1,32,1792]{3,2,1,0:T(8,128)(2,1)S(1)}, bf16[1,1,32,1792]{3,2,1,0:T(8,128)(2,1)S(1)}, u32[]{:S(2)}, u32[]{:S(2)}) collective-permute-start(bf16[1,1,32,1792]{3,2,1,0:T(8,128)(2,1)S(1)} %add_convert_fusion.9), channel_id=1, source_target_pairs={{0,8},{4,12},{8,0},{12,4},{1,9},{5,13},{9,1},{13,5},{2,10},{6,14},... | collective-permute-start | bytes 344072 | tf_op jit(solution)/shard_map/ppermute | solution.py:41
  24.2 6.6 %collective-permute-start.8 = (bf16[2,1,32,1792]{3,2,1,0:T(8,128)(2,1)S(1)}, bf16[2,1,32,1792]{3,2,1,0:T(8,128)(2,1)S(1)}, u32[]{:S(2)}, u32[]{:S(2)}) collective-permute-start(bf16[2,1,32,1792]{3,2,1,0:T(8,128)(2,1)S(1)} %get-tuple-element.75), channel_id=1, source_target_pairs={{0,4},{4,0},{8,12},{12,8},{1,5},{5,1},{9,13},{13,9},{2,6},{6,2},{1... | collective-permute-start | bytes 688136 | tf_op jit(solution)/shard_map/ppermute | solution.py:41
  24.3 5.6 %collective-permute-start.9 = (bf16[2,1,32,1792]{3,2,1,0:T(8,128)(2,1)S(1)}, bf16[2,1,32,1792]{3,2,1,0:T(8,128)(2,1)S(1)}, u32[]{:S(2)}, u32[]{:S(2)}) collective-permute-start(bf16[2,1,32,1792]{3,2,1,0:T(8,128)(2,1)S(1)} %get-tuple-element.77), channel_id=1, source_target_pairs={{0,4},{4,0},{8,12},{12,8},{1,5},{5,1},{9,13},{13,9},{2,6},{6,2},{1... | collective-permute-start | bytes 688136 | tf_op jit(solution)/shard_map/ppermute | solution.py:41
  24.8 7.4 %collective-permute-start.14 = (bf16[1,1,32,1792]{3,2,1,0:T(8,128)(2,1)S(1)}, bf16[1,1,32,1792]{3,2,1,0:T(8,128)(2,1)S(1)}, u32[]{:S(2)}, u32[]{:S(2)}) collective-permute-start(bf16[1,1,32,1792]{3,2,1,0:T(8,128)(2,1)S(1)} %add_convert_fusion.5), channel_id=1, source_target_pairs={{0,8},{4,12},{8,0},{12,4},{1,9},{5,13},{9,1},{13,5},{2,10},{6,14},... | collective-permute-start | bytes 344072 | tf_op jit(solution)/shard_map/ppermute | solution.py:41
  28.3 4.9 %collective-permute-start.16 = (bf16[32,1792]{1,0:T(8,128)(2,1)S(1)}, bf16[32,1792]{1,0:T(8,128)(2,1)S(1)}, u32[]{:S(2)}, u32[]{:S(2)}) collective-permute-start(bf16[32,1792]{1,0:T(8,128)(2,1)S(1)} %fusion.4), channel_id=1, source_target_pairs={{0,1},{1,0},{2,3},{3,2},{4,5},{5,4},{6,7},{7,6},{8,9},{9,8},{10,11... | collective-permute-start | bytes 344072 | tf_op jit(solution)/shard_map/ppermute | solution.py:41
  30.0 5.9 %collective-permute-start.12 = (bf16[1,1,32,1792]{3,2,1,0:T(8,128)(2,1)S(1)}, bf16[1,1,32,1792]{3,2,1,0:T(8,128)(2,1)S(1)}, u32[]{:S(2)}, u32[]{:S(2)}) collective-permute-start(bf16[1,1,32,1792]{3,2,1,0:T(8,128)(2,1)S(1)} %add_convert_fusion.6), channel_id=1, source_target_pairs={{0,8},{4,12},{8,0},{12,4},{1,9},{5,13},{9,1},{13,5},{2,10},{6,14},... | collective-permute-start | bytes 344072 | tf_op jit(solution)/shard_map/ppermute | solution.py:41
  30.8 6.8 %collective-permute-start.11 = (bf16[1,1,32,1792]{3,2,1,0:T(8,128)(2,1)S(1)}, bf16[1,1,32,1792]{3,2,1,0:T(8,128)(2,1)S(1)}, u32[]{:S(2)}, u32[]{:S(2)}) collective-permute-start(bf16[1,1,32,1792]{3,2,1,0:T(8,128)(2,1)S(1)} %add_convert_fusion.7), channel_id=1, source_target_pairs={{0,8},{4,12},{8,0},{12,4},{1,9},{5,13},{9,1},{13,5},{2,10},{6,14},... | collective-permute-start | bytes 344072 | tf_op jit(solution)/shard_map/ppermute | solution.py:41
  33.2 7.1 %collective-permute-start.17 = (bf16[32,1792]{1,0:T(8,128)(2,1)S(1)}, bf16[32,1792]{1,0:T(8,128)(2,1)S(1)}, u32[]{:S(2)}, u32[]{:S(2)}) collective-permute-start(bf16[32,1792]{1,0:T(8,128)(2,1)S(1)} %fusion), channel_id=1, source_target_pairs={{0,2},{1,3},{2,0},{3,1},{4,6},{5,7},{6,4},{7,5},{8,10},{9,11},{10,... | collective-permute-start | bytes 344072 | tf_op jit(solution)/shard_map/ppermute | solution.py:41
  35.9 5.0 %collective-permute-start.13 = (bf16[32,1792]{1,0:T(8,128)(2,1)S(1)}, bf16[32,1792]{1,0:T(8,128)(2,1)S(1)}, u32[]{:S(2)}, u32[]{:S(2)}) collective-permute-start(bf16[32,1792]{1,0:T(8,128)(2,1)S(1)} %fusion.3), channel_id=1, source_target_pairs={{0,1},{1,0},{2,3},{3,2},{4,5},{5,4},{6,7},{7,6},{8,9},{9,8},{10,11... | collective-permute-start | bytes 344072 | tf_op jit(solution)/shard_map/ppermute | solution.py:41

commit v13 on v12

--- a/solution.py
+++ b/solution.py
@@ -72,7 +72,7 @@
 
 def first_kernel(
     experts, ids, values, tenants, pair_slot, rows, store_b, shared_b, factor_store, factor_shared,
-    gate_weight, up_weight, gate_shared, up_shared, down, down_shared, meta, columns, *refs
+    gate_weight, up_weight, gate_shared, up_shared, down, down_shared, pack, columns, *refs
 ):
     targets, (ids_held, values_held, tenants_held, pair_slot_held, small_sems, sems) = refs[:-6], refs[-6:]
     own, own_part = lax.axis_index("expert"), lax.axis_index("tensor")
@@ -88,7 +88,9 @@
         rows, store_b, shared_b, factor_store, factor_shared, gate_weight, up_weight, gate_shared,
         up_shared, down, down_shared,
     ]
-    staged = list(zip(sources[:5], targets[:5]))
+    shared_count, (store_count, width) = shared_b.shape[0], store_b.shape
+    staged = list(zip(sources[:5], (targets[0], pack.at[pl.ds(0, store_count), pl.ds(0, width)], *targets[1:4])))
+    targets = (None, *targets)
     piece = gate_weight.shape[0] // parts
     for source, target in zip(sources[5:9], targets[5:9]):
         for k in range(parts):
@@ -109,7 +111,7 @@
 
     steps, top, size = ids_held.shape
     tenant = column_of(tenants_held[...], size)
-    lane = lax.broadcasted_iota(jnp.int32, (size, meta.shape[1]), 1)
+    lane = lax.broadcasted_iota(jnp.int32, (size, META), 1)
     for s in range(steps):
         weight = jnp.zeros(lane.shape, F32)
         for k in range(top):
@@ -121,7 +123,10 @@
         low = weight - high - middle
         found = jnp.where(lane < experts, high, jnp.where(lane < 2 * experts, middle, low))
         found = jnp.where(lane < 3 * experts, found, tenant)
-        meta[s * size : (s + 1) * size] = found.astype(BF16)
+        start = store_count + s * size
+        pack[start : start + size, :META] = found.astype(BF16)
+        if pack.shape[1] > META:
+            pack[start : start + size, META:] = jnp.zeros((size, pack.shape[1] - META), BF16)
 
     tenant_count = pair_slot_held.shape[1]
     place = lax.broadcasted_iota(jnp.int32, pair_slot_held.shape, 0)
@@ -131,7 +136,6 @@
     own_slots = column_of(own_row, tenant_count).astype(jnp.int32)
     total = columns.shape[1]
     per_device = tenant_count // lax.axis_size("expert")
-    shared_count, store_count = shared_b.shape[0], store_b.shape[0]
     rank = shared_count // per_device
     column = lax.broadcasted_iota(jnp.int32, (1, total), 1)
     shared_tenant = own * per_device + column % shared_count // rank
@@ -151,9 +155,9 @@
     steps, _, size = ids.shape
     columns = max(lax.axis_size("expert") * staged[1].shape[0], staged[2].shape[0])
     outs = [
-        jax.ShapeDtypeStruct((steps * size, META), BF16),
+        jax.ShapeDtypeStruct((staged[1].shape[0] + steps * size, max(META, staged[1].shape[1])), BF16),
         jax.ShapeDtypeStruct((8, columns), jnp.int32),
-        *[vmem_shape(value) for value in staged],
+        *[vmem_shape(value) for n, value in enumerate(staged) if n != 1],
     ]
     inputs = [ids, values, tenants, pair_slot, *staged]
     return pl.pallas_call(
@@ -184,10 +188,11 @@
 
 
 def message_kernel(chunk, *refs):
-    half = len(refs) - 5
-    rows, (factor, factor_other, store_b, meta, out) = refs[:half], refs[half:]
+    half = len(refs) - 4
+    rows, (factor, factor_other, pack, out) = refs[:half], refs[half:]
     size, depth = rows[0].shape
-    store_count, width = store_b.shape
+    store_count, width = factor.shape[0], pack.shape[1]
+    meta = pack[store_count:, :META]
     total = 0.0
     for k in range(depth // chunk):
         part = pl.ds(k * chunk, chunk)
@@ -199,7 +204,7 @@
         )
     total = total.astype(BF16)
     wide, per, lines = message_layout(2 * half, store_count)
-    out[:store_count, :width] = store_b[...]
+    out[:store_count, :width] = pack[:store_count]
     if width < wide:
         out[:store_count, width:] = jnp.zeros((store_count, wide - width), BF16)
     for line in range(lines):
@@ -207,16 +212,16 @@
             total[n * size : (n + 1) * size] if n < half else jnp.zeros((size, 2 * store_count), BF16)
             for n in range(line * per, (line + 1) * per)
         ]
-        blocks.append(meta[...] if line == 0 else jnp.zeros(meta.shape, BF16))
+        blocks.append(meta if line == 0 else jnp.zeros(meta.shape, BF16))
         start = store_count + line * size
         out[start : start + size] = jnp.concatenate(blocks, axis=1)
 
 
-def make_message(rows, factor, factor_other, store_b, meta):
+def make_message(rows, factor, factor_other, pack):
     size, depth = rows[0].shape
-    store_count = store_b.shape[0]
+    store_count = factor.shape[0]
     wide, _, lines = message_layout(2 * len(rows), store_count)
-    inputs = [*rows, factor, factor_other, store_b, meta]
+    inputs = [*rows, factor, factor_other, pack]
     return pl.pallas_call(
         functools.partial(message_kernel, 1024),
         in_specs=[VMEM_SPEC] * len(inputs),
@@ -228,8 +233,9 @@
 
 
 def gate_up_kernel(count, chunk, *refs):
-    rows, factor, weights, inner, outs = refs[:count], refs[count], refs[count + 1 : count + 5], refs[count + 5], refs[count + 6 :]
-    depth = factor.shape[1]
+    rows, factors, weights = refs[:count], refs[count : count + 3], refs[count + 3 : count + 7]
+    inner, outs = refs[count + 7], refs[count + 8 :]
+    depth = rows[0].shape[1]
     pieces = [pl.ds(k * chunk, chunk) for k in range(depth // chunk)]
     for weight, out in zip(weights, outs):
         total = jnp.zeros(out.shape, F32)
@@ -240,22 +246,24 @@
     total = jnp.zeros(inner.shape, F32)
     for part in pieces:
         block = jnp.concatenate([ref[:, part] for ref in rows], axis=0)
+        factor = jnp.concatenate([ref[:, part] for ref in factors], axis=0)
         total += lax.dot_general(
-            block, factor[:, part], (((1,), (1,)), ((), ())), preferred_element_type=F32
+            block, factor, (((1,), (1,)), ((), ())), preferred_element_type=F32
         )
     inner[...] = total.astype(BF16)
 
 
-def gate_up(rows, factor, weights):
+def gate_up(rows, factors, weights):
     depth, width = weights[0].shape
     total = rows[0].shape[0] * len(rows)
-    inputs = [*rows, factor, *weights]
+    columns = sum(factor.shape[0] for factor in factors)
+    inputs = [*rows, *factors, *weights]
     out = jax.ShapeDtypeStruct((total, width), F32)
     return pl.pallas_call(
         functools.partial(gate_up_kernel, len(rows), 1024),
         in_specs=[VMEM_SPEC] * len(inputs),
         out_specs=[VMEM_SPEC] * (1 + len(weights)),
-        out_shape=[jax.ShapeDtypeStruct((total, factor.shape[0]), BF16)] + [out] * len(weights),
+        out_shape=[jax.ShapeDtypeStruct((total, columns), BF16)] + [out] * len(weights),
         compiler_params=params(12),
         cost_estimate=cost(2 * len(weights) * total * depth * width, 2 * len(weights) * depth * width),
     )(*[in_vmem(x) for x in inputs])
@@ -292,7 +300,7 @@
 def down_kernel(experts, chunks, order, *refs):
     count = len(order)
     half = count // 2
-    inner_shared, gate, up, gate_shared, up_shared = [ref[...] for ref in refs[:5]]
+    inner, gate, up, gate_shared, up_shared = [ref[...] for ref in refs[:5]]
     refs = refs[5:]
     columns, shared_b = refs[:2]
     messages = refs[2 : 2 + count]
@@ -306,8 +314,10 @@
     wide, per, _ = message_layout(count, store_count)
     own = columns[2:3, :1]
 
+    rows = slice(store_count, store_count + size)
     meta = jnp.concatenate(
-        [ref[store_count : store_count + size, wide - META :] for ref in messages], axis=0
+        [ref[rows, :META] for ref in messages[:2]] + [ref[rows, wide - META :] for ref in messages[2:]],
+        axis=0,
     ).astype(F32)
     lane = lax.broadcasted_iota(jnp.int32, meta.shape, 1)
     mine = (lane < 3 * experts) & (lane % experts == own)
@@ -317,8 +327,8 @@
 
     lifted = []
     for k in range(count):
-        parts = []
-        for h in range(0, count, 2):
+        parts = [inner[k * size : (k + 1) * size, shared_count:]]
+        for h in range(2, count, 2):
             sender = h + k % 2
             n = (k ^ sender) // 2
             rows = slice(store_count + n // per * size, store_count + (n // per + 1) * size)
@@ -332,7 +342,7 @@
     zero = jnp.zeros((), BF16)
     lifted = jnp.where(row_tenant == columns[1:2], lifted, zero)
     shared_tenant = columns[0:1, :shared_count]
-    lifted_shared = jnp.where(row_tenant == shared_tenant, inner_shared, zero)
+    lifted_shared = jnp.where(row_tenant == shared_tenant, inner[:, :shared_count], zero)
     factor = jnp.concatenate([ref[:store_count, :width] for ref in messages], axis=0)
     upward = up + jnp.dot(lifted, factor, preferred_element_type=F32)
     hidden = (silu(gate) * upward).astype(BF16)
@@ -438,18 +448,20 @@
             shared_down,
         ],
     )
-    meta, columns, rows_held, store_b_held, shared_b_held, factor_store, factor_shared = first[:7]
-    weights, down, down_own = first[7:11], first[11], first[12]
-    arrived, rows_held, store_other = lax.optimization_barrier((arrived, rows_held, store_other))
+    pack, columns, rows_held, shared_b_held, factor_store, factor_shared = first[:6]
+    weights, down, down_own = first[6:10], first[10], first[11]
+    pack_other = swap(pack, 1)
+    arrived, rows_held, store_other, pack_other = lax.optimization_barrier(
+        (arrived, rows_held, store_other, pack_other)
+    )
     came = far_rows(arrived, rows_own)
-    message = make_message([rows_held, *came], factor_store, store_other, store_b_held, meta)
-    messages = {r: swap(message, r) for r in [*range(2, count), 1]}
-    messages = [message] + [messages[r] for r in range(1, count)]
+    message = make_message([rows_held, *came], factor_store, store_other, pack)
+    messages = [pack, pack_other] + [swap(message, r) for r in range(2, count)]
     came, message = lax.optimization_barrier((came, message))
     rows = [rows_held, swap(rows_own, 1)]
     for value in came:
         rows += [value, swap(value, 1)]
-    gated = gate_up(rows, factor_shared, weights)
+    gated = gate_up(rows, [factor_shared, factor_store, store_other], weights)
 
     order = [0]
     bit = count // 2

time: 41.7 us -> 40.6 us (0.974)
  waiting for transfers between devices: 10.5 us -> 9.48 us
    ppermute x18, waiting for transfers between devices: 10.5 us -> 9.48 us  [swap(): return lax.ppermute(value, axis, [(i, i ^ bits) for i in range(count)])]
  transfers between devices with their start and end apart: 18 -> 18, of which waited for: 7 -> 8; matrix products, arithmetic and copies ran while one was open for 1% -> 1% of each run, Pallas kernels for 29% -> 30%
where the time goes in v13:
time: 40.6 us; the launch traced here: 40.5 us
  starting transfers between devices  16.9 us (42%)
  Pallas kernels  13 us (32%)
  waiting for transfers between devices  9.48 us (23%)
  other arithmetic  0.99 us (2%)
    ppermute x18, starting transfers between devices, swap(): return lax.ppermute(value, axis, [(i, i ^ bits) for i in range(count)])  16.9 us
    ppermute x18, waiting for transfers between devices, swap(): return lax.ppermute(value, axis, [(i, i ^ bits) for i in range(count)])  9.48 us
    pallas_call x1, Pallas kernels, first_call(): pl.pallas_call(functools.partial(first_kernel, experts), in_specs=[HBM_SP...  8.19 us
    pallas_call x1, Pallas kernels, gate_up(): pl.pallas_call(functools.partial(gate_up_kernel, len(rows), 1024), in_spe...  2.67 us
    pallas_call x1, Pallas kernels, down_products(): pl.pallas_call(functools.partial(down_kernel, experts, chunks, order), in...  1 us
    convert_element_type x4, other arithmetic, total_of(): return sum((value.astype(F32) for value in values)).astype(BF16)  0.87 us
  transfers between devices with their start and end apart: 18, of which 8 were waited for; matrix products, arithmetic and copies ran while one was open for 1% of the time, Pallas kernels for 30%

profile of v13, /device:TPU:0, one launch (start us, length us, event | category | flops | bytes accessed | tf_op | source)
XLA Modules:
  0.0 40.5 jit_solution(3547107783729738445)
XLA Ops:
  0.0 3.0 %collective-permute-start = (bf16[32,7168]{1,0:T(8,128)(2,1)}, bf16[32,7168]{1,0:T(8,128)(2,1)S(1)}, u32[]{:S(2)}, u32[]{:S(2)}) collective-permute-start(bf16[32,7168]{1,0:T(8,128)(2,1)} %bitcast.34), channel_id=1, source_target_pairs={{0,8},{4,12},{8,0},{12,4},{1,9},{5,13},{9,1},{13,5},{2,10},{6,14},... | collective-permute-start | bytes 1376264 | tf_op jit(solution)/shard_map/ppermute | solution.py:41
  3.0 8.2 %shard_map.145 = (bf16[64,256]{1,0:T(8,128)(2,1)S(1)}, s32[8,128]{1,0:T(8,128)S(1)}, bf16[32,7168]{1,0:T(8,128)(2,1)S(1)}, bf16[64,256]{1,0:T(8,128)(2,1)S(1)}, ...) custom-call(s32[2,2,16]{2,1,0:T(2,128)} %bitcast.39, ...), custom_call_target="tpu_custom_call" | custom-call | bytes 23904256 | tf_op jit(solution)/shard_map/pallas_call | solution.py:163
  11.2 0.6 %collective-permute-start.2 = (bf16[64,256]{1,0:T(8,128)(2,1)S(1)}, bf16[64,256]{1,0:T(8,128)(2,1)S(1)}, u32[]{:S(2)}, u32[]{:S(2)}) collective-permute-start(bf16[64,256]{1,0:T(8,128)(2,1)S(1)} %get-tuple-element.45.refs_4_.refs_7_), channel_id=1, source_target_pairs={{0,4},{4,0},{8,12},{12,8},{1,5},{5,1},{9,13},{13,9},{2,6},{6,2},{1... | collective-permute-start | bytes 98312 | tf_op jit(solution)/shard_map/ppermute | solution.py:41
  11.7 0.1 collective-permute-start.3
  11.8 0.8 %collective-permute-done.2.refs_8_ = bf16[64,256]{1,0:T(8,128)(2,1)S(1)} collective-permute-done((bf16[64,256]{1,0:T(8,128)(2,1)S(1)}, bf16[64,256]{1,0:T(8,128)(2,1)S(1)}, u32[]{:S(2)}, u32[]{:S(2)}) %collective-permute-start.2) | collective-permute-done | bytes 32800 | tf_op jit(solution)/shard_map/ppermute | solution.py:41
  12.6 1.1 %collective-permute-done.refs_1_.refs_2_ = bf16[32,7168]{1,0:T(8,128)(2,1)S(1)} collective-permute-done((bf16[32,7168]{1,0:T(8,128)(2,1)}, bf16[32,7168]{1,0:T(8,128)(2,1)S(1)}, u32[]{:S(2)}, u32[]{:S(2)}) %collective-permute-start) | collective-permute-done | bytes 458784 | tf_op jit(solution)/shard_map/ppermute | solution.py:41
  13.7 0.5 %shard_map.146 = bf16[64,256]{1,0:T(8,128)(2,1)S(1)} custom-call(bf16[32,7168]{1,0:T(8,128)(2,1)S(1)} %get-tuple-element.46.refs_0_, bf16[32,7168]{1,0:T(8,128)(2,1)S(1)} %collective-permute-done.refs_1_.refs_2_, bf16[32,7168]{1,0:T(8,128)(2,1)S(1)} %get-tuple-element.48.refs_2_.refs_5_, bf16[32,7168]{1,0:T(8,128)(2,1)S(1)} %bitcast.27, ...), custom_call_target="tpu_custom_call" | custom-call | flops 58720256 | bytes 917504 | tf_op jit(solution)/shard_map/pallas_call | solution.py:225
  14.2 0.0 collective-permute-start.4
  14.2 1.8 %collective-permute-start.5 = (bf16[64,256]{1,0:T(8,128)(2,1)S(1)}, bf16[64,256]{1,0:T(8,128)(2,1)S(1)}, u32[]{:S(2)}, u32[]{:S(2)}) collective-permute-start(bf16[64,256]{1,0:T(8,128)(2,1)S(1)} %shard_map.146), channel_id=1, source_target_pairs={{0,8},{4,12},{8,0},{12,4},{1,9},{5,13},{9,1},{13,5},{2,10},{6,14},... | collective-permute-start | bytes 98312 | tf_op jit(solution)/shard_map/ppermute | solution.py:41
  16.0 0.1 collective-permute-start.6
  16.1 2.7 %shard_map.147 = (bf16[128,128]{1,0:T(8,128)(2,1)S(1)}, f32[128,256]{1,0:T(8,128)S(1)}, f32[128,256]{1,0:T(8,128)S(1)}, f32[128,256]{1,0:T(8,128)S(1)}, f32[128,256]{1,0:T(8,128)S(1)}) custom-call(bf16[32,7168]{1,0:T(8,128)(2,1)S(1)} %get-tuple-element.46.refs_0_, bf16[32,7168]{1,0:T(8,128)(2,1)S(1)} %collective-permute-done.3.refs_1_, ...), custom_call_target="tpu_custom_call" | custom-call | flops 1879048192 | bytes 14680064 | tf_op jit(solution)/shard_map/pallas_call | solution.py:262
  18.8 0.6 %collective-permute-done.6.refs_10_ = bf16[64,256]{1,0:T(8,128)(2,1)S(1)} collective-permute-done((bf16[64,256]{1,0:T(8,128)(2,1)S(1)}, bf16[64,256]{1,0:T(8,128)(2,1)S(1)}, u32[]{:S(2)}, u32[]{:S(2)}) %collective-permute-start.6) | collective-permute-done | bytes 32800 | tf_op jit(solution)/shard_map/ppermute | solution.py:41
  19.3 1.0 %shard_map.148 = (bf16[128,256]{1,0:T(8,128)(2,1)S(1)}, bf16[128,256]{1,0:T(8,128)(2,1)S(1)}, f32[128,128]{1,0:T(8,128)S(1)}, bf16[2,1,32,1792]{3,2,1,0:T(8,128)...) custom-call(bf16[128,128]{1,0:T(8,128)(2,1)S(1)} %get-tuple-element., ...), custom_call_target="tpu_custom_call" | custom-call | flops 469762048 | tf_op jit(solution)/shard_map/pallas_call | solution.py:379
  20.3 0.2 collective-permute-start.7
  20.6 0.4 collective-permute-start.10
  20.9 1.0 %collective-permute-done.7 = bf16[2,1,32,1792]{3,2,1,0:T(8,128)(2,1)S(1)} collective-permute-done((bf16[2,1,32,1792]{3,2,1,0:T(8,128)(2,1)S(1)}, bf16[2,1,32,1792]{3,2,1,0:T(8,128)(2,1)S(1)}, u32[]{:S(2)}, u32[]{:S(2)}) %collective-permute-start.7) | collective-permute-done | bytes 229408 | tf_op jit(solution)/shard_map/ppermute | solution.py:41
  21.9 1.2 %collective-permute-start.15 = (bf16[1,1,32,1792]{3,2,1,0:T(8,128)(2,1)S(1)}, bf16[1,1,32,1792]{3,2,1,0:T(8,128)(2,1)S(1)}, u32[]{:S(2)}, u32[]{:S(2)}) collective-permute-start(bf16[1,1,32,1792]{3,2,1,0:T(8,128)(2,1)S(1)} %add_convert_fusion.9), channel_id=1, source_target_pairs={{0,8},{4,12},{8,0},{12,4},{1,9},{5,13},{9,1},{13,5},{2,10},{6,14},... | collective-permute-start | bytes 344072 | tf_op jit(solution)/shard_map/ppermute | solution.py:41
  23.2 0.7 %shard_map.149 = (bf16[2,1,32,1792]{3,2,1,0:T(8,128)(2,1)S(1)}, bf16[2,1,32,1792]{3,2,1,0:T(8,128)(2,1)S(1)}, bf16[2,1,32,1792]{3,2,1,0:T(8,128)(2,1)S(1)}, bf16[2,1,32,1792]{3,2,1,0:T(8,128)(2,1)S(1)}) custom-call(bf16[128,256]{1,0:T(8,128)(2,1)S(1)} %get-tuple-element.71.hidden, bf16[128,256]{1,0:T(8,128)(2,1)S(1)} %get-tuple-element.72.hidden_shared, ...), custom_call_target="tpu_custom_call" | custom-call | flops 469762048 | tf_op jit(solution)/shard_map/pallas_call | solution.py:393
  23.8 0.1 collective-permute-start.8
  24.0 0.4 %collective-permute-start.9 = (bf16[2,1,32,1792]{3,2,1,0:T(8,128)(2,1)S(1)}, bf16[2,1,32,1792]{3,2,1,0:T(8,128)(2,1)S(1)}, u32[]{:S(2)}, u32[]{:S(2)}) collective-permute-start(bf16[2,1,32,1792]{3,2,1,0:T(8,128)(2,1)S(1)} %get-tuple-element.77), channel_id=1, source_target_pairs={{0,4},{4,0},{8,12},{12,8},{1,5},{5,1},{9,13},{13,9},{2,6},{6,2},{1... | collective-permute-start | bytes 688136 | tf_op jit(solution)/shard_map/ppermute | solution.py:41
  24.4 0.9 %collective-permute-start.14 = (bf16[1,1,32,1792]{3,2,1,0:T(8,128)(2,1)S(1)}, bf16[1,1,32,1792]{3,2,1,0:T(8,128)(2,1)S(1)}, u32[]{:S(2)}, u32[]{:S(2)}) collective-permute-start(bf16[1,1,32,1792]{3,2,1,0:T(8,128)(2,1)S(1)} %add_convert_fusion.5), channel_id=1, source_target_pairs={{0,8},{4,12},{8,0},{12,4},{1,9},{5,13},{9,1},{13,5},{2,10},{6,14},... | collective-permute-start | bytes 344072 | tf_op jit(solution)/shard_map/ppermute | solution.py:41
  25.4 1.8 %collective-permute-done.15 = bf16[1,1,32,1792]{3,2,1,0:T(8,128)(2,1)S(1)} collective-permute-done((bf16[1,1,32,1792]{3,2,1,0:T(8,128)(2,1)S(1)}, bf16[1,1,32,1792]{3,2,1,0:T(8,128)(2,1)S(1)}, u32[]{:S(2)}, u32[]{:S(2)}) %collective-permute-start.15) | collective-permute-done | bytes 114720 | tf_op jit(solution)/shard_map/ppermute | solution.py:41
  27.3 1.6 %collective-permute-start.16 = (bf16[32,1792]{1,0:T(8,128)(2,1)S(1)}, bf16[32,1792]{1,0:T(8,128)(2,1)S(1)}, u32[]{:S(2)}, u32[]{:S(2)}) collective-permute-start(bf16[32,1792]{1,0:T(8,128)(2,1)S(1)} %fusion.4), channel_id=1, source_target_pairs={{0,1},{1,0},{2,3},{3,2},{4,5},{5,4},{6,7},{7,6},{8,9},{9,8},{10,11... | collective-permute-start | bytes 344072 | tf_op jit(solution)/shard_map/ppermute | solution.py:41
  28.9 1.9 %collective-permute-start.12 = (bf16[1,1,32,1792]{3,2,1,0:T(8,128)(2,1)S(1)}, bf16[1,1,32,1792]{3,2,1,0:T(8,128)(2,1)S(1)}, u32[]{:S(2)}, u32[]{:S(2)}) collective-permute-start(bf16[1,1,32,1792]{3,2,1,0:T(8,128)(2,1)S(1)} %add_convert_fusion.6), channel_id=1, source_target_pairs={{0,8},{4,12},{8,0},{12,4},{1,9},{5,13},{9,1},{13,5},{2,10},{6,14},... | collective-permute-start | bytes 344072 | tf_op jit(solution)/shard_map/ppermute | solution.py:41
  30.8 0.3 collective-permute-start.11
  31.1 1.0 %collective-permute-done.16 = bf16[32,1792]{1,0:T(8,128)(2,1)S(1)} collective-permute-done((bf16[32,1792]{1,0:T(8,128)(2,1)S(1)}, bf16[32,1792]{1,0:T(8,128)(2,1)S(1)}, u32[]{:S(2)}, u32[]{:S(2)}) %collective-permute-start.16) | collective-permute-done | bytes 114720 | tf_op jit(solution)/shard_map/ppermute | solution.py:41
  32.1 0.1 fusion
  32.2 2.6 %collective-permute-start.17 = (bf16[32,1792]{1,0:T(8,128)(2,1)S(1)}, bf16[32,1792]{1,0:T(8,128)(2,1)S(1)}, u32[]{:S(2)}, u32[]{:S(2)}) collective-permute-start(bf16[32,1792]{1,0:T(8,128)(2,1)S(1)} %fusion), channel_id=1, source_target_pairs={{0,2},{1,3},{2,0},{3,1},{4,6},{5,7},{6,4},{7,5},{8,10},{9,11},{10,... | collective-permute-start | bytes 344072 | tf_op jit(solution)/shard_map/ppermute | solution.py:41
  34.9 1.6 %collective-permute-start.13 = (bf16[32,1792]{1,0:T(8,128)(2,1)S(1)}, bf16[32,1792]{1,0:T(8,128)(2,1)S(1)}, u32[]{:S(2)}, u32[]{:S(2)}) collective-permute-start(bf16[32,1792]{1,0:T(8,128)(2,1)S(1)} %fusion.3), channel_id=1, source_target_pairs={{0,1},{1,0},{2,3},{3,2},{4,5},{5,4},{6,7},{7,6},{8,9},{9,8},{10,11... | collective-permute-start | bytes 344072 | tf_op jit(solution)/shard_map/ppermute | solution.py:41
  36.5 1.6 %collective-permute-done.17 = bf16[32,1792]{1,0:T(8,128)(2,1)S(1)} collective-permute-done((bf16[32,1792]{1,0:T(8,128)(2,1)S(1)}, bf16[32,1792]{1,0:T(8,128)(2,1)S(1)}, u32[]{:S(2)}, u32[]{:S(2)}) %collective-permute-start.17) | collective-permute-done | bytes 114720 | tf_op jit(solution)/shard_map/ppermute | solution.py:41
  38.1 1.6 %collective-permute-done.13 = bf16[32,1792]{1,0:T(8,128)(2,1)S(1)} collective-permute-done((bf16[32,1792]{1,0:T(8,128)(2,1)S(1)}, bf16[32,1792]{1,0:T(8,128)(2,1)S(1)}, u32[]{:S(2)}, u32[]{:S(2)}) %collective-permute-start.13) | collective-permute-done | bytes 114720 | tf_op jit(solution)/shard_map/ppermute | solution.py:41
  39.7 0.7 %fusion.2 = bf16[32,1792]{1,0:T(8,128)(2,1)} fusion(bf16[32,1792]{1,0:T(8,128)(2,1)S(1)} %collective-permute-done.17, bf16[32,1792]{1,0:T(8,128)(2,1)S(1)} %collective-permute-done.13, bf16[1,1,32,1792]{3,2,1,0:T(8,128)(2,1)S(1)} %collective-permute-done.11, bf16[2,1,32,1792]{3,2,1,0:T(8,128)(2,1)S(1)} %collective-permute-done.8, ...), kind=kLoop, calls=%fused_computation.4 | loop fusion | flops 688128 | bytes 688128 | tf_op jit(solution)/shard_map/convert_element_type | solution.py:49
  (19 shorter events, 0.2 us)
Async XLA Ops:
  0.0 13.7 %collective-permute-start = (bf16[32,7168]{1,0:T(8,128)(2,1)}, bf16[32,7168]{1,0:T(8,128)(2,1)S(1)}, u32[]{:S(2)}, u32[]{:S(2)}) collective-permute-start(bf16[32,7168]{1,0:T(8,128)(2,1)} %bitcast.34), channel_id=1, source_target_pairs={{0,8},{4,12},{8,0},{12,4},{1,9},{5,13},{9,1},{13,5},{2,10},{6,14},... | collective-permute-start | bytes 1376264 | tf_op jit(solution)/shard_map/ppermute | solution.py:41
  3.0 10.7 %collective-permute-start.1 = (bf16[2,16,7168]{2,1,0:T(8,128)(2,1)}, bf16[2,16,7168]{2,1,0:T(8,128)(2,1)S(1)}, u32[]{:S(2)}, u32[]{:S(2)}) collective-permute-start(bf16[2,16,7168]{2,1,0:T(8,128)(2,1)} %param.25), channel_id=1, source_target_pairs={{0,4},{4,0},{8,12},{12,8},{1,5},{5,1},{9,13},{13,9},{2,6},{6,2},{1... | collective-permute-start | bytes 1376264 | tf_op jit(solution)/shard_map/ppermute | solution.py:41
  3.0 8.8 %copy-start = (bf16[2,16,7168]{2,1,0:T(8,128)(2,1)S(1)}, bf16[2,16,7168]{2,1,0:T(8,128)(2,1)}, u32[]{:S(2)}) copy-start(bf16[2,16,7168]{2,1,0:T(8,128)(2,1)} %param.15) | copy-start | bytes 1376260
  11.2 1.4 %collective-permute-start.2 = (bf16[64,256]{1,0:T(8,128)(2,1)S(1)}, bf16[64,256]{1,0:T(8,128)(2,1)S(1)}, u32[]{:S(2)}, u32[]{:S(2)}) collective-permute-start(bf16[64,256]{1,0:T(8,128)(2,1)S(1)} %get-tuple-element.45.refs_4_.refs_7_), channel_id=1, source_target_pairs={{0,4},{4,0},{8,12},{12,8},{1,5},{5,1},{9,13},{13,9},{2,6},{6,2},{1... | collective-permute-start | bytes 98312 | tf_op jit(solution)/shard_map/ppermute | solution.py:41
  11.7 4.3 %collective-permute-start.3 = (bf16[32,7168]{1,0:T(8,128)(2,1)S(1)}, bf16[32,7168]{1,0:T(8,128)(2,1)S(1)}, u32[]{:S(2)}, u32[]{:S(2)}) collective-permute-start(bf16[32,7168]{1,0:T(8,128)(2,1)S(1)} %bitcast.36), channel_id=1, source_target_pairs={{0,4},{4,0},{8,12},{12,8},{1,5},{5,1},{9,13},{13,9},{2,6},{6,2},{1... | collective-permute-start | bytes 1376264 | tf_op jit(solution)/shard_map/ppermute | solution.py:41
  14.2 1.9 %collective-permute-start.4 = (bf16[32,7168]{1,0:T(8,128)(2,1)S(1)}, bf16[32,7168]{1,0:T(8,128)(2,1)S(1)}, u32[]{:S(2)}, u32[]{:S(2)}) collective-permute-start(bf16[32,7168]{1,0:T(8,128)(2,1)S(1)} %collective-permute-done.refs_1_.refs_2_), channel_id=1, source_target_pairs={{0,4},{4,0},{8,12},{12,8},{1,5},{5,1},{9,13},{13,9},{2,6},{6,2},{1... | collective-permute-start | bytes 1376264 | tf_op jit(solution)/shard_map/ppermute | solution.py:41
  14.2 4.6 %collective-permute-start.5 = (bf16[64,256]{1,0:T(8,128)(2,1)S(1)}, bf16[64,256]{1,0:T(8,128)(2,1)S(1)}, u32[]{:S(2)}, u32[]{:S(2)}) collective-permute-start(bf16[64,256]{1,0:T(8,128)(2,1)S(1)} %shard_map.146), channel_id=1, source_target_pairs={{0,8},{4,12},{8,0},{12,4},{1,9},{5,13},{9,1},{13,5},{2,10},{6,14},... | collective-permute-start | bytes 98312 | tf_op jit(solution)/shard_map/ppermute | solution.py:41
  16.0 3.3 %collective-permute-start.6 = (bf16[64,256]{1,0:T(8,128)(2,1)S(1)}, bf16[64,256]{1,0:T(8,128)(2,1)S(1)}, u32[]{:S(2)}, u32[]{:S(2)}) collective-permute-start(bf16[64,256]{1,0:T(8,128)(2,1)S(1)} %shard_map.146), channel_id=1, source_target_pairs={{0,12},{4,8},{8,4},{12,0},{1,13},{5,9},{9,5},{13,1},{2,14},{6,10},... | collective-permute-start | bytes 98312 | tf_op jit(solution)/shard_map/ppermute | solution.py:41
  20.3 1.6 %collective-permute-start.7 = (bf16[2,1,32,1792]{3,2,1,0:T(8,128)(2,1)S(1)}, bf16[2,1,32,1792]{3,2,1,0:T(8,128)(2,1)S(1)}, u32[]{:S(2)}, u32[]{:S(2)}) collective-permute-start(bf16[2,1,32,1792]{3,2,1,0:T(8,128)(2,1)S(1)} %get-tuple-element.70), channel_id=1, source_target_pairs={{0,4},{4,0},{8,12},{12,8},{1,5},{5,1},{9,13},{13,9},{2,6},{6,2},{1... | collective-permute-start | bytes 688136 | tf_op jit(solution)/shard_map/ppermute | solution.py:41
  20.6 3.8 %collective-permute-start.10 = (bf16[2,1,32,1792]{3,2,1,0:T(8,128)(2,1)S(1)}, bf16[2,1,32,1792]{3,2,1,0:T(8,128)(2,1)S(1)}, u32[]{:S(2)}, u32[]{:S(2)}) collective-permute-start(bf16[2,1,32,1792]{3,2,1,0:T(8,128)(2,1)S(1)} %get-tuple-element.79), channel_id=1, source_target_pairs={{0,4},{4,0},{8,12},{12,8},{1,5},{5,1},{9,13},{13,9},{2,6},{6,2},{1... | collective-permute-start | bytes 688136 | tf_op jit(solution)/shard_map/ppermute | solution.py:41
  21.9 5.3 %collective-permute-start.15 = (bf16[1,1,32,1792]{3,2,1,0:T(8,128)(2,1)S(1)}, bf16[1,1,32,1792]{3,2,1,0:T(8,128)(2,1)S(1)}, u32[]{:S(2)}, u32[]{:S(2)}) collective-permute-start(bf16[1,1,32,1792]{3,2,1,0:T(8,128)(2,1)S(1)} %add_convert_fusion.9), channel_id=1, source_target_pairs={{0,8},{4,12},{8,0},{12,4},{1,9},{5,13},{9,1},{13,5},{2,10},{6,14},... | collective-permute-start | bytes 344072 | tf_op jit(solution)/shard_map/ppermute | solution.py:41
  23.8 7.0 %collective-permute-start.8 = (bf16[2,1,32,1792]{3,2,1,0:T(8,128)(2,1)S(1)}, bf16[2,1,32,1792]{3,2,1,0:T(8,128)(2,1)S(1)}, u32[]{:S(2)}, u32[]{:S(2)}) collective-permute-start(bf16[2,1,32,1792]{3,2,1,0:T(8,128)(2,1)S(1)} %get-tuple-element.75), channel_id=1, source_target_pairs={{0,4},{4,0},{8,12},{12,8},{1,5},{5,1},{9,13},{13,9},{2,6},{6,2},{1... | collective-permute-start | bytes 688136 | tf_op jit(solution)/shard_map/ppermute | solution.py:41
  24.0 4.9 %collective-permute-start.9 = (bf16[2,1,32,1792]{3,2,1,0:T(8,128)(2,1)S(1)}, bf16[2,1,32,1792]{3,2,1,0:T(8,128)(2,1)S(1)}, u32[]{:S(2)}, u32[]{:S(2)}) collective-permute-start(bf16[2,1,32,1792]{3,2,1,0:T(8,128)(2,1)S(1)} %get-tuple-element.77), channel_id=1, source_target_pairs={{0,4},{4,0},{8,12},{12,8},{1,5},{5,1},{9,13},{13,9},{2,6},{6,2},{1... | collective-permute-start | bytes 688136 | tf_op jit(solution)/shard_map/ppermute | solution.py:41
  24.4 6.7 %collective-permute-start.14 = (bf16[1,1,32,1792]{3,2,1,0:T(8,128)(2,1)S(1)}, bf16[1,1,32,1792]{3,2,1,0:T(8,128)(2,1)S(1)}, u32[]{:S(2)}, u32[]{:S(2)}) collective-permute-start(bf16[1,1,32,1792]{3,2,1,0:T(8,128)(2,1)S(1)} %add_convert_fusion.5), channel_id=1, source_target_pairs={{0,8},{4,12},{8,0},{12,4},{1,9},{5,13},{9,1},{13,5},{2,10},{6,14},... | collective-permute-start | bytes 344072 | tf_op jit(solution)/shard_map/ppermute | solution.py:41
  27.3 4.9 %collective-permute-start.16 = (bf16[32,1792]{1,0:T(8,128)(2,1)S(1)}, bf16[32,1792]{1,0:T(8,128)(2,1)S(1)}, u32[]{:S(2)}, u32[]{:S(2)}) collective-permute-start(bf16[32,1792]{1,0:T(8,128)(2,1)S(1)} %fusion.4), channel_id=1, source_target_pairs={{0,1},{1,0},{2,3},{3,2},{4,5},{5,4},{6,7},{7,6},{8,9},{9,8},{10,11... | collective-permute-start | bytes 344072 | tf_op jit(solution)/shard_map/ppermute | solution.py:41
  28.9 5.9 %collective-permute-start.12 = (bf16[1,1,32,1792]{3,2,1,0:T(8,128)(2,1)S(1)}, bf16[1,1,32,1792]{3,2,1,0:T(8,128)(2,1)S(1)}, u32[]{:S(2)}, u32[]{:S(2)}) collective-permute-start(bf16[1,1,32,1792]{3,2,1,0:T(8,128)(2,1)S(1)} %add_convert_fusion.6), channel_id=1, source_target_pairs={{0,8},{4,12},{8,0},{12,4},{1,9},{5,13},{9,1},{13,5},{2,10},{6,14},... | collective-permute-start | bytes 344072 | tf_op jit(solution)/shard_map/ppermute | solution.py:41
  30.8 5.7 %collective-permute-start.11 = (bf16[1,1,32,1792]{3,2,1,0:T(8,128)(2,1)S(1)}, bf16[1,1,32,1792]{3,2,1,0:T(8,128)(2,1)S(1)}, u32[]{:S(2)}, u32[]{:S(2)}) collective-permute-start(bf16[1,1,32,1792]{3,2,1,0:T(8,128)(2,1)S(1)} %add_convert_fusion.7), channel_id=1, source_target_pairs={{0,8},{4,12},{8,0},{12,4},{1,9},{5,13},{9,1},{13,5},{2,10},{6,14},... | collective-permute-start | bytes 344072 | tf_op jit(solution)/shard_map/ppermute | solution.py:41
  32.2 6.0 %collective-permute-start.17 = (bf16[32,1792]{1,0:T(8,128)(2,1)S(1)}, bf16[32,1792]{1,0:T(8,128)(2,1)S(1)}, u32[]{:S(2)}, u32[]{:S(2)}) collective-permute-start(bf16[32,1792]{1,0:T(8,128)(2,1)S(1)} %fusion), channel_id=1, source_target_pairs={{0,2},{1,3},{2,0},{3,1},{4,6},{5,7},{6,4},{7,5},{8,10},{9,11},{10,... | collective-permute-start | bytes 344072 | tf_op jit(solution)/shard_map/ppermute | solution.py:41
  34.9 4.9 %collective-permute-start.13 = (bf16[32,1792]{1,0:T(8,128)(2,1)S(1)}, bf16[32,1792]{1,0:T(8,128)(2,1)S(1)}, u32[]{:S(2)}, u32[]{:S(2)}) collective-permute-start(bf16[32,1792]{1,0:T(8,128)(2,1)S(1)} %fusion.3), channel_id=1, source_target_pairs={{0,1},{1,0},{2,3},{3,2},{4,5},{5,4},{6,7},{7,6},{8,9},{9,8},{10,11... | collective-permute-start | bytes 344072 | tf_op jit(solution)/shard_map/ppermute | solution.py:41

commit v14 on v13

--- a/solution.py
+++ b/solution.py
@@ -36,9 +36,14 @@
 HBM_SPEC = pl.BlockSpec(memory_space=pltpu.HBM)
 
 
+def crossed(index):
+    return index ^ ((index >> 1) & 1)
+
+
 def swap(value, bits, axis="expert"):
     count = lax.axis_size(axis)
-    return lax.ppermute(value, axis, [(i, i ^ bits) for i in range(count)])
+    number = crossed if axis == "expert" else int
+    return lax.ppermute(value, axis, [(i, number(number(i) ^ bits)) for i in range(count)])
 
 
 def add(one, other):
@@ -139,7 +144,8 @@
     rank = shared_count // per_device
     column = lax.broadcasted_iota(jnp.int32, (1, total), 1)
     shared_tenant = own * per_device + column % shared_count // rank
-    slot = (own ^ (column // store_count)) * (store_count // rank) + column % store_count // rank
+    holder = crossed(crossed(own) ^ (column // store_count))
+    slot = holder * (store_count // rank) + column % store_count // rank
     tenant_number = lax.broadcasted_iota(jnp.int32, (tenant_count, total), 0)
     slot_tenant = jnp.max(jnp.where(own_slots == slot, tenant_number, -1), axis=0, keepdims=True)
     columns[0:1] = shared_tenant

time: 40.6 us -> 44 us (1.084)
  waiting for transfers between devices: 9.48 us -> 12.8 us
    ppermute x18, waiting for transfers between devices: 9.48 us -> 12.8 us  [swap(): lax.ppermute(value, axis, [(i, number(number(i) ^ bits)) for i in range(c...]
  transfers between devices with their start and end apart: 18 -> 18, of which waited for: 8 -> 8; matrix products, arithmetic and copies ran while one was open for 1% -> 1% of each run, Pallas kernels for 30% -> 27%
where the time goes in v14:
time: 44 us; the launch traced here: 43.9 us
  starting transfers between devices  17 us (39%)
  Pallas kernels  13 us (30%)
  waiting for transfers between devices  12.8 us (29%)
  other arithmetic  0.99 us (2%)
    ppermute x18, starting transfers between devices, swap(): lax.ppermute(value, axis, [(i, number(number(i) ^ bits)) for i in range(c...  17 us
    ppermute x18, waiting for transfers between devices, swap(): lax.ppermute(value, axis, [(i, number(number(i) ^ bits)) for i in range(c...  12.8 us
    pallas_call x1, Pallas kernels, first_call(): pl.pallas_call(functools.partial(first_kernel, experts), in_specs=[HBM_SP...  8.19 us
    pallas_call x1, Pallas kernels, gate_up(): pl.pallas_call(functools.partial(gate_up_kernel, len(rows), 1024), in_spe...  2.66 us
    pallas_call x1, Pallas kernels, down_products(): pl.pallas_call(functools.partial(down_kernel, experts, chunks, order), in...  1 us
  transfers between devices with their start and end apart: 18, of which 8 were waited for; matrix products, arithmetic and copies ran while one was open for 1% of the time, Pallas kernels for 27%

profile of v14, /device:TPU:0, one launch (start us, length us, event | category | flops | bytes accessed | tf_op | source)
XLA Modules:
  0.0 43.9 jit_solution(2125241628268807617)
XLA Ops:
  0.0 2.4 %collective-permute-start = (bf16[32,7168]{1,0:T(8,128)(2,1)}, bf16[32,7168]{1,0:T(8,128)(2,1)S(1)}, u32[]{:S(2)}, u32[]{:S(2)}) collective-permute-start(bf16[32,7168]{1,0:T(8,128)(2,1)} %bitcast.34), channel_id=1, source_target_pairs={{0,12},{4,8},{8,4},{12,0},{1,13},{5,9},{9,5},{13,1},{2,14},{6,10},... | collective-permute-start | bytes 1376264 | tf_op jit(solution)/shard_map/ppermute | solution.py:46
  2.4 0.7 %collective-permute-start.1 = (bf16[2,16,7168]{2,1,0:T(8,128)(2,1)}, bf16[2,16,7168]{2,1,0:T(8,128)(2,1)S(1)}, u32[]{:S(2)}, u32[]{:S(2)}) collective-permute-start(bf16[2,16,7168]{2,1,0:T(8,128)(2,1)} %param.25), channel_id=1, source_target_pairs={{0,4},{4,0},{8,12},{12,8},{1,5},{5,1},{9,13},{13,9},{2,6},{6,2},{1... | collective-permute-start | bytes 1376264 | tf_op jit(solution)/shard_map/ppermute | solution.py:46
  3.1 8.2 %shard_map.145 = (bf16[64,256]{1,0:T(8,128)(2,1)S(1)}, s32[8,128]{1,0:T(8,128)S(1)}, bf16[32,7168]{1,0:T(8,128)(2,1)S(1)}, bf16[64,256]{1,0:T(8,128)(2,1)S(1)}, ...) custom-call(s32[2,2,16]{2,1,0:T(2,128)} %bitcast.39, ...), custom_call_target="tpu_custom_call" | custom-call | bytes 23904256 | tf_op jit(solution)/shard_map/pallas_call | solution.py:169
  11.3 0.1 collective-permute-start.2
  11.4 0.5 %collective-permute-start.3 = (bf16[32,7168]{1,0:T(8,128)(2,1)S(1)}, bf16[32,7168]{1,0:T(8,128)(2,1)S(1)}, u32[]{:S(2)}, u32[]{:S(2)}) collective-permute-start(bf16[32,7168]{1,0:T(8,128)(2,1)S(1)} %bitcast.36), channel_id=1, source_target_pairs={{0,4},{4,0},{8,12},{12,8},{1,5},{5,1},{9,13},{13,9},{2,6},{6,2},{1... | collective-permute-start | bytes 1376264 | tf_op jit(solution)/shard_map/ppermute | solution.py:46
  11.9 0.7 %collective-permute-done.2.refs_8_ = bf16[64,256]{1,0:T(8,128)(2,1)S(1)} collective-permute-done((bf16[64,256]{1,0:T(8,128)(2,1)S(1)}, bf16[64,256]{1,0:T(8,128)(2,1)S(1)}, u32[]{:S(2)}, u32[]{:S(2)}) %collective-permute-start.2) | collective-permute-done | bytes 32800 | tf_op jit(solution)/shard_map/ppermute | solution.py:46
  12.6 1.1 %collective-permute-done.refs_1_.refs_2_ = bf16[32,7168]{1,0:T(8,128)(2,1)S(1)} collective-permute-done((bf16[32,7168]{1,0:T(8,128)(2,1)}, bf16[32,7168]{1,0:T(8,128)(2,1)S(1)}, u32[]{:S(2)}, u32[]{:S(2)}) %collective-permute-start) | collective-permute-done | bytes 458784 | tf_op jit(solution)/shard_map/ppermute | solution.py:46
  13.6 0.5 %shard_map.146 = bf16[64,256]{1,0:T(8,128)(2,1)S(1)} custom-call(bf16[32,7168]{1,0:T(8,128)(2,1)S(1)} %get-tuple-element.46.refs_0_, bf16[32,7168]{1,0:T(8,128)(2,1)S(1)} %collective-permute-done.refs_1_.refs_2_, bf16[32,7168]{1,0:T(8,128)(2,1)S(1)} %get-tuple-element.48.refs_2_.refs_5_, bf16[32,7168]{1,0:T(8,128)(2,1)S(1)} %bitcast.27, ...), custom_call_target="tpu_custom_call" | custom-call | flops 58720256 | bytes 917504 | tf_op jit(solution)/shard_map/pallas_call | solution.py:231
  14.1 0.1 collective-permute-start.4
  14.2 2.4 %collective-permute-start.5 = (bf16[64,256]{1,0:T(8,128)(2,1)S(1)}, bf16[64,256]{1,0:T(8,128)(2,1)S(1)}, u32[]{:S(2)}, u32[]{:S(2)}) collective-permute-start(bf16[64,256]{1,0:T(8,128)(2,1)S(1)} %shard_map.146), channel_id=1, source_target_pairs={{0,12},{4,8},{8,4},{12,0},{1,13},{5,9},{9,5},{13,1},{2,14},{6,10},... | collective-permute-start | bytes 98312 | tf_op jit(solution)/shard_map/ppermute | solution.py:46
  16.6 2.7 %shard_map.147 = (bf16[128,128]{1,0:T(8,128)(2,1)S(1)}, f32[128,256]{1,0:T(8,128)S(1)}, f32[128,256]{1,0:T(8,128)S(1)}, f32[128,256]{1,0:T(8,128)S(1)}, f32[128,256]{1,0:T(8,128)S(1)}) custom-call(bf16[32,7168]{1,0:T(8,128)(2,1)S(1)} %get-tuple-element.46.refs_0_, bf16[32,7168]{1,0:T(8,128)(2,1)S(1)} %collective-permute-done.3.refs_1_, ...), custom_call_target="tpu_custom_call" | custom-call | flops 1879048192 | bytes 14680064 | tf_op jit(solution)/shard_map/pallas_call | solution.py:268
  19.3 1.2 %collective-permute-done.6.refs_10_ = bf16[64,256]{1,0:T(8,128)(2,1)S(1)} collective-permute-done((bf16[64,256]{1,0:T(8,128)(2,1)S(1)}, bf16[64,256]{1,0:T(8,128)(2,1)S(1)}, u32[]{:S(2)}, u32[]{:S(2)}) %collective-permute-start.6) | collective-permute-done | bytes 32800 | tf_op jit(solution)/shard_map/ppermute | solution.py:46
  20.5 1.0 %shard_map.148 = (bf16[128,256]{1,0:T(8,128)(2,1)S(1)}, bf16[128,256]{1,0:T(8,128)(2,1)S(1)}, f32[128,128]{1,0:T(8,128)S(1)}, bf16[2,1,32,1792]{3,2,1,0:T(8,128)...) custom-call(bf16[128,128]{1,0:T(8,128)(2,1)S(1)} %get-tuple-element., ...), custom_call_target="tpu_custom_call" | custom-call | flops 469762048 | tf_op jit(solution)/shard_map/pallas_call | solution.py:385
  21.5 0.1 collective-permute-start.7
  21.6 0.5 %collective-permute-start.10 = (bf16[2,1,32,1792]{3,2,1,0:T(8,128)(2,1)S(1)}, bf16[2,1,32,1792]{3,2,1,0:T(8,128)(2,1)S(1)}, u32[]{:S(2)}, u32[]{:S(2)}) collective-permute-start(bf16[2,1,32,1792]{3,2,1,0:T(8,128)(2,1)S(1)} %get-tuple-element.79), channel_id=1, source_target_pairs={{0,4},{4,0},{8,12},{12,8},{1,5},{5,1},{9,13},{13,9},{2,6},{6,2},{1... | collective-permute-start | bytes 688136 | tf_op jit(solution)/shard_map/ppermute | solution.py:46
  22.1 1.0 %collective-permute-done.7 = bf16[2,1,32,1792]{3,2,1,0:T(8,128)(2,1)S(1)} collective-permute-done((bf16[2,1,32,1792]{3,2,1,0:T(8,128)(2,1)S(1)}, bf16[2,1,32,1792]{3,2,1,0:T(8,128)(2,1)S(1)}, u32[]{:S(2)}, u32[]{:S(2)}) %collective-permute-start.7) | collective-permute-done | bytes 229408 | tf_op jit(solution)/shard_map/ppermute | solution.py:46
  23.1 0.6 %collective-permute-start.15 = (bf16[1,1,32,1792]{3,2,1,0:T(8,128)(2,1)S(1)}, bf16[1,1,32,1792]{3,2,1,0:T(8,128)(2,1)S(1)}, u32[]{:S(2)}, u32[]{:S(2)}) collective-permute-start(bf16[1,1,32,1792]{3,2,1,0:T(8,128)(2,1)S(1)} %add_convert_fusion.9), channel_id=1, source_target_pairs={{0,12},{4,8},{8,4},{12,0},{1,13},{5,9},{9,5},{13,1},{2,14},{6,10},... | collective-permute-start | bytes 344072 | tf_op jit(solution)/shard_map/ppermute | solution.py:46
  23.7 0.7 %shard_map.149 = (bf16[2,1,32,1792]{3,2,1,0:T(8,128)(2,1)S(1)}, bf16[2,1,32,1792]{3,2,1,0:T(8,128)(2,1)S(1)}, bf16[2,1,32,1792]{3,2,1,0:T(8,128)(2,1)S(1)}, bf16[2,1,32,1792]{3,2,1,0:T(8,128)(2,1)S(1)}) custom-call(bf16[128,256]{1,0:T(8,128)(2,1)S(1)} %get-tuple-element.71.hidden, bf16[128,256]{1,0:T(8,128)(2,1)S(1)} %get-tuple-element.72.hidden_shared, ...), custom_call_target="tpu_custom_call" | custom-call | flops 469762048 | tf_op jit(solution)/shard_map/pallas_call | solution.py:399
  24.4 0.4 collective-permute-start.8
  24.8 0.1 collective-permute-start.9
  25.0 1.2 %collective-permute-start.14 = (bf16[1,1,32,1792]{3,2,1,0:T(8,128)(2,1)S(1)}, bf16[1,1,32,1792]{3,2,1,0:T(8,128)(2,1)S(1)}, u32[]{:S(2)}, u32[]{:S(2)}) collective-permute-start(bf16[1,1,32,1792]{3,2,1,0:T(8,128)(2,1)S(1)} %add_convert_fusion.5), channel_id=1, source_target_pairs={{0,12},{4,8},{8,4},{12,0},{1,13},{5,9},{9,5},{13,1},{2,14},{6,10},... | collective-permute-start | bytes 344072 | tf_op jit(solution)/shard_map/ppermute | solution.py:46
  26.3 2.0 %collective-permute-done.15 = bf16[1,1,32,1792]{3,2,1,0:T(8,128)(2,1)S(1)} collective-permute-done((bf16[1,1,32,1792]{3,2,1,0:T(8,128)(2,1)S(1)}, bf16[1,1,32,1792]{3,2,1,0:T(8,128)(2,1)S(1)}, u32[]{:S(2)}, u32[]{:S(2)}) %collective-permute-start.15) | collective-permute-done | bytes 114720 | tf_op jit(solution)/shard_map/ppermute | solution.py:46
  28.3 1.6 %collective-permute-start.16 = (bf16[32,1792]{1,0:T(8,128)(2,1)S(1)}, bf16[32,1792]{1,0:T(8,128)(2,1)S(1)}, u32[]{:S(2)}, u32[]{:S(2)}) collective-permute-start(bf16[32,1792]{1,0:T(8,128)(2,1)S(1)} %fusion.4), channel_id=1, source_target_pairs={{0,1},{1,0},{2,3},{3,2},{4,5},{5,4},{6,7},{7,6},{8,9},{9,8},{10,11... | collective-permute-start | bytes 344072 | tf_op jit(solution)/shard_map/ppermute | solution.py:46
  30.0 0.7 %collective-permute-start.12 = (bf16[1,1,32,1792]{3,2,1,0:T(8,128)(2,1)S(1)}, bf16[1,1,32,1792]{3,2,1,0:T(8,128)(2,1)S(1)}, u32[]{:S(2)}, u32[]{:S(2)}) collective-permute-start(bf16[1,1,32,1792]{3,2,1,0:T(8,128)(2,1)S(1)} %add_convert_fusion.6), channel_id=1, source_target_pairs={{0,12},{4,8},{8,4},{12,0},{1,13},{5,9},{9,5},{13,1},{2,14},{6,10},... | collective-permute-start | bytes 344072 | tf_op jit(solution)/shard_map/ppermute | solution.py:46
  30.8 1.2 %collective-permute-start.11 = (bf16[1,1,32,1792]{3,2,1,0:T(8,128)(2,1)S(1)}, bf16[1,1,32,1792]{3,2,1,0:T(8,128)(2,1)S(1)}, u32[]{:S(2)}, u32[]{:S(2)}) collective-permute-start(bf16[1,1,32,1792]{3,2,1,0:T(8,128)(2,1)S(1)} %add_convert_fusion.7), channel_id=1, source_target_pairs={{0,12},{4,8},{8,4},{12,0},{1,13},{5,9},{9,5},{13,1},{2,14},{6,10},... | collective-permute-start | bytes 344072 | tf_op jit(solution)/shard_map/ppermute | solution.py:46
  31.9 2.3 %collective-permute-done.16 = bf16[32,1792]{1,0:T(8,128)(2,1)S(1)} collective-permute-done((bf16[32,1792]{1,0:T(8,128)(2,1)S(1)}, bf16[32,1792]{1,0:T(8,128)(2,1)S(1)}, u32[]{:S(2)}, u32[]{:S(2)}) %collective-permute-start.16) | collective-permute-done | bytes 114720 | tf_op jit(solution)/shard_map/ppermute | solution.py:46
  34.2 0.1 fusion
  34.3 2.7 %collective-permute-start.17 = (bf16[32,1792]{1,0:T(8,128)(2,1)S(1)}, bf16[32,1792]{1,0:T(8,128)(2,1)S(1)}, u32[]{:S(2)}, u32[]{:S(2)}) collective-permute-start(bf16[32,1792]{1,0:T(8,128)(2,1)S(1)} %fusion), channel_id=1, source_target_pairs={{0,2},{1,3},{2,0},{3,1},{4,6},{5,7},{6,4},{7,5},{8,10},{9,11},{10,... | collective-permute-start | bytes 344072 | tf_op jit(solution)/shard_map/ppermute | solution.py:46
  37.0 1.6 %collective-permute-start.13 = (bf16[32,1792]{1,0:T(8,128)(2,1)S(1)}, bf16[32,1792]{1,0:T(8,128)(2,1)S(1)}, u32[]{:S(2)}, u32[]{:S(2)}) collective-permute-start(bf16[32,1792]{1,0:T(8,128)(2,1)S(1)} %fusion.3), channel_id=1, source_target_pairs={{0,1},{1,0},{2,3},{3,2},{4,5},{5,4},{6,7},{7,6},{8,9},{9,8},{10,11... | collective-permute-start | bytes 344072 | tf_op jit(solution)/shard_map/ppermute | solution.py:46
  38.6 4.1 %collective-permute-done.17 = bf16[32,1792]{1,0:T(8,128)(2,1)S(1)} collective-permute-done((bf16[32,1792]{1,0:T(8,128)(2,1)S(1)}, bf16[32,1792]{1,0:T(8,128)(2,1)S(1)}, u32[]{:S(2)}, u32[]{:S(2)}) %collective-permute-start.17) | collective-permute-done | bytes 114720 | tf_op jit(solution)/shard_map/ppermute | solution.py:46
  42.7 0.4 collective-permute-done.13
  43.2 0.7 %fusion.2 = bf16[32,1792]{1,0:T(8,128)(2,1)} fusion(bf16[32,1792]{1,0:T(8,128)(2,1)S(1)} %collective-permute-done.17, bf16[32,1792]{1,0:T(8,128)(2,1)S(1)} %collective-permute-done.13, bf16[1,1,32,1792]{3,2,1,0:T(8,128)(2,1)S(1)} %collective-permute-done.11, bf16[2,1,32,1792]{3,2,1,0:T(8,128)(2,1)S(1)} %collective-permute-done.8, ...), kind=kLoop, calls=%fused_computation.4 | loop fusion | flops 688128 | bytes 688128 | tf_op jit(solution)/shard_map/convert_element_type | solution.py:54
  (19 shorter events, 0.3 us)
Async XLA Ops:
  0.0 13.6 %collective-permute-start = (bf16[32,7168]{1,0:T(8,128)(2,1)}, bf16[32,7168]{1,0:T(8,128)(2,1)S(1)}, u32[]{:S(2)}, u32[]{:S(2)}) collective-permute-start(bf16[32,7168]{1,0:T(8,128)(2,1)} %bitcast.34), channel_id=1, source_target_pairs={{0,12},{4,8},{8,4},{12,0},{1,13},{5,9},{9,5},{13,1},{2,14},{6,10},... | collective-permute-start | bytes 1376264 | tf_op jit(solution)/shard_map/ppermute | solution.py:46
  2.4 11.2 %collective-permute-start.1 = (bf16[2,16,7168]{2,1,0:T(8,128)(2,1)}, bf16[2,16,7168]{2,1,0:T(8,128)(2,1)S(1)}, u32[]{:S(2)}, u32[]{:S(2)}) collective-permute-start(bf16[2,16,7168]{2,1,0:T(8,128)(2,1)} %param.25), channel_id=1, source_target_pairs={{0,4},{4,0},{8,12},{12,8},{1,5},{5,1},{9,13},{13,9},{2,6},{6,2},{1... | collective-permute-start | bytes 1376264 | tf_op jit(solution)/shard_map/ppermute | solution.py:46
  3.1 8.3 %copy-start = (bf16[2,16,7168]{2,1,0:T(8,128)(2,1)S(1)}, bf16[2,16,7168]{2,1,0:T(8,128)(2,1)}, u32[]{:S(2)}) copy-start(bf16[2,16,7168]{2,1,0:T(8,128)(2,1)} %param.15) | copy-start | bytes 1376260
  11.3 1.3 %collective-permute-start.2 = (bf16[64,256]{1,0:T(8,128)(2,1)S(1)}, bf16[64,256]{1,0:T(8,128)(2,1)S(1)}, u32[]{:S(2)}, u32[]{:S(2)}) collective-permute-start(bf16[64,256]{1,0:T(8,128)(2,1)S(1)} %get-tuple-element.45.refs_4_.refs_7_), channel_id=1, source_target_pairs={{0,4},{4,0},{8,12},{12,8},{1,5},{5,1},{9,13},{13,9},{2,6},{6,2},{1... | collective-permute-start | bytes 98312 | tf_op jit(solution)/shard_map/ppermute | solution.py:46
  11.4 5.3 %collective-permute-start.3 = (bf16[32,7168]{1,0:T(8,128)(2,1)S(1)}, bf16[32,7168]{1,0:T(8,128)(2,1)S(1)}, u32[]{:S(2)}, u32[]{:S(2)}) collective-permute-start(bf16[32,7168]{1,0:T(8,128)(2,1)S(1)} %bitcast.36), channel_id=1, source_target_pairs={{0,4},{4,0},{8,12},{12,8},{1,5},{5,1},{9,13},{13,9},{2,6},{6,2},{1... | collective-permute-start | bytes 1376264 | tf_op jit(solution)/shard_map/ppermute | solution.py:46
  14.1 2.6 %collective-permute-start.4 = (bf16[32,7168]{1,0:T(8,128)(2,1)S(1)}, bf16[32,7168]{1,0:T(8,128)(2,1)S(1)}, u32[]{:S(2)}, u32[]{:S(2)}) collective-permute-start(bf16[32,7168]{1,0:T(8,128)(2,1)S(1)} %collective-permute-done.refs_1_.refs_2_), channel_id=1, source_target_pairs={{0,4},{4,0},{8,12},{12,8},{1,5},{5,1},{9,13},{13,9},{2,6},{6,2},{1... | collective-permute-start | bytes 1376264 | tf_op jit(solution)/shard_map/ppermute | solution.py:46
  14.2 5.1 %collective-permute-start.5 = (bf16[64,256]{1,0:T(8,128)(2,1)S(1)}, bf16[64,256]{1,0:T(8,128)(2,1)S(1)}, u32[]{:S(2)}, u32[]{:S(2)}) collective-permute-start(bf16[64,256]{1,0:T(8,128)(2,1)S(1)} %shard_map.146), channel_id=1, source_target_pairs={{0,12},{4,8},{8,4},{12,0},{1,13},{5,9},{9,5},{13,1},{2,14},{6,10},... | collective-permute-start | bytes 98312 | tf_op jit(solution)/shard_map/ppermute | solution.py:46
  16.6 3.9 %collective-permute-start.6 = (bf16[64,256]{1,0:T(8,128)(2,1)S(1)}, bf16[64,256]{1,0:T(8,128)(2,1)S(1)}, u32[]{:S(2)}, u32[]{:S(2)}) collective-permute-start(bf16[64,256]{1,0:T(8,128)(2,1)S(1)} %shard_map.146), channel_id=1, source_target_pairs={{0,8},{4,12},{8,0},{12,4},{1,9},{5,13},{9,1},{13,5},{2,10},{6,14},... | collective-permute-start | bytes 98312 | tf_op jit(solution)/shard_map/ppermute | solution.py:46
  21.5 1.6 %collective-permute-start.7 = (bf16[2,1,32,1792]{3,2,1,0:T(8,128)(2,1)S(1)}, bf16[2,1,32,1792]{3,2,1,0:T(8,128)(2,1)S(1)}, u32[]{:S(2)}, u32[]{:S(2)}) collective-permute-start(bf16[2,1,32,1792]{3,2,1,0:T(8,128)(2,1)S(1)} %get-tuple-element.70), channel_id=1, source_target_pairs={{0,4},{4,0},{8,12},{12,8},{1,5},{5,1},{9,13},{13,9},{2,6},{6,2},{1... | collective-permute-start | bytes 688136 | tf_op jit(solution)/shard_map/ppermute | solution.py:46
  21.6 3.4 %collective-permute-start.10 = (bf16[2,1,32,1792]{3,2,1,0:T(8,128)(2,1)S(1)}, bf16[2,1,32,1792]{3,2,1,0:T(8,128)(2,1)S(1)}, u32[]{:S(2)}, u32[]{:S(2)}) collective-permute-start(bf16[2,1,32,1792]{3,2,1,0:T(8,128)(2,1)S(1)} %get-tuple-element.79), channel_id=1, source_target_pairs={{0,4},{4,0},{8,12},{12,8},{1,5},{5,1},{9,13},{13,9},{2,6},{6,2},{1... | collective-permute-start | bytes 688136 | tf_op jit(solution)/shard_map/ppermute | solution.py:46
  23.1 5.2 %collective-permute-start.15 = (bf16[1,1,32,1792]{3,2,1,0:T(8,128)(2,1)S(1)}, bf16[1,1,32,1792]{3,2,1,0:T(8,128)(2,1)S(1)}, u32[]{:S(2)}, u32[]{:S(2)}) collective-permute-start(bf16[1,1,32,1792]{3,2,1,0:T(8,128)(2,1)S(1)} %add_convert_fusion.9), channel_id=1, source_target_pairs={{0,12},{4,8},{8,4},{12,0},{1,13},{5,9},{9,5},{13,1},{2,14},{6,10},... | collective-permute-start | bytes 344072 | tf_op jit(solution)/shard_map/ppermute | solution.py:46
  24.4 6.3 %collective-permute-start.8 = (bf16[2,1,32,1792]{3,2,1,0:T(8,128)(2,1)S(1)}, bf16[2,1,32,1792]{3,2,1,0:T(8,128)(2,1)S(1)}, u32[]{:S(2)}, u32[]{:S(2)}) collective-permute-start(bf16[2,1,32,1792]{3,2,1,0:T(8,128)(2,1)S(1)} %get-tuple-element.75), channel_id=1, source_target_pairs={{0,4},{4,0},{8,12},{12,8},{1,5},{5,1},{9,13},{13,9},{2,6},{6,2},{1... | collective-permute-start | bytes 688136 | tf_op jit(solution)/shard_map/ppermute | solution.py:46
  24.8 5.2 %collective-permute-start.9 = (bf16[2,1,32,1792]{3,2,1,0:T(8,128)(2,1)S(1)}, bf16[2,1,32,1792]{3,2,1,0:T(8,128)(2,1)S(1)}, u32[]{:S(2)}, u32[]{:S(2)}) collective-permute-start(bf16[2,1,32,1792]{3,2,1,0:T(8,128)(2,1)S(1)} %get-tuple-element.77), channel_id=1, source_target_pairs={{0,4},{4,0},{8,12},{12,8},{1,5},{5,1},{9,13},{13,9},{2,6},{6,2},{1... | collective-permute-start | bytes 688136 | tf_op jit(solution)/shard_map/ppermute | solution.py:46
  25.0 6.9 %collective-permute-start.14 = (bf16[1,1,32,1792]{3,2,1,0:T(8,128)(2,1)S(1)}, bf16[1,1,32,1792]{3,2,1,0:T(8,128)(2,1)S(1)}, u32[]{:S(2)}, u32[]{:S(2)}) collective-permute-start(bf16[1,1,32,1792]{3,2,1,0:T(8,128)(2,1)S(1)} %add_convert_fusion.5), channel_id=1, source_target_pairs={{0,12},{4,8},{8,4},{12,0},{1,13},{5,9},{9,5},{13,1},{2,14},{6,10},... | collective-permute-start | bytes 344072 | tf_op jit(solution)/shard_map/ppermute | solution.py:46
  28.3 5.9 %collective-permute-start.16 = (bf16[32,1792]{1,0:T(8,128)(2,1)S(1)}, bf16[32,1792]{1,0:T(8,128)(2,1)S(1)}, u32[]{:S(2)}, u32[]{:S(2)}) collective-permute-start(bf16[32,1792]{1,0:T(8,128)(2,1)S(1)} %fusion.4), channel_id=1, source_target_pairs={{0,1},{1,0},{2,3},{3,2},{4,5},{5,4},{6,7},{7,6},{8,9},{9,8},{10,11... | collective-permute-start | bytes 344072 | tf_op jit(solution)/shard_map/ppermute | solution.py:46
  30.0 6.9 %collective-permute-start.12 = (bf16[1,1,32,1792]{3,2,1,0:T(8,128)(2,1)S(1)}, bf16[1,1,32,1792]{3,2,1,0:T(8,128)(2,1)S(1)}, u32[]{:S(2)}, u32[]{:S(2)}) collective-permute-start(bf16[1,1,32,1792]{3,2,1,0:T(8,128)(2,1)S(1)} %add_convert_fusion.6), channel_id=1, source_target_pairs={{0,12},{4,8},{8,4},{12,0},{1,13},{5,9},{9,5},{13,1},{2,14},{6,10},... | collective-permute-start | bytes 344072 | tf_op jit(solution)/shard_map/ppermute | solution.py:46
  30.8 7.8 %collective-permute-start.11 = (bf16[1,1,32,1792]{3,2,1,0:T(8,128)(2,1)S(1)}, bf16[1,1,32,1792]{3,2,1,0:T(8,128)(2,1)S(1)}, u32[]{:S(2)}, u32[]{:S(2)}) collective-permute-start(bf16[1,1,32,1792]{3,2,1,0:T(8,128)(2,1)S(1)} %add_convert_fusion.7), channel_id=1, source_target_pairs={{0,12},{4,8},{8,4},{12,0},{1,13},{5,9},{9,5},{13,1},{2,14},{6,10},... | collective-permute-start | bytes 344072 | tf_op jit(solution)/shard_map/ppermute | solution.py:46
  34.3 8.5 %collective-permute-start.17 = (bf16[32,1792]{1,0:T(8,128)(2,1)S(1)}, bf16[32,1792]{1,0:T(8,128)(2,1)S(1)}, u32[]{:S(2)}, u32[]{:S(2)}) collective-permute-start(bf16[32,1792]{1,0:T(8,128)(2,1)S(1)} %fusion), channel_id=1, source_target_pairs={{0,2},{1,3},{2,0},{3,1},{4,6},{5,7},{6,4},{7,5},{8,10},{9,11},{10,... | collective-permute-start | bytes 344072 | tf_op jit(solution)/shard_map/ppermute | solution.py:46
  37.0 6.2 %collective-permute-start.13 = (bf16[32,1792]{1,0:T(8,128)(2,1)S(1)}, bf16[32,1792]{1,0:T(8,128)(2,1)S(1)}, u32[]{:S(2)}, u32[]{:S(2)}) collective-permute-start(bf16[32,1792]{1,0:T(8,128)(2,1)S(1)} %fusion.3), channel_id=1, source_target_pairs={{0,1},{1,0},{2,3},{3,2},{4,5},{5,4},{6,7},{7,6},{8,9},{9,8},{10,11... | collective-permute-start | bytes 344072 | tf_op jit(solution)/shard_map/ppermute | solution.py:46

commit v15 on v13

--- a/solution.py
+++ b/solution.py
@@ -288,6 +288,8 @@
                 for at, r in enumerate(order):
                     block = routed[r * size : (r + 1) * size].astype(BF16)
                     target, row = (keep, at) if at < half else (send, at - half)
+                    if at >= half and len(outs) % 2 and n == 0:
+                        target, row = (outs[-1], 0) if at == half else (send, at - half - 1)
                     target[row, place, :, c * tile : (c + 1) * tile] = block
 
 
@@ -376,6 +378,9 @@
     outs = [jax.ShapeDtypeStruct((rows, width), BF16)] * 2
     outs += [jax.ShapeDtypeStruct((rows, 128), F32)]
     outs += down_outs(rows, down.shape[1], chunks, order)
+    apart = outs[4].shape
+    outs[4] = jax.ShapeDtypeStruct((apart[0] - 1, *apart[1:]), BF16)
+    outs.append(jax.ShapeDtypeStruct((1, *apart[1:]), BF16))
     return pl.pallas_call(
         functools.partial(down_kernel, experts, chunks, order),
         in_specs=[VMEM_SPEC] * len(whole),
@@ -472,7 +477,8 @@
     hidden = down_products(
         gated, columns, shared_b_held, messages, down, down_own, experts, chunks[:-2], order
     )
-    hidden, held, leaving = hidden[:3], list(hidden[3::2]), list(hidden[4::2])
+    hidden, held, leaving, apart = hidden[:3], hidden[3:-1:2], hidden[4:-1:2], hidden[-1]
+    held, leaving = list(held), list(leaving)
     bit = 1
     while bit < count:
         half = count // (2 * bit) // 2
@@ -481,7 +487,8 @@
                 leaving[n], *_ = lax.optimization_barrier((leaving[n], leaving[n - 1]))
         arrived = [swap(value, bit) for value in leaving]
         if bit == 1:
-            ready = add(held[0][half:], arrived[0][half:])
+            ready = add(held[0][half:], arrived[0][half - 1 :])
+            arrived[0] = jnp.concatenate([swap(apart, bit), arrived[0]], axis=0)
             hidden, ready = lax.optimization_barrier((hidden, ready))
             rest = down_next(hidden, down, down_own, chunks[len(held) :], order)
             held += rest[0::2]

time: 40.6 us -> 40.4 us (level)
    ppermute x18 -> x19, waiting for transfers between devices: 9.48 us -> 9.17 us  [swap(): return lax.ppermute(value, axis, [(i, i ^ bits) for i in range(count)])]
    ppermute x18 -> x19, starting transfers between devices: 16.9 us -> 17.1 us  [swap(): return lax.ppermute(value, axis, [(i, i ^ bits) for i in range(count)])]
  transfers between devices with their start and end apart: 18 -> 19, of which waited for: 8 -> 8; matrix products, arithmetic and copies ran while one was open for 1% -> 1% of each run, Pallas kernels for 30% -> 30%
where the time goes in v15:
time: 40.4 us; the launch traced here: 40.3 us
  starting transfers between devices  17.1 us (42%)
  Pallas kernels  13 us (32%)
  waiting for transfers between devices  9.17 us (23%)
  other arithmetic  0.99 us (2%)
    ppermute x19, starting transfers between devices, swap(): return lax.ppermute(value, axis, [(i, i ^ bits) for i in range(count)])  17.1 us
    ppermute x19, waiting for transfers between devices, swap(): return lax.ppermute(value, axis, [(i, i ^ bits) for i in range(count)])  9.17 us
    pallas_call x1, Pallas kernels, first_call(): pl.pallas_call(functools.partial(first_kernel, experts), in_specs=[HBM_SP...  8.19 us
    pallas_call x1, Pallas kernels, gate_up(): pl.pallas_call(functools.partial(gate_up_kernel, len(rows), 1024), in_spe...  2.67 us
    pallas_call x1, Pallas kernels, down_products(): pl.pallas_call(functools.partial(down_kernel, experts, chunks, order), in...  1 us
    convert_element_type x4, other arithmetic, total_of(): return sum((value.astype(F32) for value in values)).astype(BF16)  0.87 us
  transfers between devices with their start and end apart: 19, of which 8 were waited for; matrix products, arithmetic and copies ran while one was open for 1% of the time, Pallas kernels for 30%

profile of v15, /device:TPU:0, one launch (start us, length us, event | category | flops | bytes accessed | tf_op | source)
XLA Modules:
  0.0 40.3 jit_solution(18095585971324421456)
XLA Ops:
  0.0 3.0 %collective-permute-start = (bf16[32,7168]{1,0:T(8,128)(2,1)}, bf16[32,7168]{1,0:T(8,128)(2,1)S(1)}, u32[]{:S(2)}, u32[]{:S(2)}) collective-permute-start(bf16[32,7168]{1,0:T(8,128)(2,1)} %bitcast.34), channel_id=1, source_target_pairs={{0,8},{4,12},{8,0},{12,4},{1,9},{5,13},{9,1},{13,5},{2,10},{6,14},... | collective-permute-start | bytes 1376264 | tf_op jit(solution)/shard_map/ppermute | solution.py:41
  3.0 8.2 %shard_map.145 = (bf16[64,256]{1,0:T(8,128)(2,1)S(1)}, s32[8,128]{1,0:T(8,128)S(1)}, bf16[32,7168]{1,0:T(8,128)(2,1)S(1)}, bf16[64,256]{1,0:T(8,128)(2,1)S(1)}, ...) custom-call(s32[2,2,16]{2,1,0:T(2,128)} %bitcast.39, ...), custom_call_target="tpu_custom_call" | custom-call | bytes 23904256 | tf_op jit(solution)/shard_map/pallas_call | solution.py:163
  11.2 0.6 %collective-permute-start.2 = (bf16[64,256]{1,0:T(8,128)(2,1)S(1)}, bf16[64,256]{1,0:T(8,128)(2,1)S(1)}, u32[]{:S(2)}, u32[]{:S(2)}) collective-permute-start(bf16[64,256]{1,0:T(8,128)(2,1)S(1)} %get-tuple-element.46.refs_4_.refs_7_), channel_id=1, source_target_pairs={{0,4},{4,0},{8,12},{12,8},{1,5},{5,1},{9,13},{13,9},{2,6},{6,2},{1... | collective-permute-start | bytes 98312 | tf_op jit(solution)/shard_map/ppermute | solution.py:41
  11.7 0.1 collective-permute-start.3
  11.8 0.8 %collective-permute-done.2.refs_8_ = bf16[64,256]{1,0:T(8,128)(2,1)S(1)} collective-permute-done((bf16[64,256]{1,0:T(8,128)(2,1)S(1)}, bf16[64,256]{1,0:T(8,128)(2,1)S(1)}, u32[]{:S(2)}, u32[]{:S(2)}) %collective-permute-start.2) | collective-permute-done | bytes 32800 | tf_op jit(solution)/shard_map/ppermute | solution.py:41
  12.6 1.1 %collective-permute-done.refs_1_.refs_2_ = bf16[32,7168]{1,0:T(8,128)(2,1)S(1)} collective-permute-done((bf16[32,7168]{1,0:T(8,128)(2,1)}, bf16[32,7168]{1,0:T(8,128)(2,1)S(1)}, u32[]{:S(2)}, u32[]{:S(2)}) %collective-permute-start) | collective-permute-done | bytes 458784 | tf_op jit(solution)/shard_map/ppermute | solution.py:41
  13.7 0.5 %shard_map.146 = bf16[64,256]{1,0:T(8,128)(2,1)S(1)} custom-call(bf16[32,7168]{1,0:T(8,128)(2,1)S(1)} %get-tuple-element.47.refs_0_, bf16[32,7168]{1,0:T(8,128)(2,1)S(1)} %collective-permute-done.refs_1_.refs_2_, bf16[32,7168]{1,0:T(8,128)(2,1)S(1)} %get-tuple-element.49.refs_2_.refs_5_, bf16[32,7168]{1,0:T(8,128)(2,1)S(1)} %bitcast.27, ...), custom_call_target="tpu_custom_call" | custom-call | flops 58720256 | bytes 917504 | tf_op jit(solution)/shard_map/pallas_call | solution.py:225
  14.2 1.8 %collective-permute-start.5 = (bf16[64,256]{1,0:T(8,128)(2,1)S(1)}, bf16[64,256]{1,0:T(8,128)(2,1)S(1)}, u32[]{:S(2)}, u32[]{:S(2)}) collective-permute-start(bf16[64,256]{1,0:T(8,128)(2,1)S(1)} %shard_map.146), channel_id=1, source_target_pairs={{0,8},{4,12},{8,0},{12,4},{1,9},{5,13},{9,1},{13,5},{2,10},{6,14},... | collective-permute-start | bytes 98312 | tf_op jit(solution)/shard_map/ppermute | solution.py:41
  16.0 0.1 collective-permute-start.6
  16.1 2.7 %shard_map.147 = (bf16[128,128]{1,0:T(8,128)(2,1)S(1)}, f32[128,256]{1,0:T(8,128)S(1)}, f32[128,256]{1,0:T(8,128)S(1)}, f32[128,256]{1,0:T(8,128)S(1)}, f32[128,256]{1,0:T(8,128)S(1)}) custom-call(bf16[32,7168]{1,0:T(8,128)(2,1)S(1)} %get-tuple-element.47.refs_0_, bf16[32,7168]{1,0:T(8,128)(2,1)S(1)} %collective-permute-done.3.refs_1_, ...), custom_call_target="tpu_custom_call" | custom-call | flops 1879048192 | bytes 14680064 | tf_op jit(solution)/shard_map/pallas_call | solution.py:262
  18.8 0.6 %collective-permute-done.6.refs_10_ = bf16[64,256]{1,0:T(8,128)(2,1)S(1)} collective-permute-done((bf16[64,256]{1,0:T(8,128)(2,1)S(1)}, bf16[64,256]{1,0:T(8,128)(2,1)S(1)}, u32[]{:S(2)}, u32[]{:S(2)}) %collective-permute-start.6) | collective-permute-done | bytes 32800 | tf_op jit(solution)/shard_map/ppermute | solution.py:41
  19.3 1.0 %shard_map.148 = (bf16[128,256]{1,0:T(8,128)(2,1)S(1)}, bf16[128,256]{1,0:T(8,128)(2,1)S(1)}, f32[128,128]{1,0:T(8,128)S(1)}, bf16[2,1,32,1792]{3,2,1,0:T(8,128)...) custom-call(bf16[128,128]{1,0:T(8,128)(2,1)S(1)} %get-tuple-element., ...), custom_call_target="tpu_custom_call" | custom-call | flops 469762048 | tf_op jit(solution)/shard_map/pallas_call | solution.py:384
  20.3 0.2 collective-permute-start.7
  20.6 0.3 collective-permute-start.10
  20.9 0.2 collective-permute-start.15
  21.1 0.6 %collective-permute-done.7 = bf16[1,1,32,1792]{3,2,1,0:T(8,128)(2,1)S(1)} collective-permute-done((bf16[1,1,32,1792]{3,2,1,0:T(8,128)(2,1)S(1)}, bf16[1,1,32,1792]{3,2,1,0:T(8,128)(2,1)S(1)}, u32[]{:S(2)}, u32[]{:S(2)}) %collective-permute-start.7) | collective-permute-done | bytes 114720 | tf_op jit(solution)/shard_map/ppermute | solution.py:41
  21.8 1.2 %collective-permute-start.16 = (bf16[1,1,32,1792]{3,2,1,0:T(8,128)(2,1)S(1)}, bf16[1,1,32,1792]{3,2,1,0:T(8,128)(2,1)S(1)}, u32[]{:S(2)}, u32[]{:S(2)}) collective-permute-start(bf16[1,1,32,1792]{3,2,1,0:T(8,128)(2,1)S(1)} %add_convert_fusion.9), channel_id=1, source_target_pairs={{0,8},{4,12},{8,0},{12,4},{1,9},{5,13},{9,1},{13,5},{2,10},{6,14},... | collective-permute-start | bytes 344072 | tf_op jit(solution)/shard_map/ppermute | solution.py:41
  23.0 0.7 %shard_map.149 = (bf16[2,1,32,1792]{3,2,1,0:T(8,128)(2,1)S(1)}, bf16[2,1,32,1792]{3,2,1,0:T(8,128)(2,1)S(1)}, bf16[2,1,32,1792]{3,2,1,0:T(8,128)(2,1)S(1)}, bf16[2,1,32,1792]{3,2,1,0:T(8,128)(2,1)S(1)}) custom-call(bf16[128,256]{1,0:T(8,128)(2,1)S(1)} %get-tuple-element.72.hidden, bf16[128,256]{1,0:T(8,128)(2,1)S(1)} %get-tuple-element.73.hidden_shared, ...), custom_call_target="tpu_custom_call" | custom-call | flops 469762048 | tf_op jit(solution)/shard_map/pallas_call | solution.py:398
  23.7 0.1 collective-permute-start.8
  23.8 0.4 %collective-permute-start.9 = (bf16[2,1,32,1792]{3,2,1,0:T(8,128)(2,1)S(1)}, bf16[2,1,32,1792]{3,2,1,0:T(8,128)(2,1)S(1)}, u32[]{:S(2)}, u32[]{:S(2)}) collective-permute-start(bf16[2,1,32,1792]{3,2,1,0:T(8,128)(2,1)S(1)} %get-tuple-element.78), channel_id=1, source_target_pairs={{0,4},{4,0},{8,12},{12,8},{1,5},{5,1},{9,13},{13,9},{2,6},{6,2},{1... | collective-permute-start | bytes 688136 | tf_op jit(solution)/shard_map/ppermute | solution.py:41
  24.3 0.9 %collective-permute-start.14 = (bf16[1,1,32,1792]{3,2,1,0:T(8,128)(2,1)S(1)}, bf16[1,1,32,1792]{3,2,1,0:T(8,128)(2,1)S(1)}, u32[]{:S(2)}, u32[]{:S(2)}) collective-permute-start(bf16[1,1,32,1792]{3,2,1,0:T(8,128)(2,1)S(1)} %add_convert_fusion.5), channel_id=1, source_target_pairs={{0,8},{4,12},{8,0},{12,4},{1,9},{5,13},{9,1},{13,5},{2,10},{6,14},... | collective-permute-start | bytes 344072 | tf_op jit(solution)/shard_map/ppermute | solution.py:41
  25.2 1.8 %collective-permute-done.16 = bf16[1,1,32,1792]{3,2,1,0:T(8,128)(2,1)S(1)} collective-permute-done((bf16[1,1,32,1792]{3,2,1,0:T(8,128)(2,1)S(1)}, bf16[1,1,32,1792]{3,2,1,0:T(8,128)(2,1)S(1)}, u32[]{:S(2)}, u32[]{:S(2)}) %collective-permute-start.16) | collective-permute-done | bytes 114720 | tf_op jit(solution)/shard_map/ppermute | solution.py:41
  27.1 1.6 %collective-permute-start.17 = (bf16[32,1792]{1,0:T(8,128)(2,1)S(1)}, bf16[32,1792]{1,0:T(8,128)(2,1)S(1)}, u32[]{:S(2)}, u32[]{:S(2)}) collective-permute-start(bf16[32,1792]{1,0:T(8,128)(2,1)S(1)} %fusion.4), channel_id=1, source_target_pairs={{0,1},{1,0},{2,3},{3,2},{4,5},{5,4},{6,7},{7,6},{8,9},{9,8},{10,11... | collective-permute-start | bytes 344072 | tf_op jit(solution)/shard_map/ppermute | solution.py:41
  28.8 1.9 %collective-permute-start.12 = (bf16[1,1,32,1792]{3,2,1,0:T(8,128)(2,1)S(1)}, bf16[1,1,32,1792]{3,2,1,0:T(8,128)(2,1)S(1)}, u32[]{:S(2)}, u32[]{:S(2)}) collective-permute-start(bf16[1,1,32,1792]{3,2,1,0:T(8,128)(2,1)S(1)} %add_convert_fusion.6), channel_id=1, source_target_pairs={{0,8},{4,12},{8,0},{12,4},{1,9},{5,13},{9,1},{13,5},{2,10},{6,14},... | collective-permute-start | bytes 344072 | tf_op jit(solution)/shard_map/ppermute | solution.py:41
  30.7 0.3 collective-permute-start.11
  31.0 1.0 %collective-permute-done.17 = bf16[32,1792]{1,0:T(8,128)(2,1)S(1)} collective-permute-done((bf16[32,1792]{1,0:T(8,128)(2,1)S(1)}, bf16[32,1792]{1,0:T(8,128)(2,1)S(1)}, u32[]{:S(2)}, u32[]{:S(2)}) %collective-permute-start.17) | collective-permute-done | bytes 114720 | tf_op jit(solution)/shard_map/ppermute | solution.py:41
  32.0 0.1 fusion
  32.0 2.6 %collective-permute-start.18 = (bf16[32,1792]{1,0:T(8,128)(2,1)S(1)}, bf16[32,1792]{1,0:T(8,128)(2,1)S(1)}, u32[]{:S(2)}, u32[]{:S(2)}) collective-permute-start(bf16[32,1792]{1,0:T(8,128)(2,1)S(1)} %fusion), channel_id=1, source_target_pairs={{0,2},{1,3},{2,0},{3,1},{4,6},{5,7},{6,4},{7,5},{8,10},{9,11},{10,... | collective-permute-start | bytes 344072 | tf_op jit(solution)/shard_map/ppermute | solution.py:41
  34.7 1.6 %collective-permute-start.13 = (bf16[32,1792]{1,0:T(8,128)(2,1)S(1)}, bf16[32,1792]{1,0:T(8,128)(2,1)S(1)}, u32[]{:S(2)}, u32[]{:S(2)}) collective-permute-start(bf16[32,1792]{1,0:T(8,128)(2,1)S(1)} %fusion.3), channel_id=1, source_target_pairs={{0,1},{1,0},{2,3},{3,2},{4,5},{5,4},{6,7},{7,6},{8,9},{9,8},{10,11... | collective-permute-start | bytes 344072 | tf_op jit(solution)/shard_map/ppermute | solution.py:41
  36.4 1.6 %collective-permute-done.18 = bf16[32,1792]{1,0:T(8,128)(2,1)S(1)} collective-permute-done((bf16[32,1792]{1,0:T(8,128)(2,1)S(1)}, bf16[32,1792]{1,0:T(8,128)(2,1)S(1)}, u32[]{:S(2)}, u32[]{:S(2)}) %collective-permute-start.18) | collective-permute-done | bytes 114720 | tf_op jit(solution)/shard_map/ppermute | solution.py:41
  38.0 1.6 %collective-permute-done.13 = bf16[32,1792]{1,0:T(8,128)(2,1)S(1)} collective-permute-done((bf16[32,1792]{1,0:T(8,128)(2,1)S(1)}, bf16[32,1792]{1,0:T(8,128)(2,1)S(1)}, u32[]{:S(2)}, u32[]{:S(2)}) %collective-permute-start.13) | collective-permute-done | bytes 114720 | tf_op jit(solution)/shard_map/ppermute | solution.py:41
  39.6 0.7 %fusion.2 = bf16[32,1792]{1,0:T(8,128)(2,1)} fusion(bf16[32,1792]{1,0:T(8,128)(2,1)S(1)} %collective-permute-done.18, bf16[32,1792]{1,0:T(8,128)(2,1)S(1)} %collective-permute-done.13, bf16[1,1,32,1792]{3,2,1,0:T(8,128)(2,1)S(1)} %collective-permute-done.11, bf16[2,1,32,1792]{3,2,1,0:T(8,128)(2,1)S(1)} %collective-permute-done.8, ...), kind=kLoop, calls=%fused_computation.4 | loop fusion | flops 688128 | bytes 688128 | tf_op jit(solution)/shard_map/convert_element_type | solution.py:49
  (21 shorter events, 0.3 us)
Async XLA Ops:
  0.0 13.7 %collective-permute-start = (bf16[32,7168]{1,0:T(8,128)(2,1)}, bf16[32,7168]{1,0:T(8,128)(2,1)S(1)}, u32[]{:S(2)}, u32[]{:S(2)}) collective-permute-start(bf16[32,7168]{1,0:T(8,128)(2,1)} %bitcast.34), channel_id=1, source_target_pairs={{0,8},{4,12},{8,0},{12,4},{1,9},{5,13},{9,1},{13,5},{2,10},{6,14},... | collective-permute-start | bytes 1376264 | tf_op jit(solution)/shard_map/ppermute | solution.py:41
  3.0 10.7 %collective-permute-start.1 = (bf16[2,16,7168]{2,1,0:T(8,128)(2,1)}, bf16[2,16,7168]{2,1,0:T(8,128)(2,1)S(1)}, u32[]{:S(2)}, u32[]{:S(2)}) collective-permute-start(bf16[2,16,7168]{2,1,0:T(8,128)(2,1)} %param.25), channel_id=1, source_target_pairs={{0,4},{4,0},{8,12},{12,8},{1,5},{5,1},{9,13},{13,9},{2,6},{6,2},{1... | collective-permute-start | bytes 1376264 | tf_op jit(solution)/shard_map/ppermute | solution.py:41
  3.0 8.8 %copy-start = (bf16[2,16,7168]{2,1,0:T(8,128)(2,1)S(1)}, bf16[2,16,7168]{2,1,0:T(8,128)(2,1)}, u32[]{:S(2)}) copy-start(bf16[2,16,7168]{2,1,0:T(8,128)(2,1)} %param.15) | copy-start | bytes 1376260
  11.2 1.4 %collective-permute-start.2 = (bf16[64,256]{1,0:T(8,128)(2,1)S(1)}, bf16[64,256]{1,0:T(8,128)(2,1)S(1)}, u32[]{:S(2)}, u32[]{:S(2)}) collective-permute-start(bf16[64,256]{1,0:T(8,128)(2,1)S(1)} %get-tuple-element.46.refs_4_.refs_7_), channel_id=1, source_target_pairs={{0,4},{4,0},{8,12},{12,8},{1,5},{5,1},{9,13},{13,9},{2,6},{6,2},{1... | collective-permute-start | bytes 98312 | tf_op jit(solution)/shard_map/ppermute | solution.py:41
  11.7 4.3 %collective-permute-start.3 = (bf16[32,7168]{1,0:T(8,128)(2,1)S(1)}, bf16[32,7168]{1,0:T(8,128)(2,1)S(1)}, u32[]{:S(2)}, u32[]{:S(2)}) collective-permute-start(bf16[32,7168]{1,0:T(8,128)(2,1)S(1)} %bitcast.36), channel_id=1, source_target_pairs={{0,4},{4,0},{8,12},{12,8},{1,5},{5,1},{9,13},{13,9},{2,6},{6,2},{1... | collective-permute-start | bytes 1376264 | tf_op jit(solution)/shard_map/ppermute | solution.py:41
  14.2 1.9 %collective-permute-start.4 = (bf16[32,7168]{1,0:T(8,128)(2,1)S(1)}, bf16[32,7168]{1,0:T(8,128)(2,1)S(1)}, u32[]{:S(2)}, u32[]{:S(2)}) collective-permute-start(bf16[32,7168]{1,0:T(8,128)(2,1)S(1)} %collective-permute-done.refs_1_.refs_2_), channel_id=1, source_target_pairs={{0,4},{4,0},{8,12},{12,8},{1,5},{5,1},{9,13},{13,9},{2,6},{6,2},{1... | collective-permute-start | bytes 1376264 | tf_op jit(solution)/shard_map/ppermute | solution.py:41
  14.2 4.6 %collective-permute-start.5 = (bf16[64,256]{1,0:T(8,128)(2,1)S(1)}, bf16[64,256]{1,0:T(8,128)(2,1)S(1)}, u32[]{:S(2)}, u32[]{:S(2)}) collective-permute-start(bf16[64,256]{1,0:T(8,128)(2,1)S(1)} %shard_map.146), channel_id=1, source_target_pairs={{0,8},{4,12},{8,0},{12,4},{1,9},{5,13},{9,1},{13,5},{2,10},{6,14},... | collective-permute-start | bytes 98312 | tf_op jit(solution)/shard_map/ppermute | solution.py:41
  16.0 3.3 %collective-permute-start.6 = (bf16[64,256]{1,0:T(8,128)(2,1)S(1)}, bf16[64,256]{1,0:T(8,128)(2,1)S(1)}, u32[]{:S(2)}, u32[]{:S(2)}) collective-permute-start(bf16[64,256]{1,0:T(8,128)(2,1)S(1)} %shard_map.146), channel_id=1, source_target_pairs={{0,12},{4,8},{8,4},{12,0},{1,13},{5,9},{9,5},{13,1},{2,14},{6,10},... | collective-permute-start | bytes 98312 | tf_op jit(solution)/shard_map/ppermute | solution.py:41
  20.3 1.4 %collective-permute-start.7 = (bf16[1,1,32,1792]{3,2,1,0:T(8,128)(2,1)S(1)}, bf16[1,1,32,1792]{3,2,1,0:T(8,128)(2,1)S(1)}, u32[]{:S(2)}, u32[]{:S(2)}) collective-permute-start(bf16[1,1,32,1792]{3,2,1,0:T(8,128)(2,1)S(1)} %get-tuple-element.71), channel_id=1, source_target_pairs={{0,4},{4,0},{8,12},{12,8},{1,5},{5,1},{9,13},{13,9},{2,6},{6,2},{1... | collective-permute-start | bytes 344072 | tf_op jit(solution)/shard_map/ppermute | solution.py:41
  20.6 3.7 %collective-permute-start.10 = (bf16[2,1,32,1792]{3,2,1,0:T(8,128)(2,1)S(1)}, bf16[2,1,32,1792]{3,2,1,0:T(8,128)(2,1)S(1)}, u32[]{:S(2)}, u32[]{:S(2)}) collective-permute-start(bf16[2,1,32,1792]{3,2,1,0:T(8,128)(2,1)S(1)} %get-tuple-element.80), channel_id=1, source_target_pairs={{0,4},{4,0},{8,12},{12,8},{1,5},{5,1},{9,13},{13,9},{2,6},{6,2},{1... | collective-permute-start | bytes 688136 | tf_op jit(solution)/shard_map/ppermute | solution.py:41
  20.9 4.3 %collective-permute-start.15 = (bf16[1,1,32,1792]{3,2,1,0:T(8,128)(2,1)S(1)}, bf16[1,1,32,1792]{3,2,1,0:T(8,128)(2,1)S(1)}, u32[]{:S(2)}, u32[]{:S(2)}) collective-permute-start(bf16[1,1,32,1792]{3,2,1,0:T(8,128)(2,1)S(1)} %get-tuple-element.84), channel_id=1, source_target_pairs={{0,4},{4,0},{8,12},{12,8},{1,5},{5,1},{9,13},{13,9},{2,6},{6,2},{1... | collective-permute-start | bytes 344072 | tf_op jit(solution)/shard_map/ppermute | solution.py:41
  21.8 5.3 %collective-permute-start.16 = (bf16[1,1,32,1792]{3,2,1,0:T(8,128)(2,1)S(1)}, bf16[1,1,32,1792]{3,2,1,0:T(8,128)(2,1)S(1)}, u32[]{:S(2)}, u32[]{:S(2)}) collective-permute-start(bf16[1,1,32,1792]{3,2,1,0:T(8,128)(2,1)S(1)} %add_convert_fusion.9), channel_id=1, source_target_pairs={{0,8},{4,12},{8,0},{12,4},{1,9},{5,13},{9,1},{13,5},{2,10},{6,14},... | collective-permute-start | bytes 344072 | tf_op jit(solution)/shard_map/ppermute | solution.py:41
  23.7 7.0 %collective-permute-start.8 = (bf16[2,1,32,1792]{3,2,1,0:T(8,128)(2,1)S(1)}, bf16[2,1,32,1792]{3,2,1,0:T(8,128)(2,1)S(1)}, u32[]{:S(2)}, u32[]{:S(2)}) collective-permute-start(bf16[2,1,32,1792]{3,2,1,0:T(8,128)(2,1)S(1)} %get-tuple-element.76), channel_id=1, source_target_pairs={{0,4},{4,0},{8,12},{12,8},{1,5},{5,1},{9,13},{13,9},{2,6},{6,2},{1... | collective-permute-start | bytes 688136 | tf_op jit(solution)/shard_map/ppermute | solution.py:41
  23.8 4.9 %collective-permute-start.9 = (bf16[2,1,32,1792]{3,2,1,0:T(8,128)(2,1)S(1)}, bf16[2,1,32,1792]{3,2,1,0:T(8,128)(2,1)S(1)}, u32[]{:S(2)}, u32[]{:S(2)}) collective-permute-start(bf16[2,1,32,1792]{3,2,1,0:T(8,128)(2,1)S(1)} %get-tuple-element.78), channel_id=1, source_target_pairs={{0,4},{4,0},{8,12},{12,8},{1,5},{5,1},{9,13},{13,9},{2,6},{6,2},{1... | collective-permute-start | bytes 688136 | tf_op jit(solution)/shard_map/ppermute | solution.py:41
  24.3 6.7 %collective-permute-start.14 = (bf16[1,1,32,1792]{3,2,1,0:T(8,128)(2,1)S(1)}, bf16[1,1,32,1792]{3,2,1,0:T(8,128)(2,1)S(1)}, u32[]{:S(2)}, u32[]{:S(2)}) collective-permute-start(bf16[1,1,32,1792]{3,2,1,0:T(8,128)(2,1)S(1)} %add_convert_fusion.5), channel_id=1, source_target_pairs={{0,8},{4,12},{8,0},{12,4},{1,9},{5,13},{9,1},{13,5},{2,10},{6,14},... | collective-permute-start | bytes 344072 | tf_op jit(solution)/shard_map/ppermute | solution.py:41
  27.1 4.9 %collective-permute-start.17 = (bf16[32,1792]{1,0:T(8,128)(2,1)S(1)}, bf16[32,1792]{1,0:T(8,128)(2,1)S(1)}, u32[]{:S(2)}, u32[]{:S(2)}) collective-permute-start(bf16[32,1792]{1,0:T(8,128)(2,1)S(1)} %fusion.4), channel_id=1, source_target_pairs={{0,1},{1,0},{2,3},{3,2},{4,5},{5,4},{6,7},{7,6},{8,9},{9,8},{10,11... | collective-permute-start | bytes 344072 | tf_op jit(solution)/shard_map/ppermute | solution.py:41
  28.8 5.9 %collective-permute-start.12 = (bf16[1,1,32,1792]{3,2,1,0:T(8,128)(2,1)S(1)}, bf16[1,1,32,1792]{3,2,1,0:T(8,128)(2,1)S(1)}, u32[]{:S(2)}, u32[]{:S(2)}) collective-permute-start(bf16[1,1,32,1792]{3,2,1,0:T(8,128)(2,1)S(1)} %add_convert_fusion.6), channel_id=1, source_target_pairs={{0,8},{4,12},{8,0},{12,4},{1,9},{5,13},{9,1},{13,5},{2,10},{6,14},... | collective-permute-start | bytes 344072 | tf_op jit(solution)/shard_map/ppermute | solution.py:41
  30.7 5.7 %collective-permute-start.11 = (bf16[1,1,32,1792]{3,2,1,0:T(8,128)(2,1)S(1)}, bf16[1,1,32,1792]{3,2,1,0:T(8,128)(2,1)S(1)}, u32[]{:S(2)}, u32[]{:S(2)}) collective-permute-start(bf16[1,1,32,1792]{3,2,1,0:T(8,128)(2,1)S(1)} %add_convert_fusion.7), channel_id=1, source_target_pairs={{0,8},{4,12},{8,0},{12,4},{1,9},{5,13},{9,1},{13,5},{2,10},{6,14},... | collective-permute-start | bytes 344072 | tf_op jit(solution)/shard_map/ppermute | solution.py:41
  32.0 6.0 %collective-permute-start.18 = (bf16[32,1792]{1,0:T(8,128)(2,1)S(1)}, bf16[32,1792]{1,0:T(8,128)(2,1)S(1)}, u32[]{:S(2)}, u32[]{:S(2)}) collective-permute-start(bf16[32,1792]{1,0:T(8,128)(2,1)S(1)} %fusion), channel_id=1, source_target_pairs={{0,2},{1,3},{2,0},{3,1},{4,6},{5,7},{6,4},{7,5},{8,10},{9,11},{10,... | collective-permute-start | bytes 344072 | tf_op jit(solution)/shard_map/ppermute | solution.py:41
  34.7 4.9 %collective-permute-start.13 = (bf16[32,1792]{1,0:T(8,128)(2,1)S(1)}, bf16[32,1792]{1,0:T(8,128)(2,1)S(1)}, u32[]{:S(2)}, u32[]{:S(2)}) collective-permute-start(bf16[32,1792]{1,0:T(8,128)(2,1)S(1)} %fusion.3), channel_id=1, source_target_pairs={{0,1},{1,0},{2,3},{3,2},{4,5},{5,4},{6,7},{7,6},{8,9},{9,8},{10,11... | collective-permute-start | bytes 344072 | tf_op jit(solution)/shard_map/ppermute | solution.py:41
